TPU v7x, 32 devices: a whole 2x2x4 slice. The times are simulated.
32 devices in a mesh: grp: 2 (over y), sp: 4 (over z), fr: 2 (over x), dr: 2 (over core).
Axes of the slice: x: 2, y: 2, z: 4, core: 2. Of those that a mesh axis runs over, the one named last changes fastest.
Arguments:
- grid_spec: float32 [36, 36, 32, 128], P('fr', 'dr', ('grp', 'sp')), parts along dimension 2, may hold values from 0 to 2
- mesh_spec: float32 [36, 36, 4096], P('fr', 'dr', ('grp', 'sp')), parts along dimension 2, may hold values from 0 to 2
- grid_sea: int32 [32, 128], P(('grp', 'sp')), parts along dimension 0, may hold values 0 or 1
- grid_speed: float32 [32, 128], P(('grp', 'sp')), parts along dimension 0, may hold values from 0.5 to 1
- nb_index: int32 [4, 4096], P(None, ('grp', 'sp')), parts along dimension 1, may hold values from 0 to 767, as said below
- nb_angle: float32 [4, 4096], P(None, ('grp', 'sp')), parts along dimension 1, may hold values from -3.140625 to 3.140625
- nb_coef: float32 [4, 4096], P(None, ('grp', 'sp')), parts along dimension 1, may hold values from 0.05 to 0.35
- halo_list: int32 [2, 1024], P(None, ('grp', 'sp')), parts along dimension 1, may hold values from 0 to 511
- w_in: bfloat16 [36, 36, 256], P('fr', 'dr'), may hold values from -0.15625 to 0.15625
- w_out: bfloat16 [256, 36, 36], P(None, 'fr', 'dr'), may hold values from -0.375 to 0.375
- g2m_index: int32 [4, 8, 4, 128], P(None, ('grp', 'sp')), parts along dimension 1, may hold values from 0 to 511
- g2m_weight: float32 [4, 8, 4, 128], P(None, ('grp', 'sp')), parts along dimension 1, may hold values from 0.05 to 0.3
- g2m_count: int32 [8, 4], P(('grp', 'sp')), parts along dimension 0, may hold values from 0 to 128, as said below
- g2m_target: int32 [8, 4, 128], P(('grp', 'sp')), parts along dimension 0, may hold values from 0 to 511
- m2g_index: int32 [3, 8, 4, 128], P(None, ('grp', 'sp')), parts along dimension 1, may hold values from 0 to 511
- m2g_weight: float32 [3, 8, 4, 128], P(None, ('grp', 'sp')), parts along dimension 1, may hold values from 0.05 to 0.4
- m2g_count: int32 [8, 4], P(('grp', 'sp')), parts along dimension 0, may hold values from 0 to 128, as said below
- m2g_target: int32 [8, 4, 128], P(('grp', 'sp')), parts along dimension 0, may hold values from 0 to 511
Outputs:
- grid_out: float32 [36, 36, 32, 128], P('fr', 'dr', ('grp', 'sp')), parts along dimension 2
- mesh_out: float32 [36, 36, 4096], P('fr', 'dr', ('grp', 'sp')), parts along dimension 2
There are 2 independent parts, one for each index of `grp`. A program takes and returns all parts, laid end to end along the dimension named above; an argument that names none is the same for every part. Nothing has to cross between parts.
Inputs may be any that keep to these rules, and one draw needn't show every extreme that they name: `nb_index`: each entry is a position in its sp index's extended list: below 512 an own node, 512 + i the i-th node from the next lower index, 640 + i the i-th from the next higher index. `g2m_count`: every sender has some receiver with all 128 slots live. `m2g_count`: every sender has some receiver with all 128 slots live.
All inputs are finite; a program needn't handle non-finite values. No bound on the sum of `grid_sea` on one device may be relied on, other than what follows from the above.
Results may differ from a plain program's by a relative error of at most 0.0015.
Values may be sent and summed in bfloat16 or wider, within the bound.
No kernel may reach another device: no remote copies, remote signals or barrier semaphores. Data moves between devices by JAX's collectives and lax.ppermute only.
A program may use at most 64 MiB of HBM per device.

v0:
```python
import jax
import jax.numpy as jnp
from jax import lax
from jax.sharding import PartitionSpec as P

ND = 36
NSUB = 2


DT_STEP = 0.1
BLEND_RATE = 0.5
EXACT = lax.Precision.HIGHEST


def from_behind(array, axis, by):
    length = lax.axis_size(axis)
    pairs = [(i, i + by) for i in range(length) if 0 <= i + by < length]
    return lax.ppermute(array, axis, pairs)


def with_halo(array, sides, width):
    for axis, dim in sides:
        size, length = (lax.axis_size(axis), array.shape[dim])
        up = [(i, (i + 1) % size) for i in range(size - 1)]
        down = [(j, i) for i, j in up]
        last = lax.slice_in_dim(array, length - width, length, axis=dim)
        leading = lax.slice_in_dim(array, 0, width, axis=dim)
        before = lax.ppermute(last, axis, up)
        after = lax.ppermute(leading, axis, down)
        array = jnp.concatenate([before, array, after], axis=dim)
    return array


def upwind(field, lower_x, upper_x, sea_mask, grid_speed, group_speed, headings):
    along_x = (
        group_speed[:, None, None, None]
        * jnp.cos(headings)[None, :, None, None]
        * grid_speed[None, None]
    )
    along_y = (
        group_speed[:, None, None, None]
        * jnp.sin(headings)[None, :, None, None]
        * grid_speed[None, None]
    )
    padded_y = jnp.pad(field, ((0, 0), (0, 0), (0, 0), (1, 1)))
    lower_y = padded_y[:, :, :, :-2]
    upper_y = padded_y[:, :, :, 2:]
    moved = (
        field
        - jnp.maximum(along_x, 0.0) * (field - lower_x)
        - jnp.maximum(-along_x, 0.0) * (field - upper_x)
    )
    moved = (
        moved
        - jnp.maximum(along_y, 0.0) * (field - lower_y)
        - jnp.maximum(-along_y, 0.0) * (field - upper_y)
    )
    return moved * sea_mask


def one_hot_rows(positions, length):
    return (jnp.arange(length)[:, None] == positions[None, :]).astype(jnp.float32)


def pick_columns(source, positions):
    selector = one_hot_rows(positions, source.shape[2])
    return jnp.einsum("fdp,pn->fdn", source, selector, precision=EXACT)


def mesh_step(mesh, nb_index, nb_angle, nb_coef, halo_list, group_speed, headings):
    to_lower = pick_columns(mesh, halo_list[0])
    to_upper = pick_columns(mesh, halo_list[1])
    from_lower = from_behind(to_upper.astype(jnp.bfloat16), "sp", 1).astype(to_upper.dtype)
    from_upper = from_behind(to_lower.astype(jnp.bfloat16), "sp", -1).astype(to_lower.dtype)
    extended = jnp.concatenate([mesh, from_lower, from_upper], axis=2)
    result = mesh
    for k in range(nb_index.shape[0]):
        nearby = pick_columns(extended, nb_index[k])
        weight = (
            group_speed[:, None, None]
            * nb_coef[k]
            * jnp.maximum(-jnp.cos(headings[:, None] - nb_angle[k]), 0.0)
        )
        result = result + weight * (nearby - mesh)
    return result


def pack_slots(source, index, weight, count):
    freq_count, dir_count, length = source.shape
    peers, slots = (index.shape[2], index.shape[3])
    live = (jnp.arange(slots)[None, :] < count[0][:, None]).astype(jnp.float32)
    scaled = weight[:, 0] * live[None]
    mixing = jnp.zeros((length, peers * slots), jnp.float32)
    for j in range(index.shape[0]):
        mixing = (
            mixing + one_hot_rows(index[j, 0].reshape(-1), length) * scaled[j].reshape(-1)[None, :]
        )
    values = jnp.einsum("fdp,ps->fds", source, mixing, precision=EXACT).reshape(
        freq_count, dir_count, peers, slots
    )
    return (values, jnp.sum(scaled, axis=0)[None, None])


def land_slots(values, weight_sums, target, state):
    freq_count, dir_count, length = state.shape
    spots = target[0].reshape(-1)
    landing = (spots[:, None] == jnp.arange(length)[None, :]).astype(jnp.float32)
    gathered_sum = jnp.einsum(
        "fds,sl->fdl", values.reshape(freq_count, dir_count, -1), landing, precision=EXACT
    )
    coverage = jnp.dot(weight_sums.reshape(-1), landing, precision=EXACT)
    return state + BLEND_RATE * (gathered_sum - coverage * state) / (1.0 + coverage)


def per_device(
    grid_spec,
    mesh_spec,
    grid_sea,
    grid_speed,
    nb_index,
    nb_angle,
    nb_coef,
    halo_list,
    w_in,
    w_out,
    g2m_index,
    g2m_weight,
    g2m_count,
    g2m_target,
    m2g_index,
    m2g_weight,
    m2g_count,
    m2g_target,
):
    band_freqs, band_dirs, tile_rows, tile_cols = grid_spec.shape
    grid_points = tile_rows * tile_cols
    freq_index = lax.axis_index("fr") * band_freqs + jnp.arange(band_freqs)
    dir_index = lax.axis_index("dr") * band_dirs + jnp.arange(band_dirs)
    group_speed = 0.7 * jnp.power(1.1, -freq_index.astype(jnp.float32))
    headings = 2.0 * jnp.pi * (dir_index.astype(jnp.float32) + 0.5) / ND
    sea_mask = grid_sea.astype(jnp.float32)
    grid = grid_spec
    mesh = mesh_spec
    for substep in range(NSUB):
        padded_x = with_halo(grid, (("sp", 2),), 1)
        grid = upwind(
            grid,
            padded_x[:, :, :-2],
            padded_x[:, :, 2:],
            sea_mask,
            grid_speed,
            group_speed,
            headings,
        )
        mesh = mesh_step(mesh, nb_index, nb_angle, nb_coef, halo_list, group_speed, headings)
        features = jnp.concatenate(
            [grid.reshape(band_freqs, band_dirs, grid_points), mesh], axis=2
        ).astype(jnp.bfloat16)
        summed = lax.psum_scatter(
            jnp.einsum("fdp,fdh->ph", features, w_in, preferred_element_type=jnp.float32).astype(
                jnp.bfloat16
            ),
            ("fr", "dr"),
            scatter_dimension=0,
            tiled=True,
        ).astype(jnp.float32)
        hidden = jax.nn.silu(summed).astype(jnp.bfloat16)
        transfer = jnp.einsum(
            "ph,hfd->fdp",
            lax.all_gather(hidden, ("fr", "dr"), axis=0, tiled=True),
            w_out,
            preferred_element_type=jnp.float32,
        ).astype(jnp.bfloat16)
        grid = grid + DT_STEP * transfer[:, :, :grid_points].astype(jnp.float32).reshape(grid.shape)
        mesh = mesh + DT_STEP * transfer[:, :, grid_points:].astype(jnp.float32)
    grid_flat = grid.reshape(band_freqs, band_dirs, grid_points)
    grid_values, grid_sums = pack_slots(grid_flat, g2m_index, g2m_weight, g2m_count)
    mesh_values, mesh_sums = pack_slots(mesh, m2g_index, m2g_weight, m2g_count)
    got_grid, got_grid_sums, got_mesh, got_mesh_sums = (
        lax.all_to_all(
            grid_values.astype(jnp.bfloat16), "sp", split_axis=2, concat_axis=2, tiled=True
        ).astype(grid_values.dtype),
        lax.all_to_all(
            grid_sums.astype(jnp.bfloat16), "sp", split_axis=2, concat_axis=2, tiled=True
        ).astype(grid_sums.dtype),
        lax.all_to_all(
            mesh_values.astype(jnp.bfloat16), "sp", split_axis=2, concat_axis=2, tiled=True
        ).astype(mesh_values.dtype),
        lax.all_to_all(
            mesh_sums.astype(jnp.bfloat16), "sp", split_axis=2, concat_axis=2, tiled=True
        ).astype(mesh_sums.dtype),
    )
    mesh_out = land_slots(got_grid, got_grid_sums, g2m_target, mesh)
    grid_out = (
        land_slots(got_mesh, got_mesh_sums, m2g_target, grid_flat).reshape(grid.shape) * sea_mask
    )
    return (grid_out, mesh_out)


def solution(mesh):
    return jax.shard_map(
        per_device,
        mesh=mesh,
        in_specs=(
            P("fr", "dr", ("grp", "sp"), None),
            P("fr", "dr", ("grp", "sp")),
            P(("grp", "sp"), None),
            P(("grp", "sp"), None),
            P(None, ("grp", "sp")),
            P(None, ("grp", "sp")),
            P(None, ("grp", "sp")),
            P(None, ("grp", "sp")),
            P("fr", "dr", None),
            P(None, "fr", "dr"),
            P(None, ("grp", "sp"), None, None),
            P(None, ("grp", "sp"), None, None),
            P(("grp", "sp"), None),
            P(("grp", "sp"), None, None),
            P(None, ("grp", "sp"), None, None),
            P(None, ("grp", "sp"), None, None),
            P(("grp", "sp"), None),
            P(("grp", "sp"), None, None),
        ),
        out_specs=(P("fr", "dr", ("grp", "sp"), None), P("fr", "dr", ("grp", "sp"))),
        check_vma=False,
    )
```

profile of v0, /device:TPU:0, one launch (start us, length us, event | category | flops | bytes accessed | tf_op | source)
XLA Modules:
  0.0 173.4 jit_solution(9250501268792892361)
XLA Ops:
  7.2 1.3 copy.53
  8.5 1.3 collective-permute-start.1
  9.8 5.6 %collective-permute-start = (f32[18,18,1,128]{3,1,2,0:T(8,128)S(1)}, f32[18,18,1,128]{3,1,2,0:T(8,128)S(1)}, u32[]{:S(2)}, u32[]{:S(2)}) collective-permute-start(f32[18,18,1,128]{3,1,2,0:T(8,128)S(1)} %get-tuple-element.18), channel_id=1, source_target_pairs={{0,4},{4,8},{8,12},{1,5},{5,9},{9,13},{2,6},{6,10},{10,14},{3,7},{... | collective-permute-start | bytes 497672 | tf_op jit(solution)/shard_map/ppermute | solution.py:28
  15.5 0.6 fusion.107
  16.1 1.3 collective-permute-start.3
  17.4 1.2 fusion.106
  18.6 4.5 %collective-permute-start.2 = (bf16[18,18,128]{2,1,0:T(8,128)(2,1)}, bf16[18,18,128]{2,1,0:T(8,128)(2,1)S(1)}, u32[]{:S(2)}, u32[]{:S(2)}) collective-permute-start(bf16[18,18,128]{2,1,0:T(8,128)(2,1)} %fusion.106), channel_id=1, source_target_pairs={{0,4},{4,8},{8,12},{1,5},{5,9},{9,13},{2,6},{6,10},{10,14},{3,7},{... | collective-permute-start | bytes 248840 | tf_op jit(solution)/shard_map/ppermute | solution.py:18
  23.2 0.6 copy.67
  23.8 4.3 %all-to-all-start.1 = ((bf16[1,1,4,128]{3,1,0,2:T(2,128)(2,1)}), bf16[1,1,4,128]{3,1,0,2:T(2,128)(2,1)}, u32[]{:S(2)}, u32[]{:S(2)}) async-start(bf16[1,1,4,128]{3,1,0,2:T(2,128)(2,1)} %copy.67), calls=%async_computation.3 | async-start | bytes 4096 | tf_op jit(solution)/shard_map/all_to_all | solution.py:189
  28.5 0.7 negate_maximum_fusion
  29.4 1.4 fusion.81
  30.8 1.4 fusion.66
  32.3 1.4 fusion.48
  33.8 2.4 %fusion.239 = (bf16[18,18,512]{2,1,0:T(8,128)(2,1)S(1)}, f32[18,18,512]{2,1,0:T(8,128)}) fusion(f32[18,18,512]{2,1,0:T(8,128)S(1)} %fusion.48, f32[18,18,512]{2,1,0:T(8,128)S(1)} %copy-done.1, s32[512]{0:T(512)S(1)} %bitcast.194, f32[18,18,128]{2,1,0:T(8,128)S(1)} %convert_element_type.189, f32[18,18,128]{2,1,0:T(8,128)S(1)} %convert_element_type.186, ...), kind=kOutput, calls=%fused_computation.263 | convolution fusion | flops 1530544128 | bytes 2729984 | tf_op jit(solution)/shard_map/fdp,pn->fdn/dot_general | solution.py:67
  36.2 0.9 fusion.232
  37.4 0.6 copy-done.45
  38.0 1.3 fusion.100
  39.5 0.6 slice_bitcast_fusion.6
  40.1 0.6 fusion.228
  40.7 0.6 slice_bitcast_fusion.3
  41.3 0.6 slice_bitcast_fusion.10
  41.9 20.8 %reduce-scatter.3.cloned.1.call-done = bf16[256,256]{1,0:T(8,128)(2,1)} async-done(((bf16[1024,256]{1,0:T(8,128)(2,1)}), bf16[256,256]{1,0:T(8,128)(2,1)}) %reduce-scatter.3.cloned.1.call-update) | async-done | bytes 131088 | tf_op jit(solution)/shard_map/reduce_scatter | solution.py:159
  62.6 1.0 fusion.194
  63.6 7.0 %all_gather.6 = bf16[1024,256]{1,0:T(8,128)(2,1)S(1)} all-gather(bf16[256,256]{1,0:T(8,128)(2,1)S(1)} %fusion.194), channel_id=1, replica_groups=mesh['grp'=2,'sp'=4,'fr'=2,'dr'=2] {'fr','dr'}, dimensions={0}, use_global_device_ids=true | all-gather | bytes 655360 | tf_op jit(solution)/shard_map/all_gather | solution.py:170
  70.6 0.4 fusion.22
  71.0 0.7 copy-done.2
  72.0 1.2 convolution_convert_fusion.4
  73.2 1.2 convolution_convert_fusion.5
  74.7 1.3 collective-permute-start.7
  76.0 4.6 %collective-permute-start.6 = (bf16[18,18,128]{2,1,0:T(8,128)(2,1)}, bf16[18,18,128]{2,1,0:T(8,128)(2,1)S(1)}, u32[]{:S(2)}, u32[]{:S(2)}) collective-permute-start(bf16[18,18,128]{2,1,0:T(8,128)(2,1)} %convolution_convert_fusion.5), channel_id=1, source_target_pairs={{0,4},{4,8},{8,12},{1,5},{5,9},{9,13},{2,6},{6,10},{10,14},{3,7},{... | collective-permute-start | bytes 248840 | tf_op jit(solution)/shard_map/ppermute | solution.py:18
  80.7 1.3 collective-permute-start.5
  82.0 4.6 %collective-permute-start.4 = (f32[18,18,1,128]{3,1,2,0:T(8,128)S(1)}, f32[18,18,1,128]{3,1,2,0:T(8,128)S(1)}, u32[]{:S(2)}, u32[]{:S(2)}) collective-permute-start(f32[18,18,1,128]{3,1,2,0:T(8,128)S(1)} %get-tuple-element.16), channel_id=1, source_target_pairs={{0,4},{4,8},{8,12},{1,5},{5,9},{9,13},{2,6},{6,10},{10,14},{3,7},{... | collective-permute-start | bytes 497672 | tf_op jit(solution)/shard_map/ppermute | solution.py:28
  86.7 1.4 fusion.72
  88.2 1.5 fusion.93
  89.7 1.4 fusion.57
  91.2 2.4 %fusion.240 = (bf16[18,18,512]{2,1,0:T(8,128)(2,1)S(1)}, f32[18,18,512]{2,1,0:T(8,128)}) fusion(f32[18,18,512]{2,1,0:T(8,128)S(1)} %fusion.57, f32[18,18,512]{2,1,0:T(8,128)S(1)} %get-tuple-element.14, s32[512]{0:T(512)S(1)} %bitcast.195, f32[18,18,128]{2,1,0:T(8,128)S(1)} %convert_element_type.200, f32[18,18,128]{2,1,0:T(8,128)S(1)} %convert_element_type.198, ...), kind=kOutput, calls=%fused_computation.264 | convolution fusion | flops 1530544128 | bytes 2729984 | tf_op jit(solution)/shard_map/fdp,pn->fdn/dot_general | solution.py:67
  93.6 0.8 fusion.230
  94.7 0.6 copy-done.46
  95.4 1.3 fusion.101
  96.7 0.6 slice_bitcast_fusion.13
  97.3 0.6 copy.71
  97.9 3.7 %all-to-all-start.3 = ((bf16[1,1,4,128]{3,1,0,2:T(2,128)(2,1)}), bf16[1,1,4,128]{3,1,0,2:T(2,128)(2,1)S(1)}, u32[]{:S(2)}, u32[]{:S(2)}) async-start(bf16[1,1,4,128]{3,1,0,2:T(2,128)(2,1)} %copy.71), calls=%async_computation.5 | async-start | bytes 4096 | tf_op jit(solution)/shard_map/all_to_all | solution.py:183
  101.6 1.0 fusion.119
  102.6 0.6 broadcast_add_fusion.1
  103.2 3.9 %all-to-all-done.3 = bf16[1,1,4,128]{3,1,0,2:T(2,128)(2,1)S(1)} async-done(((bf16[1,1,4,128]{3,1,0,2:T(2,128)(2,1)}), bf16[1,1,4,128]{3,1,0,2:T(2,128)(2,1)S(1)}, u32[]{:S(2)}, u32[]{:S(2)}) %all-to-all-start.3) | async-done | bytes 1056 | tf_op jit(solution)/shard_map/all_to_all | solution.py:183
  107.1 0.3 fusion.110
  107.5 10.5 %reduce-scatter.5.cloned.1.call-done = bf16[256,256]{1,0:T(8,128)(2,1)} async-done(((bf16[1024,256]{1,0:T(8,128)(2,1)}), bf16[256,256]{1,0:T(8,128)(2,1)}) %reduce-scatter.5.cloned.1.call-update) | async-done | bytes 131088 | tf_op jit(solution)/shard_map/reduce_scatter | solution.py:159
  118.0 1.0 fusion.198
  118.9 7.0 %all_gather.7 = bf16[1024,256]{1,0:T(8,128)(2,1)S(1)} all-gather(bf16[256,256]{1,0:T(8,128)(2,1)S(1)} %fusion.198), channel_id=1, replica_groups=mesh['grp'=2,'sp'=4,'fr'=2,'dr'=2] {'fr','dr'}, dimensions={0}, use_global_device_ids=true | all-gather | bytes 655360 | tf_op jit(solution)/shard_map/all_gather | solution.py:170
  126.0 0.4 fusion.23
  126.7 3.2 %convolution_convert_fusion.3 = bf16[18,18,512]{2,1,0:T(8,128)(2,1)S(1)} fusion(f32[18,18,512]{2,1,0:T(8,128)} %get-tuple-element.61, f32[512]{0:T(512)} %get-tuple-element.44, s32[512]{0:T(512)} %get-tuple-element.41, f32[512]{0:T(512)} %get-tuple-element.45, s32[512]{0:T(512)} %get-tuple-element.42, f32[512]{0:T(512)} %get-tuple-element.43, ...), kind=kOutput, calls=%fused_computation.67 | convolution fusion | flops 1021976576 | bytes 1449984 | tf_op jit(solution)/shard_map/fdp,ps->fds/dot_general | solution.py:98
  130.1 0.8 copy.65
  130.9 4.6 %all-to-all-start = ((bf16[18,18,4,128]{3,1,0,2:T(8,128)(2,1)}), bf16[18,18,4,128]{3,1,0,2:T(8,128)(2,1)}, u32[]{:S(2)}, u32[]{:S(2)}) async-start(bf16[18,18,4,128]{3,1,0,2:T(8,128)(2,1)} %copy.65), calls=%async_computation.2 | async-start | bytes 884736 | tf_op jit(solution)/shard_map/all_to_all | solution.py:186
  135.8 0.3 reshape.551
  136.4 3.2 %convolution_convert_fusion.2 = bf16[18,18,4,128]{3,1,2,0:T(8,128)(2,1)S(1)} fusion(f32[18,18,512,1]{2,1,0,3:T(8,128)S(1)} %reshape.571, f32[4,128]{1,0:T(4,128)} %get-tuple-element.25, s32[4,128]{1,0:T(4,128)} %get-tuple-element.22, f32[4,128]{1,0:T(4,128)} %get-tuple-element.26, s32[4,128]{1,0:T(4,128)} %get-tuple-element.23, ...), kind=kOutput, calls=%fused_computation.66 | convolution fusion | flops 1022265344 | bytes 1011712 | tf_op jit(solution)/shard_map/fdp,ps->fds/dot_general | solution.py:98
  139.6 0.8 copy.69
  140.4 8.5 %all-to-all-done = bf16[18,18,4,128]{3,1,0,2:T(8,128)(2,1)} async-done(((bf16[18,18,4,128]{3,1,0,2:T(8,128)(2,1)}), bf16[18,18,4,128]{3,1,0,2:T(8,128)(2,1)}, u32[]{:S(2)}, u32[]{:S(2)}) %all-to-all-start) | async-done | bytes 331808 | tf_op jit(solution)/shard_map/all_to_all | solution.py:186
  148.9 3.5 %all-to-all-start.2 = ((bf16[18,18,4,128]{3,1,0,2:T(8,128)(2,1)}), bf16[18,18,4,128]{3,1,0,2:T(8,128)(2,1)S(1)}, u32[]{:S(2)}, u32[]{:S(2)}) async-start(bf16[18,18,4,128]{3,1,0,2:T(8,128)(2,1)} %copy.69), calls=%async_computation.4 | async-start | bytes 884736 | tf_op jit(solution)/shard_map/all_to_all | solution.py:180
  152.4 1.1 copy.66
  153.5 0.9 reshape.552
  154.4 1.6 fusion.97
  156.3 1.0 copy.72
  157.3 7.4 %all-to-all-done.2 = bf16[18,18,4,128]{3,1,0,2:T(8,128)(2,1)S(1)} async-done(((bf16[18,18,4,128]{3,1,0,2:T(8,128)(2,1)}), bf16[18,18,4,128]{3,1,0,2:T(8,128)(2,1)S(1)}, u32[]{:S(2)}, u32[]{:S(2)}) %all-to-all-start.2) | async-done | bytes 331808 | tf_op jit(solution)/shard_map/all_to_all | solution.py:180
  165.0 1.5 fusion.99
  (148 shorter events, 3.7 us)
Async XLA Ops:
  7.2 63.4 %copy-start = (bf16[256,18,18]{0,2,1:T(8,128)(2,1)S(1)}, bf16[256,18,18]{0,2,1:T(8,128)(2,1)}, u32[]{:S(2)}) copy-start(bf16[256,18,18]{0,2,1:T(8,128)(2,1)} %param.27) | copy-start | bytes 497668
  7.2 8.2 %copy-start.42 = (s32[2,128]{1,0:T(2,128)S(1)}, s32[2,128]{1,0:T(2,128)}, u32[]{:S(2)}) copy-start(s32[2,128]{1,0:T(2,128)} %param.25) | copy-start | bytes 3076
  7.2 8.2 %copy-start.1 = (f32[18,18,512]{2,1,0:T(8,128)S(1)}, f32[18,18,512]{2,1,0:T(8,128)}, u32[]{:S(2)}) copy-start(f32[18,18,512]{2,1,0:T(8,128)} %param.19) | copy-start | bytes 1990660
  8.5 27.7 %collective-permute-start.1 = (f32[18,18,1,128]{3,1,2,0:T(8,128)S(1)}, f32[18,18,1,128]{3,1,2,0:T(8,128)S(1)}, u32[]{:S(2)}, u32[]{:S(2)}) collective-permute-start(f32[18,18,1,128]{3,1,2,0:T(8,128)S(1)} %get-tuple-element.19), channel_id=1, source_target_pairs={{4,0},{8,4},{12,8},{5,1},{9,5},{13,9},{6,2},{10,6},{14,10},{7,3},{... | collective-permute-start | bytes 497672 | tf_op jit(solution)/shard_map/ppermute | solution.py:29
  9.8 26.4 %collective-permute-start = (f32[18,18,1,128]{3,1,2,0:T(8,128)S(1)}, f32[18,18,1,128]{3,1,2,0:T(8,128)S(1)}, u32[]{:S(2)}, u32[]{:S(2)}) collective-permute-start(f32[18,18,1,128]{3,1,2,0:T(8,128)S(1)} %get-tuple-element.18), channel_id=1, source_target_pairs={{0,4},{4,8},{8,12},{1,5},{5,9},{9,13},{2,6},{6,10},{10,14},{3,7},{... | collective-permute-start | bytes 497672 | tf_op jit(solution)/shard_map/ppermute | solution.py:28
  15.4 7.7 %copy-start.43 = (s32[1,4]{1,0:T(1,128)S(1)}, s32[1,4]{1,0:T(1,128)}, u32[]{:S(2)}) copy-start(s32[1,4]{1,0:T(1,128)} %param.34) | copy-start | bytes 52
  15.4 7.8 %copy-start.38 = (f32[3,1,4,128]{3,2,1,0:T(4,128)S(1)}, f32[3,1,4,128]{3,2,1,0:T(4,128)}, u32[]{:S(2)}) copy-start(f32[3,1,4,128]{3,2,1,0:T(4,128)} %param.33) | copy-start | bytes 18436
  15.4 12.8 %copy-start.30 = (f32[4,512]{1,0:T(4,128)S(1)}, f32[4,512]{1,0:T(4,128)}, u32[]{:S(2)}) copy-start(f32[4,512]{1,0:T(4,128)} %param.23) | copy-start | bytes 24580
  15.5 12.8 %copy-start.31 = (f32[4,512]{1,0:T(4,128)S(1)}, f32[4,512]{1,0:T(4,128)}, u32[]{:S(2)}) copy-start(f32[4,512]{1,0:T(4,128)} %param.24) | copy-start | bytes 24580
  16.0 13.1 %copy-start.32 = (s32[4,512]{1,0:T(4,128)S(1)}, s32[4,512]{1,0:T(4,128)}, u32[]{:S(2)}) copy-start(s32[4,512]{1,0:T(4,128)} %param.22) | copy-start | bytes 24580
  16.1 13.2 %copy-start.40 = (s32[4,128]{1,0:T(4,128)S(1)}, s32[4,128]{1,0:T(4,128)}, u32[]{:S(2)}) copy-start(s32[4,128]{1,0:T(4,128)} %param.20) | copy-start | bytes 6148
  16.1 13.2 %collective-permute-start.3 = (bf16[18,18,128]{2,1,0:T(8,128)(2,1)S(1)}, bf16[18,18,128]{2,1,0:T(8,128)(2,1)S(1)}, u32[]{:S(2)}, u32[]{:S(2)}) collective-permute-start(bf16[18,18,128]{2,1,0:T(8,128)(2,1)S(1)} %fusion.107), channel_id=1, source_target_pairs={{4,0},{8,4},{12,8},{5,1},{9,5},{13,9},{6,2},{10,6},{14,10},{7,3},{... | collective-permute-start | bytes 248840 | tf_op jit(solution)/shard_map/ppermute | solution.py:18
  18.6 10.8 %collective-permute-start.2 = (bf16[18,18,128]{2,1,0:T(8,128)(2,1)}, bf16[18,18,128]{2,1,0:T(8,128)(2,1)S(1)}, u32[]{:S(2)}, u32[]{:S(2)}) collective-permute-start(bf16[18,18,128]{2,1,0:T(8,128)(2,1)} %fusion.106), channel_id=1, source_target_pairs={{0,4},{4,8},{8,12},{1,5},{5,9},{9,13},{2,6},{6,10},{10,14},{3,7},{... | collective-permute-start | bytes 248840 | tf_op jit(solution)/shard_map/ppermute | solution.py:18
  23.8 74.1 %all-to-all-start.1 = ((bf16[1,1,4,128]{3,1,0,2:T(2,128)(2,1)}), bf16[1,1,4,128]{3,1,0,2:T(2,128)(2,1)}, u32[]{:S(2)}, u32[]{:S(2)}) async-start(bf16[1,1,4,128]{3,1,0,2:T(2,128)(2,1)} %copy.67), calls=%async_computation.3 | async-start | bytes 4096 | tf_op jit(solution)/shard_map/all_to_all | solution.py:189
  28.1 34.5 %reduce-scatter.3.cloned.1.call-start = ((), (), s32[]{:S(2)}) async-start(), calls=%async_computation.6 | async-start | bytes 655360 | tf_op jit(solution)/shard_map/reduce_scatter | solution.py:159
  28.3 7.8 %copy-start.20 = (f32[18,18]{1,0:T(8,128)}, f32[18,18]{1,0:T(8,128)S(1)}, u32[]{:S(2)}) copy-start(f32[18,18]{1,0:T(8,128)S(1)} %get-tuple-element.57) | copy-start | bytes 3892
  28.4 2.4 %copy-start.12 = (f32[18,512]{1,0:T(8,128)}, f32[18,512]{1,0:T(8,128)S(1)}, u32[]{:S(2)}) copy-start(f32[18,512]{1,0:T(8,128)S(1)} %get-tuple-element.51) | copy-start | bytes 110596
  28.4 2.4 %copy-start.14 = (f32[18,512]{1,0:T(8,128)}, f32[18,512]{1,0:T(8,128)S(1)}, u32[]{:S(2)}) copy-start(f32[18,512]{1,0:T(8,128)S(1)} %get-tuple-element.49) | copy-start | bytes 110596
  28.4 3.8 %copy-start.6 = (f32[18,512]{1,0:T(8,128)}, f32[18,512]{1,0:T(8,128)S(1)}, u32[]{:S(2)}) copy-start(f32[18,512]{1,0:T(8,128)S(1)} %get-tuple-element.50) | copy-start | bytes 110596
  28.5 5.3 %copy-start.4 = (f32[18,512]{1,0:T(8,128)}, f32[18,512]{1,0:T(8,128)S(1)}, u32[]{:S(2)}) copy-start(f32[18,512]{1,0:T(8,128)S(1)} %get-tuple-element.48) | copy-start | bytes 110596
  29.2 1.6 copy-start.16
  29.2 1.6 copy-start.18
  29.2 3.1 %copy-start.10 = (f32[18,512]{1,0:T(8,128)}, f32[18,512]{1,0:T(8,128)S(1)}, u32[]{:S(2)}) copy-start(f32[18,512]{1,0:T(8,128)S(1)} %get-tuple-element.55) | copy-start | bytes 110596
  29.2 4.5 %copy-start.8 = (f32[18,512]{1,0:T(8,128)}, f32[18,512]{1,0:T(8,128)S(1)}, u32[]{:S(2)}) copy-start(f32[18,512]{1,0:T(8,128)S(1)} %get-tuple-element.52) | copy-start | bytes 110596
  29.3 1.5 copy-start.26
  29.3 1.6 copy-start.28
  29.3 3.0 %copy-start.22 = (s32[1,512]{1,0:T(1,128)}, s32[1,512]{1,0:T(1,128)S(1)}, u32[]{:S(2)}) copy-start(s32[1,512]{1,0:T(1,128)S(1)} %get-tuple-element.39) | copy-start | bytes 6148
  29.3 4.5 %copy-start.24 = (s32[1,512]{1,0:T(1,128)}, s32[1,512]{1,0:T(1,128)S(1)}, u32[]{:S(2)}) copy-start(s32[1,512]{1,0:T(1,128)S(1)} %get-tuple-element.36) | copy-start | bytes 6148
  33.8 2.4 %copy-start.35 = (f32[4,128]{1,0:T(4,128)S(1)}, f32[4,128]{1,0:T(4,128)}, u32[]{:S(2)}) copy-start(f32[4,128]{1,0:T(4,128)} %param.21) | copy-start | bytes 6148
  38.0 1.4 copy-start.44
  38.0 2.1 %copy-start.33 = (f32[4,1,4,128]{3,2,1,0:T(4,128)S(1)}, f32[4,1,4,128]{3,2,1,0:T(4,128)}, u32[]{:S(2)}) copy-start(f32[4,1,4,128]{3,2,1,0:T(4,128)} %param.29) | copy-start | bytes 24580
  38.0 3.3 %copy-start.34 = (s32[4,1,4,128]{3,2,1,0:T(4,128)S(1)}, s32[4,1,4,128]{3,2,1,0:T(4,128)}, u32[]{:S(2)}) copy-start(s32[4,1,4,128]{3,2,1,0:T(4,128)} %param.28) | copy-start | bytes 24580
  39.3 78.6 %reduce-scatter.5.cloned.1.call-start = ((), (), s32[]{:S(2)}) async-start(), calls=%async_computation.7 | async-start | bytes 655360 | tf_op jit(solution)/shard_map/reduce_scatter | solution.py:159
  70.6 1.2 copy-start.2
  74.7 11.9 %collective-permute-start.7 = (bf16[18,18,128]{2,1,0:T(8,128)(2,1)}, bf16[18,18,128]{2,1,0:T(8,128)(2,1)S(1)}, u32[]{:S(2)}, u32[]{:S(2)}) collective-permute-start(bf16[18,18,128]{2,1,0:T(8,128)(2,1)} %convolution_convert_fusion.4), channel_id=1, source_target_pairs={{4,0},{8,4},{12,8},{5,1},{9,5},{13,9},{6,2},{10,6},{14,10},{7,3},{... | collective-permute-start | bytes 248840 | tf_op jit(solution)/shard_map/ppermute | solution.py:18
  76.0 10.7 %collective-permute-start.6 = (bf16[18,18,128]{2,1,0:T(8,128)(2,1)}, bf16[18,18,128]{2,1,0:T(8,128)(2,1)S(1)}, u32[]{:S(2)}, u32[]{:S(2)}) collective-permute-start(bf16[18,18,128]{2,1,0:T(8,128)(2,1)} %convolution_convert_fusion.5), channel_id=1, source_target_pairs={{0,4},{4,8},{8,12},{1,5},{5,9},{9,13},{2,6},{6,10},{10,14},{3,7},{... | collective-permute-start | bytes 248840 | tf_op jit(solution)/shard_map/ppermute | solution.py:18
  80.7 6.0 %copy-start.15 = (f32[18,512]{1,0:T(8,128)S(1)}, f32[18,512]{1,0:T(8,128)}, u32[]{:S(2)}) copy-start(f32[18,512]{1,0:T(8,128)} %copy-done.14) | copy-start | bytes 110596
  80.7 6.0 %copy-start.19 = (f32[18,512]{1,0:T(8,128)S(1)}, f32[18,512]{1,0:T(8,128)}, u32[]{:S(2)}) copy-start(f32[18,512]{1,0:T(8,128)} %copy-done.18) | copy-start | bytes 110596
  80.7 6.0 %copy-start.29 = (s32[1,512]{1,0:T(1,128)S(1)}, s32[1,512]{1,0:T(1,128)}, u32[]{:S(2)}) copy-start(s32[1,512]{1,0:T(1,128)} %copy-done.28) | copy-start | bytes 6148
  80.7 12.8 %collective-permute-start.5 = (f32[18,18,1,128]{3,1,2,0:T(8,128)S(1)}, f32[18,18,1,128]{3,1,2,0:T(8,128)S(1)}, u32[]{:S(2)}, u32[]{:S(2)}) collective-permute-start(f32[18,18,1,128]{3,1,2,0:T(8,128)S(1)} %get-tuple-element.17), channel_id=1, source_target_pairs={{4,0},{8,4},{12,8},{5,1},{9,5},{13,9},{6,2},{10,6},{14,10},{7,3},{... | collective-permute-start | bytes 497672 | tf_op jit(solution)/shard_map/ppermute | solution.py:29
  82.0 11.5 %collective-permute-start.4 = (f32[18,18,1,128]{3,1,2,0:T(8,128)S(1)}, f32[18,18,1,128]{3,1,2,0:T(8,128)S(1)}, u32[]{:S(2)}, u32[]{:S(2)}) collective-permute-start(f32[18,18,1,128]{3,1,2,0:T(8,128)S(1)} %get-tuple-element.16), channel_id=1, source_target_pairs={{0,4},{4,8},{8,12},{1,5},{5,9},{9,13},{2,6},{6,10},{10,14},{3,7},{... | collective-permute-start | bytes 497672 | tf_op jit(solution)/shard_map/ppermute | solution.py:28
  86.7 1.4 copy-start.13
  86.7 1.4 copy-start.17
  86.7 1.4 copy-start.27
  88.1 1.5 copy-start.7
  88.2 1.5 copy-start.11
  88.2 1.5 copy-start.23
  89.7 1.5 copy-start.5
  89.7 1.5 copy-start.9
  89.7 1.5 copy-start.25
  91.2 2.4 %copy-start.21 = (f32[18,18]{1,0:T(8,128)S(1)}, f32[18,18]{1,0:T(8,128)}, u32[]{:S(2)}) copy-start(f32[18,18]{1,0:T(8,128)} %copy-done.20) | copy-start | bytes 3892
  91.2 2.4 %copy-start.36 = (f32[4,128]{1,0:T(4,128)S(1)}, f32[4,128]{1,0:T(4,128)}, u32[]{:S(2)}) copy-start(f32[4,128]{1,0:T(4,128)} %param.21) | copy-start | bytes 6148
  94.4 0.9 copy-start.46
  95.4 1.3 copy-start.37
  95.4 1.9 %copy-start.39 = (bf16[4,128]{1,0:T(4,128)(2,1)S(1)}, bf16[4,128]{1,0:T(4,128)(2,1)}, u32[]{:S(2)}) copy-start(bf16[4,128]{1,0:T(4,128)(2,1)} %get-tuple-element.6) | copy-start | bytes 3076
  95.4 6.2 %copy-start.47 = (s32[1,4,128]{2,1,0:T(4,128)S(1)}, s32[1,4,128]{2,1,0:T(4,128)}, u32[]{:S(2)}) copy-start(s32[1,4,128]{2,1,0:T(4,128)} %param.35) | copy-start | bytes 6148
  95.4 11.7 %copy-start.49 = (s32[1,4,128]{2,1,0:T(4,128)S(1)}, s32[1,4,128]{2,1,0:T(4,128)}, u32[]{:S(2)}) copy-start(s32[1,4,128]{2,1,0:T(4,128)} %param.31) | copy-start | bytes 6148
  97.9 9.2 %all-to-all-start.3 = ((bf16[1,1,4,128]{3,1,0,2:T(2,128)(2,1)}), bf16[1,1,4,128]{3,1,0,2:T(2,128)(2,1)S(1)}, u32[]{:S(2)}, u32[]{:S(2)}) async-start(bf16[1,1,4,128]{3,1,0,2:T(2,128)(2,1)} %copy.71), calls=%async_computation.5 | async-start | bytes 4096 | tf_op jit(solution)/shard_map/all_to_all | solution.py:183
  130.9 18.0 %all-to-all-start = ((bf16[18,18,4,128]{3,1,0,2:T(8,128)(2,1)}), bf16[18,18,4,128]{3,1,0,2:T(8,128)(2,1)}, u32[]{:S(2)}, u32[]{:S(2)}) async-start(bf16[18,18,4,128]{3,1,0,2:T(8,128)(2,1)} %copy.65), calls=%async_computation.2 | async-start | bytes 884736 | tf_op jit(solution)/shard_map/all_to_all | solution.py:186
  148.9 15.8 %all-to-all-start.2 = ((bf16[18,18,4,128]{3,1,0,2:T(8,128)(2,1)}), bf16[18,18,4,128]{3,1,0,2:T(8,128)(2,1)S(1)}, u32[]{:S(2)}, u32[]{:S(2)}) async-start(bf16[18,18,4,128]{3,1,0,2:T(8,128)(2,1)} %copy.69), calls=%async_computation.4 | async-start | bytes 884736 | tf_op jit(solution)/shard_map/all_to_all | solution.py:180
  152.3 2.1 %copy-start.41 = (f32[512]{0:T(512)S(1)}, f32[512]{0:T(512)}, u32[]{:S(2)}) copy-start(f32[512]{0:T(512)} %broadcast_add_fusion.1) | copy-start | bytes 6148
  152.4 2.1 %copy-start.48 = (s32[1,4,128]{2,1,0:T(4,128)S(1)}, s32[1,4,128]{2,1,0:T(4,128)}, u32[]{:S(2)}) copy-start(s32[1,4,128]{2,1,0:T(4,128)} %param.35) | copy-start | bytes 6148
  157.3 7.7 %copy-start.3 = (f32[18,18,512]{2,1,0:T(8,128)S(1)}, f32[18,18,512]{2,1,0:T(8,128)}, u32[]{:S(2)}) copy-start(f32[18,18,512]{2,1,0:T(8,128)} %get-tuple-element.61) | copy-start | bytes 1990660
  157.3 7.7 %copy-start.50 = (s32[1,4,128]{2,1,0:T(4,128)S(1)}, s32[1,4,128]{2,1,0:T(4,128)}, u32[]{:S(2)}) copy-start(s32[1,4,128]{2,1,0:T(4,128)} %param.31) | copy-start | bytes 6148
  (1 other events, 0.9 us)
Sparse Core Ops, SparseCore 0:
  39.4 23.1 reduce-scatter.2
  96.8 21.0 reduce-scatter.4
where the time goes:
time: 174 us; the launch traced here: 173 us
  waiting for transfers between devices  51.1 us (29%)
  starting transfers between devices  40.5 us (23%)
  matrix products  31.8 us (18%)
  between operations  15.1 us (9%)
  local copies, waits for them, and re-layouts  14.2 us (8%)
  blocking collectives  14 us (8%)
  other arithmetic  6.72 us (4%)
    reduce_scatter x2, waiting for transfers between devices, per_device(): lax.psum_scatter(jnp.einsum('fdp,fdh->ph', features, w_in, preferred_elem...  31.3 us
    dot_general x12, matrix products, pick_columns(): return jnp.einsum('fdp,pn->fdn', source, selector, precision=EXACT)  17.5 us
    all_gather x2, blocking collectives, per_device(): lax.all_gather(hidden, ('fr', 'dr'), axis=0, tiled=True)  14 us
    ppermute x4, starting transfers between devices, from_behind(): return lax.ppermute(array, axis, pairs)  11.7 us
    ppermute x2, starting transfers between devices, with_halo(): before = lax.ppermute(last, axis, up)  10.1 us
    all_to_all x1, waiting for transfers between devices, per_device(): lax.all_to_all(mesh_values.astype(jnp.bfloat16), 'sp', split_axis=2, conc...  8.48 us
    all_to_all x1, waiting for transfers between devices, per_device(): lax.all_to_all(grid_values.astype(jnp.bfloat16), 'sp', split_axis=2, conc...  7.38 us
    dot_general x2, matrix products, pack_slots(): jnp.einsum('fdp,ps->fds', source, mixing, precision=EXACT)  6.41 us
  transfers between devices with their start and end apart: 14, of which 5 were waited for; matrix products, arithmetic and copies ran while one was open for 24% of the time, Pallas kernels for 0%

commit v1 on v0

v1 whole, which is shorter than its diff:
```python
import functools

import jax
import jax.numpy as jnp
import numpy as np
from jax import lax
from jax.experimental import pallas as pl
from jax.experimental.pallas import tpu as pltpu
from jax.sharding import PartitionSpec as P

NSUB = 2
DT_STEP = 0.1
BLEND_RATE = 0.5
F32 = jnp.float32
BF16 = jnp.bfloat16
CHUNK = 16


def kernel_call(body, outs, scratch=(), flops=0, nbytes=4 << 20):
    spec = pl.BlockSpec(memory_space=pltpu.VMEM)

    def run(*args):
        return pl.pallas_call(
            body,
            out_shape=[jax.ShapeDtypeStruct(s, t) for s, t in outs],
            in_specs=[spec] * len(args),
            out_specs=[spec] * len(outs),
            scratch_shapes=[pltpu.VMEM(s, t) for s, t in scratch],
            compiler_params=pltpu.CompilerParams(vmem_limit_bytes=24 << 20),
            cost_estimate=pl.CostEstimate(flops=flops, bytes_accessed=nbytes, transcendentals=0),
        )(*args)

    return run


def dot(a, b):
    return jnp.dot(a, b, preferred_element_type=F32)


def one_hot(row, length):
    spots = lax.broadcasted_iota(jnp.int32, (length, row.shape[1]), 0)
    return jnp.where(spots == row, 1.0, 0.0).astype(BF16)


def shift(array, axis, by):
    size = lax.axis_size(axis)
    return lax.ppermute(array, axis, [(i, i + by) for i in range(size) if 0 <= i + by < size])


def peer_pairs(size, step):
    if size & (size - 1) == 0:
        return [(i, i ^ step) for i in range(size)]
    return [(i, (step - i) % size) for i in range(size)]


def peer_of(me, size, step):
    if size & (size - 1) == 0:
        return lax.bitwise_xor(me, step)
    return lax.rem(step - me + size, size)


def messages(state_ref, halo_ref, up_ref, down_ref, grid_points, cols):
    nodes = state_ref.shape[1] - grid_points
    listed = halo_ref.shape[1]
    mesh = state_ref[:, grid_points:].astype(BF16)
    for msg, row, which in ((up_ref, grid_points - cols, 1), (down_ref, 0, 0)):
        msg[:, :cols] = state_ref[:, row : row + cols].astype(BF16)
        picked = dot(mesh, one_hot(halo_ref[which : which + 1, :], nodes))
        msg[:, cols : cols + listed] = picked.astype(BF16)


def begin_kernel(grid_ref, mesh_ref, halo_ref, state_ref, up_ref, down_ref, *, rows, cols):
    freqs, dirs, _ = mesh_ref.shape
    bands = freqs * dirs
    gp = rows * cols
    padded = state_ref.shape[0]
    state_ref[bands:, :] = jnp.zeros((padded - bands, state_ref.shape[1]), F32)
    for x in range(rows):
        state_ref[:bands, x * cols : (x + 1) * cols] = grid_ref[pl.ds(x, bands, stride=rows), :]
    for f in range(freqs):
        state_ref[f * dirs : (f + 1) * dirs, gp:] = mesh_ref[f]
    messages(state_ref, halo_ref, up_ref, down_ref, gp, cols)


def hot_kernel(index_ref, hot_ref):
    for k in range(index_ref.shape[0]):
        hot_ref[k] = one_hot(index_ref[k : k + 1, :], hot_ref.shape[1])


def move_kernel(
    state_ref, lower_ref, upper_ref, hot_ref, pq_ref, band_ref, sea_ref, speed_ref, win_ref,
    moved_ref, keep_ref, send_ref, ext_ref, near_ref, feat_ref,
):
    padded, points = state_ref.shape
    rows, cols = sea_ref.shape
    gp = rows * cols
    nodes = points - gp
    neighbours = hot_ref.shape[0]
    listed = lower_ref.shape[1] - cols
    ext_ref[:, :nodes] = state_ref[:, gp:].astype(BF16)
    ext_ref[:, nodes : nodes + listed] = lower_ref[:, cols:]
    ext_ref[:, nodes + listed :] = upper_ref[:, cols:]
    for k in range(neighbours):
        near_ref[k] = dot(ext_ref[...], hot_ref[k])
    sea = sea_ref[...].astype(F32)
    lane = lax.broadcasted_iota(jnp.int32, (CHUNK, cols), 1)
    for c in range(padded // CHUNK):
        here = slice(c * CHUNK, (c + 1) * CHUNK)
        cx = band_ref[here, 0:1]
        cy = band_ref[here, 1:2]
        for x in range(rows):
            g = state_ref[here, x * cols : (x + 1) * cols]
            if x == 0:
                low = lower_ref[here, :cols].astype(F32)
            else:
                low = state_ref[here, (x - 1) * cols : x * cols]
            if x == rows - 1:
                high = upper_ref[here, :cols].astype(F32)
            else:
                high = state_ref[here, (x + 1) * cols : (x + 2) * cols]
            west = jnp.where(lane == 0, 0.0, pltpu.roll(g, 1, 1))
            east = jnp.where(lane == cols - 1, 0.0, pltpu.roll(g, cols - 1, 1))
            out = g - jnp.abs(cx) * speed_ref[x : x + 1, :] * (g - jnp.where(cx > 0, low, high))
            out = out - jnp.abs(cy) * speed_ref[x : x + 1, :] * (g - jnp.where(cy > 0, west, east))
            out = out * sea[x : x + 1, :]
            moved_ref[here, x * cols : (x + 1) * cols] = out
            feat_ref[here, x * cols : (x + 1) * cols] = out.astype(BF16)
        e = state_ref[here, gp:]
        out = e
        for k in range(neighbours):
            w = cx * pq_ref[k : k + 1, :] + cy * pq_ref[neighbours + k : neighbours + k + 1, :]
            out = out + jnp.maximum(w, 0.0) * (near_ref[k, here, :] - e)
        moved_ref[here, gp:] = out
        feat_ref[here, gp:] = out.astype(BF16)
    half = keep_ref.shape[0]
    keep_ref[...] = dot(win_ref[:half, :], feat_ref[...])
    send_ref[...] = dot(win_ref[half:, :], feat_ref[...]).astype(BF16)


def add_transfer(moved_ref, mine_ref, other_ref, wout_ref, hid_ref, state_ref):
    half = mine_ref.shape[0]
    hid_ref[:half, :] = mine_ref[...]
    hid_ref[half:, :] = other_ref[...]
    state_ref[...] = moved_ref[...] + DT_STEP * dot(wout_ref[...], hid_ref[...])


def next_kernel(
    moved_ref, mine_ref, other_ref, wout_ref, halo_ref, state_ref, up_ref, down_ref, hid_ref,
    *, grid_points, cols,
):
    add_transfer(moved_ref, mine_ref, other_ref, wout_ref, hid_ref, state_ref)
    messages(state_ref, halo_ref, up_ref, down_ref, grid_points, cols)


def slots_kernel(
    gi_ref, gw_ref, gc_ref, gt_ref, mi_ref, mw_ref, mc_ref, mt_ref,
    gmix_ref, mmix_ref, sums_ref, gland_ref, mland_ref,
):
    me = lax.axis_index("sp")
    _, _, peers, cap = gi_ref.shape
    groups = (
        (gi_ref, gw_ref, gc_ref, gt_ref, gmix_ref, gland_ref, 0),
        (mi_ref, mw_ref, mc_ref, mt_ref, mmix_ref, mland_ref, 1),
    )
    for index_ref, weight_ref, count_ref, target_ref, mix_ref, land_ref, kind in groups:
        length = mix_ref.shape[0]
        spots = lax.broadcasted_iota(jnp.int32, (length, cap), 0)
        slot = lax.broadcasted_iota(jnp.int32, (1, cap), 1)
        for p in range(peers):
            peer = peer_of(me, peers, p)
            count = jnp.sum(
                jnp.where(
                    lax.broadcasted_iota(jnp.int32, (1, peers), 1) == peer, count_ref[...], 0
                ),
                axis=1,
                keepdims=True,
            )
            live = jnp.where(slot < count, 1.0, 0.0)
            mix = jnp.zeros((length, cap), F32)
            total = jnp.zeros((1, cap), F32)
            for j in range(index_ref.shape[0]):
                scaled = weight_ref[j, 0, pl.ds(peer, 1), :] * live
                mix = mix + jnp.where(spots == index_ref[j, 0, pl.ds(peer, 1), :], scaled, 0.0)
                total = total + scaled
            mix_ref[:, p * cap : (p + 1) * cap] = mix.astype(BF16)
            sums_ref[kind : kind + 1, p * cap : (p + 1) * cap] = total
            land_ref[:, p * cap : (p + 1) * cap] = one_hot(
                target_ref[0, pl.ds(peer, 1), :], land_ref.shape[0]
            )


def mix_kernel(
    moved_ref, mine_ref, other_ref, wout_ref, gmix_ref, mmix_ref, sums_ref, state_ref, *rest,
    bands,
):
    out_refs, hid_ref = rest[:-1], rest[-1]
    add_transfer(moved_ref, mine_ref, other_ref, wout_ref, hid_ref, state_ref)
    gp = gmix_ref.shape[0]
    peers = len(out_refs)
    cap = gmix_ref.shape[1] // peers
    grid = state_ref[:, :gp].astype(BF16)
    mesh = state_ref[:, gp:].astype(BF16)
    row = lax.broadcasted_iota(jnp.int32, (state_ref.shape[0], cap), 0)
    for p in range(peers):
        cut = slice(p * cap, (p + 1) * cap)
        for kind, source, mix_ref in ((0, grid, gmix_ref), (1, mesh, mmix_ref)):
            value = dot(source, mix_ref[:, cut])
            value = jnp.where(row == bands, sums_ref[kind : kind + 1, cut], value)
            out_refs[p][:, kind * cap : (kind + 1) * cap] = value.astype(BF16)


def land(values, land_ref):
    return lax.dot_general(
        values, land_ref[...], (((1,), (1,)), ((), ())), preferred_element_type=F32
    )


def end_kernel(state_ref, gland_ref, mland_ref, sea_ref, *rest, bands):
    got_refs, (grid_ref, mesh_ref, values_ref, sum_ref) = rest[:-4], rest[-4:]
    rows, cols = sea_ref.shape
    gp = rows * cols
    freqs, dirs, _ = mesh_ref.shape
    cap = got_refs[0].shape[1] // 2
    for kind in (0, 1):
        for p, got in enumerate(got_refs):
            values_ref[kind, :, p * cap : (p + 1) * cap] = got[:, kind * cap : (kind + 1) * cap]
    sum_ref[:, :gp] = land(values_ref[1], mland_ref)
    sum_ref[:, gp:] = land(values_ref[0], gland_ref)
    cover = sum_ref[bands : bands + 1, :]
    rate = BLEND_RATE / (1.0 + cover)
    sea = sea_ref[...].astype(F32)
    for x in range(rows):
        cut = slice(x * cols, (x + 1) * cols)
        g = state_ref[:bands, cut]
        out = g + rate[:, cut] * (sum_ref[:bands, cut] - cover[:, cut] * g)
        grid_ref[pl.ds(x, bands, stride=rows), :] = out * sea[x : x + 1, :]
    for f in range(freqs):
        here = slice(f * dirs, (f + 1) * dirs)
        e = state_ref[here, gp:]
        mesh_ref[f] = e + rate[:, gp:] * (sum_ref[here, gp:] - cover[:, gp:] * e)


def band_table(freqs, dirs, n_fr, n_dr, padded):
    speed = (0.7 * np.power(np.float32(1.1), -np.arange(freqs * n_fr, dtype=np.float32))).astype(np.float32)
    total = dirs * n_dr
    heading = (2.0 * np.pi * (np.arange(total, dtype=np.float64) + 0.5) / total)
    table = np.zeros((n_fr, n_dr, padded, 2), np.float32)
    for i in range(n_fr):
        for j in range(n_dr):
            s = speed[i * freqs : (i + 1) * freqs, None]
            h = heading[None, j * dirs : (j + 1) * dirs]
            table[i, j, : freqs * dirs, 0] = (s * np.cos(h)).reshape(-1)
            table[i, j, : freqs * dirs, 1] = (s * np.sin(h)).reshape(-1)
    return table


def reduce_hidden(keep, send):
    got = lax.ppermute(send, "dr", [(0, 1), (1, 0)])
    total = keep + got.astype(F32)
    size = lax.axis_size("fr")
    step = 1
    while step < size:
        total = total + lax.ppermute(
            total.astype(BF16), "fr", [(i, i ^ step) for i in range(size)]
        ).astype(F32)
        step *= 2
    hidden = (total / (1.0 + jnp.exp(-total))).astype(BF16)
    return hidden, lax.ppermute(hidden, "dr", [(0, 1), (1, 0)])


def per_device(
    grid_spec, mesh_spec, grid_sea, grid_speed, nb_index, nb_angle, nb_coef, halo_list, w_in, w_out,
    g2m_index, g2m_weight, g2m_count, g2m_target, m2g_index, m2g_weight, m2g_count, m2g_target,
):
    freqs, dirs, rows, cols = grid_spec.shape
    nodes = mesh_spec.shape[2]
    listed = halo_list.shape[1]
    hid = w_in.shape[2]
    half = hid // 2
    bands = freqs * dirs
    padded = (bands // CHUNK + 1) * CHUNK
    gp = rows * cols
    points = gp + nodes
    neighbours = nb_index.shape[0]
    peers, cap = g2m_index.shape[2:]
    n_fr, n_dr = lax.axis_size("fr"), lax.axis_size("dr")
    dr = lax.axis_index("dr")

    table = jnp.asarray(band_table(freqs, dirs, n_fr, n_dr, padded))
    band = table[lax.axis_index("fr"), dr]
    pq = jnp.concatenate([-nb_coef * jnp.cos(nb_angle), -nb_coef * jnp.sin(nb_angle)], axis=0)
    pad = ((0, padded - bands), (0, 0))
    win = jnp.pad(w_in.reshape(bands, hid), pad).T
    wout = jnp.pad(w_out.reshape(hid, bands).T, pad)
    win = jnp.where(dr == 0, win, jnp.roll(win, half, axis=0))
    wout = jnp.where(dr == 0, wout, jnp.roll(wout, half, axis=1))

    message = ((padded, cols + listed), BF16)
    state_shape = ((padded, points), F32)
    hid_scratch = ((hid, points), BF16)
    state, up, down = kernel_call(
        functools.partial(begin_kernel, rows=rows, cols=cols),
        [state_shape, message, message],
        flops=2 * padded * nodes * 2 * listed,
    )(grid_spec.reshape(bands * rows, cols), mesh_spec, halo_list)
    (hot,) = kernel_call(hot_kernel, [((neighbours, nodes + 2 * listed, nodes), BF16)])(nb_index)
    gmix, mmix, sums, gland, mland = kernel_call(
        slots_kernel,
        [
            ((gp, peers * cap), BF16),
            ((nodes, peers * cap), BF16),
            ((2, peers * cap), F32),
            ((nodes, peers * cap), BF16),
            ((gp, peers * cap), BF16),
        ],
    )(g2m_index, g2m_weight, g2m_count, g2m_target, m2g_index, m2g_weight, m2g_count, m2g_target)

    for substep in range(NSUB):
        lower = shift(up, "sp", 1)
        upper = shift(down, "sp", -1)
        moved, keep, send = kernel_call(
            move_kernel,
            [state_shape, ((half, points), F32), ((half, points), BF16)],
            [
                ((padded, nodes + 2 * listed), BF16),
                ((neighbours, padded, nodes), F32),
                ((padded, points), BF16),
            ],
            flops=2 * padded * (neighbours * nodes * (nodes + 2 * listed) + hid * points),
        )(state, lower, upper, hot, pq, band, grid_sea, grid_speed, win)
        mine, other = reduce_hidden(keep, send)
        if substep < NSUB - 1:
            state, up, down = kernel_call(
                functools.partial(next_kernel, grid_points=gp, cols=cols),
                [state_shape, message, message],
                [hid_scratch],
                flops=2 * padded * hid * points,
            )(moved, mine, other, wout, halo_list)

    state, *values = kernel_call(
        functools.partial(mix_kernel, bands=bands),
        [state_shape] + [((padded, 2 * cap), BF16)] * peers,
        [hid_scratch],
        flops=2 * padded * (hid * points + points * peers * cap),
    )(moved, mine, other, wout, gmix, mmix, sums)
    got = [
        lax.ppermute(v, "sp", peer_pairs(peers, p)) if p else v for p, v in enumerate(values)
    ]
    if peers & (peers - 1):
        got[0] = lax.ppermute(values[0], "sp", peer_pairs(peers, 0))
    grid_out, mesh_out = kernel_call(
        functools.partial(end_kernel, bands=bands),
        [((bands * rows, cols), F32), ((freqs, dirs, nodes), F32)],
        [((2, padded, peers * cap), BF16), state_shape],
        flops=2 * padded * points * peers * cap,
    )(state, gland, mland, grid_sea, *got)
    return grid_out.reshape(grid_spec.shape), mesh_out


def solution(mesh):
    return jax.shard_map(
        per_device,
        mesh=mesh,
        in_specs=(
            P("fr", "dr", ("grp", "sp"), None),
            P("fr", "dr", ("grp", "sp")),
            P(("grp", "sp"), None),
            P(("grp", "sp"), None),
            P(None, ("grp", "sp")),
            P(None, ("grp", "sp")),
            P(None, ("grp", "sp")),
            P(None, ("grp", "sp")),
            P("fr", "dr", None),
            P(None, "fr", "dr"),
            P(None, ("grp", "sp"), None, None),
            P(None, ("grp", "sp"), None, None),
            P(("grp", "sp"), None),
            P(("grp", "sp"), None, None),
            P(None, ("grp", "sp"), None, None),
            P(None, ("grp", "sp"), None, None),
            P(("grp", "sp"), None),
            P(("grp", "sp"), None, None),
        ),
        out_specs=(P("fr", "dr", ("grp", "sp"), None), P("fr", "dr", ("grp", "sp"))),
        check_vma=False,
    )
```

time: 174 us -> 88.4 us (0.51)
  matrix products: 31.8 us -> 0 us
  starting transfers between devices: 40.5 us -> 19.1 us
  Pallas kernels: 0 us -> 14.6 us
  between operations: 15.1 us -> 1.08 us
  blocking collectives: 14 us -> 0 us
  waiting for transfers between devices: 51.1 us -> 40 us
  other arithmetic: 6.72 us -> 2.31 us
  local copies, waits for them, and re-layouts: 14.2 us -> 10.3 us
    ppermute x8 -> x13, waiting for transfers between devices: 0.02 us -> 40 us  [the longest x2 13.7 us: reduce_hidden(): lax.ppermute(total.astype(BF16), 'fr', [(i, i ^ step) for i in range(size)])]
    dot_general x22 -> x0, matrix products: 31.8 us -> none  [the longest x12 17.5 us: pick_columns(): return jnp.einsum('fdp,pn->fdn', source, selector, precision=EXACT)]
    reduce_scatter x2 -> x0, waiting for transfers between devices: 31.3 us -> none  [per_device(): lax.psum_scatter(jnp.einsum('fdp,fdh->ph', features, w_in, preferred_elem...]
    all_to_all x4 -> x0, waiting for transfers between devices: 19.8 us -> none  [the longest x1 8.48 us: per_device(): lax.all_to_all(mesh_values.astype(jnp.bfloat16), 'sp', split_axis=2, conc...]
    all_to_all x4 -> x0, starting transfers between devices: 16 us -> none  [the longest x1 4.62 us: per_device(): lax.all_to_all(mesh_values.astype(jnp.bfloat16), 'sp', split_axis=2, conc...]
    pallas_call x0 -> x8, Pallas kernels: none -> 14.6 us  [run(): pl.pallas_call(body, out_shape=[jax.ShapeDtypeStruct(s, t) for s, t in ou...]
    all_gather x2 -> x0, blocking collectives: 14 us -> none  [per_device(): lax.all_gather(hidden, ('fr', 'dr'), axis=0, tiled=True)]
    ppermute x8 -> x13, starting transfers between devices: 24.4 us -> 19.1 us  [the longest x4 11.3 us: shift(): lax.ppermute(array, axis, [(i, i + by) for i in range(size) if 0 <= i + b...]
  transfers between devices with their start and end apart: 14 -> 13, of which waited for: 5 -> 9; matrix products, arithmetic and copies ran while one was open for 24% -> 6% of each run, Pallas kernels for 0% -> 3%
where the time goes in v1:
time: 88.4 us; the launch traced here: 87.4 us
  waiting for transfers between devices  40 us (45%)
  starting transfers between devices  19.1 us (22%)
  Pallas kernels  14.6 us (17%)
  local copies, waits for them, and re-layouts  10.3 us (12%)
  other arithmetic  2.31 us (3%)
  between operations  1.08 us (1%)
    pallas_call x8, Pallas kernels, run(): pl.pallas_call(body, out_shape=[jax.ShapeDtypeStruct(s, t) for s, t in ou...  14.6 us
    ppermute x2, waiting for transfers between devices, reduce_hidden(): lax.ppermute(total.astype(BF16), 'fr', [(i, i ^ step) for i in range(size)])  13.7 us
    ppermute x3, waiting for transfers between devices, per_device(): lax.ppermute(v, 'sp', peer_pairs(peers, p))  12.7 us
    ppermute x4, starting transfers between devices, shift(): lax.ppermute(array, axis, [(i, i + by) for i in range(size) if 0 <= i + b...  11.3 us
    ppermute x4, waiting for transfers between devices, shift(): lax.ppermute(array, axis, [(i, i + by) for i in range(size) if 0 <= i + b...  10.5 us
    unnamed x52, local copies, waits for them, and re-layouts  5.83 us
    ppermute x3, starting transfers between devices, per_device(): lax.ppermute(v, 'sp', peer_pairs(peers, p))  4.45 us
    ppermute x2, starting transfers between devices, reduce_hidden(): lax.ppermute(total.astype(BF16), 'fr', [(i, i ^ step) for i in range(size)])  3.11 us
  transfers between devices with their start and end apart: 13, of which 9 were waited for; matrix products, arithmetic and copies ran while one was open for 6% of the time, Pallas kernels for 3%

profile of v1, /device:TPU:0, one launch (start us, length us, event | category | flops | bytes accessed | tf_op | source)
XLA Modules:
  0.0 87.4 jit_solution(14433611212305580083)
XLA Ops:
  0.6 1.2 %copy-done.4 = f32[18,18,512]{2,1,0:T(8,128)S(1)} copy-done((f32[18,18,512]{2,1,0:T(8,128)S(1)}, f32[18,18,512]{2,1,0:T(8,128)}, u32[]{:S(2)}) %copy-start.4) | copy-done | bytes 663576
  1.8 1.1 %copy-done.5 = f32[18,18,4,128]{3,2,1,0:T(4,128)S(1)} copy-done((f32[18,18,4,128]{3,2,1,0:T(4,128)S(1)}, f32[18,18,4,128]{3,2,1,0:T(4,128)}, u32[]{:S(2)}) %copy-start.5) | copy-done | bytes 663576
  2.9 0.7 copy-done.13
  3.6 1.1 %shard_map.194 = (f32[336,1024]{1,0:T(8,128)S(1)}, bf16[336,256]{1,0:T(8,128)(2,1)}, bf16[336,256]{1,0:T(8,128)(2,1)}) custom-call(f32[1296,128]{1,0:T(8,128)S(1)} %bitcast.11, f32[18,18,512]{2,1,0:T(8,128)S(1)} %copy-done.4, s32[2,128]{1,0:T(2,128)S(1)} %copy-done.13), custom_call_target="tpu_custom_call" | custom-call | flops 88080384 | bytes 4194304 | tf_op jit(solution)/shard_map/pallas_call | solution.py:23
  4.7 1.1 %copy-done.2 = f32[336,1024]{1,0:T(8,128)} copy-done((f32[336,1024]{1,0:T(8,128)}, f32[336,1024]{1,0:T(8,128)S(1)}, u32[]{:S(2)}) %copy-start.2) | copy-done | bytes 1376280
  5.8 5.7 %collective-permute-start = (bf16[336,256]{1,0:T(8,128)(2,1)}, bf16[336,256]{1,0:T(8,128)(2,1)}, u32[]{:S(2)}, u32[]{:S(2)}) collective-permute-start(bf16[336,256]{1,0:T(8,128)(2,1)} %get-tuple-element.27), channel_id=1, source_target_pairs={{0,4},{4,8},{8,12},{1,5},{5,9},{9,13},{2,6},{6,10},{10,14},{3,7},{... | collective-permute-start | bytes 516104 | tf_op jit(solution)/shard_map/ppermute | solution.py:47
  11.5 1.3 %collective-permute-start.1 = (bf16[336,256]{1,0:T(8,128)(2,1)}, bf16[336,256]{1,0:T(8,128)(2,1)}, u32[]{:S(2)}, u32[]{:S(2)}) collective-permute-start(bf16[336,256]{1,0:T(8,128)(2,1)} %get-tuple-element.28), channel_id=1, source_target_pairs={{4,0},{8,4},{12,8},{5,1},{9,5},{13,9},{6,2},{10,6},{14,10},{7,3},{... | collective-permute-start | bytes 516104 | tf_op jit(solution)/shard_map/ppermute | solution.py:47
  12.8 0.1 reshape.17
  12.9 0.2 copy.22
  13.1 0.0 copy-start.19
  13.1 0.7 fusion.2
  13.8 0.1 cosine_multiply_fusion
  13.9 0.9 %dynamic-slice_bitcast_fusion.band_ref = f32[336,2]{1,0:T(8,128)S(1)} fusion(f32[2,2,336,2]{3,2,1,0:T(8,128)} %constant.16.clone, s32[]{:T(128)S(6)} %select_n.22, s32[]{:T(128)S(6)} %select_n.23), kind=kLoop, calls=%fused_computation.9 | loop fusion | bytes 5384 | tf_op jit(solution)/shard_map/squeeze | solution.py:290
  14.9 0.0 copy-start.20
  14.9 0.0 copy-start.6
  14.9 0.0 copy-start.8
  14.9 0.6 shard_map.195.hot_ref
  15.6 0.2 copy-done.20
  15.8 0.1 copy-done.21
  15.9 0.0 copy-done.22
  15.9 0.1 maximum_select_fusion.win_ref
  16.0 0.0 collective-permute-done.lower_ref
  16.0 3.6 %collective-permute-done.1.upper_ref = bf16[336,256]{1,0:T(8,128)(2,1)} collective-permute-done((bf16[336,256]{1,0:T(8,128)(2,1)}, bf16[336,256]{1,0:T(8,128)(2,1)}, u32[]{:S(2)}, u32[]{:S(2)}) %collective-permute-start.1) | collective-permute-done | bytes 172064 | tf_op jit(solution)/shard_map/ppermute | solution.py:47
  19.6 3.3 %shard_map.196 = (f32[336,1024]{1,0:T(8,128)S(1)}, f32[128,1024]{1,0:T(8,128)S(1)}, bf16[128,1024]{1,0:T(8,128)(2,1)S(1)}) custom-call(f32[336,1024]{1,0:T(8,128)S(1)} %copy-done.3, bf16[336,256]{1,0:T(8,128)(2,1)} %collective-permute-done.lower_ref, bf16[336,256]{1,0:T(8,128)(2,1)} %collective-permute-done.1.upper_ref, ...), custom_call_target="tpu_custom_call" | custom-call | flops 1233125376 | bytes 4194304 | tf_op jit(solution)/shard_map/pallas_call | solution.py:23
  22.9 0.1 collective-permute-start.2
  22.9 1.5 %collective-permute-done.2 = bf16[128,1024]{1,0:T(8,128)(2,1)S(1)} collective-permute-done((bf16[128,1024]{1,0:T(8,128)(2,1)S(1)}, bf16[128,1024]{1,0:T(8,128)(2,1)S(1)}, u32[]{:S(2)}, u32[]{:S(2)}) %collective-permute-start.2) | collective-permute-done | bytes 262176 | tf_op jit(solution)/shard_map/ppermute | solution.py:258
  24.5 0.1 fusion
  24.5 0.0 copy-start.14
  24.5 1.6 %collective-permute-start.3 = (bf16[128,1024]{1,0:T(8,128)(2,1)S(1)}, bf16[128,1024]{1,0:T(8,128)(2,1)S(1)}, u32[]{:S(2)}, u32[]{:S(2)}) collective-permute-start(bf16[128,1024]{1,0:T(8,128)(2,1)S(1)} %fusion), channel_id=1, source_target_pairs={{0,2},{2,0},{1,3},{3,1},{4,6},{6,4},{5,7},{7,5},{8,10},{10,8},{9,1... | collective-permute-start | bytes 786440 | tf_op jit(solution)/shard_map/ppermute | solution.py:263
  26.1 6.9 %collective-permute-done.3 = bf16[128,1024]{1,0:T(8,128)(2,1)S(1)} collective-permute-done((bf16[128,1024]{1,0:T(8,128)(2,1)S(1)}, bf16[128,1024]{1,0:T(8,128)(2,1)S(1)}, u32[]{:S(2)}, u32[]{:S(2)}) %collective-permute-start.3) | collective-permute-done | bytes 262176 | tf_op jit(solution)/shard_map/ppermute | solution.py:263
  33.0 0.9 %divide_convert_fusion.1.mine_ref = bf16[128,1024]{1,0:T(8,128)(2,1)} fusion(bf16[128,1024]{1,0:T(8,128)(2,1)S(1)} %collective-permute-done.3, f32[128,1024]{1,0:T(8,128)S(1)} %get-tuple-element.30, bf16[128,1024]{1,0:T(8,128)(2,1)S(1)} %collective-permute-done.2), kind=kLoop, calls=%fused_computation.2 | loop fusion | flops 1048576 | bytes 1310720 | tf_op jit(solution)/shard_map/convert_element_type | solution.py:267
  33.9 0.0 collective-permute-start.4
  33.9 1.7 %reshape.18 = bf16[256,324]{0,1:T(8,128)(2,1)} reshape(bf16[256,18,18]{0,2,1:T(8,128)(2,1)} %param.28) | data formatting | bytes 331776 | tf_op jit(solution)/shard_map/reshape | solution.py:294
  35.5 0.9 %pad_slice_fusion.1 = (bf16[336,128]{1,0:T(8,128)(2,1)S(1)}, bf16[336,128]{1,0:T(8,128)(2,1)S(1)}) fusion(bf16[324,256]{1,0:T(8,128)(2,1)} %bitcast.12), kind=kLoop, calls=%fused_computation.11 | loop fusion | bytes 337920 | tf_op jit(solution)/shard_map/jit(_roll_static)/slice | solution.py:296
  36.5 1.0 %maximum_select_fusion.1.wout_ref = bf16[336,256]{1,0:T(8,128)(2,1)S(1)} fusion(bf16[336,128]{1,0:T(8,128)(2,1)S(1)} %get-tuple-element.53, bf16[336,128]{1,0:T(8,128)(2,1)S(1)} %get-tuple-element.52, pred[]{:T(512)S(6)} %eq.4, bf16[324,256]{1,0:T(8,128)(2,1)} %bitcast.13), kind=kLoop, calls=%fused_computation.8 | loop fusion | flops 430080 | bytes 509953 | tf_op jit(solution)/shard_map/jit(_where)/select_n | solution.py:296
  37.5 1.3 %copy-done.1 = f32[336,1024]{1,0:T(8,128)S(1)} copy-done((f32[336,1024]{1,0:T(8,128)S(1)}, f32[336,1024]{1,0:T(8,128)}, u32[]{:S(2)}) %copy-start.1) | copy-done | bytes 1376280
  38.8 1.6 %shard_map.197 = (f32[336,1024]{1,0:T(8,128)S(1)}, bf16[336,256]{1,0:T(8,128)(2,1)S(1)}, bf16[336,256]{1,0:T(8,128)(2,1)S(1)}) custom-call(f32[336,1024]{1,0:T(8,128)S(1)} %copy-done.1, bf16[128,1024]{1,0:T(8,128)(2,1)} %divide_convert_fusion.1.mine_ref, bf16[128,1024]{1,0:T(8,128)(2,1)} %collective-permute-done.4.other_ref, ...), custom_call_target="tpu_custom_call" | custom-call | flops 176160768 | bytes 4194304 | tf_op jit(solution)/shard_map/pallas_call | solution.py:23
  40.4 2.9 %collective-permute-start.5 = (bf16[336,256]{1,0:T(8,128)(2,1)S(1)}, bf16[336,256]{1,0:T(8,128)(2,1)S(1)}, u32[]{:S(2)}, u32[]{:S(2)}) collective-permute-start(bf16[336,256]{1,0:T(8,128)(2,1)S(1)} %get-tuple-element.33), channel_id=1, source_target_pairs={{0,4},{4,8},{8,12},{1,5},{5,9},{9,13},{2,6},{6,10},{10,14},{3,7},{... | collective-permute-start | bytes 516104 | tf_op jit(solution)/shard_map/ppermute | solution.py:47
  43.3 1.5 %collective-permute-start.6 = (bf16[336,256]{1,0:T(8,128)(2,1)S(1)}, bf16[336,256]{1,0:T(8,128)(2,1)S(1)}, u32[]{:S(2)}, u32[]{:S(2)}) collective-permute-start(bf16[336,256]{1,0:T(8,128)(2,1)S(1)} %get-tuple-element.34), channel_id=1, source_target_pairs={{4,0},{8,4},{12,8},{5,1},{9,5},{13,9},{6,2},{10,6},{14,10},{7,3},{... | collective-permute-start | bytes 516104 | tf_op jit(solution)/shard_map/ppermute | solution.py:47
  44.8 2.8 %collective-permute-done.5.lower_ref = bf16[336,256]{1,0:T(8,128)(2,1)S(1)} collective-permute-done((bf16[336,256]{1,0:T(8,128)(2,1)S(1)}, bf16[336,256]{1,0:T(8,128)(2,1)S(1)}, u32[]{:S(2)}, u32[]{:S(2)}) %collective-permute-start.5) | collective-permute-done | bytes 172064 | tf_op jit(solution)/shard_map/ppermute | solution.py:47
  47.6 4.1 %collective-permute-done.6.upper_ref = bf16[336,256]{1,0:T(8,128)(2,1)S(1)} collective-permute-done((bf16[336,256]{1,0:T(8,128)(2,1)S(1)}, bf16[336,256]{1,0:T(8,128)(2,1)S(1)}, u32[]{:S(2)}, u32[]{:S(2)}) %collective-permute-start.6) | collective-permute-done | bytes 172064 | tf_op jit(solution)/shard_map/ppermute | solution.py:47
  51.7 2.3 %shard_map.198 = (f32[336,1024]{1,0:T(8,128)S(1)}, f32[128,1024]{1,0:T(8,128)S(1)}, bf16[128,1024]{1,0:T(8,128)(2,1)S(1)}) custom-call(f32[336,1024]{1,0:T(8,128)S(1)} %get-tuple-element.32.state_ref, bf16[336,256]{1,0:T(8,128)(2,1)S(1)} %collective-permute-done.5.lower_ref, bf16[336,256]{1,0:T(8,128)(2,1)S(1)} %collective-permute-done.6.upper_ref, ...), custom_call_target="tpu_custom_call" | custom-call | flops 1233125376 | bytes 4194304 | tf_op jit(solution)/shard_map/pallas_call | solution.py:23
  54.0 0.0 copy-start.9
  54.0 0.0 copy-start.10
  54.0 0.0 copy-start.11
  54.0 0.0 copy-start.12
  54.0 0.0 copy-start.15
  54.0 0.0 copy-start.16
  54.0 0.0 copy-start.17
  54.1 0.0 copy-start.18
  54.1 0.1 collective-permute-start.7
  54.1 1.5 %collective-permute-done.7 = bf16[128,1024]{1,0:T(8,128)(2,1)S(1)} collective-permute-done((bf16[128,1024]{1,0:T(8,128)(2,1)S(1)}, bf16[128,1024]{1,0:T(8,128)(2,1)S(1)}, u32[]{:S(2)}, u32[]{:S(2)}) %collective-permute-start.7) | collective-permute-done | bytes 262176 | tf_op jit(solution)/shard_map/ppermute | solution.py:258
  55.7 0.1 fusion.1
  55.7 1.6 %collective-permute-start.8 = (bf16[128,1024]{1,0:T(8,128)(2,1)S(1)}, bf16[128,1024]{1,0:T(8,128)(2,1)S(1)}, u32[]{:S(2)}, u32[]{:S(2)}) collective-permute-start(bf16[128,1024]{1,0:T(8,128)(2,1)S(1)} %fusion.1), channel_id=1, source_target_pairs={{0,2},{2,0},{1,3},{3,1},{4,6},{6,4},{5,7},{7,5},{8,10},{10,8},{9,1... | collective-permute-start | bytes 786440 | tf_op jit(solution)/shard_map/ppermute | solution.py:263
  57.3 6.9 %collective-permute-done.8 = bf16[128,1024]{1,0:T(8,128)(2,1)S(1)} collective-permute-done((bf16[128,1024]{1,0:T(8,128)(2,1)S(1)}, bf16[128,1024]{1,0:T(8,128)(2,1)S(1)}, u32[]{:S(2)}, u32[]{:S(2)}) %collective-permute-start.8) | collective-permute-done | bytes 262176 | tf_op jit(solution)/shard_map/ppermute | solution.py:263
  64.1 0.2 divide_convert_fusion.mine_ref
  64.3 0.1 collective-permute-start.9
  64.5 2.2 %shard_map.199 = (bf16[512,512]{1,0:T(8,128)(2,1)S(1)}, bf16[512,512]{1,0:T(8,128)(2,1)S(1)}, f32[2,512]{1,0:T(2,128)S(1)}, bf16[512,512]{1,0:T(8,128)(2,1)S(1)}, bf16[512,512]{1,0:T(8,128)(2,1)S(1)}) custom-call(s32[4,1,4,128]{3,2,1,0:T(4,128)S(1)} %copy-done.9, f32[4,1,4,128]{3,2,1,0:T(4,128)S(1)} %copy-done.10, s32[1,4]{1,0:T(1,128)S(1)} %copy-done.17, ...), custom_call_target="tpu_custom_call" | custom-call | bytes 4194304 | tf_op jit(solution)/shard_map/pallas_call | solution.py:23
  66.7 1.1 %shard_map.200 = (f32[336,1024]{1,0:T(8,128)S(1)}, bf16[336,256]{1,0:T(8,128)(2,1)S(1)}, bf16[336,256]{1,0:T(8,128)(2,1)S(1)}, bf16[336,256]{1,0:T(8,128)(2,1)S(1)}, bf16[336,256]{1,0:T(8,128)(2,1)S(1)}) custom-call(f32[336,1024]{1,0:T(8,128)S(1)} %get-tuple-element.35.moved_ref, bf16[128,1024]{1,0:T(8,128)(2,1)S(1)} %divide_convert_fusion.mine_ref, ...), custom_call_target="tpu_custom_call" | custom-call | flops 528482304 | bytes 4194304 | tf_op jit(solution)/shard_map/pallas_call | solution.py:23
  67.8 1.6 %collective-permute-start.10 = (bf16[336,256]{1,0:T(8,128)(2,1)S(1)}, bf16[336,256]{1,0:T(8,128)(2,1)S(1)}, u32[]{:S(2)}, u32[]{:S(2)}) collective-permute-start(bf16[336,256]{1,0:T(8,128)(2,1)S(1)} %get-tuple-element.45), channel_id=1, source_target_pairs={{0,4},{4,0},{8,12},{12,8},{1,5},{5,1},{9,13},{13,9},{2,6},{6,2},{1... | collective-permute-start | bytes 516104 | tf_op jit(solution)/shard_map/ppermute | solution.py:347
  69.4 2.8 %collective-permute-start.12 = (bf16[336,256]{1,0:T(8,128)(2,1)S(1)}, bf16[336,256]{1,0:T(8,128)(2,1)S(1)}, u32[]{:S(2)}, u32[]{:S(2)}) collective-permute-start(bf16[336,256]{1,0:T(8,128)(2,1)S(1)} %get-tuple-element.47), channel_id=1, source_target_pairs={{0,12},{4,8},{8,4},{12,0},{1,13},{5,9},{9,5},{13,1},{2,14},{6,10},... | collective-permute-start | bytes 516104 | tf_op jit(solution)/shard_map/ppermute | solution.py:347
  72.3 4.6 %collective-permute-done.10.rest_1_ = bf16[336,256]{1,0:T(8,128)(2,1)S(1)} collective-permute-done((bf16[336,256]{1,0:T(8,128)(2,1)S(1)}, bf16[336,256]{1,0:T(8,128)(2,1)S(1)}, u32[]{:S(2)}, u32[]{:S(2)}) %collective-permute-start.10) | collective-permute-done | bytes 172064 | tf_op jit(solution)/shard_map/ppermute | solution.py:347
  76.9 8.1 %collective-permute-done.11.rest_2_ = bf16[336,256]{1,0:T(8,128)(2,1)S(1)} collective-permute-done((bf16[336,256]{1,0:T(8,128)(2,1)S(1)}, bf16[336,256]{1,0:T(8,128)(2,1)S(1)}, u32[]{:S(2)}, u32[]{:S(2)}) %collective-permute-start.11) | collective-permute-done | bytes 172064 | tf_op jit(solution)/shard_map/ppermute | solution.py:347
  85.0 2.4 %shard_map.201 = (f32[1296,128]{1,0:T(8,128)}, f32[18,18,512]{2,1,0:T(8,128)}) custom-call(f32[336,1024]{1,0:T(8,128)S(1)} %get-tuple-element.41.state_ref, bf16[512,512]{1,0:T(8,128)(2,1)S(1)} %get-tuple-element.42.gland_ref, bf16[512,512]{1,0:T(8,128)(2,1)S(1)} %get-tuple-element.43.mland_ref, s32[4,128]{1,0:T(4,128)S(1)} %copy-done.6, ...), custom_call_target="tpu_custom_call" | custom-call | flops 352321536 | bytes 4194304 | tf_op jit(solution)/shard_map/pallas_call | solution.py:23
  (37 shorter events, 0.1 us)
Async XLA Ops:
  0.6 1.2 %copy-start.4 = (f32[18,18,512]{2,1,0:T(8,128)S(1)}, f32[18,18,512]{2,1,0:T(8,128)}, u32[]{:S(2)}) copy-start(f32[18,18,512]{2,1,0:T(8,128)} %mesh_ref.1) | copy-start | bytes 1990660
  1.8 1.1 %copy-start.5 = (f32[18,18,4,128]{3,2,1,0:T(4,128)S(1)}, f32[18,18,4,128]{3,2,1,0:T(4,128)}, u32[]{:S(2)}) copy-start(f32[18,18,4,128]{3,2,1,0:T(4,128)} %param.19) | copy-start | bytes 1990660
  2.9 0.7 copy-start.13
  3.6 9.2 %copy-start.23 = (bf16[18,18,256]{2,1,0:T(8,128)(2,1)S(1)}, bf16[18,18,256]{2,1,0:T(8,128)(2,1)}, u32[]{:S(2)}) copy-start(bf16[18,18,256]{2,1,0:T(8,128)(2,1)} %param.27) | copy-start | bytes 497668
  3.6 10.2 %copy-start.24 = (f32[4,512]{1,0:T(4,128)S(1)}, f32[4,512]{1,0:T(4,128)}, u32[]{:S(2)}) copy-start(f32[4,512]{1,0:T(4,128)} %param.24) | copy-start | bytes 24580
  3.6 10.2 %copy-start.25 = (f32[4,512]{1,0:T(4,128)S(1)}, f32[4,512]{1,0:T(4,128)}, u32[]{:S(2)}) copy-start(f32[4,512]{1,0:T(4,128)} %param.25) | copy-start | bytes 24580
  4.7 1.1 %copy-start.2 = (f32[336,1024]{1,0:T(8,128)}, f32[336,1024]{1,0:T(8,128)S(1)}, u32[]{:S(2)}) copy-start(f32[336,1024]{1,0:T(8,128)S(1)} %get-tuple-element.26.state_ref) | copy-start | bytes 4128772
  5.8 9.1 %copy-start.7 = (s32[4,512]{1,0:T(4,128)S(1)}, s32[4,512]{1,0:T(4,128)}, u32[]{:S(2)}) copy-start(s32[4,512]{1,0:T(4,128)} %index_ref.1) | copy-start | bytes 24580
  5.8 10.2 %collective-permute-start = (bf16[336,256]{1,0:T(8,128)(2,1)}, bf16[336,256]{1,0:T(8,128)(2,1)}, u32[]{:S(2)}, u32[]{:S(2)}) collective-permute-start(bf16[336,256]{1,0:T(8,128)(2,1)} %get-tuple-element.27), channel_id=1, source_target_pairs={{0,4},{4,8},{8,12},{1,5},{5,9},{9,13},{2,6},{6,10},{10,14},{3,7},{... | collective-permute-start | bytes 516104 | tf_op jit(solution)/shard_map/ppermute | solution.py:47
  11.5 8.0 %collective-permute-start.1 = (bf16[336,256]{1,0:T(8,128)(2,1)}, bf16[336,256]{1,0:T(8,128)(2,1)}, u32[]{:S(2)}, u32[]{:S(2)}) collective-permute-start(bf16[336,256]{1,0:T(8,128)(2,1)} %get-tuple-element.28), channel_id=1, source_target_pairs={{4,0},{8,4},{12,8},{5,1},{9,5},{13,9},{6,2},{10,6},{14,10},{7,3},{... | collective-permute-start | bytes 516104 | tf_op jit(solution)/shard_map/ppermute | solution.py:47
  13.1 1.8 %copy-start.19 = (bf16[324,256]{0,1:T(8,128)(2,1)}, bf16[324,256]{0,1:T(8,128)(2,1)S(1)}, u32[]{:S(2)}) copy-start(bf16[324,256]{0,1:T(8,128)(2,1)S(1)} %copy.22) | copy-start | bytes 497668
  14.9 0.9 %copy-start.20 = (bf16[324,256]{0,1:T(8,128)(2,1)S(1)}, bf16[324,256]{0,1:T(8,128)(2,1)}, u32[]{:S(2)}) copy-start(bf16[324,256]{0,1:T(8,128)(2,1)} %copy-done.19) | copy-start | bytes 497668
  14.9 1.0 %copy-start.21 = (bf16[128,336]{1,0:T(8,128)(2,1)S(1)}, bf16[128,336]{1,0:T(8,128)(2,1)}, u32[]{:S(2)}) copy-start(bf16[128,336]{1,0:T(8,128)(2,1)} %get-tuple-element.50) | copy-start | bytes 258052
  14.9 1.0 %copy-start.22 = (bf16[128,336]{1,0:T(8,128)(2,1)S(1)}, bf16[128,336]{1,0:T(8,128)(2,1)}, u32[]{:S(2)}) copy-start(bf16[128,336]{1,0:T(8,128)(2,1)} %get-tuple-element.51) | copy-start | bytes 258052
  14.9 4.7 %copy-start.3 = (f32[336,1024]{1,0:T(8,128)S(1)}, f32[336,1024]{1,0:T(8,128)}, u32[]{:S(2)}) copy-start(f32[336,1024]{1,0:T(8,128)} %copy-done.2) | copy-start | bytes 4128772
  14.9 4.6 %copy-start.6 = (s32[4,128]{1,0:T(4,128)S(1)}, s32[4,128]{1,0:T(4,128)}, u32[]{:S(2)}) copy-start(s32[4,128]{1,0:T(4,128)} %sea_ref.5) | copy-start | bytes 6148
  14.9 4.6 %copy-start.8 = (f32[4,128]{1,0:T(4,128)S(1)}, f32[4,128]{1,0:T(4,128)}, u32[]{:S(2)}) copy-start(f32[4,128]{1,0:T(4,128)} %speed_ref.3) | copy-start | bytes 6148
  22.8 11.0 %copy-start = (f32[336,1024]{1,0:T(8,128)}, f32[336,1024]{1,0:T(8,128)S(1)}, u32[]{:S(2)}) copy-start(f32[336,1024]{1,0:T(8,128)S(1)} %get-tuple-element.29.moved_ref) | copy-start | bytes 4128772
  22.9 1.6 %collective-permute-start.2 = (bf16[128,1024]{1,0:T(8,128)(2,1)S(1)}, bf16[128,1024]{1,0:T(8,128)(2,1)S(1)}, u32[]{:S(2)}, u32[]{:S(2)}) collective-permute-start(bf16[128,1024]{1,0:T(8,128)(2,1)S(1)} %get-tuple-element.31), channel_id=1, source_target_pairs={{0,1},{1,0},{2,3},{3,2},{4,5},{5,4},{6,7},{7,6},{8,9},{9,8},{10,11... | collective-permute-start | bytes 786440 | tf_op jit(solution)/shard_map/ppermute | solution.py:258
  24.5 12.9 %copy-start.14 = (s32[2,128]{1,0:T(2,128)S(1)}, s32[2,128]{1,0:T(2,128)}, u32[]{:S(2)}) copy-start(s32[2,128]{1,0:T(2,128)} %halo_ref.3) | copy-start | bytes 3076
  24.5 8.4 %collective-permute-start.3 = (bf16[128,1024]{1,0:T(8,128)(2,1)S(1)}, bf16[128,1024]{1,0:T(8,128)(2,1)S(1)}, u32[]{:S(2)}, u32[]{:S(2)}) collective-permute-start(bf16[128,1024]{1,0:T(8,128)(2,1)S(1)} %fusion), channel_id=1, source_target_pairs={{0,2},{2,0},{1,3},{3,1},{4,6},{6,4},{5,7},{7,5},{8,10},{10,8},{9,1... | collective-permute-start | bytes 786440 | tf_op jit(solution)/shard_map/ppermute | solution.py:263
  33.9 3.6 %collective-permute-start.4 = (bf16[128,1024]{1,0:T(8,128)(2,1)}, bf16[128,1024]{1,0:T(8,128)(2,1)}, u32[]{:S(2)}, u32[]{:S(2)}) collective-permute-start(bf16[128,1024]{1,0:T(8,128)(2,1)} %divide_convert_fusion.1.mine_ref), channel_id=1, source_target_pairs={{0,1},{1,0},{2,3},{3,2},{4,5},{5,4},{6,7},{7,6},{8,9},{9,8},{10,11... | collective-permute-start | bytes 786440 | tf_op jit(solution)/shard_map/ppermute | solution.py:268
  37.5 1.3 %copy-start.1 = (f32[336,1024]{1,0:T(8,128)S(1)}, f32[336,1024]{1,0:T(8,128)}, u32[]{:S(2)}) copy-start(f32[336,1024]{1,0:T(8,128)} %copy-done) | copy-start | bytes 4128772
  40.4 7.1 %collective-permute-start.5 = (bf16[336,256]{1,0:T(8,128)(2,1)S(1)}, bf16[336,256]{1,0:T(8,128)(2,1)S(1)}, u32[]{:S(2)}, u32[]{:S(2)}) collective-permute-start(bf16[336,256]{1,0:T(8,128)(2,1)S(1)} %get-tuple-element.33), channel_id=1, source_target_pairs={{0,4},{4,8},{8,12},{1,5},{5,9},{9,13},{2,6},{6,10},{10,14},{3,7},{... | collective-permute-start | bytes 516104 | tf_op jit(solution)/shard_map/ppermute | solution.py:47
  43.3 8.4 %collective-permute-start.6 = (bf16[336,256]{1,0:T(8,128)(2,1)S(1)}, bf16[336,256]{1,0:T(8,128)(2,1)S(1)}, u32[]{:S(2)}, u32[]{:S(2)}) collective-permute-start(bf16[336,256]{1,0:T(8,128)(2,1)S(1)} %get-tuple-element.34), channel_id=1, source_target_pairs={{4,0},{8,4},{12,8},{5,1},{9,5},{13,9},{6,2},{10,6},{14,10},{7,3},{... | collective-permute-start | bytes 516104 | tf_op jit(solution)/shard_map/ppermute | solution.py:47
  54.0 10.4 %copy-start.9 = (s32[4,1,4,128]{3,2,1,0:T(4,128)S(1)}, s32[4,1,4,128]{3,2,1,0:T(4,128)}, u32[]{:S(2)}) copy-start(s32[4,1,4,128]{3,2,1,0:T(4,128)} %gi_ref.1) | copy-start | bytes 24580
  54.0 10.4 %copy-start.10 = (f32[4,1,4,128]{3,2,1,0:T(4,128)S(1)}, f32[4,1,4,128]{3,2,1,0:T(4,128)}, u32[]{:S(2)}) copy-start(f32[4,1,4,128]{3,2,1,0:T(4,128)} %gw_ref.1) | copy-start | bytes 24580
  54.0 10.4 %copy-start.11 = (s32[3,1,4,128]{3,2,1,0:T(4,128)S(1)}, s32[3,1,4,128]{3,2,1,0:T(4,128)}, u32[]{:S(2)}) copy-start(s32[3,1,4,128]{3,2,1,0:T(4,128)} %mi_ref.1) | copy-start | bytes 18436
  54.0 10.4 %copy-start.12 = (f32[3,1,4,128]{3,2,1,0:T(4,128)S(1)}, f32[3,1,4,128]{3,2,1,0:T(4,128)}, u32[]{:S(2)}) copy-start(f32[3,1,4,128]{3,2,1,0:T(4,128)} %mw_ref.1) | copy-start | bytes 18436
  54.0 10.4 %copy-start.15 = (s32[1,4,128]{2,1,0:T(4,128)S(1)}, s32[1,4,128]{2,1,0:T(4,128)}, u32[]{:S(2)}) copy-start(s32[1,4,128]{2,1,0:T(4,128)} %gt_ref.1) | copy-start | bytes 6148
  54.0 10.4 %copy-start.16 = (s32[1,4,128]{2,1,0:T(4,128)S(1)}, s32[1,4,128]{2,1,0:T(4,128)}, u32[]{:S(2)}) copy-start(s32[1,4,128]{2,1,0:T(4,128)} %mt_ref.1) | copy-start | bytes 6148
  54.0 10.4 %copy-start.17 = (s32[1,4]{1,0:T(1,128)S(1)}, s32[1,4]{1,0:T(1,128)}, u32[]{:S(2)}) copy-start(s32[1,4]{1,0:T(1,128)} %gc_ref.1) | copy-start | bytes 52
  54.1 10.4 %copy-start.18 = (s32[1,4]{1,0:T(1,128)S(1)}, s32[1,4]{1,0:T(1,128)}, u32[]{:S(2)}) copy-start(s32[1,4]{1,0:T(1,128)} %mc_ref.1) | copy-start | bytes 52
  54.1 1.6 %collective-permute-start.7 = (bf16[128,1024]{1,0:T(8,128)(2,1)S(1)}, bf16[128,1024]{1,0:T(8,128)(2,1)S(1)}, u32[]{:S(2)}, u32[]{:S(2)}) collective-permute-start(bf16[128,1024]{1,0:T(8,128)(2,1)S(1)} %get-tuple-element.37), channel_id=1, source_target_pairs={{0,1},{1,0},{2,3},{3,2},{4,5},{5,4},{6,7},{7,6},{8,9},{9,8},{10,11... | collective-permute-start | bytes 786440 | tf_op jit(solution)/shard_map/ppermute | solution.py:258
  55.7 8.4 %collective-permute-start.8 = (bf16[128,1024]{1,0:T(8,128)(2,1)S(1)}, bf16[128,1024]{1,0:T(8,128)(2,1)S(1)}, u32[]{:S(2)}, u32[]{:S(2)}) collective-permute-start(bf16[128,1024]{1,0:T(8,128)(2,1)S(1)} %fusion.1), channel_id=1, source_target_pairs={{0,2},{2,0},{1,3},{3,1},{4,6},{6,4},{5,7},{7,5},{8,10},{10,8},{9,1... | collective-permute-start | bytes 786440 | tf_op jit(solution)/shard_map/ppermute | solution.py:263
  64.3 2.3 %collective-permute-start.9 = (bf16[128,1024]{1,0:T(8,128)(2,1)S(1)}, bf16[128,1024]{1,0:T(8,128)(2,1)S(1)}, u32[]{:S(2)}, u32[]{:S(2)}) collective-permute-start(bf16[128,1024]{1,0:T(8,128)(2,1)S(1)} %divide_convert_fusion.mine_ref), channel_id=1, source_target_pairs={{0,1},{1,0},{2,3},{3,2},{4,5},{5,4},{6,7},{7,6},{8,9},{9,8},{10,11... | collective-permute-start | bytes 786440 | tf_op jit(solution)/shard_map/ppermute | solution.py:268
  67.8 9.1 %collective-permute-start.10 = (bf16[336,256]{1,0:T(8,128)(2,1)S(1)}, bf16[336,256]{1,0:T(8,128)(2,1)S(1)}, u32[]{:S(2)}, u32[]{:S(2)}) collective-permute-start(bf16[336,256]{1,0:T(8,128)(2,1)S(1)} %get-tuple-element.45), channel_id=1, source_target_pairs={{0,4},{4,0},{8,12},{12,8},{1,5},{5,1},{9,13},{13,9},{2,6},{6,2},{1... | collective-permute-start | bytes 516104 | tf_op jit(solution)/shard_map/ppermute | solution.py:347
  69.4 15.5 %collective-permute-start.11 = (bf16[336,256]{1,0:T(8,128)(2,1)S(1)}, bf16[336,256]{1,0:T(8,128)(2,1)S(1)}, u32[]{:S(2)}, u32[]{:S(2)}) collective-permute-start(bf16[336,256]{1,0:T(8,128)(2,1)S(1)} %get-tuple-element.46), channel_id=1, source_target_pairs={{0,8},{4,12},{8,0},{12,4},{1,9},{5,13},{9,1},{13,5},{2,10},{6,14},... | collective-permute-start | bytes 516104 | tf_op jit(solution)/shard_map/ppermute | solution.py:347
  69.4 15.5 %collective-permute-start.12 = (bf16[336,256]{1,0:T(8,128)(2,1)S(1)}, bf16[336,256]{1,0:T(8,128)(2,1)S(1)}, u32[]{:S(2)}, u32[]{:S(2)}) collective-permute-start(bf16[336,256]{1,0:T(8,128)(2,1)S(1)} %get-tuple-element.47), channel_id=1, source_target_pairs={{0,12},{4,8},{8,4},{12,0},{1,13},{5,9},{9,5},{13,1},{2,14},{6,10},... | collective-permute-start | bytes 516104 | tf_op jit(solution)/shard_map/ppermute | solution.py:347

commit v2 on v1

--- a/solution.py
+++ b/solution.py
@@ -16,17 +16,20 @@
 CHUNK = 16
 
 
-def kernel_call(body, outs, scratch=(), flops=0, nbytes=4 << 20):
-    spec = pl.BlockSpec(memory_space=pltpu.VMEM)
-
+VMEM = pltpu.MemorySpace.VMEM
+HBM = pltpu.MemorySpace.HBM
+
+
+def kernel_call(body, outs, scratch=(), flops=0, nbytes=2 << 20, spaces=None):
     def run(*args):
+        where = spaces or [VMEM] * len(args)
         return pl.pallas_call(
             body,
             out_shape=[jax.ShapeDtypeStruct(s, t) for s, t in outs],
-            in_specs=[spec] * len(args),
-            out_specs=[spec] * len(outs),
-            scratch_shapes=[pltpu.VMEM(s, t) for s, t in scratch],
-            compiler_params=pltpu.CompilerParams(vmem_limit_bytes=24 << 20),
+            in_specs=[pl.BlockSpec(memory_space=space) for space in where],
+            out_specs=[pl.BlockSpec(memory_space=VMEM)] * len(outs),
+            scratch_shapes=[s if hasattr(s, "dtype") else pltpu.VMEM(*s) for s in scratch],
+            compiler_params=pltpu.CompilerParams(vmem_limit_bytes=16 << 20),
             cost_estimate=pl.CostEstimate(flops=flops, bytes_accessed=nbytes, transcendentals=0),
         )(*args)
 
@@ -42,9 +45,10 @@
     return jnp.where(spots == row, 1.0, 0.0).astype(BF16)
 
 
-def shift(array, axis, by):
+def pair_swap(array, axis, first):
     size = lax.axis_size(axis)
-    return lax.ppermute(array, axis, [(i, i + by) for i in range(size) if 0 <= i + by < size])
+    pairs = [(i, i + 1) for i in range(first, size - 1, 2)]
+    return lax.ppermute(array, axis, pairs + [(j, i) for i, j in pairs])
 
 
 def peer_pairs(size, step):
@@ -59,77 +63,175 @@
     return lax.rem(step - me + size, size)
 
 
-def messages(state_ref, halo_ref, up_ref, down_ref, grid_points, cols):
-    nodes = state_ref.shape[1] - grid_points
-    listed = halo_ref.shape[1]
-    mesh = state_ref[:, grid_points:].astype(BF16)
-    for msg, row, which in ((up_ref, grid_points - cols, 1), (down_ref, 0, 0)):
-        msg[:, :cols] = state_ref[:, row : row + cols].astype(BF16)
-        picked = dot(mesh, one_hot(halo_ref[which : which + 1, :], nodes))
-        msg[:, cols : cols + listed] = picked.astype(BF16)
-
-
-def begin_kernel(grid_ref, mesh_ref, halo_ref, state_ref, up_ref, down_ref, *, rows, cols):
-    freqs, dirs, _ = mesh_ref.shape
-    bands = freqs * dirs
-    gp = rows * cols
-    padded = state_ref.shape[0]
-    state_ref[bands:, :] = jnp.zeros((padded - bands, state_ref.shape[1]), F32)
-    for x in range(rows):
-        state_ref[:bands, x * cols : (x + 1) * cols] = grid_ref[pl.ds(x, bands, stride=rows), :]
+def on_even():
+    return lax.rem(lax.axis_index("sp"), 2) == 0
+
+
+def messages(mesh, low_row, high_row, halo_ref, even_ref, odd_ref):
+    even = on_even()
+    nodes = mesh.shape[1]
+    cols = low_row.shape[1]
+    to_lower = dot(mesh, one_hot(halo_ref[0:1, :], nodes)).astype(BF16)
+    to_upper = dot(mesh, one_hot(halo_ref[1:2, :], nodes)).astype(BF16)
+    even_ref[:, :cols] = jnp.where(even, high_row, low_row)
+    odd_ref[:, :cols] = jnp.where(even, low_row, high_row)
+    even_ref[:, cols:] = jnp.where(even, to_upper, to_lower)
+    odd_ref[:, cols:] = jnp.where(even, to_lower, to_upper)
+
+
+def pack_rows(source_ref, packed_ref, at):
+    freqs, dirs, width = source_ref.shape
     for f in range(freqs):
-        state_ref[f * dirs : (f + 1) * dirs, gp:] = mesh_ref[f]
-    messages(state_ref, halo_ref, up_ref, down_ref, gp, cols)
-
-
-def hot_kernel(index_ref, hot_ref):
-    for k in range(index_ref.shape[0]):
-        hot_ref[k] = one_hot(index_ref[k : k + 1, :], hot_ref.shape[1])
-
-
-def move_kernel(
-    state_ref, lower_ref, upper_ref, hot_ref, pq_ref, band_ref, sea_ref, speed_ref, win_ref,
-    moved_ref, keep_ref, send_ref, ext_ref, near_ref, feat_ref,
-):
-    padded, points = state_ref.shape
+        packed_ref[f * dirs : (f + 1) * dirs, at : at + width] = source_ref[f].astype(F32)
+    packed_ref[freqs * dirs :, at : at + width] = jnp.zeros(
+        (packed_ref.shape[0] - freqs * dirs, width), F32
+    )
+
+
+def begin_kernel(
+    grid_hbm, mesh_hbm, halo_hbm, even_ref, odd_ref, grid_ref, mesh_ref, halo_ref, packed_ref, sem,
+    *, rows,
+):
+    copies = [
+        pltpu.make_async_copy(halo_hbm, halo_ref, sem.at[0]),
+        pltpu.make_async_copy(mesh_hbm, mesh_ref, sem.at[1]),
+        pltpu.make_async_copy(grid_hbm, grid_ref, sem.at[2]),
+    ]
+    for copy in copies:
+        copy.start()
+    bands = grid_ref.shape[0] // rows
+    blank = jnp.zeros((packed_ref.shape[0] - bands, grid_ref.shape[1]), F32)
+    copies[0].wait()
+    copies[1].wait()
+    pack_rows(mesh_ref, packed_ref, 0)
+    copies[2].wait()
+    low = jnp.concatenate([grid_ref[pl.ds(0, bands, stride=rows), :], blank], axis=0)
+    high = jnp.concatenate([grid_ref[pl.ds(rows - 1, bands, stride=rows), :], blank], axis=0)
+    messages(
+        packed_ref[...].astype(BF16), low.astype(BF16), high.astype(BF16), halo_ref, even_ref, odd_ref
+    )
+
+
+def own_grid(state_ref, band_ref, sea_ref, speed_ref, part_ref):
     rows, cols = sea_ref.shape
-    gp = rows * cols
-    nodes = points - gp
-    neighbours = hot_ref.shape[0]
-    listed = lower_ref.shape[1] - cols
-    ext_ref[:, :nodes] = state_ref[:, gp:].astype(BF16)
-    ext_ref[:, nodes : nodes + listed] = lower_ref[:, cols:]
-    ext_ref[:, nodes + listed :] = upper_ref[:, cols:]
-    for k in range(neighbours):
-        near_ref[k] = dot(ext_ref[...], hot_ref[k])
     sea = sea_ref[...].astype(F32)
     lane = lax.broadcasted_iota(jnp.int32, (CHUNK, cols), 1)
-    for c in range(padded // CHUNK):
+    for c in range(state_ref.shape[0] // CHUNK):
         here = slice(c * CHUNK, (c + 1) * CHUNK)
         cx = band_ref[here, 0:1]
         cy = band_ref[here, 1:2]
         for x in range(rows):
             g = state_ref[here, x * cols : (x + 1) * cols]
-            if x == 0:
-                low = lower_ref[here, :cols].astype(F32)
-            else:
-                low = state_ref[here, (x - 1) * cols : x * cols]
-            if x == rows - 1:
-                high = upper_ref[here, :cols].astype(F32)
-            else:
-                high = state_ref[here, (x + 1) * cols : (x + 2) * cols]
+            low = 0.0 if x == 0 else state_ref[here, (x - 1) * cols : x * cols]
+            high = 0.0 if x == rows - 1 else state_ref[here, (x + 1) * cols : (x + 2) * cols]
             west = jnp.where(lane == 0, 0.0, pltpu.roll(g, 1, 1))
             east = jnp.where(lane == cols - 1, 0.0, pltpu.roll(g, cols - 1, 1))
             out = g - jnp.abs(cx) * speed_ref[x : x + 1, :] * (g - jnp.where(cx > 0, low, high))
             out = out - jnp.abs(cy) * speed_ref[x : x + 1, :] * (g - jnp.where(cy > 0, west, east))
-            out = out * sea[x : x + 1, :]
-            moved_ref[here, x * cols : (x + 1) * cols] = out
-            feat_ref[here, x * cols : (x + 1) * cols] = out.astype(BF16)
+            part_ref[here, x * cols : (x + 1) * cols] = out * sea[x : x + 1, :]
+
+
+def own_mesh(state_ref, hot_ref, weight_ref, part_ref, near_ref):
+    neighbours, padded, nodes = weight_ref.shape
+    gp = state_ref.shape[1] - nodes
+    mesh = state_ref[:, gp:].astype(BF16)
+    for k in range(neighbours):
+        near_ref[k] = dot(mesh, hot_ref[k, :nodes, :])
+    for c in range(padded // CHUNK):
+        here = slice(c * CHUNK, (c + 1) * CHUNK)
         e = state_ref[here, gp:]
         out = e
         for k in range(neighbours):
+            out = out + weight_ref[k, here, :] * (near_ref[k, here, :] - e)
+        part_ref[here, gp:] = out
+
+
+def prepare_kernel(
+    grid_hbm, mesh_hbm, table_hbm, win_hbm, wout_hbm, index_ref, pq_ref, sea_ref, speed_ref,
+    part_ref, hot_ref, weight_ref, band_ref, win_ref, wout_ref,
+    grid_ref, mesh_ref, layer_ref, state_ref, near_ref, pack_ref, sem,
+):
+    fr, dr = lax.axis_index("fr"), lax.axis_index("dr")
+    rows, cols = sea_ref.shape
+    gp = rows * cols
+    padded = state_ref.shape[0]
+    bands = grid_ref.shape[0] // rows
+    copies = [
+        pltpu.make_async_copy(table_hbm.at[fr, dr], band_ref, sem.at[0]),
+        pltpu.make_async_copy(mesh_hbm, mesh_ref, sem.at[1]),
+        pltpu.make_async_copy(grid_hbm, grid_ref, sem.at[2]),
+        pltpu.make_async_copy(win_hbm, layer_ref.at[0], sem.at[3]),
+        pltpu.make_async_copy(wout_hbm, layer_ref.at[1], sem.at[4]),
+    ]
+    for copy in copies:
+        copy.start()
+    neighbours = index_ref.shape[0]
+    for k in range(neighbours):
+        hot_ref[k] = one_hot(index_ref[k : k + 1, :], hot_ref.shape[1])
+    copies[0].wait()
+    for c in range(padded // CHUNK):
+        here = slice(c * CHUNK, (c + 1) * CHUNK)
+        cx = band_ref[here, 0:1]
+        cy = band_ref[here, 1:2]
+        for k in range(neighbours):
             w = cx * pq_ref[k : k + 1, :] + cy * pq_ref[neighbours + k : neighbours + k + 1, :]
-            out = out + jnp.maximum(w, 0.0) * (near_ref[k, here, :] - e)
+            weight_ref[k, here, :] = jnp.maximum(w, 0.0)
+    copies[1].wait()
+    pack_rows(mesh_ref, state_ref, gp)
+    own_mesh(state_ref, hot_ref, weight_ref, part_ref, near_ref)
+    copies[2].wait()
+    state_ref[bands:, :gp] = jnp.zeros((padded - bands, gp), F32)
+    for x in range(rows):
+        state_ref[:bands, x * cols : (x + 1) * cols] = grid_ref[pl.ds(x, bands, stride=rows), :]
+    own_grid(state_ref, band_ref, sea_ref, speed_ref, part_ref)
+    half = pack_ref.shape[1] // 2
+    copies[3].wait()
+    pack_rows(layer_ref.at[0], pack_ref, 0)
+    one, two = pack_ref[:, :half].T.astype(BF16), pack_ref[:, half:].T.astype(BF16)
+    win_ref[:half, :] = jnp.where(dr == 0, one, two)
+    win_ref[half:, :] = jnp.where(dr == 0, two, one)
+    copies[4].wait()
+    pack_rows(layer_ref.at[1], pack_ref, 0)
+    one, two = pack_ref[:, :half].astype(BF16), pack_ref[:, half:].astype(BF16)
+    wout_ref[:, :half] = jnp.where(dr == 0, one, two)
+    wout_ref[:, half:] = jnp.where(dr == 0, two, one)
+
+
+def own_kernel(state_ref, hot_ref, weight_ref, band_ref, sea_ref, speed_ref, part_ref, near_ref):
+    own_mesh(state_ref, hot_ref, weight_ref, part_ref, near_ref)
+    own_grid(state_ref, band_ref, sea_ref, speed_ref, part_ref)
+
+
+def halo_kernel(
+    part_ref, even_ref, odd_ref, hot_ref, weight_ref, band_ref, sea_ref, speed_ref, win_ref,
+    moved_ref, keep_ref, send_ref, ext_ref, near_ref, feat_ref,
+):
+    neighbours, padded, nodes = weight_ref.shape
+    rows, cols = sea_ref.shape
+    gp = rows * cols
+    listed = even_ref.shape[1] - cols
+    even = on_even()
+    ext_ref[:, :listed] = jnp.where(even, odd_ref[:, cols:], even_ref[:, cols:])
+    ext_ref[:, listed:] = jnp.where(even, even_ref[:, cols:], odd_ref[:, cols:])
+    for k in range(neighbours):
+        near_ref[k] = dot(ext_ref[...], hot_ref[k, nodes:, :])
+    scale = sea_ref[...].astype(F32) * speed_ref[...]
+    for c in range(padded // CHUNK):
+        here = slice(c * CHUNK, (c + 1) * CHUNK)
+        cx = band_ref[here, 0:1]
+        a, b = even_ref[here, :cols].astype(F32), odd_ref[here, :cols].astype(F32)
+        for x in range(rows):
+            cut = slice(x * cols, (x + 1) * cols)
+            out = part_ref[here, cut]
+            if x == 0:
+                out = out + jnp.maximum(cx, 0.0) * scale[x : x + 1, :] * jnp.where(even, b, a)
+            if x == rows - 1:
+                out = out + jnp.maximum(-cx, 0.0) * scale[x : x + 1, :] * jnp.where(even, a, b)
+            moved_ref[here, cut] = out
+            feat_ref[here, cut] = out.astype(BF16)
+        out = part_ref[here, gp:]
+        for k in range(neighbours):
+            out = out + weight_ref[k, here, :] * near_ref[k, here, :]
         moved_ref[here, gp:] = out
         feat_ref[here, gp:] = out.astype(BF16)
     half = keep_ref.shape[0]
@@ -145,15 +247,22 @@
 
 
 def next_kernel(
-    moved_ref, mine_ref, other_ref, wout_ref, halo_ref, state_ref, up_ref, down_ref, hid_ref,
+    moved_ref, mine_ref, other_ref, wout_ref, halo_ref, state_ref, even_ref, odd_ref, hid_ref,
     *, grid_points, cols,
 ):
     add_transfer(moved_ref, mine_ref, other_ref, wout_ref, hid_ref, state_ref)
-    messages(state_ref, halo_ref, up_ref, down_ref, grid_points, cols)
+    messages(
+        state_ref[:, grid_points:].astype(BF16),
+        state_ref[:, :cols].astype(BF16),
+        state_ref[:, grid_points - cols : grid_points].astype(BF16),
+        halo_ref,
+        even_ref,
+        odd_ref,
+    )
 
 
 def slots_kernel(
-    gi_ref, gw_ref, gc_ref, gt_ref, mi_ref, mw_ref, mc_ref, mt_ref,
+    gi_ref, gw_ref, gc_ref, gt_ref, mi_ref, mw_ref, mc_ref, mt_ref, after_ref,
     gmix_ref, mmix_ref, sums_ref, gland_ref, mland_ref,
 ):
     me = lax.axis_index("sp")
@@ -254,18 +363,19 @@
     return table
 
 
-def reduce_hidden(keep, send):
-    got = lax.ppermute(send, "dr", [(0, 1), (1, 0)])
-    total = keep + got.astype(F32)
+def core_swap(array):
+    return lax.ppermute(array, "dr", [(0, 1), (1, 0)])
+
+
+def fr_swap(array, step):
     size = lax.axis_size("fr")
-    step = 1
-    while step < size:
-        total = total + lax.ppermute(
-            total.astype(BF16), "fr", [(i, i ^ step) for i in range(size)]
-        ).astype(F32)
-        step *= 2
-    hidden = (total / (1.0 + jnp.exp(-total))).astype(BF16)
-    return hidden, lax.ppermute(hidden, "dr", [(0, 1), (1, 0)])
+    return lax.ppermute(array, "fr", [(i, i ^ step) for i in range(size)])
+
+
+def silu_kernel(total_ref, got_ref, *rest):
+    out_ref = rest[-1]
+    total = total_ref[...] + got_ref[...].astype(F32)
+    out_ref[...] = (total / (1.0 + jnp.exp(-total))).astype(BF16)
 
 
 def per_device(
@@ -284,53 +394,103 @@
     neighbours = nb_index.shape[0]
     peers, cap = g2m_index.shape[2:]
     n_fr, n_dr = lax.axis_size("fr"), lax.axis_size("dr")
-    dr = lax.axis_index("dr")
-
-    table = jnp.asarray(band_table(freqs, dirs, n_fr, n_dr, padded))
-    band = table[lax.axis_index("fr"), dr]
-    pq = jnp.concatenate([-nb_coef * jnp.cos(nb_angle), -nb_coef * jnp.sin(nb_angle)], axis=0)
-    pad = ((0, padded - bands), (0, 0))
-    win = jnp.pad(w_in.reshape(bands, hid), pad).T
-    wout = jnp.pad(w_out.reshape(hid, bands).T, pad)
-    win = jnp.where(dr == 0, win, jnp.roll(win, half, axis=0))
-    wout = jnp.where(dr == 0, wout, jnp.roll(wout, half, axis=1))
 
     message = ((padded, cols + listed), BF16)
     state_shape = ((padded, points), F32)
+    half_shape = (half, points)
     hid_scratch = ((hid, points), BF16)
-    state, up, down = kernel_call(
-        functools.partial(begin_kernel, rows=rows, cols=cols),
-        [state_shape, message, message],
+    near_scratch = ((neighbours, padded, nodes), F32)
+    grid_flat = grid_spec.reshape(bands * rows, cols)
+    even, odd = kernel_call(
+        functools.partial(begin_kernel, rows=rows),
+        [message, message],
+        [
+            (grid_flat.shape, F32),
+            (mesh_spec.shape, F32),
+            (halo_list.shape, jnp.int32),
+            ((padded, nodes), F32),
+            pltpu.SemaphoreType.DMA((3,)),
+        ],
         flops=2 * padded * nodes * 2 * listed,
-    )(grid_spec.reshape(bands * rows, cols), mesh_spec, halo_list)
-    (hot,) = kernel_call(hot_kernel, [((neighbours, nodes + 2 * listed, nodes), BF16)])(nb_index)
-    gmix, mmix, sums, gland, mland = kernel_call(
-        slots_kernel,
-        [
-            ((gp, peers * cap), BF16),
-            ((nodes, peers * cap), BF16),
-            ((2, peers * cap), F32),
-            ((nodes, peers * cap), BF16),
-            ((gp, peers * cap), BF16),
-        ],
-    )(g2m_index, g2m_weight, g2m_count, g2m_target, m2g_index, m2g_weight, m2g_count, m2g_target)
-
+        spaces=[HBM] * 3,
+    )(grid_flat, mesh_spec, halo_list)
+
+    table = jnp.asarray(band_table(freqs, dirs, n_fr, n_dr, padded))
+    pq = jnp.concatenate([-nb_coef * jnp.cos(nb_angle), -nb_coef * jnp.sin(nb_angle)], axis=0)
     for substep in range(NSUB):
-        lower = shift(up, "sp", 1)
-        upper = shift(down, "sp", -1)
-        moved, keep, send = kernel_call(
-            move_kernel,
-            [state_shape, ((half, points), F32), ((half, points), BF16)],
-            [
-                ((padded, nodes + 2 * listed), BF16),
-                ((neighbours, padded, nodes), F32),
-                ((padded, points), BF16),
-            ],
-            flops=2 * padded * (neighbours * nodes * (nodes + 2 * listed) + hid * points),
-        )(state, lower, upper, hot, pq, band, grid_sea, grid_speed, win)
-        mine, other = reduce_hidden(keep, send)
+        from_even = pair_swap(even, "sp", 0)
+        from_odd = pair_swap(odd, "sp", 1)
+        own_flops = 2 * padded * neighbours * nodes * nodes
+        if substep == 0:
+            part, hot, weight, band, win, wout = kernel_call(
+                prepare_kernel,
+                [
+                    state_shape,
+                    ((neighbours, nodes + 2 * listed, nodes), BF16),
+                    near_scratch,
+                    ((padded, 2), F32),
+                    ((hid, padded), BF16),
+                    ((padded, hid), BF16),
+                ],
+                [
+                    (grid_flat.shape, F32),
+                    (mesh_spec.shape, F32),
+                    ((2,) + w_in.shape, BF16),
+                    state_shape,
+                    near_scratch,
+                    ((padded, hid), F32),
+                    pltpu.SemaphoreType.DMA((5,)),
+                ],
+                flops=3 * own_flops,
+                spaces=[HBM] * 5 + [VMEM] * 4,
+            )(
+                grid_flat, mesh_spec, table, w_in, jnp.transpose(w_out, (1, 2, 0)),
+                nb_index, pq, grid_sea, grid_speed,
+            )
+        else:
+            (part,) = kernel_call(own_kernel, [state_shape], [near_scratch], flops=own_flops)(
+                state, hot, weight, band, grid_sea, grid_speed
+            )
+        moved, total, send = kernel_call(
+            halo_kernel,
+            [state_shape, (half_shape, F32), (half_shape, BF16)],
+            [((padded, 2 * listed), BF16), near_scratch, ((padded, points), BF16)],
+            flops=2 * padded * (neighbours * nodes * 2 * listed + hid * points),
+        )(part, from_even, from_odd, hot, weight, band, grid_sea, grid_speed, win)
+
+        total = total + core_swap(send).astype(F32)
+        rounded = total.astype(BF16)
+        got = fr_swap(rounded, 1)
+        step = 2
+        while step < n_fr:
+            total = total + got.astype(F32)
+            rounded = total.astype(BF16)
+            got = fr_swap(rounded, step)
+            step *= 2
+        extra = []
+        if substep == 0:
+            gmix, mmix, sums, gland, mland = kernel_call(
+                slots_kernel,
+                [
+                    ((gp, peers * cap), BF16),
+                    ((nodes, peers * cap), BF16),
+                    ((2, peers * cap), F32),
+                    ((nodes, peers * cap), BF16),
+                    ((gp, peers * cap), BF16),
+                ],
+                flops=2 << 30,
+                spaces=[VMEM] * 8 + [pl.ANY],
+            )(
+                g2m_index, g2m_weight, g2m_count, g2m_target,
+                m2g_index, m2g_weight, m2g_count, m2g_target, rounded,
+            )
+            extra = [sums]
+        (mine,) = kernel_call(
+            silu_kernel, [(half_shape, BF16)], spaces=[VMEM, VMEM] + [pl.ANY] * len(extra)
+        )(total, got, *extra)
+        other = core_swap(mine)
         if substep < NSUB - 1:
-            state, up, down = kernel_call(
+            state, even, odd = kernel_call(
                 functools.partial(next_kernel, grid_points=gp, cols=cols),
                 [state_shape, message, message],
                 [hid_scratch],

time: 88.4 us -> 71.8 us (0.81)
  local copies, waits for them, and re-layouts: 10.3 us -> 3.02 us
  waiting for transfers between devices: 40 us -> 32.9 us
  other arithmetic: 2.31 us -> 0.24 us
  Pallas kernels: 14.6 us -> 15.7 us
    ppermute x10, waiting for transfers between devices: 27.2 us -> 19.8 us  [the longest x2 11.5 us: fr_swap(): return lax.ppermute(array, 'fr', [(i, i ^ step) for i in range(size)])]
    unnamed x52 -> x40, local copies, waits for them, and re-layouts: 5.83 us -> 3.02 us
    ppermute x10, starting transfers between devices: 14.7 us -> 12.4 us  [the longest x4 9.04 us: pair_swap(): return lax.ppermute(array, axis, pairs + [(j, i) for i, j in pairs])]
    reshape x3 -> x0, local copies, waits for them, and re-layouts: 1.88 us -> none  [the longest x1 1.66 us: per_device(): wout = jnp.pad(w_out.reshape(hid, bands).T, pad)]
    ppermute x3, starting transfers between devices: 4.45 us -> 6.15 us  [per_device(): lax.ppermute(v, 'sp', peer_pairs(peers, p))]
    slice x2 -> x0, local copies, waits for them, and re-layouts: 1.65 us -> none  [the longest x1 0.94 us: per_device(): wout = jnp.where(dr == 0, wout, jnp.roll(wout, half, axis=1))]
    pallas_call x8 -> x11, Pallas kernels: 14.6 us -> 15.7 us  [run(): pl.pallas_call(body, out_shape=[jax.ShapeDtypeStruct(s, t) for s, t in ou...]
    select_n x2 -> x0, other arithmetic: 1.03 us -> none  [the longest x1 0.97 us: per_device(): wout = jnp.where(dr == 0, wout, jnp.roll(wout, half, axis=1))]
  transfers between devices with their start and end apart: 13 -> 13, of which waited for: 9 -> 9; matrix products, arithmetic and copies ran while one was open for 6% -> 0% of each run, Pallas kernels for 3% -> 11%
where the time goes in v2:
time: 71.8 us; the launch traced here: 71.5 us
  waiting for transfers between devices  32.9 us (46%)
  starting transfers between devices  18.6 us (26%)
  Pallas kernels  15.7 us (22%)
  local copies, waits for them, and re-layouts  3.02 us (4%)
  between operations  1.01 us (1%)
    pallas_call x11, Pallas kernels, run(): pl.pallas_call(body, out_shape=[jax.ShapeDtypeStruct(s, t) for s, t in ou...  15.7 us
    ppermute x3, waiting for transfers between devices, per_device(): lax.ppermute(v, 'sp', peer_pairs(peers, p))  13.1 us
    ppermute x2, waiting for transfers between devices, fr_swap(): return lax.ppermute(array, 'fr', [(i, i ^ step) for i in range(size)])  11.5 us
    ppermute x4, starting transfers between devices, pair_swap(): return lax.ppermute(array, axis, pairs + [(j, i) for i, j in pairs])  9.04 us
    ppermute x3, starting transfers between devices, per_device(): lax.ppermute(v, 'sp', peer_pairs(peers, p))  6.15 us
    ppermute x4, waiting for transfers between devices, core_swap(): return lax.ppermute(array, 'dr', [(0, 1), (1, 0)])  6.09 us
    ppermute x2, starting transfers between devices, fr_swap(): return lax.ppermute(array, 'fr', [(i, i ^ step) for i in range(size)])  3.11 us
    unnamed x40, local copies, waits for them, and re-layouts  3.02 us
  transfers between devices with their start and end apart: 13, of which 9 were waited for; matrix products, arithmetic and copies ran while one was open for 0% of the time, Pallas kernels for 11%

profile of v2, /device:TPU:0, one launch (start us, length us, event | category | flops | bytes accessed | tf_op | source)
XLA Modules:
  0.0 71.5 jit_solution(8373713192506552850)
XLA Ops:
  0.6 0.0 copy-start
  0.6 1.2 %copy-done = f32[18,18,512]{2,1,0:T(8,128)S(1)} copy-done((f32[18,18,512]{2,1,0:T(8,128)S(1)}, f32[18,18,512]{2,1,0:T(8,128)}, u32[]{:S(2)}) %copy-start) | copy-done | bytes 663576
  1.8 1.1 %copy-done.1 = f32[18,18,4,128]{3,2,1,0:T(4,128)S(1)} copy-done((f32[18,18,4,128]{3,2,1,0:T(4,128)S(1)}, f32[18,18,4,128]{3,2,1,0:T(4,128)}, u32[]{:S(2)}) %copy-start.1) | copy-done | bytes 663576
  2.9 0.7 copy-done.4
  3.6 0.0 copy-start.6
  3.6 0.0 copy-start.17
  3.6 0.9 %shard_map.195 = (bf16[336,256]{1,0:T(8,128)(2,1)S(1)}, bf16[336,256]{1,0:T(8,128)(2,1)S(1)}) custom-call(f32[1296,128]{1,0:T(8,128)S(1)} %bitcast.3, f32[18,18,512]{2,1,0:T(8,128)S(1)} %copy-done, s32[2,128]{1,0:T(2,128)S(1)} %copy-done.4), custom_call_target="tpu_custom_call" | custom-call | flops 88080384 | bytes 2097152 | tf_op jit(solution)/shard_map/pallas_call | solution.py:26
  4.5 3.1 %collective-permute-start = (bf16[336,256]{1,0:T(8,128)(2,1)S(1)}, bf16[336,256]{1,0:T(8,128)(2,1)S(1)}, u32[]{:S(2)}, u32[]{:S(2)}) collective-permute-start(bf16[336,256]{1,0:T(8,128)(2,1)S(1)} %get-tuple-element.32), channel_id=1, source_target_pairs={{0,4},{8,12},{4,0},{12,8},{1,5},{9,13},{5,1},{13,9},{2,6},{10,14},... | collective-permute-start | bytes 516104 | tf_op jit(solution)/shard_map/ppermute | solution.py:51
  7.6 0.7 collective-permute-start.1
  8.3 0.1 cosine_multiply_fusion
  8.4 0.0 copy-done.2
  8.4 0.0 copy-done.3
  8.4 0.0 copy-done.6
  8.4 0.0 copy-done.7
  8.4 0.0 copy-done.8
  8.4 0.0 copy-done.17
  8.5 4.4 %shard_map.194 = (f32[336,1024]{1,0:T(8,128)S(1)}, bf16[4,768,512]{2,1,0:T(8,128)(2,1)S(1)}, f32[4,336,512]{2,1,0:T(8,128)S(1)}, f32[336,2]{1,0:T(8,128)S(1)}, b...) custom-call(f32[1296,128]{1,0:T(8,128)S(1)} %bitcast.4, f32[18,18,512]{2,1,0:T(8,128)S(1)} %copy-done, ...), custom_call_target="tpu_custom_call" | custom-call | flops 2113929216 | bytes 2097152 | tf_op jit(solution)/shard_map/pallas_call | solution.py:26
  12.9 0.0 collective-permute-done.even_ref
  12.9 0.0 collective-permute-done.1.odd_ref
  12.9 1.1 %shard_map.196 = (f32[336,1024]{1,0:T(8,128)S(1)}, f32[128,1024]{1,0:T(8,128)S(1)}, bf16[128,1024]{1,0:T(8,128)(2,1)S(1)}) custom-call(f32[336,1024]{1,0:T(8,128)S(1)} %get-tuple-element.31.part_ref, bf16[336,256]{1,0:T(8,128)(2,1)S(1)} %collective-permute-done.even_ref, bf16[336,256]{1,0:T(8,128)(2,1)S(1)} %collective-permute-done.1.odd_ref, ...), custom_call_target="tpu_custom_call" | custom-call | flops 528482304 | bytes 2097152 | tf_op jit(solution)/shard_map/pallas_call | solution.py:26
  14.0 0.0 copy-start.9
  14.0 0.0 copy-start.10
  14.0 0.0 copy-start.11
  14.0 0.0 copy-start.12
  14.1 0.0 copy-start.13
  14.1 0.0 copy-start.14
  14.1 0.0 copy-start.15
  14.1 0.0 copy-start.16
  14.1 0.1 collective-permute-start.2
  14.2 1.5 %collective-permute-done.2 = bf16[128,1024]{1,0:T(8,128)(2,1)S(1)} collective-permute-done((bf16[128,1024]{1,0:T(8,128)(2,1)S(1)}, bf16[128,1024]{1,0:T(8,128)(2,1)S(1)}, u32[]{:S(2)}, u32[]{:S(2)}) %collective-permute-start.2) | collective-permute-done | bytes 262176 | tf_op jit(solution)/shard_map/ppermute | solution.py:367
  15.7 0.1 fusion.1
  15.8 0.0 copy-start.5
  15.8 1.6 %collective-permute-start.3 = (bf16[128,1024]{1,0:T(8,128)(2,1)S(1)}, bf16[128,1024]{1,0:T(8,128)(2,1)S(1)}, u32[]{:S(2)}, u32[]{:S(2)}) collective-permute-start(bf16[128,1024]{1,0:T(8,128)(2,1)S(1)} %get-tuple-element.62.after_ref), channel_id=1, source_target_pairs={{0,2},{2,0},{1,3},{3,1},{4,6},{6,4},{5,7},{7,5},{8,10},{10,8},{9,1... | collective-permute-start | bytes 786440 | tf_op jit(solution)/shard_map/ppermute | solution.py:372
  17.4 0.0 copy-done.10
  17.4 0.0 copy-done.12
  17.4 2.2 %shard_map.197 = (bf16[512,512]{1,0:T(8,128)(2,1)S(1)}, bf16[512,512]{1,0:T(8,128)(2,1)S(1)}, f32[2,512]{1,0:T(2,128)S(1)}, bf16[512,512]{1,0:T(8,128)(2,1)S(1)}, bf16[512,512]{1,0:T(8,128)(2,1)S(1)}) custom-call(s32[4,1,4,128]{3,2,1,0:T(4,128)S(1)} %copy-done.9, f32[4,1,4,128]{3,2,1,0:T(4,128)S(1)} %copy-done.10, s32[1,4]{1,0:T(1,128)S(1)} %copy-done.15, ...), custom_call_target="tpu_custom_call" | custom-call | flops 2147483648 | bytes 2097152 | tf_op jit(solution)/shard_map/pallas_call | solution.py:26
  19.6 4.6 %collective-permute-done.3.got_ref = bf16[128,1024]{1,0:T(8,128)(2,1)S(1)} collective-permute-done((bf16[128,1024]{1,0:T(8,128)(2,1)S(1)}, bf16[128,1024]{1,0:T(8,128)(2,1)S(1)}, u32[]{:S(2)}, u32[]{:S(2)}) %collective-permute-start.3) | collective-permute-done | bytes 262176 | tf_op jit(solution)/shard_map/ppermute | solution.py:372
  24.2 0.2 shard_map.198.mine_ref
  24.4 0.1 collective-permute-start.4
  24.5 1.5 %collective-permute-done.4.other_ref = bf16[128,1024]{1,0:T(8,128)(2,1)S(1)} collective-permute-done((bf16[128,1024]{1,0:T(8,128)(2,1)S(1)}, bf16[128,1024]{1,0:T(8,128)(2,1)S(1)}, u32[]{:S(2)}, u32[]{:S(2)}) %collective-permute-start.4) | collective-permute-done | bytes 262176 | tf_op jit(solution)/shard_map/ppermute | solution.py:367
  26.0 0.0 copy-done.5
  26.0 0.6 shard_map.199
  26.6 4.5 %collective-permute-start.5 = (bf16[336,256]{1,0:T(8,128)(2,1)S(1)}, bf16[336,256]{1,0:T(8,128)(2,1)S(1)}, u32[]{:S(2)}, u32[]{:S(2)}) collective-permute-start(bf16[336,256]{1,0:T(8,128)(2,1)S(1)} %get-tuple-element.44), channel_id=1, source_target_pairs={{0,4},{8,12},{4,0},{12,8},{1,5},{9,13},{5,1},{13,9},{2,6},{10,14},... | collective-permute-start | bytes 516104 | tf_op jit(solution)/shard_map/ppermute | solution.py:51
  31.1 0.8 %collective-permute-start.6 = (bf16[336,256]{1,0:T(8,128)(2,1)S(1)}, bf16[336,256]{1,0:T(8,128)(2,1)S(1)}, u32[]{:S(2)}, u32[]{:S(2)}) collective-permute-start(bf16[336,256]{1,0:T(8,128)(2,1)S(1)} %get-tuple-element.45), channel_id=1, source_target_pairs={{4,8},{8,4},{5,9},{9,5},{6,10},{10,6},{7,11},{11,7},{20,24},{24,20... | collective-permute-start | bytes 516104 | tf_op jit(solution)/shard_map/ppermute | solution.py:51
  31.9 1.6 %shard_map.200.part_ref = f32[336,1024]{1,0:T(8,128)S(1)} custom-call(f32[336,1024]{1,0:T(8,128)S(1)} %get-tuple-element.43.state_ref, bf16[4,768,512]{2,1,0:T(8,128)(2,1)S(1)} %get-tuple-element.34.hot_ref, f32[4,336,512]{2,1,0:T(8,128)S(1)} %get-tuple-element.35.weight_ref, f32[336,2]{1,0:T(8,128)S(1)} %get-tuple-element.36.band_ref, ...), custom_call_target="tpu_custom_call" | custom-call | flops 704643072 | bytes 2097152 | tf_op jit(solution)/shard_map/pallas_call | solution.py:26
  33.5 2.3 %collective-permute-done.5.even_ref = bf16[336,256]{1,0:T(8,128)(2,1)S(1)} collective-permute-done((bf16[336,256]{1,0:T(8,128)(2,1)S(1)}, bf16[336,256]{1,0:T(8,128)(2,1)S(1)}, u32[]{:S(2)}, u32[]{:S(2)}) %collective-permute-start.5) | collective-permute-done | bytes 172064 | tf_op jit(solution)/shard_map/ppermute | solution.py:51
  35.7 0.0 collective-permute-done.6.odd_ref
  35.7 1.1 %shard_map.201 = (f32[336,1024]{1,0:T(8,128)S(1)}, f32[128,1024]{1,0:T(8,128)S(1)}, bf16[128,1024]{1,0:T(8,128)(2,1)S(1)}) custom-call(f32[336,1024]{1,0:T(8,128)S(1)} %shard_map.200.part_ref, bf16[336,256]{1,0:T(8,128)(2,1)S(1)} %collective-permute-done.5.even_ref, bf16[336,256]{1,0:T(8,128)(2,1)S(1)} %collective-permute-done.6.odd_ref, ...), custom_call_target="tpu_custom_call" | custom-call | flops 528482304 | bytes 2097152 | tf_op jit(solution)/shard_map/pallas_call | solution.py:26
  36.8 0.1 collective-permute-start.7
  36.9 1.5 %collective-permute-done.7 = bf16[128,1024]{1,0:T(8,128)(2,1)S(1)} collective-permute-done((bf16[128,1024]{1,0:T(8,128)(2,1)S(1)}, bf16[128,1024]{1,0:T(8,128)(2,1)S(1)}, u32[]{:S(2)}, u32[]{:S(2)}) %collective-permute-start.7) | collective-permute-done | bytes 262176 | tf_op jit(solution)/shard_map/ppermute | solution.py:367
  38.4 0.1 fusion
  38.5 1.6 %collective-permute-start.8 = (bf16[128,1024]{1,0:T(8,128)(2,1)S(1)}, bf16[128,1024]{1,0:T(8,128)(2,1)S(1)}, u32[]{:S(2)}, u32[]{:S(2)}) collective-permute-start(bf16[128,1024]{1,0:T(8,128)(2,1)S(1)} %get-tuple-element.60), channel_id=1, source_target_pairs={{0,2},{2,0},{1,3},{3,1},{4,6},{6,4},{5,7},{7,5},{8,10},{10,8},{9,1... | collective-permute-start | bytes 786440 | tf_op jit(solution)/shard_map/ppermute | solution.py:372
  40.1 6.9 %collective-permute-done.8.got_ref = bf16[128,1024]{1,0:T(8,128)(2,1)S(1)} collective-permute-done((bf16[128,1024]{1,0:T(8,128)(2,1)S(1)}, bf16[128,1024]{1,0:T(8,128)(2,1)S(1)}, u32[]{:S(2)}, u32[]{:S(2)}) %collective-permute-start.8) | collective-permute-done | bytes 262176 | tf_op jit(solution)/shard_map/ppermute | solution.py:372
  46.9 0.2 shard_map.202.mine_ref
  47.1 0.1 collective-permute-start.9
  47.2 1.5 %collective-permute-done.9.other_ref = bf16[128,1024]{1,0:T(8,128)(2,1)S(1)} collective-permute-done((bf16[128,1024]{1,0:T(8,128)(2,1)S(1)}, bf16[128,1024]{1,0:T(8,128)(2,1)S(1)}, u32[]{:S(2)}, u32[]{:S(2)}) %collective-permute-start.9) | collective-permute-done | bytes 262176 | tf_op jit(solution)/shard_map/ppermute | solution.py:367
  48.7 1.1 %shard_map.203 = (f32[336,1024]{1,0:T(8,128)S(1)}, bf16[336,256]{1,0:T(8,128)(2,1)S(1)}, bf16[336,256]{1,0:T(8,128)(2,1)S(1)}, bf16[336,256]{1,0:T(8,128)(2,1)S(1)}, bf16[336,256]{1,0:T(8,128)(2,1)S(1)}) custom-call(f32[336,1024]{1,0:T(8,128)S(1)} %get-tuple-element.46.moved_ref, bf16[128,1024]{1,0:T(8,128)(2,1)S(1)} %shard_map.202.mine_ref, ...), custom_call_target="tpu_custom_call" | custom-call | flops 528482304 | bytes 2097152 | tf_op jit(solution)/shard_map/pallas_call | solution.py:26
  49.8 3.7 %collective-permute-start.10 = (bf16[336,256]{1,0:T(8,128)(2,1)S(1)}, bf16[336,256]{1,0:T(8,128)(2,1)S(1)}, u32[]{:S(2)}, u32[]{:S(2)}) collective-permute-start(bf16[336,256]{1,0:T(8,128)(2,1)S(1)} %get-tuple-element.55), channel_id=1, source_target_pairs={{0,4},{4,0},{8,12},{12,8},{1,5},{5,1},{9,13},{13,9},{2,6},{6,2},{1... | collective-permute-start | bytes 516104 | tf_op jit(solution)/shard_map/ppermute | solution.py:507
  53.5 0.7 collective-permute-start.11
  54.2 1.8 %collective-permute-start.12 = (bf16[336,256]{1,0:T(8,128)(2,1)S(1)}, bf16[336,256]{1,0:T(8,128)(2,1)S(1)}, u32[]{:S(2)}, u32[]{:S(2)}) collective-permute-start(bf16[336,256]{1,0:T(8,128)(2,1)S(1)} %get-tuple-element.57), channel_id=1, source_target_pairs={{0,12},{4,8},{8,4},{12,0},{1,13},{5,9},{9,5},{13,1},{2,14},{6,10},... | collective-permute-start | bytes 516104 | tf_op jit(solution)/shard_map/ppermute | solution.py:507
  56.0 5.1 %collective-permute-done.10.rest_1_ = bf16[336,256]{1,0:T(8,128)(2,1)S(1)} collective-permute-done((bf16[336,256]{1,0:T(8,128)(2,1)S(1)}, bf16[336,256]{1,0:T(8,128)(2,1)S(1)}, u32[]{:S(2)}, u32[]{:S(2)}) %collective-permute-start.10) | collective-permute-done | bytes 172064 | tf_op jit(solution)/shard_map/ppermute | solution.py:507
  61.1 8.0 %collective-permute-done.11.rest_2_ = bf16[336,256]{1,0:T(8,128)(2,1)S(1)} collective-permute-done((bf16[336,256]{1,0:T(8,128)(2,1)S(1)}, bf16[336,256]{1,0:T(8,128)(2,1)S(1)}, u32[]{:S(2)}, u32[]{:S(2)}) %collective-permute-start.11) | collective-permute-done | bytes 172064 | tf_op jit(solution)/shard_map/ppermute | solution.py:507
  69.0 0.0 collective-permute-done.12.rest_3_
  69.1 2.4 %shard_map.204 = (f32[1296,128]{1,0:T(8,128)}, f32[18,18,512]{2,1,0:T(8,128)}) custom-call(f32[336,1024]{1,0:T(8,128)S(1)} %get-tuple-element.51.state_ref, bf16[512,512]{1,0:T(8,128)(2,1)S(1)} %get-tuple-element.52.gland_ref, bf16[512,512]{1,0:T(8,128)(2,1)S(1)} %get-tuple-element.53.mland_ref, s32[4,128]{1,0:T(4,128)S(1)} %copy-done.2, ...), custom_call_target="tpu_custom_call" | custom-call | flops 352321536 | bytes 2097152 | tf_op jit(solution)/shard_map/pallas_call | solution.py:26
  (17 shorter events, 0.0 us)
Async XLA Ops:
  0.6 1.2 %copy-start = (f32[18,18,512]{2,1,0:T(8,128)S(1)}, f32[18,18,512]{2,1,0:T(8,128)}, u32[]{:S(2)}) copy-start(f32[18,18,512]{2,1,0:T(8,128)} %mesh_hbm.3) | copy-start | bytes 1990660
  1.8 1.1 %copy-start.1 = (f32[18,18,4,128]{3,2,1,0:T(4,128)S(1)}, f32[18,18,4,128]{3,2,1,0:T(4,128)}, u32[]{:S(2)}) copy-start(f32[18,18,4,128]{3,2,1,0:T(4,128)} %param.19) | copy-start | bytes 1990660
  2.9 0.7 copy-start.4
  3.6 4.7 %copy-start.18 = (f32[4,512]{1,0:T(4,128)S(1)}, f32[4,512]{1,0:T(4,128)}, u32[]{:S(2)}) copy-start(f32[4,512]{1,0:T(4,128)} %param.24) | copy-start | bytes 24580
  3.6 4.7 %copy-start.19 = (f32[4,512]{1,0:T(4,128)S(1)}, f32[4,512]{1,0:T(4,128)}, u32[]{:S(2)}) copy-start(f32[4,512]{1,0:T(4,128)} %param.25) | copy-start | bytes 24580
  3.6 4.8 %copy-start.2 = (s32[4,128]{1,0:T(4,128)S(1)}, s32[4,128]{1,0:T(4,128)}, u32[]{:S(2)}) copy-start(s32[4,128]{1,0:T(4,128)} %sea_ref.9) | copy-start | bytes 6148
  3.6 4.8 %copy-start.3 = (f32[4,128]{1,0:T(4,128)S(1)}, f32[4,128]{1,0:T(4,128)}, u32[]{:S(2)}) copy-start(f32[4,128]{1,0:T(4,128)} %speed_ref.7) | copy-start | bytes 6148
  3.6 4.8 %copy-start.6 = (bf16[18,18,256]{2,1,0:T(8,128)(2,1)S(1)}, bf16[18,18,256]{2,1,0:T(8,128)(2,1)}, u32[]{:S(2)}) copy-start(bf16[18,18,256]{2,1,0:T(8,128)(2,1)} %win_hbm.1) | copy-start | bytes 497668
  3.6 4.8 %copy-start.7 = (bf16[256,18,18]{0,2,1:T(8,128)(2,1)S(1)}, bf16[256,18,18]{0,2,1:T(8,128)(2,1)}, u32[]{:S(2)}) copy-start(bf16[256,18,18]{0,2,1:T(8,128)(2,1)} %param.28) | copy-start | bytes 497668
  3.6 4.8 %copy-start.8 = (s32[4,512]{1,0:T(4,128)S(1)}, s32[4,512]{1,0:T(4,128)}, u32[]{:S(2)}) copy-start(s32[4,512]{1,0:T(4,128)} %index_ref.1) | copy-start | bytes 24580
  3.6 4.8 %copy-start.17 = (f32[2,2,336,2]{3,2,1,0:T(8,128)S(1)}, f32[2,2,336,2]{3,2,1,0:T(8,128)}, u32[]{:S(2)}) copy-start(f32[2,2,336,2]{3,2,1,0:T(8,128)} %constant.2.clone.table_hbm) | copy-start | bytes 32260
  4.5 8.4 %collective-permute-start = (bf16[336,256]{1,0:T(8,128)(2,1)S(1)}, bf16[336,256]{1,0:T(8,128)(2,1)S(1)}, u32[]{:S(2)}, u32[]{:S(2)}) collective-permute-start(bf16[336,256]{1,0:T(8,128)(2,1)S(1)} %get-tuple-element.32), channel_id=1, source_target_pairs={{0,4},{8,12},{4,0},{12,8},{1,5},{9,13},{5,1},{13,9},{2,6},{10,14},... | collective-permute-start | bytes 516104 | tf_op jit(solution)/shard_map/ppermute | solution.py:51
  7.6 5.3 %collective-permute-start.1 = (bf16[336,256]{1,0:T(8,128)(2,1)S(1)}, bf16[336,256]{1,0:T(8,128)(2,1)S(1)}, u32[]{:S(2)}, u32[]{:S(2)}) collective-permute-start(bf16[336,256]{1,0:T(8,128)(2,1)S(1)} %get-tuple-element.33), channel_id=1, source_target_pairs={{4,8},{8,4},{5,9},{9,5},{6,10},{10,6},{7,11},{11,7},{20,24},{24,20... | collective-permute-start | bytes 516104 | tf_op jit(solution)/shard_map/ppermute | solution.py:51
  14.0 3.4 %copy-start.9 = (s32[4,1,4,128]{3,2,1,0:T(4,128)S(1)}, s32[4,1,4,128]{3,2,1,0:T(4,128)}, u32[]{:S(2)}) copy-start(s32[4,1,4,128]{3,2,1,0:T(4,128)} %gi_ref.1) | copy-start | bytes 24580
  14.0 3.3 %copy-start.10 = (f32[4,1,4,128]{3,2,1,0:T(4,128)S(1)}, f32[4,1,4,128]{3,2,1,0:T(4,128)}, u32[]{:S(2)}) copy-start(f32[4,1,4,128]{3,2,1,0:T(4,128)} %gw_ref.1) | copy-start | bytes 24580
  14.0 3.3 %copy-start.11 = (s32[3,1,4,128]{3,2,1,0:T(4,128)S(1)}, s32[3,1,4,128]{3,2,1,0:T(4,128)}, u32[]{:S(2)}) copy-start(s32[3,1,4,128]{3,2,1,0:T(4,128)} %mi_ref.1) | copy-start | bytes 18436
  14.0 3.3 %copy-start.12 = (f32[3,1,4,128]{3,2,1,0:T(4,128)S(1)}, f32[3,1,4,128]{3,2,1,0:T(4,128)}, u32[]{:S(2)}) copy-start(f32[3,1,4,128]{3,2,1,0:T(4,128)} %mw_ref.1) | copy-start | bytes 18436
  14.1 3.3 %copy-start.13 = (s32[1,4,128]{2,1,0:T(4,128)S(1)}, s32[1,4,128]{2,1,0:T(4,128)}, u32[]{:S(2)}) copy-start(s32[1,4,128]{2,1,0:T(4,128)} %gt_ref.1) | copy-start | bytes 6148
  14.1 3.3 %copy-start.14 = (s32[1,4,128]{2,1,0:T(4,128)S(1)}, s32[1,4,128]{2,1,0:T(4,128)}, u32[]{:S(2)}) copy-start(s32[1,4,128]{2,1,0:T(4,128)} %mt_ref.1) | copy-start | bytes 6148
  14.1 3.3 %copy-start.15 = (s32[1,4]{1,0:T(1,128)S(1)}, s32[1,4]{1,0:T(1,128)}, u32[]{:S(2)}) copy-start(s32[1,4]{1,0:T(1,128)} %gc_ref.1) | copy-start | bytes 52
  14.1 3.3 %copy-start.16 = (s32[1,4]{1,0:T(1,128)S(1)}, s32[1,4]{1,0:T(1,128)}, u32[]{:S(2)}) copy-start(s32[1,4]{1,0:T(1,128)} %mc_ref.1) | copy-start | bytes 52
  14.1 1.6 %collective-permute-start.2 = (bf16[128,1024]{1,0:T(8,128)(2,1)S(1)}, bf16[128,1024]{1,0:T(8,128)(2,1)S(1)}, u32[]{:S(2)}, u32[]{:S(2)}) collective-permute-start(bf16[128,1024]{1,0:T(8,128)(2,1)S(1)} %get-tuple-element.40), channel_id=1, source_target_pairs={{0,1},{1,0},{2,3},{3,2},{4,5},{5,4},{6,7},{7,6},{8,9},{9,8},{10,11... | collective-permute-start | bytes 786440 | tf_op jit(solution)/shard_map/ppermute | solution.py:367
  15.8 10.2 %copy-start.5 = (s32[2,128]{1,0:T(2,128)S(1)}, s32[2,128]{1,0:T(2,128)}, u32[]{:S(2)}) copy-start(s32[2,128]{1,0:T(2,128)} %halo_ref.1) | copy-start | bytes 3076
  15.8 8.4 %collective-permute-start.3 = (bf16[128,1024]{1,0:T(8,128)(2,1)S(1)}, bf16[128,1024]{1,0:T(8,128)(2,1)S(1)}, u32[]{:S(2)}, u32[]{:S(2)}) collective-permute-start(bf16[128,1024]{1,0:T(8,128)(2,1)S(1)} %get-tuple-element.62.after_ref), channel_id=1, source_target_pairs={{0,2},{2,0},{1,3},{3,1},{4,6},{6,4},{5,7},{7,5},{8,10},{10,8},{9,1... | collective-permute-start | bytes 786440 | tf_op jit(solution)/shard_map/ppermute | solution.py:372
  24.4 1.6 %collective-permute-start.4 = (bf16[128,1024]{1,0:T(8,128)(2,1)S(1)}, bf16[128,1024]{1,0:T(8,128)(2,1)S(1)}, u32[]{:S(2)}, u32[]{:S(2)}) collective-permute-start(bf16[128,1024]{1,0:T(8,128)(2,1)S(1)} %shard_map.198.mine_ref), channel_id=1, source_target_pairs={{0,1},{1,0},{2,3},{3,2},{4,5},{5,4},{6,7},{7,6},{8,9},{9,8},{10,11... | collective-permute-start | bytes 786440 | tf_op jit(solution)/shard_map/ppermute | solution.py:367
  26.6 9.1 %collective-permute-start.5 = (bf16[336,256]{1,0:T(8,128)(2,1)S(1)}, bf16[336,256]{1,0:T(8,128)(2,1)S(1)}, u32[]{:S(2)}, u32[]{:S(2)}) collective-permute-start(bf16[336,256]{1,0:T(8,128)(2,1)S(1)} %get-tuple-element.44), channel_id=1, source_target_pairs={{0,4},{8,12},{4,0},{12,8},{1,5},{9,13},{5,1},{13,9},{2,6},{10,14},... | collective-permute-start | bytes 516104 | tf_op jit(solution)/shard_map/ppermute | solution.py:51
  31.1 4.7 %collective-permute-start.6 = (bf16[336,256]{1,0:T(8,128)(2,1)S(1)}, bf16[336,256]{1,0:T(8,128)(2,1)S(1)}, u32[]{:S(2)}, u32[]{:S(2)}) collective-permute-start(bf16[336,256]{1,0:T(8,128)(2,1)S(1)} %get-tuple-element.45), channel_id=1, source_target_pairs={{4,8},{8,4},{5,9},{9,5},{6,10},{10,6},{7,11},{11,7},{20,24},{24,20... | collective-permute-start | bytes 516104 | tf_op jit(solution)/shard_map/ppermute | solution.py:51
  36.8 1.6 %collective-permute-start.7 = (bf16[128,1024]{1,0:T(8,128)(2,1)S(1)}, bf16[128,1024]{1,0:T(8,128)(2,1)S(1)}, u32[]{:S(2)}, u32[]{:S(2)}) collective-permute-start(bf16[128,1024]{1,0:T(8,128)(2,1)S(1)} %get-tuple-element.48), channel_id=1, source_target_pairs={{0,1},{1,0},{2,3},{3,2},{4,5},{5,4},{6,7},{7,6},{8,9},{9,8},{10,11... | collective-permute-start | bytes 786440 | tf_op jit(solution)/shard_map/ppermute | solution.py:367
  38.5 8.4 %collective-permute-start.8 = (bf16[128,1024]{1,0:T(8,128)(2,1)S(1)}, bf16[128,1024]{1,0:T(8,128)(2,1)S(1)}, u32[]{:S(2)}, u32[]{:S(2)}) collective-permute-start(bf16[128,1024]{1,0:T(8,128)(2,1)S(1)} %get-tuple-element.60), channel_id=1, source_target_pairs={{0,2},{2,0},{1,3},{3,1},{4,6},{6,4},{5,7},{7,5},{8,10},{10,8},{9,1... | collective-permute-start | bytes 786440 | tf_op jit(solution)/shard_map/ppermute | solution.py:372
  47.1 1.6 %collective-permute-start.9 = (bf16[128,1024]{1,0:T(8,128)(2,1)S(1)}, bf16[128,1024]{1,0:T(8,128)(2,1)S(1)}, u32[]{:S(2)}, u32[]{:S(2)}) collective-permute-start(bf16[128,1024]{1,0:T(8,128)(2,1)S(1)} %shard_map.202.mine_ref), channel_id=1, source_target_pairs={{0,1},{1,0},{2,3},{3,2},{4,5},{5,4},{6,7},{7,6},{8,9},{9,8},{10,11... | collective-permute-start | bytes 786440 | tf_op jit(solution)/shard_map/ppermute | solution.py:367
  49.8 11.3 %collective-permute-start.10 = (bf16[336,256]{1,0:T(8,128)(2,1)S(1)}, bf16[336,256]{1,0:T(8,128)(2,1)S(1)}, u32[]{:S(2)}, u32[]{:S(2)}) collective-permute-start(bf16[336,256]{1,0:T(8,128)(2,1)S(1)} %get-tuple-element.55), channel_id=1, source_target_pairs={{0,4},{4,0},{8,12},{12,8},{1,5},{5,1},{9,13},{13,9},{2,6},{6,2},{1... | collective-permute-start | bytes 516104 | tf_op jit(solution)/shard_map/ppermute | solution.py:507
  53.5 15.5 %collective-permute-start.11 = (bf16[336,256]{1,0:T(8,128)(2,1)S(1)}, bf16[336,256]{1,0:T(8,128)(2,1)S(1)}, u32[]{:S(2)}, u32[]{:S(2)}) collective-permute-start(bf16[336,256]{1,0:T(8,128)(2,1)S(1)} %get-tuple-element.56), channel_id=1, source_target_pairs={{0,8},{4,12},{8,0},{12,4},{1,9},{5,13},{9,1},{13,5},{2,10},{6,14},... | collective-permute-start | bytes 516104 | tf_op jit(solution)/shard_map/ppermute | solution.py:507
  54.2 14.9 %collective-permute-start.12 = (bf16[336,256]{1,0:T(8,128)(2,1)S(1)}, bf16[336,256]{1,0:T(8,128)(2,1)S(1)}, u32[]{:S(2)}, u32[]{:S(2)}) collective-permute-start(bf16[336,256]{1,0:T(8,128)(2,1)S(1)} %get-tuple-element.57), channel_id=1, source_target_pairs={{0,12},{4,8},{8,4},{12,0},{1,13},{5,9},{9,5},{13,1},{2,14},{6,10},... | collective-permute-start | bytes 516104 | tf_op jit(solution)/shard_map/ppermute | solution.py:507

commit v3 on v2

--- a/solution.py
+++ b/solution.py
@@ -20,14 +20,18 @@
 HBM = pltpu.MemorySpace.HBM
 
 
-def kernel_call(body, outs, scratch=(), flops=0, nbytes=2 << 20, spaces=None):
+def kernel_call(body, outs, scratch=(), flops=0, nbytes=2 << 20, spaces=None, out_space=VMEM):
     def run(*args):
         where = spaces or [VMEM] * len(args)
+        args = [
+            pltpu.with_memory_space_constraint(a, HBM) if space == HBM else a
+            for a, space in zip(args, where)
+        ]
         return pl.pallas_call(
             body,
             out_shape=[jax.ShapeDtypeStruct(s, t) for s, t in outs],
             in_specs=[pl.BlockSpec(memory_space=space) for space in where],
-            out_specs=[pl.BlockSpec(memory_space=VMEM)] * len(outs),
+            out_specs=[pl.BlockSpec(memory_space=out_space)] * len(outs),
             scratch_shapes=[s if hasattr(s, "dtype") else pltpu.VMEM(*s) for s in scratch],
             compiler_params=pltpu.CompilerParams(vmem_limit_bytes=16 << 20),
             cost_estimate=pl.CostEstimate(flops=flops, bytes_accessed=nbytes, transcendentals=0),
@@ -51,16 +55,9 @@
     return lax.ppermute(array, axis, pairs + [(j, i) for i, j in pairs])
 
 
-def peer_pairs(size, step):
-    if size & (size - 1) == 0:
-        return [(i, i ^ step) for i in range(size)]
-    return [(i, (step - i) % size) for i in range(size)]
-
-
-def peer_of(me, size, step):
-    if size & (size - 1) == 0:
-        return lax.bitwise_xor(me, step)
-    return lax.rem(step - me + size, size)
+def peer_swap(array, axis, step):
+    size = lax.axis_size(axis)
+    return lax.ppermute(array, axis, [(i, i ^ step) for i in range(size)])
 
 
 def on_even():
@@ -276,7 +273,7 @@
         spots = lax.broadcasted_iota(jnp.int32, (length, cap), 0)
         slot = lax.broadcasted_iota(jnp.int32, (1, cap), 1)
         for p in range(peers):
-            peer = peer_of(me, peers, p)
+            peer = lax.bitwise_xor(me, p)
             count = jnp.sum(
                 jnp.where(
                     lax.broadcasted_iota(jnp.int32, (1, peers), 1) == peer, count_ref[...], 0
@@ -318,6 +315,11 @@
             out_refs[p][:, kind * cap : (kind + 1) * cap] = value.astype(BF16)
 
 
+def silu_kernel(total_ref, got_ref, *rest):
+    total = total_ref[...] + got_ref[...].astype(F32)
+    rest[-1][...] = (total / (1.0 + jnp.exp(-total))).astype(BF16)
+
+
 def land(values, land_ref):
     return lax.dot_general(
         values, land_ref[...], (((1,), (1,)), ((), ())), preferred_element_type=F32
@@ -325,7 +327,8 @@
 
 
 def end_kernel(state_ref, gland_ref, mland_ref, sea_ref, *rest, bands):
-    got_refs, (grid_ref, mesh_ref, values_ref, sum_ref) = rest[:-4], rest[-4:]
+    got_refs, rest = rest[-8::-1], rest[-7:]
+    grid_hbm, mesh_hbm, values_ref, sum_ref, grid_ref, mesh_ref, sem = rest
     rows, cols = sea_ref.shape
     gp = rows * cols
     freqs, dirs, _ = mesh_ref.shape
@@ -333,20 +336,29 @@
     for kind in (0, 1):
         for p, got in enumerate(got_refs):
             values_ref[kind, :, p * cap : (p + 1) * cap] = got[:, kind * cap : (kind + 1) * cap]
+    sum_ref[:, gp:] = land(values_ref[0], gland_ref)
+    cover = sum_ref[bands : bands + 1, gp:]
+    rate = BLEND_RATE / (1.0 + cover)
+    keep = 1.0 - rate * cover
+    for f in range(freqs):
+        here = slice(f * dirs, (f + 1) * dirs)
+        mesh_ref[f] = keep * state_ref[here, gp:] + rate * sum_ref[here, gp:]
+    mesh_copy = pltpu.make_async_copy(mesh_ref, mesh_hbm, sem.at[0])
+    mesh_copy.start()
     sum_ref[:, :gp] = land(values_ref[1], mland_ref)
-    sum_ref[:, gp:] = land(values_ref[0], gland_ref)
-    cover = sum_ref[bands : bands + 1, :]
+    cover = sum_ref[bands : bands + 1, :gp]
     rate = BLEND_RATE / (1.0 + cover)
+    keep = 1.0 - rate * cover
     sea = sea_ref[...].astype(F32)
     for x in range(rows):
         cut = slice(x * cols, (x + 1) * cols)
-        g = state_ref[:bands, cut]
-        out = g + rate[:, cut] * (sum_ref[:bands, cut] - cover[:, cut] * g)
-        grid_ref[pl.ds(x, bands, stride=rows), :] = out * sea[x : x + 1, :]
-    for f in range(freqs):
-        here = slice(f * dirs, (f + 1) * dirs)
-        e = state_ref[here, gp:]
-        mesh_ref[f] = e + rate[:, gp:] * (sum_ref[here, gp:] - cover[:, gp:] * e)
+        wet = sea[x : x + 1, :]
+        out = keep[:, cut] * wet * state_ref[:bands, cut] + rate[:, cut] * wet * sum_ref[:bands, cut]
+        grid_ref[pl.ds(x, bands, stride=rows), :] = out
+    grid_copy = pltpu.make_async_copy(grid_ref, grid_hbm, sem.at[1])
+    grid_copy.start()
+    mesh_copy.wait()
+    grid_copy.wait()
 
 
 def band_table(freqs, dirs, n_fr, n_dr, padded):
@@ -365,17 +377,6 @@
 
 def core_swap(array):
     return lax.ppermute(array, "dr", [(0, 1), (1, 0)])
-
-
-def fr_swap(array, step):
-    size = lax.axis_size("fr")
-    return lax.ppermute(array, "fr", [(i, i ^ step) for i in range(size)])
-
-
-def silu_kernel(total_ref, got_ref, *rest):
-    out_ref = rest[-1]
-    total = total_ref[...] + got_ref[...].astype(F32)
-    out_ref[...] = (total / (1.0 + jnp.exp(-total))).astype(BF16)
 
 
 def per_device(
@@ -460,12 +461,12 @@
 
         total = total + core_swap(send).astype(F32)
         rounded = total.astype(BF16)
-        got = fr_swap(rounded, 1)
+        got = peer_swap(rounded, "fr", 1)
         step = 2
         while step < n_fr:
             total = total + got.astype(F32)
             rounded = total.astype(BF16)
-            got = fr_swap(rounded, step)
+            got = peer_swap(rounded, "fr", step)
             step *= 2
         extra = []
         if substep == 0:
@@ -503,17 +504,21 @@
         [hid_scratch],
         flops=2 * padded * (hid * points + points * peers * cap),
     )(moved, mine, other, wout, gmix, mmix, sums)
-    got = [
-        lax.ppermute(v, "sp", peer_pairs(peers, p)) if p else v for p, v in enumerate(values)
-    ]
-    if peers & (peers - 1):
-        got[0] = lax.ppermute(values[0], "sp", peer_pairs(peers, 0))
+    for p in reversed(range(1, peers)):
+        values[p] = peer_swap(values[p], "sp", p)
     grid_out, mesh_out = kernel_call(
         functools.partial(end_kernel, bands=bands),
-        [((bands * rows, cols), F32), ((freqs, dirs, nodes), F32)],
-        [((2, padded, peers * cap), BF16), state_shape],
+        [(grid_flat.shape, F32), (mesh_spec.shape, F32)],
+        [
+            ((2, padded, peers * cap), BF16),
+            state_shape,
+            (grid_flat.shape, F32),
+            (mesh_spec.shape, F32),
+            pltpu.SemaphoreType.DMA((2,)),
+        ],
         flops=2 * padded * points * peers * cap,
-    )(state, gland, mland, grid_sea, *got)
+        out_space=pl.ANY,
+    )(state, gland, mland, grid_sea, *values[::-1])
     return grid_out.reshape(grid_spec.shape), mesh_out
 
 

time: 71.8 us -> 68.8 us (0.958)
  local copies, waits for them, and re-layouts: 3.02 us -> 0.08 us
  waiting for transfers between devices: 32.9 us -> 33.7 us
    unnamed x40 -> x28, local copies, waits for them, and re-layouts: 3.02 us -> 0.08 us
  transfers between devices with their start and end apart: 13 -> 13, of which waited for: 9 -> 10; matrix products, arithmetic and copies ran while one was open for 0% -> 0% of each run, Pallas kernels for 11% -> 10%
where the time goes in v3:
time: 68.8 us; the launch traced here: 68.6 us
  waiting for transfers between devices  33.7 us (49%)
  starting transfers between devices  18.4 us (27%)
  Pallas kernels  15 us (22%)
  between operations  1.12 us (2%)
    ppermute x5, waiting for transfers between devices, peer_swap(): return lax.ppermute(array, axis, [(i, i ^ step) for i in range(size)])  25.2 us
    pallas_call x11, Pallas kernels, run(): pl.pallas_call(body, out_shape=[jax.ShapeDtypeStruct(s, t) for s, t in ou...  15 us
    ppermute x4, starting transfers between devices, pair_swap(): return lax.ppermute(array, axis, pairs + [(j, i) for i, j in pairs])  9.41 us
    ppermute x5, starting transfers between devices, peer_swap(): return lax.ppermute(array, axis, [(i, i ^ step) for i in range(size)])  8.73 us
    ppermute x4, waiting for transfers between devices, core_swap(): return lax.ppermute(array, 'dr', [(0, 1), (1, 0)])  6.09 us
    ppermute x4, waiting for transfers between devices, pair_swap(): return lax.ppermute(array, axis, pairs + [(j, i) for i, j in pairs])  2.46 us
  transfers between devices with their start and end apart: 13, of which 10 were waited for; matrix products, arithmetic and copies ran while one was open for 0% of the time, Pallas kernels for 10%

profile of v3, /device:TPU:0, one launch (start us, length us, event | category | flops | bytes accessed | tf_op | source)
XLA Modules:
  0.0 68.6 jit_solution(5980903635214237298)
XLA Ops:
  0.6 0.0 copy-start.13
  0.6 0.0 copy-start.12
  0.7 0.0 copy-start
  0.7 0.0 copy-start.1
  0.7 0.0 copy-start.3
  0.7 1.8 %shard_map.195 = (bf16[336,256]{1,0:T(8,128)(2,1)S(1)}, bf16[336,256]{1,0:T(8,128)(2,1)S(1)}) custom-call(f32[1296,128]{1,0:T(8,128)} %bitcast.3, f32[18,18,512]{2,1,0:T(8,128)} %mesh_hbm.3, s32[2,128]{1,0:T(2,128)} %halo_ref.1), custom_call_target="tpu_custom_call" | custom-call | flops 88080384 | bytes 2097152 | tf_op jit(solution)/shard_map/pallas_call | solution.py:30
  2.5 3.1 %collective-permute-start = (bf16[336,256]{1,0:T(8,128)(2,1)S(1)}, bf16[336,256]{1,0:T(8,128)(2,1)S(1)}, u32[]{:S(2)}, u32[]{:S(2)}) collective-permute-start(bf16[336,256]{1,0:T(8,128)(2,1)S(1)} %get-tuple-element.32), channel_id=1, source_target_pairs={{0,4},{8,12},{4,0},{12,8},{1,5},{9,13},{5,1},{13,9},{2,6},{10,14},... | collective-permute-start | bytes 516104 | tf_op jit(solution)/shard_map/ppermute | solution.py:55
  5.6 0.7 collective-permute-start.1
  6.3 0.0 copy-done.13
  6.3 0.0 copy-done.12
  6.3 0.1 cosine_multiply_fusion
  6.4 0.0 copy-done
  6.4 0.0 copy-done.1
  6.4 0.0 copy-done.3
  6.4 3.4 %shard_map.194 = (f32[336,1024]{1,0:T(8,128)S(1)}, bf16[4,768,512]{2,1,0:T(8,128)(2,1)S(1)}, f32[4,336,512]{2,1,0:T(8,128)S(1)}, f32[336,2]{1,0:T(8,128)S(1)}, b...) custom-call(f32[1296,128]{1,0:T(8,128)} %bitcast.4, f32[18,18,512]{2,1,0:T(8,128)} %mesh_hbm.3, ...), custom_call_target="tpu_custom_call" | custom-call | flops 2113929216 | bytes 2097152 | tf_op jit(solution)/shard_map/pallas_call | solution.py:30
  9.8 0.1 collective-permute-done.even_ref
  10.0 0.0 collective-permute-done.1.odd_ref
  10.0 1.1 %shard_map.196 = (f32[336,1024]{1,0:T(8,128)S(1)}, f32[128,1024]{1,0:T(8,128)S(1)}, bf16[128,1024]{1,0:T(8,128)(2,1)S(1)}) custom-call(f32[336,1024]{1,0:T(8,128)S(1)} %get-tuple-element.31.part_ref, bf16[336,256]{1,0:T(8,128)(2,1)S(1)} %collective-permute-done.even_ref, bf16[336,256]{1,0:T(8,128)(2,1)S(1)} %collective-permute-done.1.odd_ref, ...), custom_call_target="tpu_custom_call" | custom-call | flops 528482304 | bytes 2097152 | tf_op jit(solution)/shard_map/pallas_call | solution.py:30
  11.1 0.0 copy-start.4
  11.1 0.0 copy-start.5
  11.1 0.0 copy-start.6
  11.1 0.0 copy-start.7
  11.1 0.0 copy-start.8
  11.1 0.0 copy-start.9
  11.1 0.0 copy-start.10
  11.1 0.0 copy-start.11
  11.2 0.1 collective-permute-start.2
  11.2 1.5 %collective-permute-done.2 = bf16[128,1024]{1,0:T(8,128)(2,1)S(1)} collective-permute-done((bf16[128,1024]{1,0:T(8,128)(2,1)S(1)}, bf16[128,1024]{1,0:T(8,128)(2,1)S(1)}, u32[]{:S(2)}, u32[]{:S(2)}) %collective-permute-start.2) | collective-permute-done | bytes 262176 | tf_op jit(solution)/shard_map/ppermute | solution.py:379
  12.8 0.1 fusion.1
  12.8 0.0 copy-start.2
  12.9 1.7 %collective-permute-start.3 = (bf16[128,1024]{1,0:T(8,128)(2,1)S(1)}, bf16[128,1024]{1,0:T(8,128)(2,1)S(1)}, u32[]{:S(2)}, u32[]{:S(2)}) collective-permute-start(bf16[128,1024]{1,0:T(8,128)(2,1)S(1)} %get-tuple-element.62.after_ref), channel_id=1, source_target_pairs={{0,2},{2,0},{1,3},{3,1},{4,6},{6,4},{5,7},{7,5},{8,10},{10,8},{9,1... | collective-permute-start | bytes 786440 | tf_op jit(solution)/shard_map/ppermute | solution.py:60
  14.6 0.0 copy-done.4
  14.6 0.0 copy-done.5
  14.6 0.0 copy-done.6
  14.6 0.0 copy-done.7
  14.6 0.0 copy-done.8
  14.6 2.2 %shard_map.197 = (bf16[512,512]{1,0:T(8,128)(2,1)S(1)}, bf16[512,512]{1,0:T(8,128)(2,1)S(1)}, f32[2,512]{1,0:T(2,128)S(1)}, bf16[512,512]{1,0:T(8,128)(2,1)S(1)}, bf16[512,512]{1,0:T(8,128)(2,1)S(1)}) custom-call(s32[4,1,4,128]{3,2,1,0:T(4,128)S(1)} %copy-done.4, f32[4,1,4,128]{3,2,1,0:T(4,128)S(1)} %copy-done.5, s32[1,4]{1,0:T(1,128)S(1)} %copy-done.10, ...), custom_call_target="tpu_custom_call" | custom-call | flops 2147483648 | bytes 2097152 | tf_op jit(solution)/shard_map/pallas_call | solution.py:30
  16.8 4.5 %collective-permute-done.3.got_ref = bf16[128,1024]{1,0:T(8,128)(2,1)S(1)} collective-permute-done((bf16[128,1024]{1,0:T(8,128)(2,1)S(1)}, bf16[128,1024]{1,0:T(8,128)(2,1)S(1)}, u32[]{:S(2)}, u32[]{:S(2)}) %collective-permute-start.3) | collective-permute-done | bytes 262176 | tf_op jit(solution)/shard_map/ppermute | solution.py:60
  21.3 0.2 shard_map.198.mine_ref
  21.4 0.1 collective-permute-start.4
  21.5 1.5 %collective-permute-done.4.other_ref = bf16[128,1024]{1,0:T(8,128)(2,1)S(1)} collective-permute-done((bf16[128,1024]{1,0:T(8,128)(2,1)S(1)}, bf16[128,1024]{1,0:T(8,128)(2,1)S(1)}, u32[]{:S(2)}, u32[]{:S(2)}) %collective-permute-start.4) | collective-permute-done | bytes 262176 | tf_op jit(solution)/shard_map/ppermute | solution.py:379
  23.0 0.6 shard_map.199
  23.6 4.8 %collective-permute-start.5 = (bf16[336,256]{1,0:T(8,128)(2,1)S(1)}, bf16[336,256]{1,0:T(8,128)(2,1)S(1)}, u32[]{:S(2)}, u32[]{:S(2)}) collective-permute-start(bf16[336,256]{1,0:T(8,128)(2,1)S(1)} %get-tuple-element.44), channel_id=1, source_target_pairs={{0,4},{8,12},{4,0},{12,8},{1,5},{9,13},{5,1},{13,9},{2,6},{10,14},... | collective-permute-start | bytes 516104 | tf_op jit(solution)/shard_map/ppermute | solution.py:55
  28.5 0.8 %collective-permute-start.6 = (bf16[336,256]{1,0:T(8,128)(2,1)S(1)}, bf16[336,256]{1,0:T(8,128)(2,1)S(1)}, u32[]{:S(2)}, u32[]{:S(2)}) collective-permute-start(bf16[336,256]{1,0:T(8,128)(2,1)S(1)} %get-tuple-element.45), channel_id=1, source_target_pairs={{4,8},{8,4},{5,9},{9,5},{6,10},{10,6},{7,11},{11,7},{20,24},{24,20... | collective-permute-start | bytes 516104 | tf_op jit(solution)/shard_map/ppermute | solution.py:55
  29.3 1.5 %shard_map.200.part_ref = f32[336,1024]{1,0:T(8,128)S(1)} custom-call(f32[336,1024]{1,0:T(8,128)S(1)} %get-tuple-element.43.state_ref, bf16[4,768,512]{2,1,0:T(8,128)(2,1)S(1)} %get-tuple-element.34.hot_ref, f32[4,336,512]{2,1,0:T(8,128)S(1)} %get-tuple-element.35.weight_ref, f32[336,2]{1,0:T(8,128)S(1)} %get-tuple-element.36.band_ref, ...), custom_call_target="tpu_custom_call" | custom-call | flops 704643072 | bytes 2097152 | tf_op jit(solution)/shard_map/pallas_call | solution.py:30
  30.8 2.3 %collective-permute-done.5.even_ref = bf16[336,256]{1,0:T(8,128)(2,1)S(1)} collective-permute-done((bf16[336,256]{1,0:T(8,128)(2,1)S(1)}, bf16[336,256]{1,0:T(8,128)(2,1)S(1)}, u32[]{:S(2)}, u32[]{:S(2)}) %collective-permute-start.5) | collective-permute-done | bytes 172064 | tf_op jit(solution)/shard_map/ppermute | solution.py:55
  33.1 0.0 collective-permute-done.6.odd_ref
  33.1 1.1 %shard_map.201 = (f32[336,1024]{1,0:T(8,128)S(1)}, f32[128,1024]{1,0:T(8,128)S(1)}, bf16[128,1024]{1,0:T(8,128)(2,1)S(1)}) custom-call(f32[336,1024]{1,0:T(8,128)S(1)} %shard_map.200.part_ref, bf16[336,256]{1,0:T(8,128)(2,1)S(1)} %collective-permute-done.5.even_ref, bf16[336,256]{1,0:T(8,128)(2,1)S(1)} %collective-permute-done.6.odd_ref, ...), custom_call_target="tpu_custom_call" | custom-call | flops 528482304 | bytes 2097152 | tf_op jit(solution)/shard_map/pallas_call | solution.py:30
  34.2 0.1 collective-permute-start.7
  34.3 1.5 %collective-permute-done.7 = bf16[128,1024]{1,0:T(8,128)(2,1)S(1)} collective-permute-done((bf16[128,1024]{1,0:T(8,128)(2,1)S(1)}, bf16[128,1024]{1,0:T(8,128)(2,1)S(1)}, u32[]{:S(2)}, u32[]{:S(2)}) %collective-permute-start.7) | collective-permute-done | bytes 262176 | tf_op jit(solution)/shard_map/ppermute | solution.py:379
  35.8 0.1 fusion
  35.9 1.6 %collective-permute-start.8 = (bf16[128,1024]{1,0:T(8,128)(2,1)S(1)}, bf16[128,1024]{1,0:T(8,128)(2,1)S(1)}, u32[]{:S(2)}, u32[]{:S(2)}) collective-permute-start(bf16[128,1024]{1,0:T(8,128)(2,1)S(1)} %get-tuple-element.60), channel_id=1, source_target_pairs={{0,2},{2,0},{1,3},{3,1},{4,6},{6,4},{5,7},{7,5},{8,10},{10,8},{9,1... | collective-permute-start | bytes 786440 | tf_op jit(solution)/shard_map/ppermute | solution.py:60
  37.5 6.9 %collective-permute-done.8.got_ref = bf16[128,1024]{1,0:T(8,128)(2,1)S(1)} collective-permute-done((bf16[128,1024]{1,0:T(8,128)(2,1)S(1)}, bf16[128,1024]{1,0:T(8,128)(2,1)S(1)}, u32[]{:S(2)}, u32[]{:S(2)}) %collective-permute-start.8) | collective-permute-done | bytes 262176 | tf_op jit(solution)/shard_map/ppermute | solution.py:60
  44.3 0.2 shard_map.202.mine_ref
  44.5 0.1 collective-permute-start.9
  44.6 1.5 %collective-permute-done.9.other_ref = bf16[128,1024]{1,0:T(8,128)(2,1)S(1)} collective-permute-done((bf16[128,1024]{1,0:T(8,128)(2,1)S(1)}, bf16[128,1024]{1,0:T(8,128)(2,1)S(1)}, u32[]{:S(2)}, u32[]{:S(2)}) %collective-permute-start.9) | collective-permute-done | bytes 262176 | tf_op jit(solution)/shard_map/ppermute | solution.py:379
  46.1 1.1 %shard_map.203 = (f32[336,1024]{1,0:T(8,128)S(1)}, bf16[336,256]{1,0:T(8,128)(2,1)S(1)}, bf16[336,256]{1,0:T(8,128)(2,1)S(1)}, bf16[336,256]{1,0:T(8,128)(2,1)S(1)}, bf16[336,256]{1,0:T(8,128)(2,1)S(1)}) custom-call(f32[336,1024]{1,0:T(8,128)S(1)} %get-tuple-element.46.moved_ref, bf16[128,1024]{1,0:T(8,128)(2,1)S(1)} %shard_map.202.mine_ref, ...), custom_call_target="tpu_custom_call" | custom-call | flops 528482304 | bytes 2097152 | tf_op jit(solution)/shard_map/pallas_call | solution.py:30
  47.2 2.7 %collective-permute-start.10 = (bf16[336,256]{1,0:T(8,128)(2,1)S(1)}, bf16[336,256]{1,0:T(8,128)(2,1)S(1)}, u32[]{:S(2)}, u32[]{:S(2)}) collective-permute-start(bf16[336,256]{1,0:T(8,128)(2,1)S(1)} %get-tuple-element.54), channel_id=1, source_target_pairs={{0,12},{4,8},{8,4},{12,0},{1,13},{5,9},{9,5},{13,1},{2,14},{6,10},... | collective-permute-start | bytes 516104 | tf_op jit(solution)/shard_map/ppermute | solution.py:60
  49.9 2.5 %collective-permute-start.11 = (bf16[336,256]{1,0:T(8,128)(2,1)S(1)}, bf16[336,256]{1,0:T(8,128)(2,1)S(1)}, u32[]{:S(2)}, u32[]{:S(2)}) collective-permute-start(bf16[336,256]{1,0:T(8,128)(2,1)S(1)} %get-tuple-element.55), channel_id=1, source_target_pairs={{0,8},{4,12},{8,0},{12,4},{1,9},{5,13},{9,1},{13,5},{2,10},{6,14},... | collective-permute-start | bytes 516104 | tf_op jit(solution)/shard_map/ppermute | solution.py:60
  52.4 0.3 collective-permute-start.12
  52.7 3.0 %collective-permute-done.10.rest_0_ = bf16[336,256]{1,0:T(8,128)(2,1)S(1)} collective-permute-done((bf16[336,256]{1,0:T(8,128)(2,1)S(1)}, bf16[336,256]{1,0:T(8,128)(2,1)S(1)}, u32[]{:S(2)}, u32[]{:S(2)}) %collective-permute-start.10) | collective-permute-done | bytes 172064 | tf_op jit(solution)/shard_map/ppermute | solution.py:60
  55.7 10.9 %collective-permute-done.11.rest_1_ = bf16[336,256]{1,0:T(8,128)(2,1)S(1)} collective-permute-done((bf16[336,256]{1,0:T(8,128)(2,1)S(1)}, bf16[336,256]{1,0:T(8,128)(2,1)S(1)}, u32[]{:S(2)}, u32[]{:S(2)}) %collective-permute-start.11) | collective-permute-done | bytes 172064 | tf_op jit(solution)/shard_map/ppermute | solution.py:60
  66.6 0.0 collective-permute-done.12.rest_2_
  66.6 1.9 %shard_map.204 = (f32[1296,128]{1,0:T(8,128)}, f32[18,18,512]{2,1,0:T(8,128)}) custom-call(f32[336,1024]{1,0:T(8,128)S(1)} %get-tuple-element.51.state_ref, bf16[512,512]{1,0:T(8,128)(2,1)S(1)} %get-tuple-element.52.gland_ref, bf16[512,512]{1,0:T(8,128)(2,1)S(1)} %get-tuple-element.53.mland_ref, s32[4,128]{1,0:T(4,128)S(1)} %copy-done, ...), custom_call_target="tpu_custom_call" | custom-call | flops 352321536 | bytes 2097152 | tf_op jit(solution)/shard_map/pallas_call | solution.py:30
  (5 shorter events, 0.0 us)
Async XLA Ops:
  0.6 5.6 %copy-start.13 = (f32[4,512]{1,0:T(4,128)S(1)}, f32[4,512]{1,0:T(4,128)}, u32[]{:S(2)}) copy-start(f32[4,512]{1,0:T(4,128)} %param.25) | copy-start | bytes 24580
  0.6 5.6 %copy-start.12 = (f32[4,512]{1,0:T(4,128)S(1)}, f32[4,512]{1,0:T(4,128)}, u32[]{:S(2)}) copy-start(f32[4,512]{1,0:T(4,128)} %param.24) | copy-start | bytes 24580
  0.7 5.7 %copy-start = (s32[4,128]{1,0:T(4,128)S(1)}, s32[4,128]{1,0:T(4,128)}, u32[]{:S(2)}) copy-start(s32[4,128]{1,0:T(4,128)} %sea_ref.9) | copy-start | bytes 6148
  0.7 5.7 %copy-start.1 = (f32[4,128]{1,0:T(4,128)S(1)}, f32[4,128]{1,0:T(4,128)}, u32[]{:S(2)}) copy-start(f32[4,128]{1,0:T(4,128)} %speed_ref.7) | copy-start | bytes 6148
  0.7 5.7 %copy-start.3 = (s32[4,512]{1,0:T(4,128)S(1)}, s32[4,512]{1,0:T(4,128)}, u32[]{:S(2)}) copy-start(s32[4,512]{1,0:T(4,128)} %index_ref.1) | copy-start | bytes 24580
  2.5 7.5 %collective-permute-start = (bf16[336,256]{1,0:T(8,128)(2,1)S(1)}, bf16[336,256]{1,0:T(8,128)(2,1)S(1)}, u32[]{:S(2)}, u32[]{:S(2)}) collective-permute-start(bf16[336,256]{1,0:T(8,128)(2,1)S(1)} %get-tuple-element.32), channel_id=1, source_target_pairs={{0,4},{8,12},{4,0},{12,8},{1,5},{9,13},{5,1},{13,9},{2,6},{10,14},... | collective-permute-start | bytes 516104 | tf_op jit(solution)/shard_map/ppermute | solution.py:55
  5.6 4.4 %collective-permute-start.1 = (bf16[336,256]{1,0:T(8,128)(2,1)S(1)}, bf16[336,256]{1,0:T(8,128)(2,1)S(1)}, u32[]{:S(2)}, u32[]{:S(2)}) collective-permute-start(bf16[336,256]{1,0:T(8,128)(2,1)S(1)} %get-tuple-element.33), channel_id=1, source_target_pairs={{4,8},{8,4},{5,9},{9,5},{6,10},{10,6},{7,11},{11,7},{20,24},{24,20... | collective-permute-start | bytes 516104 | tf_op jit(solution)/shard_map/ppermute | solution.py:55
  11.1 3.5 %copy-start.4 = (s32[4,1,4,128]{3,2,1,0:T(4,128)S(1)}, s32[4,1,4,128]{3,2,1,0:T(4,128)}, u32[]{:S(2)}) copy-start(s32[4,1,4,128]{3,2,1,0:T(4,128)} %gi_ref.1) | copy-start | bytes 24580
  11.1 3.5 %copy-start.5 = (f32[4,1,4,128]{3,2,1,0:T(4,128)S(1)}, f32[4,1,4,128]{3,2,1,0:T(4,128)}, u32[]{:S(2)}) copy-start(f32[4,1,4,128]{3,2,1,0:T(4,128)} %gw_ref.1) | copy-start | bytes 24580
  11.1 3.5 %copy-start.6 = (s32[3,1,4,128]{3,2,1,0:T(4,128)S(1)}, s32[3,1,4,128]{3,2,1,0:T(4,128)}, u32[]{:S(2)}) copy-start(s32[3,1,4,128]{3,2,1,0:T(4,128)} %mi_ref.1) | copy-start | bytes 18436
  11.1 3.5 %copy-start.7 = (f32[3,1,4,128]{3,2,1,0:T(4,128)S(1)}, f32[3,1,4,128]{3,2,1,0:T(4,128)}, u32[]{:S(2)}) copy-start(f32[3,1,4,128]{3,2,1,0:T(4,128)} %mw_ref.1) | copy-start | bytes 18436
  11.1 3.5 %copy-start.8 = (s32[1,4,128]{2,1,0:T(4,128)S(1)}, s32[1,4,128]{2,1,0:T(4,128)}, u32[]{:S(2)}) copy-start(s32[1,4,128]{2,1,0:T(4,128)} %gt_ref.1) | copy-start | bytes 6148
  11.1 3.5 %copy-start.9 = (s32[1,4,128]{2,1,0:T(4,128)S(1)}, s32[1,4,128]{2,1,0:T(4,128)}, u32[]{:S(2)}) copy-start(s32[1,4,128]{2,1,0:T(4,128)} %mt_ref.1) | copy-start | bytes 6148
  11.1 3.5 %copy-start.10 = (s32[1,4]{1,0:T(1,128)S(1)}, s32[1,4]{1,0:T(1,128)}, u32[]{:S(2)}) copy-start(s32[1,4]{1,0:T(1,128)} %gc_ref.1) | copy-start | bytes 52
  11.1 3.5 %copy-start.11 = (s32[1,4]{1,0:T(1,128)S(1)}, s32[1,4]{1,0:T(1,128)}, u32[]{:S(2)}) copy-start(s32[1,4]{1,0:T(1,128)} %mc_ref.1) | copy-start | bytes 52
  11.2 1.6 %collective-permute-start.2 = (bf16[128,1024]{1,0:T(8,128)(2,1)S(1)}, bf16[128,1024]{1,0:T(8,128)(2,1)S(1)}, u32[]{:S(2)}, u32[]{:S(2)}) collective-permute-start(bf16[128,1024]{1,0:T(8,128)(2,1)S(1)} %get-tuple-element.40), channel_id=1, source_target_pairs={{0,1},{1,0},{2,3},{3,2},{4,5},{5,4},{6,7},{7,6},{8,9},{9,8},{10,11... | collective-permute-start | bytes 786440 | tf_op jit(solution)/shard_map/ppermute | solution.py:379
  12.8 10.2 %copy-start.2 = (s32[2,128]{1,0:T(2,128)S(1)}, s32[2,128]{1,0:T(2,128)}, u32[]{:S(2)}) copy-start(s32[2,128]{1,0:T(2,128)} %halo_ref.1) | copy-start | bytes 3076
  12.9 8.4 %collective-permute-start.3 = (bf16[128,1024]{1,0:T(8,128)(2,1)S(1)}, bf16[128,1024]{1,0:T(8,128)(2,1)S(1)}, u32[]{:S(2)}, u32[]{:S(2)}) collective-permute-start(bf16[128,1024]{1,0:T(8,128)(2,1)S(1)} %get-tuple-element.62.after_ref), channel_id=1, source_target_pairs={{0,2},{2,0},{1,3},{3,1},{4,6},{6,4},{5,7},{7,5},{8,10},{10,8},{9,1... | collective-permute-start | bytes 786440 | tf_op jit(solution)/shard_map/ppermute | solution.py:60
  21.4 1.6 %collective-permute-start.4 = (bf16[128,1024]{1,0:T(8,128)(2,1)S(1)}, bf16[128,1024]{1,0:T(8,128)(2,1)S(1)}, u32[]{:S(2)}, u32[]{:S(2)}) collective-permute-start(bf16[128,1024]{1,0:T(8,128)(2,1)S(1)} %shard_map.198.mine_ref), channel_id=1, source_target_pairs={{0,1},{1,0},{2,3},{3,2},{4,5},{5,4},{6,7},{7,6},{8,9},{9,8},{10,11... | collective-permute-start | bytes 786440 | tf_op jit(solution)/shard_map/ppermute | solution.py:379
  23.6 9.5 %collective-permute-start.5 = (bf16[336,256]{1,0:T(8,128)(2,1)S(1)}, bf16[336,256]{1,0:T(8,128)(2,1)S(1)}, u32[]{:S(2)}, u32[]{:S(2)}) collective-permute-start(bf16[336,256]{1,0:T(8,128)(2,1)S(1)} %get-tuple-element.44), channel_id=1, source_target_pairs={{0,4},{8,12},{4,0},{12,8},{1,5},{9,13},{5,1},{13,9},{2,6},{10,14},... | collective-permute-start | bytes 516104 | tf_op jit(solution)/shard_map/ppermute | solution.py:55
  28.5 4.7 %collective-permute-start.6 = (bf16[336,256]{1,0:T(8,128)(2,1)S(1)}, bf16[336,256]{1,0:T(8,128)(2,1)S(1)}, u32[]{:S(2)}, u32[]{:S(2)}) collective-permute-start(bf16[336,256]{1,0:T(8,128)(2,1)S(1)} %get-tuple-element.45), channel_id=1, source_target_pairs={{4,8},{8,4},{5,9},{9,5},{6,10},{10,6},{7,11},{11,7},{20,24},{24,20... | collective-permute-start | bytes 516104 | tf_op jit(solution)/shard_map/ppermute | solution.py:55
  34.2 1.6 %collective-permute-start.7 = (bf16[128,1024]{1,0:T(8,128)(2,1)S(1)}, bf16[128,1024]{1,0:T(8,128)(2,1)S(1)}, u32[]{:S(2)}, u32[]{:S(2)}) collective-permute-start(bf16[128,1024]{1,0:T(8,128)(2,1)S(1)} %get-tuple-element.48), channel_id=1, source_target_pairs={{0,1},{1,0},{2,3},{3,2},{4,5},{5,4},{6,7},{7,6},{8,9},{9,8},{10,11... | collective-permute-start | bytes 786440 | tf_op jit(solution)/shard_map/ppermute | solution.py:379
  35.9 8.4 %collective-permute-start.8 = (bf16[128,1024]{1,0:T(8,128)(2,1)S(1)}, bf16[128,1024]{1,0:T(8,128)(2,1)S(1)}, u32[]{:S(2)}, u32[]{:S(2)}) collective-permute-start(bf16[128,1024]{1,0:T(8,128)(2,1)S(1)} %get-tuple-element.60), channel_id=1, source_target_pairs={{0,2},{2,0},{1,3},{3,1},{4,6},{6,4},{5,7},{7,5},{8,10},{10,8},{9,1... | collective-permute-start | bytes 786440 | tf_op jit(solution)/shard_map/ppermute | solution.py:60
  44.5 1.6 %collective-permute-start.9 = (bf16[128,1024]{1,0:T(8,128)(2,1)S(1)}, bf16[128,1024]{1,0:T(8,128)(2,1)S(1)}, u32[]{:S(2)}, u32[]{:S(2)}) collective-permute-start(bf16[128,1024]{1,0:T(8,128)(2,1)S(1)} %shard_map.202.mine_ref), channel_id=1, source_target_pairs={{0,1},{1,0},{2,3},{3,2},{4,5},{5,4},{6,7},{7,6},{8,9},{9,8},{10,11... | collective-permute-start | bytes 786440 | tf_op jit(solution)/shard_map/ppermute | solution.py:379
  47.2 8.5 %collective-permute-start.10 = (bf16[336,256]{1,0:T(8,128)(2,1)S(1)}, bf16[336,256]{1,0:T(8,128)(2,1)S(1)}, u32[]{:S(2)}, u32[]{:S(2)}) collective-permute-start(bf16[336,256]{1,0:T(8,128)(2,1)S(1)} %get-tuple-element.54), channel_id=1, source_target_pairs={{0,12},{4,8},{8,4},{12,0},{1,13},{5,9},{9,5},{13,1},{2,14},{6,10},... | collective-permute-start | bytes 516104 | tf_op jit(solution)/shard_map/ppermute | solution.py:60
  49.9 16.6 %collective-permute-start.11 = (bf16[336,256]{1,0:T(8,128)(2,1)S(1)}, bf16[336,256]{1,0:T(8,128)(2,1)S(1)}, u32[]{:S(2)}, u32[]{:S(2)}) collective-permute-start(bf16[336,256]{1,0:T(8,128)(2,1)S(1)} %get-tuple-element.55), channel_id=1, source_target_pairs={{0,8},{4,12},{8,0},{12,4},{1,9},{5,13},{9,1},{13,5},{2,10},{6,14},... | collective-permute-start | bytes 516104 | tf_op jit(solution)/shard_map/ppermute | solution.py:60
  52.4 14.2 %collective-permute-start.12 = (bf16[336,256]{1,0:T(8,128)(2,1)S(1)}, bf16[336,256]{1,0:T(8,128)(2,1)S(1)}, u32[]{:S(2)}, u32[]{:S(2)}) collective-permute-start(bf16[336,256]{1,0:T(8,128)(2,1)S(1)} %get-tuple-element.56), channel_id=1, source_target_pairs={{0,4},{4,0},{8,12},{12,8},{1,5},{5,1},{9,13},{13,9},{2,6},{6,2},{1... | collective-permute-start | bytes 516104 | tf_op jit(solution)/shard_map/ppermute | solution.py:60

commit v4 on v3

--- a/solution.py
+++ b/solution.py
@@ -295,29 +295,59 @@
             )
 
 
+def slot_values(source_refs, mix_refs, sums_ref, p, cap, bands, out_ref):
+    cut = slice(p * cap, (p + 1) * cap)
+    for kind in (0, 1):
+        value = dot(source_refs[kind], mix_refs[kind][:, cut])
+        if bands is not None:
+            row = lax.broadcasted_iota(jnp.int32, value.shape, 0)
+            value = jnp.where(row == bands, sums_ref[kind : kind + 1, cut], value)
+        out_ref[:, kind * cap : (kind + 1) * cap] = value.astype(BF16)
+
+
+def early_kernel(moved_ref, gmix_ref, mmix_ref, sums_ref, out_ref, *, bands, peer):
+    gp = gmix_ref.shape[0]
+    cap = out_ref.shape[1] // 2
+    parts = (moved_ref[:, :gp].astype(BF16), moved_ref[:, gp:].astype(BF16))
+    slot_values(parts, (gmix_ref, mmix_ref), sums_ref, peer, cap, bands, out_ref)
+
+
 def mix_kernel(
     moved_ref, mine_ref, other_ref, wout_ref, gmix_ref, mmix_ref, sums_ref, state_ref, *rest,
-    bands,
+    bands, which,
 ):
     out_refs, hid_ref = rest[:-1], rest[-1]
     add_transfer(moved_ref, mine_ref, other_ref, wout_ref, hid_ref, state_ref)
     gp = gmix_ref.shape[0]
-    peers = len(out_refs)
-    cap = gmix_ref.shape[1] // peers
-    grid = state_ref[:, :gp].astype(BF16)
-    mesh = state_ref[:, gp:].astype(BF16)
-    row = lax.broadcasted_iota(jnp.int32, (state_ref.shape[0], cap), 0)
-    for p in range(peers):
-        cut = slice(p * cap, (p + 1) * cap)
-        for kind, source, mix_ref in ((0, grid, gmix_ref), (1, mesh, mmix_ref)):
-            value = dot(source, mix_ref[:, cut])
-            value = jnp.where(row == bands, sums_ref[kind : kind + 1, cut], value)
-            out_refs[p][:, kind * cap : (kind + 1) * cap] = value.astype(BF16)
+    cap = out_refs[0].shape[1] // 2
+    parts = (state_ref[:, :gp].astype(BF16), state_ref[:, gp:].astype(BF16))
+    for p, out_ref in zip(which, out_refs):
+        slot_values(parts, (gmix_ref, mmix_ref), sums_ref, p, cap, bands, out_ref)
+
+
+def silu(total_ref, got_ref):
+    total = total_ref[...] + got_ref[...].astype(F32)
+    return (total / (1.0 + jnp.exp(-total))).astype(BF16)
 
 
 def silu_kernel(total_ref, got_ref, *rest):
-    total = total_ref[...] + got_ref[...].astype(F32)
-    rest[-1][...] = (total / (1.0 + jnp.exp(-total))).astype(BF16)
+    rest[-1][...] = silu(total_ref, got_ref)
+
+
+def silu_mix_kernel(
+    total_ref, got_ref, gmix_ref, mmix_ref, after_ref, mine_ref, mixed_ref, *, peer
+):
+    gp = gmix_ref.shape[0]
+    cap = mixed_ref.shape[1] // 2
+    mine_ref[...] = silu(total_ref, got_ref)
+    parts = (mine_ref[:, :gp], mine_ref[:, gp:])
+    slot_values(parts, (gmix_ref, mmix_ref), None, peer, cap, None, mixed_ref)
+
+
+def join_kernel(early_ref, mine_ref, other_ref, wout_ref, out_ref):
+    half = mine_ref.shape[0]
+    moved = dot(wout_ref[:, :half], mine_ref[...]) + dot(wout_ref[:, half:], other_ref[...])
+    out_ref[...] = (early_ref[...].astype(F32) + DT_STEP * moved).astype(BF16)
 
 
 def land(values, land_ref):
@@ -486,11 +516,11 @@
                 m2g_index, m2g_weight, m2g_count, m2g_target, rounded,
             )
             extra = [sums]
-        (mine,) = kernel_call(
-            silu_kernel, [(half_shape, BF16)], spaces=[VMEM, VMEM] + [pl.ANY] * len(extra)
-        )(total, got, *extra)
-        other = core_swap(mine)
         if substep < NSUB - 1:
+            (mine,) = kernel_call(
+                silu_kernel, [(half_shape, BF16)], spaces=[VMEM, VMEM] + [pl.ANY] * len(extra)
+            )(total, got, *extra)
+            other = core_swap(mine)
             state, even, odd = kernel_call(
                 functools.partial(next_kernel, grid_points=gp, cols=cols),
                 [state_shape, message, message],
@@ -498,14 +528,37 @@
                 flops=2 * padded * hid * points,
             )(moved, mine, other, wout, halo_list)
 
+    split = peers // 2
+    slot_shape = ((padded, 2 * cap), BF16)
+    (early,) = kernel_call(
+        functools.partial(early_kernel, bands=bands, peer=split),
+        [slot_shape],
+        flops=2 * padded * points * cap,
+    )(moved, gmix, mmix, sums)
+    early = peer_swap(early, "sp", split)
+    mine, mixed = kernel_call(
+        functools.partial(silu_mix_kernel, peer=split),
+        [(half_shape, BF16), ((half, 2 * cap), BF16)],
+        flops=2 * half * points * cap,
+        spaces=[VMEM] * 4 + [pl.ANY],
+    )(total, got, gmix, mmix, early)
+    other = core_swap(mine)
+    mixed = peer_swap(mixed, "sp", split)
+    which = [p for p in range(peers) if p != split]
     state, *values = kernel_call(
-        functools.partial(mix_kernel, bands=bands),
-        [state_shape] + [((padded, 2 * cap), BF16)] * peers,
+        functools.partial(mix_kernel, bands=bands, which=which),
+        [state_shape] + [slot_shape] * len(which),
         [hid_scratch],
-        flops=2 * padded * (hid * points + points * peers * cap),
+        flops=2 * padded * (hid * points + points * len(which) * cap),
     )(moved, mine, other, wout, gmix, mmix, sums)
-    for p in reversed(range(1, peers)):
+    values = dict(zip(which, values))
+    mixed, state = lax.optimization_barrier((mixed, state))
+    for p in which[1:]:
         values[p] = peer_swap(values[p], "sp", p)
+    (values[split],) = kernel_call(join_kernel, [slot_shape], flops=900 << 20)(
+        early, mixed, core_swap(mixed), wout
+    )
+    values = [values[p] for p in range(peers)]
     grid_out, mesh_out = kernel_call(
         functools.partial(end_kernel, bands=bands),
         [(grid_flat.shape, F32), (mesh_spec.shape, F32)],

time: 68.8 us -> 66.9 us (0.972)
  waiting for transfers between devices: 33.7 us -> 29.8 us
  starting transfers between devices: 18.4 us -> 20 us
    ppermute x5 -> x6, waiting for transfers between devices: 25.2 us -> 20 us  [peer_swap(): return lax.ppermute(array, axis, [(i, i ^ step) for i in range(size)])]
    ppermute x5 -> x6, starting transfers between devices: 8.73 us -> 10.3 us  [peer_swap(): return lax.ppermute(array, axis, [(i, i ^ step) for i in range(size)])]
    ppermute x4 -> x5, waiting for transfers between devices: 6.09 us -> 7.26 us  [core_swap(): return lax.ppermute(array, 'dr', [(0, 1), (1, 0)])]
    pallas_call x11 -> x13, Pallas kernels: 15 us -> 15.5 us  [run(): pl.pallas_call(body, out_shape=[jax.ShapeDtypeStruct(s, t) for s, t in ou...]
  transfers between devices with their start and end apart: 13 -> 15, of which waited for: 10 -> 12; matrix products, arithmetic and copies ran while one was open for 0% -> 0% of each run, Pallas kernels for 10% -> 13%
where the time goes in v4:
time: 66.9 us; the launch traced here: 66.8 us
  waiting for transfers between devices  29.8 us (45%)
  starting transfers between devices  20 us (30%)
  Pallas kernels  15.5 us (23%)
  between operations  1.15 us (2%)
    ppermute x6, waiting for transfers between devices, peer_swap(): return lax.ppermute(array, axis, [(i, i ^ step) for i in range(size)])  20 us
    pallas_call x13, Pallas kernels, run(): pl.pallas_call(body, out_shape=[jax.ShapeDtypeStruct(s, t) for s, t in ou...  15.5 us
    ppermute x6, starting transfers between devices, peer_swap(): return lax.ppermute(array, axis, [(i, i ^ step) for i in range(size)])  10.3 us
    ppermute x4, starting transfers between devices, pair_swap(): return lax.ppermute(array, axis, pairs + [(j, i) for i, j in pairs])  9.41 us
    ppermute x5, waiting for transfers between devices, core_swap(): return lax.ppermute(array, 'dr', [(0, 1), (1, 0)])  7.26 us
    ppermute x4, waiting for transfers between devices, pair_swap(): return lax.ppermute(array, axis, pairs + [(j, i) for i, j in pairs])  2.46 us
  transfers between devices with their start and end apart: 15, of which 12 were waited for; matrix products, arithmetic and copies ran while one was open for 0% of the time, Pallas kernels for 13%

profile of v4, /device:TPU:0, one launch (start us, length us, event | category | flops | bytes accessed | tf_op | source)
XLA Modules:
  0.0 66.8 jit_solution(15758747973870051279)
XLA Ops:
  0.6 0.0 copy-start.13
  0.6 0.0 copy-start.12
  0.7 0.0 copy-start
  0.7 0.0 copy-start.1
  0.7 0.0 copy-start.3
  0.7 1.8 %shard_map.195 = (bf16[336,256]{1,0:T(8,128)(2,1)S(1)}, bf16[336,256]{1,0:T(8,128)(2,1)S(1)}) custom-call(f32[1296,128]{1,0:T(8,128)} %bitcast.3, f32[18,18,512]{2,1,0:T(8,128)} %mesh_hbm.3, s32[2,128]{1,0:T(2,128)} %halo_ref.1), custom_call_target="tpu_custom_call" | custom-call | flops 88080384 | bytes 2097152 | tf_op jit(solution)/shard_map/pallas_call | solution.py:30
  2.5 3.1 %collective-permute-start = (bf16[336,256]{1,0:T(8,128)(2,1)S(1)}, bf16[336,256]{1,0:T(8,128)(2,1)S(1)}, u32[]{:S(2)}, u32[]{:S(2)}) collective-permute-start(bf16[336,256]{1,0:T(8,128)(2,1)S(1)} %get-tuple-element.35), channel_id=1, source_target_pairs={{0,4},{8,12},{4,0},{12,8},{1,5},{9,13},{5,1},{13,9},{2,6},{10,14},... | collective-permute-start | bytes 516104 | tf_op jit(solution)/shard_map/ppermute | solution.py:55
  5.6 0.7 collective-permute-start.1
  6.3 0.0 copy-done.13
  6.3 0.0 copy-done.12
  6.3 0.1 cosine_multiply_fusion
  6.4 0.0 copy-done
  6.4 0.0 copy-done.1
  6.4 3.4 %shard_map.194 = (f32[336,1024]{1,0:T(8,128)S(1)}, bf16[4,768,512]{2,1,0:T(8,128)(2,1)S(1)}, f32[4,336,512]{2,1,0:T(8,128)S(1)}, f32[336,2]{1,0:T(8,128)S(1)}, b...) custom-call(f32[1296,128]{1,0:T(8,128)} %bitcast.4, f32[18,18,512]{2,1,0:T(8,128)} %mesh_hbm.3, ...), custom_call_target="tpu_custom_call" | custom-call | flops 2113929216 | bytes 2097152 | tf_op jit(solution)/shard_map/pallas_call | solution.py:30
  9.8 0.1 collective-permute-done.even_ref
  10.0 0.0 collective-permute-done.1.odd_ref
  10.0 1.1 %shard_map.196 = (f32[336,1024]{1,0:T(8,128)S(1)}, f32[128,1024]{1,0:T(8,128)S(1)}, bf16[128,1024]{1,0:T(8,128)(2,1)S(1)}) custom-call(f32[336,1024]{1,0:T(8,128)S(1)} %get-tuple-element.34.part_ref, bf16[336,256]{1,0:T(8,128)(2,1)S(1)} %collective-permute-done.even_ref, bf16[336,256]{1,0:T(8,128)(2,1)S(1)} %collective-permute-done.1.odd_ref, ...), custom_call_target="tpu_custom_call" | custom-call | flops 528482304 | bytes 2097152 | tf_op jit(solution)/shard_map/pallas_call | solution.py:30
  11.1 0.0 copy-start.4
  11.1 0.0 copy-start.5
  11.1 0.0 copy-start.6
  11.1 0.0 copy-start.7
  11.1 0.0 copy-start.8
  11.1 0.0 copy-start.9
  11.1 0.0 copy-start.10
  11.1 0.0 copy-start.11
  11.2 0.1 collective-permute-start.2
  11.2 1.5 %collective-permute-done.2 = bf16[128,1024]{1,0:T(8,128)(2,1)S(1)} collective-permute-done((bf16[128,1024]{1,0:T(8,128)(2,1)S(1)}, bf16[128,1024]{1,0:T(8,128)(2,1)S(1)}, u32[]{:S(2)}, u32[]{:S(2)}) %collective-permute-start.2) | collective-permute-done | bytes 262176 | tf_op jit(solution)/shard_map/ppermute | solution.py:409
  12.8 0.1 fusion.1
  12.8 0.0 copy-start.2
  12.9 1.7 %collective-permute-start.3 = (bf16[128,1024]{1,0:T(8,128)(2,1)S(1)}, bf16[128,1024]{1,0:T(8,128)(2,1)S(1)}, u32[]{:S(2)}, u32[]{:S(2)}) collective-permute-start(bf16[128,1024]{1,0:T(8,128)(2,1)S(1)} %get-tuple-element.68.after_ref), channel_id=1, source_target_pairs={{0,2},{2,0},{1,3},{3,1},{4,6},{6,4},{5,7},{7,5},{8,10},{10,8},{9,1... | collective-permute-start | bytes 786440 | tf_op jit(solution)/shard_map/ppermute | solution.py:60
  14.6 2.2 %shard_map.197 = (bf16[512,512]{1,0:T(8,128)(2,1)S(1)}, bf16[512,512]{1,0:T(8,128)(2,1)S(1)}, f32[2,512]{1,0:T(2,128)S(1)}, bf16[512,512]{1,0:T(8,128)(2,1)S(1)}, bf16[512,512]{1,0:T(8,128)(2,1)S(1)}) custom-call(s32[4,1,4,128]{3,2,1,0:T(4,128)S(1)} %copy-done.4, f32[4,1,4,128]{3,2,1,0:T(4,128)S(1)} %copy-done.5, s32[1,4]{1,0:T(1,128)S(1)} %copy-done.10, ...), custom_call_target="tpu_custom_call" | custom-call | flops 2147483648 | bytes 2097152 | tf_op jit(solution)/shard_map/pallas_call | solution.py:30
  16.8 4.5 %collective-permute-done.3.got_ref = bf16[128,1024]{1,0:T(8,128)(2,1)S(1)} collective-permute-done((bf16[128,1024]{1,0:T(8,128)(2,1)S(1)}, bf16[128,1024]{1,0:T(8,128)(2,1)S(1)}, u32[]{:S(2)}, u32[]{:S(2)}) %collective-permute-start.3) | collective-permute-done | bytes 262176 | tf_op jit(solution)/shard_map/ppermute | solution.py:60
  21.3 0.2 shard_map.198.mine_ref
  21.4 0.1 collective-permute-start.4
  21.5 1.5 %collective-permute-done.4.other_ref = bf16[128,1024]{1,0:T(8,128)(2,1)S(1)} collective-permute-done((bf16[128,1024]{1,0:T(8,128)(2,1)S(1)}, bf16[128,1024]{1,0:T(8,128)(2,1)S(1)}, u32[]{:S(2)}, u32[]{:S(2)}) %collective-permute-start.4) | collective-permute-done | bytes 262176 | tf_op jit(solution)/shard_map/ppermute | solution.py:409
  23.0 0.6 shard_map.199
  23.6 4.8 %collective-permute-start.5 = (bf16[336,256]{1,0:T(8,128)(2,1)S(1)}, bf16[336,256]{1,0:T(8,128)(2,1)S(1)}, u32[]{:S(2)}, u32[]{:S(2)}) collective-permute-start(bf16[336,256]{1,0:T(8,128)(2,1)S(1)} %get-tuple-element.47), channel_id=1, source_target_pairs={{0,4},{8,12},{4,0},{12,8},{1,5},{9,13},{5,1},{13,9},{2,6},{10,14},... | collective-permute-start | bytes 516104 | tf_op jit(solution)/shard_map/ppermute | solution.py:55
  28.5 0.8 %collective-permute-start.6 = (bf16[336,256]{1,0:T(8,128)(2,1)S(1)}, bf16[336,256]{1,0:T(8,128)(2,1)S(1)}, u32[]{:S(2)}, u32[]{:S(2)}) collective-permute-start(bf16[336,256]{1,0:T(8,128)(2,1)S(1)} %get-tuple-element.48), channel_id=1, source_target_pairs={{4,8},{8,4},{5,9},{9,5},{6,10},{10,6},{7,11},{11,7},{20,24},{24,20... | collective-permute-start | bytes 516104 | tf_op jit(solution)/shard_map/ppermute | solution.py:55
  29.3 1.5 %shard_map.200.part_ref = f32[336,1024]{1,0:T(8,128)S(1)} custom-call(f32[336,1024]{1,0:T(8,128)S(1)} %get-tuple-element.46.state_ref, bf16[4,768,512]{2,1,0:T(8,128)(2,1)S(1)} %get-tuple-element.37.hot_ref, f32[4,336,512]{2,1,0:T(8,128)S(1)} %get-tuple-element.38.weight_ref, f32[336,2]{1,0:T(8,128)S(1)} %get-tuple-element.39.band_ref, ...), custom_call_target="tpu_custom_call" | custom-call | flops 704643072 | bytes 2097152 | tf_op jit(solution)/shard_map/pallas_call | solution.py:30
  30.8 2.3 %collective-permute-done.5.even_ref = bf16[336,256]{1,0:T(8,128)(2,1)S(1)} collective-permute-done((bf16[336,256]{1,0:T(8,128)(2,1)S(1)}, bf16[336,256]{1,0:T(8,128)(2,1)S(1)}, u32[]{:S(2)}, u32[]{:S(2)}) %collective-permute-start.5) | collective-permute-done | bytes 172064 | tf_op jit(solution)/shard_map/ppermute | solution.py:55
  33.1 0.0 collective-permute-done.6.odd_ref
  33.1 1.1 %shard_map.201 = (f32[336,1024]{1,0:T(8,128)S(1)}, f32[128,1024]{1,0:T(8,128)S(1)}, bf16[128,1024]{1,0:T(8,128)(2,1)S(1)}) custom-call(f32[336,1024]{1,0:T(8,128)S(1)} %shard_map.200.part_ref, bf16[336,256]{1,0:T(8,128)(2,1)S(1)} %collective-permute-done.5.even_ref, bf16[336,256]{1,0:T(8,128)(2,1)S(1)} %collective-permute-done.6.odd_ref, ...), custom_call_target="tpu_custom_call" | custom-call | flops 528482304 | bytes 2097152 | tf_op jit(solution)/shard_map/pallas_call | solution.py:30
  34.2 0.1 collective-permute-start.7
  34.3 1.5 %collective-permute-done.7 = bf16[128,1024]{1,0:T(8,128)(2,1)S(1)} collective-permute-done((bf16[128,1024]{1,0:T(8,128)(2,1)S(1)}, bf16[128,1024]{1,0:T(8,128)(2,1)S(1)}, u32[]{:S(2)}, u32[]{:S(2)}) %collective-permute-start.7) | collective-permute-done | bytes 262176 | tf_op jit(solution)/shard_map/ppermute | solution.py:409
  35.8 0.1 fusion
  35.9 1.6 %collective-permute-start.8 = (bf16[128,1024]{1,0:T(8,128)(2,1)S(1)}, bf16[128,1024]{1,0:T(8,128)(2,1)S(1)}, u32[]{:S(2)}, u32[]{:S(2)}) collective-permute-start(bf16[128,1024]{1,0:T(8,128)(2,1)S(1)} %get-tuple-element.66), channel_id=1, source_target_pairs={{0,2},{2,0},{1,3},{3,1},{4,6},{6,4},{5,7},{7,5},{8,10},{10,8},{9,1... | collective-permute-start | bytes 786440 | tf_op jit(solution)/shard_map/ppermute | solution.py:60
  37.5 0.3 shard_map.202
  37.8 4.9 %collective-permute-start.9 = (bf16[336,256]{1,0:T(8,128)(2,1)S(1)}, bf16[336,256]{1,0:T(8,128)(2,1)S(1)}, u32[]{:S(2)}, u32[]{:S(2)}) collective-permute-start(bf16[336,256]{1,0:T(8,128)(2,1)S(1)} %shard_map.202), channel_id=1, source_target_pairs={{0,8},{4,12},{8,0},{12,4},{1,9},{5,13},{9,1},{13,5},{2,10},{6,14},... | collective-permute-start | bytes 516104 | tf_op jit(solution)/shard_map/ppermute | solution.py:60
  42.7 8.1 %collective-permute-done.9.after_ref.early_ref = bf16[336,256]{1,0:T(8,128)(2,1)S(1)} collective-permute-done((bf16[336,256]{1,0:T(8,128)(2,1)S(1)}, bf16[336,256]{1,0:T(8,128)(2,1)S(1)}, u32[]{:S(2)}, u32[]{:S(2)}) %collective-permute-start.9) | collective-permute-done | bytes 172064 | tf_op jit(solution)/shard_map/ppermute | solution.py:60
  50.8 0.0 collective-permute-done.8.got_ref
  50.8 0.3 shard_map.203
  51.1 0.1 collective-permute-start.11
  51.2 0.1 collective-permute-start.10
  51.3 1.4 %collective-permute-done.11.other_ref = bf16[128,1024]{1,0:T(8,128)(2,1)S(1)} collective-permute-done((bf16[128,1024]{1,0:T(8,128)(2,1)S(1)}, bf16[128,1024]{1,0:T(8,128)(2,1)S(1)}, u32[]{:S(2)}, u32[]{:S(2)}) %collective-permute-start.11) | collective-permute-done | bytes 262176 | tf_op jit(solution)/shard_map/ppermute | solution.py:409
  52.7 0.9 %shard_map.204 = (f32[336,1024]{1,0:T(8,128)S(1)}, bf16[336,256]{1,0:T(8,128)(2,1)S(1)}, bf16[336,256]{1,0:T(8,128)(2,1)S(1)}, bf16[336,256]{1,0:T(8,128)(2,1)S(1)}) custom-call(f32[336,1024]{1,0:T(8,128)S(1)} %get-tuple-element.53.moved_ref, bf16[128,1024]{1,0:T(8,128)(2,1)S(1)} %get-tuple-element.55.mine_ref, ...), custom_call_target="tpu_custom_call" | custom-call | flops 440401920 | bytes 2097152 | tf_op jit(solution)/shard_map/pallas_call | solution.py:30
  53.6 1.3 %collective-permute-start.12 = (bf16[336,256]{1,0:T(8,128)(2,1)S(1)}, bf16[336,256]{1,0:T(8,128)(2,1)S(1)}, u32[]{:S(2)}, u32[]{:S(2)}) collective-permute-start(bf16[336,256]{1,0:T(8,128)(2,1)S(1)} %get-tuple-element.60), channel_id=1, source_target_pairs={{0,12},{4,8},{8,4},{12,0},{1,13},{5,9},{9,5},{13,1},{2,14},{6,10},... | collective-permute-start | bytes 516104 | tf_op jit(solution)/shard_map/ppermute | solution.py:60
  54.9 0.8 %collective-permute-start.14 = (bf16[336,256]{1,0:T(8,128)(2,1)S(1)}, bf16[336,256]{1,0:T(8,128)(2,1)S(1)}, u32[]{:S(2)}, u32[]{:S(2)}) collective-permute-start(bf16[336,256]{1,0:T(8,128)(2,1)S(1)} %get-tuple-element.62), channel_id=1, source_target_pairs={{0,4},{4,0},{8,12},{12,8},{1,5},{5,1},{9,13},{13,9},{2,6},{6,2},{1... | collective-permute-start | bytes 516104 | tf_op jit(solution)/shard_map/ppermute | solution.py:60
  55.7 1.2 %collective-permute-done.10.mine_ref = bf16[128,256]{1,0:T(8,128)(2,1)S(1)} collective-permute-done((bf16[128,256]{1,0:T(8,128)(2,1)S(1)}, bf16[128,256]{1,0:T(8,128)(2,1)S(1)}, u32[]{:S(2)}, u32[]{:S(2)}) %collective-permute-start.10) | collective-permute-done | bytes 65568 | tf_op jit(solution)/shard_map/ppermute | solution.py:60
  57.0 0.0 collective-permute-start.13
  57.0 1.3 %collective-permute-done.13.other_ref = bf16[128,256]{1,0:T(8,128)(2,1)S(1)} collective-permute-done((bf16[128,256]{1,0:T(8,128)(2,1)S(1)}, bf16[128,256]{1,0:T(8,128)(2,1)S(1)}, u32[]{:S(2)}, u32[]{:S(2)}) %collective-permute-start.13) | collective-permute-done | bytes 65568 | tf_op jit(solution)/shard_map/ppermute | solution.py:409
  58.2 0.2 shard_map.205.rest_1_
  58.4 4.3 %collective-permute-done.12.rest_0_ = bf16[336,256]{1,0:T(8,128)(2,1)S(1)} collective-permute-done((bf16[336,256]{1,0:T(8,128)(2,1)S(1)}, bf16[336,256]{1,0:T(8,128)(2,1)S(1)}, u32[]{:S(2)}, u32[]{:S(2)}) %collective-permute-start.12) | collective-permute-done | bytes 172064 | tf_op jit(solution)/shard_map/ppermute | solution.py:60
  62.8 1.9 %collective-permute-done.14.rest_2_ = bf16[336,256]{1,0:T(8,128)(2,1)S(1)} collective-permute-done((bf16[336,256]{1,0:T(8,128)(2,1)S(1)}, bf16[336,256]{1,0:T(8,128)(2,1)S(1)}, u32[]{:S(2)}, u32[]{:S(2)}) %collective-permute-start.14) | collective-permute-done | bytes 172064 | tf_op jit(solution)/shard_map/ppermute | solution.py:60
  64.7 1.9 %shard_map.206 = (f32[1296,128]{1,0:T(8,128)}, f32[18,18,512]{2,1,0:T(8,128)}) custom-call(f32[336,1024]{1,0:T(8,128)S(1)} %get-tuple-element.57.state_ref, bf16[512,512]{1,0:T(8,128)(2,1)S(1)} %get-tuple-element.58.gland_ref, bf16[512,512]{1,0:T(8,128)(2,1)S(1)} %get-tuple-element.59.mland_ref, s32[4,128]{1,0:T(4,128)S(1)} %copy-done, ...), custom_call_target="tpu_custom_call" | custom-call | flops 352321536 | bytes 2097152 | tf_op jit(solution)/shard_map/pallas_call | solution.py:30
  (11 shorter events, 0.0 us)
Async XLA Ops:
  0.6 5.6 %copy-start.13 = (f32[4,512]{1,0:T(4,128)S(1)}, f32[4,512]{1,0:T(4,128)}, u32[]{:S(2)}) copy-start(f32[4,512]{1,0:T(4,128)} %param.25) | copy-start | bytes 24580
  0.6 5.6 %copy-start.12 = (f32[4,512]{1,0:T(4,128)S(1)}, f32[4,512]{1,0:T(4,128)}, u32[]{:S(2)}) copy-start(f32[4,512]{1,0:T(4,128)} %param.24) | copy-start | bytes 24580
  0.7 5.7 %copy-start = (s32[4,128]{1,0:T(4,128)S(1)}, s32[4,128]{1,0:T(4,128)}, u32[]{:S(2)}) copy-start(s32[4,128]{1,0:T(4,128)} %sea_ref.9) | copy-start | bytes 6148
  0.7 5.7 %copy-start.1 = (f32[4,128]{1,0:T(4,128)S(1)}, f32[4,128]{1,0:T(4,128)}, u32[]{:S(2)}) copy-start(f32[4,128]{1,0:T(4,128)} %speed_ref.7) | copy-start | bytes 6148
  0.7 5.7 %copy-start.3 = (s32[4,512]{1,0:T(4,128)S(1)}, s32[4,512]{1,0:T(4,128)}, u32[]{:S(2)}) copy-start(s32[4,512]{1,0:T(4,128)} %index_ref.1) | copy-start | bytes 24580
  2.5 7.5 %collective-permute-start = (bf16[336,256]{1,0:T(8,128)(2,1)S(1)}, bf16[336,256]{1,0:T(8,128)(2,1)S(1)}, u32[]{:S(2)}, u32[]{:S(2)}) collective-permute-start(bf16[336,256]{1,0:T(8,128)(2,1)S(1)} %get-tuple-element.35), channel_id=1, source_target_pairs={{0,4},{8,12},{4,0},{12,8},{1,5},{9,13},{5,1},{13,9},{2,6},{10,14},... | collective-permute-start | bytes 516104 | tf_op jit(solution)/shard_map/ppermute | solution.py:55
  5.6 4.4 %collective-permute-start.1 = (bf16[336,256]{1,0:T(8,128)(2,1)S(1)}, bf16[336,256]{1,0:T(8,128)(2,1)S(1)}, u32[]{:S(2)}, u32[]{:S(2)}) collective-permute-start(bf16[336,256]{1,0:T(8,128)(2,1)S(1)} %get-tuple-element.36), channel_id=1, source_target_pairs={{4,8},{8,4},{5,9},{9,5},{6,10},{10,6},{7,11},{11,7},{20,24},{24,20... | collective-permute-start | bytes 516104 | tf_op jit(solution)/shard_map/ppermute | solution.py:55
  11.1 3.5 %copy-start.4 = (s32[4,1,4,128]{3,2,1,0:T(4,128)S(1)}, s32[4,1,4,128]{3,2,1,0:T(4,128)}, u32[]{:S(2)}) copy-start(s32[4,1,4,128]{3,2,1,0:T(4,128)} %gi_ref.1) | copy-start | bytes 24580
  11.1 3.5 %copy-start.5 = (f32[4,1,4,128]{3,2,1,0:T(4,128)S(1)}, f32[4,1,4,128]{3,2,1,0:T(4,128)}, u32[]{:S(2)}) copy-start(f32[4,1,4,128]{3,2,1,0:T(4,128)} %gw_ref.1) | copy-start | bytes 24580
  11.1 3.5 %copy-start.6 = (s32[3,1,4,128]{3,2,1,0:T(4,128)S(1)}, s32[3,1,4,128]{3,2,1,0:T(4,128)}, u32[]{:S(2)}) copy-start(s32[3,1,4,128]{3,2,1,0:T(4,128)} %mi_ref.1) | copy-start | bytes 18436
  11.1 3.5 %copy-start.7 = (f32[3,1,4,128]{3,2,1,0:T(4,128)S(1)}, f32[3,1,4,128]{3,2,1,0:T(4,128)}, u32[]{:S(2)}) copy-start(f32[3,1,4,128]{3,2,1,0:T(4,128)} %mw_ref.1) | copy-start | bytes 18436
  11.1 3.5 %copy-start.8 = (s32[1,4,128]{2,1,0:T(4,128)S(1)}, s32[1,4,128]{2,1,0:T(4,128)}, u32[]{:S(2)}) copy-start(s32[1,4,128]{2,1,0:T(4,128)} %gt_ref.1) | copy-start | bytes 6148
  11.1 3.5 %copy-start.9 = (s32[1,4,128]{2,1,0:T(4,128)S(1)}, s32[1,4,128]{2,1,0:T(4,128)}, u32[]{:S(2)}) copy-start(s32[1,4,128]{2,1,0:T(4,128)} %mt_ref.1) | copy-start | bytes 6148
  11.1 3.5 %copy-start.10 = (s32[1,4]{1,0:T(1,128)S(1)}, s32[1,4]{1,0:T(1,128)}, u32[]{:S(2)}) copy-start(s32[1,4]{1,0:T(1,128)} %gc_ref.1) | copy-start | bytes 52
  11.1 3.5 %copy-start.11 = (s32[1,4]{1,0:T(1,128)S(1)}, s32[1,4]{1,0:T(1,128)}, u32[]{:S(2)}) copy-start(s32[1,4]{1,0:T(1,128)} %mc_ref.1) | copy-start | bytes 52
  11.2 1.6 %collective-permute-start.2 = (bf16[128,1024]{1,0:T(8,128)(2,1)S(1)}, bf16[128,1024]{1,0:T(8,128)(2,1)S(1)}, u32[]{:S(2)}, u32[]{:S(2)}) collective-permute-start(bf16[128,1024]{1,0:T(8,128)(2,1)S(1)} %get-tuple-element.43), channel_id=1, source_target_pairs={{0,1},{1,0},{2,3},{3,2},{4,5},{5,4},{6,7},{7,6},{8,9},{9,8},{10,11... | collective-permute-start | bytes 786440 | tf_op jit(solution)/shard_map/ppermute | solution.py:409
  12.8 10.2 %copy-start.2 = (s32[2,128]{1,0:T(2,128)S(1)}, s32[2,128]{1,0:T(2,128)}, u32[]{:S(2)}) copy-start(s32[2,128]{1,0:T(2,128)} %halo_ref.1) | copy-start | bytes 3076
  12.9 8.4 %collective-permute-start.3 = (bf16[128,1024]{1,0:T(8,128)(2,1)S(1)}, bf16[128,1024]{1,0:T(8,128)(2,1)S(1)}, u32[]{:S(2)}, u32[]{:S(2)}) collective-permute-start(bf16[128,1024]{1,0:T(8,128)(2,1)S(1)} %get-tuple-element.68.after_ref), channel_id=1, source_target_pairs={{0,2},{2,0},{1,3},{3,1},{4,6},{6,4},{5,7},{7,5},{8,10},{10,8},{9,1... | collective-permute-start | bytes 786440 | tf_op jit(solution)/shard_map/ppermute | solution.py:60
  21.4 1.6 %collective-permute-start.4 = (bf16[128,1024]{1,0:T(8,128)(2,1)S(1)}, bf16[128,1024]{1,0:T(8,128)(2,1)S(1)}, u32[]{:S(2)}, u32[]{:S(2)}) collective-permute-start(bf16[128,1024]{1,0:T(8,128)(2,1)S(1)} %shard_map.198.mine_ref), channel_id=1, source_target_pairs={{0,1},{1,0},{2,3},{3,2},{4,5},{5,4},{6,7},{7,6},{8,9},{9,8},{10,11... | collective-permute-start | bytes 786440 | tf_op jit(solution)/shard_map/ppermute | solution.py:409
  23.6 9.5 %collective-permute-start.5 = (bf16[336,256]{1,0:T(8,128)(2,1)S(1)}, bf16[336,256]{1,0:T(8,128)(2,1)S(1)}, u32[]{:S(2)}, u32[]{:S(2)}) collective-permute-start(bf16[336,256]{1,0:T(8,128)(2,1)S(1)} %get-tuple-element.47), channel_id=1, source_target_pairs={{0,4},{8,12},{4,0},{12,8},{1,5},{9,13},{5,1},{13,9},{2,6},{10,14},... | collective-permute-start | bytes 516104 | tf_op jit(solution)/shard_map/ppermute | solution.py:55
  28.5 4.7 %collective-permute-start.6 = (bf16[336,256]{1,0:T(8,128)(2,1)S(1)}, bf16[336,256]{1,0:T(8,128)(2,1)S(1)}, u32[]{:S(2)}, u32[]{:S(2)}) collective-permute-start(bf16[336,256]{1,0:T(8,128)(2,1)S(1)} %get-tuple-element.48), channel_id=1, source_target_pairs={{4,8},{8,4},{5,9},{9,5},{6,10},{10,6},{7,11},{11,7},{20,24},{24,20... | collective-permute-start | bytes 516104 | tf_op jit(solution)/shard_map/ppermute | solution.py:55
  34.2 1.6 %collective-permute-start.7 = (bf16[128,1024]{1,0:T(8,128)(2,1)S(1)}, bf16[128,1024]{1,0:T(8,128)(2,1)S(1)}, u32[]{:S(2)}, u32[]{:S(2)}) collective-permute-start(bf16[128,1024]{1,0:T(8,128)(2,1)S(1)} %get-tuple-element.50), channel_id=1, source_target_pairs={{0,1},{1,0},{2,3},{3,2},{4,5},{5,4},{6,7},{7,6},{8,9},{9,8},{10,11... | collective-permute-start | bytes 786440 | tf_op jit(solution)/shard_map/ppermute | solution.py:409
  35.9 14.9 %collective-permute-start.8 = (bf16[128,1024]{1,0:T(8,128)(2,1)S(1)}, bf16[128,1024]{1,0:T(8,128)(2,1)S(1)}, u32[]{:S(2)}, u32[]{:S(2)}) collective-permute-start(bf16[128,1024]{1,0:T(8,128)(2,1)S(1)} %get-tuple-element.66), channel_id=1, source_target_pairs={{0,2},{2,0},{1,3},{3,1},{4,6},{6,4},{5,7},{7,5},{8,10},{10,8},{9,1... | collective-permute-start | bytes 786440 | tf_op jit(solution)/shard_map/ppermute | solution.py:60
  37.8 13.0 %collective-permute-start.9 = (bf16[336,256]{1,0:T(8,128)(2,1)S(1)}, bf16[336,256]{1,0:T(8,128)(2,1)S(1)}, u32[]{:S(2)}, u32[]{:S(2)}) collective-permute-start(bf16[336,256]{1,0:T(8,128)(2,1)S(1)} %shard_map.202), channel_id=1, source_target_pairs={{0,8},{4,12},{8,0},{12,4},{1,9},{5,13},{9,1},{13,5},{2,10},{6,14},... | collective-permute-start | bytes 516104 | tf_op jit(solution)/shard_map/ppermute | solution.py:60
  51.1 1.6 %collective-permute-start.11 = (bf16[128,1024]{1,0:T(8,128)(2,1)S(1)}, bf16[128,1024]{1,0:T(8,128)(2,1)S(1)}, u32[]{:S(2)}, u32[]{:S(2)}) collective-permute-start(bf16[128,1024]{1,0:T(8,128)(2,1)S(1)} %get-tuple-element.55.mine_ref), channel_id=1, source_target_pairs={{0,1},{1,0},{2,3},{3,2},{4,5},{5,4},{6,7},{7,6},{8,9},{9,8},{10,11... | collective-permute-start | bytes 786440 | tf_op jit(solution)/shard_map/ppermute | solution.py:409
  51.2 5.8 %collective-permute-start.10 = (bf16[128,256]{1,0:T(8,128)(2,1)S(1)}, bf16[128,256]{1,0:T(8,128)(2,1)S(1)}, u32[]{:S(2)}, u32[]{:S(2)}) collective-permute-start(bf16[128,256]{1,0:T(8,128)(2,1)S(1)} %get-tuple-element.54), channel_id=1, source_target_pairs={{0,8},{4,12},{8,0},{12,4},{1,9},{5,13},{9,1},{13,5},{2,10},{6,14},... | collective-permute-start | bytes 196616 | tf_op jit(solution)/shard_map/ppermute | solution.py:60
  53.6 9.1 %collective-permute-start.12 = (bf16[336,256]{1,0:T(8,128)(2,1)S(1)}, bf16[336,256]{1,0:T(8,128)(2,1)S(1)}, u32[]{:S(2)}, u32[]{:S(2)}) collective-permute-start(bf16[336,256]{1,0:T(8,128)(2,1)S(1)} %get-tuple-element.60), channel_id=1, source_target_pairs={{0,12},{4,8},{8,4},{12,0},{1,13},{5,9},{9,5},{13,1},{2,14},{6,10},... | collective-permute-start | bytes 516104 | tf_op jit(solution)/shard_map/ppermute | solution.py:60
  54.9 9.8 %collective-permute-start.14 = (bf16[336,256]{1,0:T(8,128)(2,1)S(1)}, bf16[336,256]{1,0:T(8,128)(2,1)S(1)}, u32[]{:S(2)}, u32[]{:S(2)}) collective-permute-start(bf16[336,256]{1,0:T(8,128)(2,1)S(1)} %get-tuple-element.62), channel_id=1, source_target_pairs={{0,4},{4,0},{8,12},{12,8},{1,5},{5,1},{9,13},{13,9},{2,6},{6,2},{1... | collective-permute-start | bytes 516104 | tf_op jit(solution)/shard_map/ppermute | solution.py:60
  57.0 1.3 %collective-permute-start.13 = (bf16[128,256]{1,0:T(8,128)(2,1)S(1)}, bf16[128,256]{1,0:T(8,128)(2,1)S(1)}, u32[]{:S(2)}, u32[]{:S(2)}) collective-permute-start(bf16[128,256]{1,0:T(8,128)(2,1)S(1)} %collective-permute-done.10.mine_ref), channel_id=1, source_target_pairs={{0,1},{1,0},{2,3},{3,2},{4,5},{5,4},{6,7},{7,6},{8,9},{9,8},{10,11... | collective-permute-start | bytes 196616 | tf_op jit(solution)/shard_map/ppermute | solution.py:409

commit v5 on v4

--- a/solution.py
+++ b/solution.py
@@ -14,13 +14,14 @@
 F32 = jnp.float32
 BF16 = jnp.bfloat16
 CHUNK = 16
+FLOPS_PER_US = 1.15e9
 
 
 VMEM = pltpu.MemorySpace.VMEM
 HBM = pltpu.MemorySpace.HBM
 
 
-def kernel_call(body, outs, scratch=(), flops=0, nbytes=2 << 20, spaces=None, out_space=VMEM):
+def kernel_call(body, outs, scratch, expected_us, spaces=None, out_space=VMEM):
     def run(*args):
         where = spaces or [VMEM] * len(args)
         args = [
@@ -34,7 +35,9 @@
             out_specs=[pl.BlockSpec(memory_space=out_space)] * len(outs),
             scratch_shapes=[s if hasattr(s, "dtype") else pltpu.VMEM(*s) for s in scratch],
             compiler_params=pltpu.CompilerParams(vmem_limit_bytes=16 << 20),
-            cost_estimate=pl.CostEstimate(flops=flops, bytes_accessed=nbytes, transcendentals=0),
+            cost_estimate=pl.CostEstimate(
+                flops=int(expected_us * FLOPS_PER_US), bytes_accessed=0, transcendentals=0
+            ),
         )(*args)
 
     return run
@@ -128,30 +131,27 @@
             part_ref[here, x * cols : (x + 1) * cols] = out * sea[x : x + 1, :]
 
 
-def own_mesh(state_ref, hot_ref, weight_ref, part_ref, near_ref):
+def own_mesh(mesh, hot_ref, weight_ref, mesh_ref, part_ref, near_ref):
     neighbours, padded, nodes = weight_ref.shape
-    gp = state_ref.shape[1] - nodes
-    mesh = state_ref[:, gp:].astype(BF16)
     for k in range(neighbours):
         near_ref[k] = dot(mesh, hot_ref[k, :nodes, :])
     for c in range(padded // CHUNK):
         here = slice(c * CHUNK, (c + 1) * CHUNK)
-        e = state_ref[here, gp:]
+        e = mesh_ref[here, :]
         out = e
         for k in range(neighbours):
             out = out + weight_ref[k, here, :] * (near_ref[k, here, :] - e)
-        part_ref[here, gp:] = out
+        part_ref[here, :] = out
 
 
 def prepare_kernel(
     grid_hbm, mesh_hbm, table_hbm, win_hbm, wout_hbm, index_ref, pq_ref, sea_ref, speed_ref,
-    part_ref, hot_ref, weight_ref, band_ref, win_ref, wout_ref,
-    grid_ref, mesh_ref, layer_ref, state_ref, near_ref, pack_ref, sem,
+    gpart_ref, mpart_ref, hot_ref, weight_ref, band_ref, win_ref, wout_ref,
+    grid_ref, mesh_ref, layer_ref, gstate_ref, mstate_ref, near_ref, pack_ref, sem,
 ):
     fr, dr = lax.axis_index("fr"), lax.axis_index("dr")
     rows, cols = sea_ref.shape
-    gp = rows * cols
-    padded = state_ref.shape[0]
+    padded = gstate_ref.shape[0]
     bands = grid_ref.shape[0] // rows
     copies = [
         pltpu.make_async_copy(table_hbm.at[fr, dr], band_ref, sem.at[0]),
@@ -174,13 +174,13 @@
             w = cx * pq_ref[k : k + 1, :] + cy * pq_ref[neighbours + k : neighbours + k + 1, :]
             weight_ref[k, here, :] = jnp.maximum(w, 0.0)
     copies[1].wait()
-    pack_rows(mesh_ref, state_ref, gp)
-    own_mesh(state_ref, hot_ref, weight_ref, part_ref, near_ref)
+    pack_rows(mesh_ref, mstate_ref, 0)
+    own_mesh(mstate_ref[...].astype(BF16), hot_ref, weight_ref, mstate_ref, mpart_ref, near_ref)
     copies[2].wait()
-    state_ref[bands:, :gp] = jnp.zeros((padded - bands, gp), F32)
+    gstate_ref[bands:, :] = jnp.zeros((padded - bands, gstate_ref.shape[1]), F32)
     for x in range(rows):
-        state_ref[:bands, x * cols : (x + 1) * cols] = grid_ref[pl.ds(x, bands, stride=rows), :]
-    own_grid(state_ref, band_ref, sea_ref, speed_ref, part_ref)
+        gstate_ref[:bands, x * cols : (x + 1) * cols] = grid_ref[pl.ds(x, bands, stride=rows), :]
+    own_grid(gstate_ref, band_ref, sea_ref, speed_ref, gpart_ref)
     half = pack_ref.shape[1] // 2
     copies[3].wait()
     pack_rows(layer_ref.at[0], pack_ref, 0)
@@ -194,26 +194,24 @@
     wout_ref[:, half:] = jnp.where(dr == 0, two, one)
 
 
-def own_kernel(state_ref, hot_ref, weight_ref, band_ref, sea_ref, speed_ref, part_ref, near_ref):
-    own_mesh(state_ref, hot_ref, weight_ref, part_ref, near_ref)
-    own_grid(state_ref, band_ref, sea_ref, speed_ref, part_ref)
-
-
-def halo_kernel(
-    part_ref, even_ref, odd_ref, hot_ref, weight_ref, band_ref, sea_ref, speed_ref, win_ref,
-    moved_ref, keep_ref, send_ref, ext_ref, near_ref, feat_ref,
-):
-    neighbours, padded, nodes = weight_ref.shape
+def own_mesh_kernel(state_ref, hot_ref, weight_ref, part_ref, near_ref):
+    own_mesh(state_ref[...].astype(BF16), hot_ref, weight_ref, state_ref, part_ref, near_ref)
+
+
+def first_layer(win_ref, feat_ref, keep_ref, send_ref):
+    half = keep_ref.shape[0]
+    send_ref[...] = dot(win_ref[half:, :], feat_ref[...]).astype(BF16)
+    keep_ref[...] = dot(win_ref[:half, :], feat_ref[...])
+
+
+def halo_grid_kernel(
+    part_ref, even_ref, odd_ref, band_ref, sea_ref, speed_ref, win_ref,
+    moved_ref, keep_ref, send_ref, feat_ref,
+):
     rows, cols = sea_ref.shape
-    gp = rows * cols
-    listed = even_ref.shape[1] - cols
     even = on_even()
-    ext_ref[:, :listed] = jnp.where(even, odd_ref[:, cols:], even_ref[:, cols:])
-    ext_ref[:, listed:] = jnp.where(even, even_ref[:, cols:], odd_ref[:, cols:])
-    for k in range(neighbours):
-        near_ref[k] = dot(ext_ref[...], hot_ref[k, nodes:, :])
     scale = sea_ref[...].astype(F32) * speed_ref[...]
-    for c in range(padded // CHUNK):
+    for c in range(part_ref.shape[0] // CHUNK):
         here = slice(c * CHUNK, (c + 1) * CHUNK)
         cx = band_ref[here, 0:1]
         a, b = even_ref[here, :cols].astype(F32), odd_ref[here, :cols].astype(F32)
@@ -226,36 +224,64 @@
                 out = out + jnp.maximum(-cx, 0.0) * scale[x : x + 1, :] * jnp.where(even, a, b)
             moved_ref[here, cut] = out
             feat_ref[here, cut] = out.astype(BF16)
-        out = part_ref[here, gp:]
+    first_layer(win_ref, feat_ref, keep_ref, send_ref)
+
+
+def halo_mesh_kernel(
+    part_ref, even_ref, odd_ref, hot_ref, weight_ref, win_ref, after_ref,
+    moved_ref, keep_ref, send_ref, ext_ref, near_ref, feat_ref,
+):
+    neighbours, padded, nodes = weight_ref.shape
+    listed = ext_ref.shape[1] // 2
+    first = even_ref.shape[1] - listed
+    even = on_even()
+    ext_ref[:, :listed] = jnp.where(even, odd_ref[:, first:], even_ref[:, first:])
+    ext_ref[:, listed:] = jnp.where(even, even_ref[:, first:], odd_ref[:, first:])
+    for k in range(neighbours):
+        near_ref[k] = dot(ext_ref[...], hot_ref[k, nodes:, :])
+    for c in range(padded // CHUNK):
+        here = slice(c * CHUNK, (c + 1) * CHUNK)
+        out = part_ref[here, :]
         for k in range(neighbours):
             out = out + weight_ref[k, here, :] * near_ref[k, here, :]
-        moved_ref[here, gp:] = out
-        feat_ref[here, gp:] = out.astype(BF16)
-    half = keep_ref.shape[0]
-    keep_ref[...] = dot(win_ref[:half, :], feat_ref[...])
-    send_ref[...] = dot(win_ref[half:, :], feat_ref[...]).astype(BF16)
-
-
-def add_transfer(moved_ref, mine_ref, other_ref, wout_ref, hid_ref, state_ref):
+        moved_ref[here, :] = out
+        feat_ref[here, :] = out.astype(BF16)
+    first_layer(win_ref, feat_ref, keep_ref, send_ref)
+
+
+def transferred(moved_ref, mine_ref, other_ref, wout_ref, hid_ref):
     half = mine_ref.shape[0]
     hid_ref[:half, :] = mine_ref[...]
     hid_ref[half:, :] = other_ref[...]
-    state_ref[...] = moved_ref[...] + DT_STEP * dot(wout_ref[...], hid_ref[...])
-
-
-def next_kernel(
-    moved_ref, mine_ref, other_ref, wout_ref, halo_ref, state_ref, even_ref, odd_ref, hid_ref,
-    *, grid_points, cols,
-):
-    add_transfer(moved_ref, mine_ref, other_ref, wout_ref, hid_ref, state_ref)
-    messages(
-        state_ref[:, grid_points:].astype(BF16),
-        state_ref[:, :cols].astype(BF16),
-        state_ref[:, grid_points - cols : grid_points].astype(BF16),
-        halo_ref,
-        even_ref,
-        odd_ref,
-    )
+    return moved_ref[...] + DT_STEP * dot(wout_ref[...], hid_ref[...])
+
+
+def next_grid_kernel(
+    moved_ref, mine_ref, other_ref, wout_ref, state_ref, even_ref, odd_ref, hid_ref
+):
+    state_ref[...] = transferred(moved_ref, mine_ref, other_ref, wout_ref, hid_ref)
+    even = on_even()
+    cols = even_ref.shape[1]
+    low, high = state_ref[:, :cols], state_ref[:, state_ref.shape[1] - cols :]
+    even_ref[...] = jnp.where(even, high, low).astype(BF16)
+    odd_ref[...] = jnp.where(even, low, high).astype(BF16)
+
+
+def next_mesh_kernel(
+    moved_ref, mine_ref, other_ref, wout_ref, halo_ref, state_ref, even_ref, odd_ref, hid_ref
+):
+    state_ref[...] = transferred(moved_ref, mine_ref, other_ref, wout_ref, hid_ref)
+    even = on_even()
+    mesh = state_ref[...].astype(BF16)
+    nodes = mesh.shape[1]
+    to_lower = dot(mesh, one_hot(halo_ref[0:1, :], nodes))
+    to_upper = dot(mesh, one_hot(halo_ref[1:2, :], nodes))
+    even_ref[...] = jnp.where(even, to_upper, to_lower).astype(BF16)
+    odd_ref[...] = jnp.where(even, to_lower, to_upper).astype(BF16)
+
+
+def state_kernel(moved_ref, mine_ref, other_ref, wout_ref, state_ref, hid_ref):
+    state_ref[...] = transferred(moved_ref, mine_ref, other_ref, wout_ref, hid_ref)
 
 
 def slots_kernel(
@@ -298,29 +324,27 @@
 def slot_values(source_refs, mix_refs, sums_ref, p, cap, bands, out_ref):
     cut = slice(p * cap, (p + 1) * cap)
     for kind in (0, 1):
-        value = dot(source_refs[kind], mix_refs[kind][:, cut])
+        value = dot(source_refs[kind][...], mix_refs[kind][:, cut])
         if bands is not None:
             row = lax.broadcasted_iota(jnp.int32, value.shape, 0)
             value = jnp.where(row == bands, sums_ref[kind : kind + 1, cut], value)
         out_ref[:, kind * cap : (kind + 1) * cap] = value.astype(BF16)
 
 
-def early_kernel(moved_ref, gmix_ref, mmix_ref, sums_ref, out_ref, *, bands, peer):
-    gp = gmix_ref.shape[0]
+def early_kernel(grid_ref, mesh_ref, gmix_ref, mmix_ref, sums_ref, out_ref, *, bands, peer):
     cap = out_ref.shape[1] // 2
-    parts = (moved_ref[:, :gp].astype(BF16), moved_ref[:, gp:].astype(BF16))
+    parts = (grid_ref[...].astype(BF16), mesh_ref[...].astype(BF16))
     slot_values(parts, (gmix_ref, mmix_ref), sums_ref, peer, cap, bands, out_ref)
 
 
 def mix_kernel(
-    moved_ref, mine_ref, other_ref, wout_ref, gmix_ref, mmix_ref, sums_ref, state_ref, *rest,
-    bands, which,
+    grid_ref, moved_ref, mine_ref, other_ref, wout_ref, gmix_ref, mmix_ref, sums_ref, state_ref,
+    *rest, bands, which,
 ):
     out_refs, hid_ref = rest[:-1], rest[-1]
-    add_transfer(moved_ref, mine_ref, other_ref, wout_ref, hid_ref, state_ref)
-    gp = gmix_ref.shape[0]
+    state_ref[...] = transferred(moved_ref, mine_ref, other_ref, wout_ref, hid_ref)
     cap = out_refs[0].shape[1] // 2
-    parts = (state_ref[:, :gp].astype(BF16), state_ref[:, gp:].astype(BF16))
+    parts = (grid_ref[...].astype(BF16), state_ref[...].astype(BF16))
     for p, out_ref in zip(which, out_refs):
         slot_values(parts, (gmix_ref, mmix_ref), sums_ref, p, cap, bands, out_ref)
 
@@ -335,13 +359,11 @@
 
 
 def silu_mix_kernel(
-    total_ref, got_ref, gmix_ref, mmix_ref, after_ref, mine_ref, mixed_ref, *, peer
-):
-    gp = gmix_ref.shape[0]
+    total_ref, got_ref, grid_ref, gmix_ref, mmix_ref, after_ref, mine_ref, mixed_ref, *, peer
+):
     cap = mixed_ref.shape[1] // 2
     mine_ref[...] = silu(total_ref, got_ref)
-    parts = (mine_ref[:, :gp], mine_ref[:, gp:])
-    slot_values(parts, (gmix_ref, mmix_ref), None, peer, cap, None, mixed_ref)
+    slot_values((grid_ref, mine_ref[...]), (gmix_ref, mmix_ref), None, peer, cap, None, mixed_ref)
 
 
 def join_kernel(early_ref, mine_ref, other_ref, wout_ref, out_ref):
@@ -356,7 +378,7 @@
     )
 
 
-def end_kernel(state_ref, gland_ref, mland_ref, sea_ref, *rest, bands):
+def end_kernel(gstate_ref, mstate_ref, gland_ref, mland_ref, sea_ref, *rest, bands):
     got_refs, rest = rest[-8::-1], rest[-7:]
     grid_hbm, mesh_hbm, values_ref, sum_ref, grid_ref, mesh_ref, sem = rest
     rows, cols = sea_ref.shape
@@ -372,7 +394,7 @@
     keep = 1.0 - rate * cover
     for f in range(freqs):
         here = slice(f * dirs, (f + 1) * dirs)
-        mesh_ref[f] = keep * state_ref[here, gp:] + rate * sum_ref[here, gp:]
+        mesh_ref[f] = keep * mstate_ref[here, :] + rate * sum_ref[here, gp:]
     mesh_copy = pltpu.make_async_copy(mesh_ref, mesh_hbm, sem.at[0])
     mesh_copy.start()
     sum_ref[:, :gp] = land(values_ref[1], mland_ref)
@@ -383,7 +405,7 @@
     for x in range(rows):
         cut = slice(x * cols, (x + 1) * cols)
         wet = sea[x : x + 1, :]
-        out = keep[:, cut] * wet * state_ref[:bands, cut] + rate[:, cut] * wet * sum_ref[:bands, cut]
+        out = keep[:, cut] * wet * gstate_ref[:bands, cut] + rate[:, cut] * wet * sum_ref[:bands, cut]
         grid_ref[pl.ds(x, bands, stride=rows), :] = out
     grid_copy = pltpu.make_async_copy(grid_ref, grid_hbm, sem.at[1])
     grid_copy.start()
@@ -427,9 +449,8 @@
     n_fr, n_dr = lax.axis_size("fr"), lax.axis_size("dr")
 
     message = ((padded, cols + listed), BF16)
-    state_shape = ((padded, points), F32)
-    half_shape = (half, points)
-    hid_scratch = ((hid, points), BF16)
+    grid_shape = ((padded, gp), F32)
+    mesh_shape = ((padded, nodes), F32)
     near_scratch = ((neighbours, padded, nodes), F32)
     grid_flat = grid_spec.reshape(bands * rows, cols)
     even, odd = kernel_call(
@@ -439,56 +460,46 @@
             (grid_flat.shape, F32),
             (mesh_spec.shape, F32),
             (halo_list.shape, jnp.int32),
-            ((padded, nodes), F32),
+            mesh_shape,
             pltpu.SemaphoreType.DMA((3,)),
         ],
-        flops=2 * padded * nodes * 2 * listed,
+        1.8,
         spaces=[HBM] * 3,
     )(grid_flat, mesh_spec, halo_list)
-
     table = jnp.asarray(band_table(freqs, dirs, n_fr, n_dr, padded))
     pq = jnp.concatenate([-nb_coef * jnp.cos(nb_angle), -nb_coef * jnp.sin(nb_angle)], axis=0)
-    for substep in range(NSUB):
-        from_even = pair_swap(even, "sp", 0)
-        from_odd = pair_swap(odd, "sp", 1)
-        own_flops = 2 * padded * neighbours * nodes * nodes
-        if substep == 0:
-            part, hot, weight, band, win, wout = kernel_call(
-                prepare_kernel,
-                [
-                    state_shape,
-                    ((neighbours, nodes + 2 * listed, nodes), BF16),
-                    near_scratch,
-                    ((padded, 2), F32),
-                    ((hid, padded), BF16),
-                    ((padded, hid), BF16),
-                ],
-                [
-                    (grid_flat.shape, F32),
-                    (mesh_spec.shape, F32),
-                    ((2,) + w_in.shape, BF16),
-                    state_shape,
-                    near_scratch,
-                    ((padded, hid), F32),
-                    pltpu.SemaphoreType.DMA((5,)),
-                ],
-                flops=3 * own_flops,
-                spaces=[HBM] * 5 + [VMEM] * 4,
-            )(
-                grid_flat, mesh_spec, table, w_in, jnp.transpose(w_out, (1, 2, 0)),
-                nb_index, pq, grid_sea, grid_speed,
-            )
-        else:
-            (part,) = kernel_call(own_kernel, [state_shape], [near_scratch], flops=own_flops)(
-                state, hot, weight, band, grid_sea, grid_speed
-            )
-        moved, total, send = kernel_call(
-            halo_kernel,
-            [state_shape, (half_shape, F32), (half_shape, BF16)],
-            [((padded, 2 * listed), BF16), near_scratch, ((padded, points), BF16)],
-            flops=2 * padded * (neighbours * nodes * 2 * listed + hid * points),
-        )(part, from_even, from_odd, hot, weight, band, grid_sea, grid_speed, win)
-
+    from_even = pair_swap(even, "sp", 0)
+    from_odd = pair_swap(odd, "sp", 1)
+    gfrom, mfrom = (from_even, from_odd), (from_even, from_odd)
+    gpart, mpart, hot, weight, band, win, wout = kernel_call(
+        prepare_kernel,
+        [
+            grid_shape,
+            mesh_shape,
+            ((neighbours, nodes + 2 * listed, nodes), BF16),
+            near_scratch,
+            ((padded, 2), F32),
+            ((hid, padded), BF16),
+            ((padded, hid), BF16),
+        ],
+        [
+            (grid_flat.shape, F32),
+            (mesh_spec.shape, F32),
+            ((2,) + w_in.shape, BF16),
+            grid_shape,
+            mesh_shape,
+            near_scratch,
+            ((padded, hid), F32),
+            pltpu.SemaphoreType.DMA((5,)),
+        ],
+        3.4,
+        spaces=[HBM] * 5 + [VMEM] * 4,
+    )(
+        grid_flat, mesh_spec, table, w_in, jnp.transpose(w_out, (1, 2, 0)),
+        nb_index, pq, grid_sea, grid_speed,
+    )
+
+    def summed(total, send):
         total = total + core_swap(send).astype(F32)
         rounded = total.astype(BF16)
         got = peer_swap(rounded, "fr", 1)
@@ -498,8 +509,31 @@
             rounded = total.astype(BF16)
             got = peer_swap(rounded, "fr", step)
             step *= 2
-        extra = []
-        if substep == 0:
+        return total, rounded, got
+
+    def activated(total, got, *after):
+        (mine,) = kernel_call(
+            silu_kernel, [(total.shape, BF16)], (), 0.1, spaces=[VMEM] * 2 + [pl.ANY] * len(after)
+        )(total, got, *after)
+        return mine
+
+    for substep in range(NSUB):
+        gmoved, gtotal, gsend = kernel_call(
+            halo_grid_kernel,
+            [grid_shape, ((half, gp), F32), ((half, gp), BF16)],
+            [((padded, gp), BF16)],
+            0.4,
+        )(gpart, *gfrom, band, grid_sea, grid_speed, win)
+        gtotal, ground, ggot = summed(gtotal, gsend)
+        mmoved, mtotal, msend = kernel_call(
+            halo_mesh_kernel,
+            [mesh_shape, ((half, nodes), F32), ((half, nodes), BF16)],
+            [((padded, 2 * listed), BF16), near_scratch, ((padded, nodes), BF16)],
+            0.8,
+            spaces=[VMEM] * 6 + [pl.ANY],
+        )(mpart, *mfrom, hot, weight, win, gsend)
+        mtotal, mround, mgot = summed(mtotal, msend)
+        if substep < NSUB - 1:
             gmix, mmix, sums, gland, mland = kernel_call(
                 slots_kernel,
                 [
@@ -509,53 +543,67 @@
                     ((nodes, peers * cap), BF16),
                     ((gp, peers * cap), BF16),
                 ],
-                flops=2 << 30,
+                (),
+                0.5,
                 spaces=[VMEM] * 8 + [pl.ANY],
             )(
                 g2m_index, g2m_weight, g2m_count, g2m_target,
-                m2g_index, m2g_weight, m2g_count, m2g_target, rounded,
+                m2g_index, m2g_weight, m2g_count, m2g_target, ground,
             )
-            extra = [sums]
-        if substep < NSUB - 1:
-            (mine,) = kernel_call(
-                silu_kernel, [(half_shape, BF16)], spaces=[VMEM, VMEM] + [pl.ANY] * len(extra)
-            )(total, got, *extra)
-            other = core_swap(mine)
-            state, even, odd = kernel_call(
-                functools.partial(next_kernel, grid_points=gp, cols=cols),
-                [state_shape, message, message],
-                [hid_scratch],
-                flops=2 * padded * hid * points,
-            )(moved, mine, other, wout, halo_list)
+            gmine = activated(gtotal, ggot, sums)
+            gstate, even, odd = kernel_call(
+                next_grid_kernel,
+                [grid_shape, ((padded, cols), BF16), ((padded, cols), BF16)],
+                [((hid, gp), BF16)],
+                0.4,
+            )(gmoved, gmine, core_swap(gmine), wout)
+            gfrom = (pair_swap(even, "sp", 0), pair_swap(odd, "sp", 1))
+            (gpart,) = kernel_call(own_grid, [grid_shape], (), 0.5)(
+                gstate, band, grid_sea, grid_speed
+            )
+            mmine = activated(mtotal, mgot)
+            mstate, even, odd = kernel_call(
+                next_mesh_kernel,
+                [mesh_shape, ((padded, listed), BF16), ((padded, listed), BF16)],
+                [((hid, nodes), BF16)],
+                0.5,
+            )(mmoved, mmine, core_swap(mmine), wout, halo_list)
+            mfrom = (pair_swap(even, "sp", 0), pair_swap(odd, "sp", 1))
+            (mpart,) = kernel_call(own_mesh_kernel, [mesh_shape], [near_scratch], 1.0)(
+                mstate, hot, weight
+            )
 
     split = peers // 2
     slot_shape = ((padded, 2 * cap), BF16)
     (early,) = kernel_call(
-        functools.partial(early_kernel, bands=bands, peer=split),
-        [slot_shape],
-        flops=2 * padded * points * cap,
-    )(moved, gmix, mmix, sums)
+        functools.partial(early_kernel, bands=bands, peer=split), [slot_shape], (), 0.4
+    )(gmoved, mmoved, gmix, mmix, sums)
     early = peer_swap(early, "sp", split)
-    mine, mixed = kernel_call(
+    gmine = activated(gtotal, ggot)
+    (gstate,) = kernel_call(state_kernel, [grid_shape], [((hid, gp), BF16)], 0.3)(
+        gmoved, gmine, core_swap(gmine), wout
+    )
+    mmine, mixed = kernel_call(
         functools.partial(silu_mix_kernel, peer=split),
-        [(half_shape, BF16), ((half, 2 * cap), BF16)],
-        flops=2 * half * points * cap,
-        spaces=[VMEM] * 4 + [pl.ANY],
-    )(total, got, gmix, mmix, early)
-    other = core_swap(mine)
+        [((half, nodes), BF16), ((half, 2 * cap), BF16)],
+        (),
+        0.3,
+        spaces=[VMEM] * 5 + [pl.ANY],
+    )(mtotal, mgot, gmine, gmix, mmix, early)
+    mother = core_swap(mmine)
     mixed = peer_swap(mixed, "sp", split)
     which = [p for p in range(peers) if p != split]
-    state, *values = kernel_call(
+    mstate, *values = kernel_call(
         functools.partial(mix_kernel, bands=bands, which=which),
-        [state_shape] + [slot_shape] * len(which),
-        [hid_scratch],
-        flops=2 * padded * (hid * points + points * len(which) * cap),
-    )(moved, mine, other, wout, gmix, mmix, sums)
+        [mesh_shape] + [slot_shape] * len(which),
+        [((hid, nodes), BF16)],
+        0.8,
+    )(gstate, mmoved, mmine, mother, wout, gmix, mmix, sums)
     values = dict(zip(which, values))
-    mixed, state = lax.optimization_barrier((mixed, state))
+    mixed, mstate = lax.optimization_barrier((mixed, mstate))
     for p in which[1:]:
         values[p] = peer_swap(values[p], "sp", p)
-    (values[split],) = kernel_call(join_kernel, [slot_shape], flops=900 << 20)(
+    (values[split],) = kernel_call(join_kernel, [slot_shape], (), 0.85)(
         early, mixed, core_swap(mixed), wout
     )
     values = [values[p] for p in range(peers)]
@@ -564,14 +612,14 @@
         [(grid_flat.shape, F32), (mesh_spec.shape, F32)],
         [
             ((2, padded, peers * cap), BF16),
-            state_shape,
+            ((padded, points), F32),
             (grid_flat.shape, F32),
             (mesh_spec.shape, F32),
             pltpu.SemaphoreType.DMA((2,)),
         ],
-        flops=2 * padded * points * peers * cap,
+        1.9,
         out_space=pl.ANY,
-    )(state, gland, mland, grid_sea, *values[::-1])
+    )(gstate, mstate, gland, mland, grid_sea, *values[::-1])
     return grid_out.reshape(grid_spec.shape), mesh_out
 
 

time: 66.9 us -> 63.3 us (0.946)
  waiting for transfers between devices: 29.8 us -> 19.9 us
  starting transfers between devices: 20 us -> 25.1 us
  Pallas kernels: 15.5 us -> 16.6 us
    ppermute x5 -> x9, waiting for transfers between devices: 7.26 us -> 2.14 us  [core_swap(): return lax.ppermute(array, 'dr', [(0, 1), (1, 0)])]
    ppermute x4 -> x6, starting transfers between devices: 9.41 us -> 13.1 us  [pair_swap(): return lax.ppermute(array, axis, pairs + [(j, i) for i, j in pairs])]
    ppermute x6 -> x8, waiting for transfers between devices: 20 us -> 17.6 us  [peer_swap(): return lax.ppermute(array, axis, [(i, i ^ step) for i in range(size)])]
    ppermute x4 -> x6, waiting for transfers between devices: 2.46 us -> 0.15 us  [pair_swap(): return lax.ppermute(array, axis, pairs + [(j, i) for i, j in pairs])]
    ppermute x5 -> x9, starting transfers between devices: 0.29 us -> 1.55 us  [core_swap(): return lax.ppermute(array, 'dr', [(0, 1), (1, 0)])]
    pallas_call x13 -> x20, Pallas kernels: 15.5 us -> 16.6 us  [run(): pl.pallas_call(body, out_shape=[jax.ShapeDtypeStruct(s, t) for s, t in ou...]
    ppermute x6 -> x8, starting transfers between devices: 10.3 us -> 10.4 us  [peer_swap(): return lax.ppermute(array, axis, [(i, i ^ step) for i in range(size)])]
  transfers between devices with their start and end apart: 15 -> 23, of which waited for: 12 -> 10; matrix products, arithmetic and copies ran while one was open for 0% -> 0% of each run, Pallas kernels for 13% -> 20%
where the time goes in v5:
time: 63.3 us; the launch traced here: 63.1 us
  starting transfers between devices  25.1 us (40%)
  waiting for transfers between devices  19.9 us (31%)
  Pallas kernels  16.6 us (26%)
  between operations  1.26 us (2%)
    ppermute x8, waiting for transfers between devices, peer_swap(): return lax.ppermute(array, axis, [(i, i ^ step) for i in range(size)])  17.6 us
    pallas_call x20, Pallas kernels, run(): pl.pallas_call(body, out_shape=[jax.ShapeDtypeStruct(s, t) for s, t in ou...  16.6 us
    ppermute x6, starting transfers between devices, pair_swap(): return lax.ppermute(array, axis, pairs + [(j, i) for i, j in pairs])  13.1 us
    ppermute x8, starting transfers between devices, peer_swap(): return lax.ppermute(array, axis, [(i, i ^ step) for i in range(size)])  10.4 us
    ppermute x9, waiting for transfers between devices, core_swap(): return lax.ppermute(array, 'dr', [(0, 1), (1, 0)])  2.14 us
    ppermute x9, starting transfers between devices, core_swap(): return lax.ppermute(array, 'dr', [(0, 1), (1, 0)])  1.55 us
  transfers between devices with their start and end apart: 23, of which 10 were waited for; matrix products, arithmetic and copies ran while one was open for 0% of the time, Pallas kernels for 20%

profile of v5, /device:TPU:0, one launch (start us, length us, event | category | flops | bytes accessed | tf_op | source)
XLA Modules:
  0.0 63.1 jit_solution(9683863373192835339)
XLA Ops:
  0.7 1.8 %shard_map.195 = (bf16[336,256]{1,0:T(8,128)(2,1)S(1)}, bf16[336,256]{1,0:T(8,128)(2,1)S(1)}) custom-call(f32[1296,128]{1,0:T(8,128)} %bitcast.3, f32[18,18,512]{2,1,0:T(8,128)} %mesh_hbm.3, s32[2,128]{1,0:T(2,128)} %halo_ref.1), custom_call_target="tpu_custom_call" | custom-call | flops 2070000000 | tf_op jit(solution)/shard_map/pallas_call | solution.py:31
  2.5 3.1 %collective-permute-start = (bf16[336,256]{1,0:T(8,128)(2,1)S(1)}, bf16[336,256]{1,0:T(8,128)(2,1)S(1)}, u32[]{:S(2)}, u32[]{:S(2)}) collective-permute-start(bf16[336,256]{1,0:T(8,128)(2,1)S(1)} %get-tuple-element.45), channel_id=1, source_target_pairs={{0,4},{8,12},{4,0},{12,8},{1,5},{9,13},{5,1},{13,9},{2,6},{10,14},... | collective-permute-start | bytes 516104 | tf_op jit(solution)/shard_map/ppermute | solution.py:58
  5.6 0.7 %collective-permute-start.1 = (bf16[336,256]{1,0:T(8,128)(2,1)S(1)}, bf16[336,256]{1,0:T(8,128)(2,1)S(1)}, u32[]{:S(2)}, u32[]{:S(2)}) collective-permute-start(bf16[336,256]{1,0:T(8,128)(2,1)S(1)} %get-tuple-element.46), channel_id=1, source_target_pairs={{4,8},{8,4},{5,9},{9,5},{6,10},{10,6},{7,11},{11,7},{20,24},{24,20... | collective-permute-start | bytes 516104 | tf_op jit(solution)/shard_map/ppermute | solution.py:58
  6.3 0.1 cosine_multiply_fusion
  6.4 3.4 %shard_map.194 = (f32[336,512]{1,0:T(8,128)S(1)}, f32[336,512]{1,0:T(8,128)S(1)}, bf16[4,768,512]{2,1,0:T(8,128)(2,1)S(1)}, f32[4,336,512]{2,1,0:T(8,128)S(1)}, ...) custom-call(f32[1296,128]{1,0:T(8,128)} %bitcast.4, f32[18,18,512]{2,1,0:T(8,128)} %mesh_hbm.3, ...), custom_call_target="tpu_custom_call" | custom-call | flops 3910000128 | tf_op jit(solution)/shard_map/pallas_call | solution.py:31
  9.8 0.1 collective-permute-done.even_ref
  10.0 0.0 collective-permute-done.1.odd_ref
  10.0 0.4 shard_map.196
  10.4 0.1 collective-permute-start.2
  10.5 0.0 copy-start.1
  10.5 0.0 copy-start.2
  10.5 0.0 copy-start.3
  10.5 0.0 copy-start.4
  10.5 0.0 copy-start.5
  10.6 0.0 copy-start.6
  10.6 0.0 copy-start.10
  10.6 0.0 copy-start.11
  10.6 0.8 %shard_map.204 = (f32[336,512]{1,0:T(8,128)S(1)}, f32[128,512]{1,0:T(8,128)S(1)}, bf16[128,512]{1,0:T(8,128)(2,1)S(1)}) custom-call(f32[336,512]{1,0:T(8,128)S(1)} %get-tuple-element.60.part_ref, bf16[336,256]{1,0:T(8,128)(2,1)S(1)} %collective-permute-done.even_ref, bf16[336,256]{1,0:T(8,128)(2,1)S(1)} %collective-permute-done.1.odd_ref, ...), custom_call_target="tpu_custom_call" | custom-call | flops 920000000 | tf_op jit(solution)/shard_map/pallas_call | solution.py:31
  11.4 0.5 collective-permute-start.10
  12.0 0.0 collective-permute-done.2
  12.0 1.7 %collective-permute-start.3 = (bf16[128,512]{1,0:T(8,128)(2,1)S(1)}, bf16[128,512]{1,0:T(8,128)(2,1)S(1)}, u32[]{:S(2)}, u32[]{:S(2)}) collective-permute-start(bf16[128,512]{1,0:T(8,128)(2,1)S(1)} %get-tuple-element.92.after_ref), channel_id=1, source_target_pairs={{0,2},{2,0},{1,3},{3,1},{4,6},{6,4},{5,7},{7,5},{8,10},{10,8},{9,1... | collective-permute-start | bytes 393224 | tf_op jit(solution)/shard_map/ppermute | solution.py:63
  13.8 0.9 %collective-permute-start.11 = (bf16[128,512]{1,0:T(8,128)(2,1)S(1)}, bf16[128,512]{1,0:T(8,128)(2,1)S(1)}, u32[]{:S(2)}, u32[]{:S(2)}) collective-permute-start(bf16[128,512]{1,0:T(8,128)(2,1)S(1)} %get-tuple-element.88), channel_id=1, source_target_pairs={{0,2},{2,0},{1,3},{3,1},{4,6},{6,4},{5,7},{7,5},{8,10},{10,8},{9,1... | collective-permute-start | bytes 393224 | tf_op jit(solution)/shard_map/ppermute | solution.py:63
  14.8 2.2 %shard_map.197 = (bf16[512,512]{1,0:T(8,128)(2,1)S(1)}, bf16[512,512]{1,0:T(8,128)(2,1)S(1)}, f32[2,512]{1,0:T(2,128)S(1)}, bf16[512,512]{1,0:T(8,128)(2,1)S(1)}, bf16[512,512]{1,0:T(8,128)(2,1)S(1)}) custom-call(s32[4,1,4,128]{3,2,1,0:T(4,128)S(1)} %copy-done.1, f32[4,1,4,128]{3,2,1,0:T(4,128)S(1)} %copy-done.2, s32[1,4]{1,0:T(1,128)S(1)} %copy-done.10, ...), custom_call_target="tpu_custom_call" | custom-call | flops 575000000 | tf_op jit(solution)/shard_map/pallas_call | solution.py:31
  16.9 1.5 %collective-permute-done.3.got_ref = bf16[128,512]{1,0:T(8,128)(2,1)S(1)} collective-permute-done((bf16[128,512]{1,0:T(8,128)(2,1)S(1)}, bf16[128,512]{1,0:T(8,128)(2,1)S(1)}, u32[]{:S(2)}, u32[]{:S(2)}) %collective-permute-start.3) | collective-permute-done | bytes 131104 | tf_op jit(solution)/shard_map/ppermute | solution.py:63
  18.4 0.1 shard_map.198.mine_ref
  18.5 0.1 collective-permute-start.4
  18.6 1.7 %collective-permute-done.11.got_ref = bf16[128,512]{1,0:T(8,128)(2,1)S(1)} collective-permute-done((bf16[128,512]{1,0:T(8,128)(2,1)S(1)}, bf16[128,512]{1,0:T(8,128)(2,1)S(1)}, u32[]{:S(2)}, u32[]{:S(2)}) %collective-permute-start.11) | collective-permute-done | bytes 131104 | tf_op jit(solution)/shard_map/ppermute | solution.py:63
  20.3 0.1 shard_map.205.mine_ref
  20.4 0.1 collective-permute-start.12
  20.5 0.3 shard_map.199
  20.8 4.8 %collective-permute-start.5 = (bf16[336,128]{1,0:T(8,128)(2,1)S(1)}, bf16[336,128]{1,0:T(8,128)(2,1)S(1)}, u32[]{:S(2)}, u32[]{:S(2)}) collective-permute-start(bf16[336,128]{1,0:T(8,128)(2,1)S(1)} %get-tuple-element.55), channel_id=1, source_target_pairs={{0,4},{8,12},{4,0},{12,8},{1,5},{9,13},{5,1},{13,9},{2,6},{10,14},... | collective-permute-start | bytes 258056 | tf_op jit(solution)/shard_map/ppermute | solution.py:58
  25.6 0.7 %collective-permute-start.6 = (bf16[336,128]{1,0:T(8,128)(2,1)S(1)}, bf16[336,128]{1,0:T(8,128)(2,1)S(1)}, u32[]{:S(2)}, u32[]{:S(2)}) collective-permute-start(bf16[336,128]{1,0:T(8,128)(2,1)S(1)} %get-tuple-element.56), channel_id=1, source_target_pairs={{4,8},{8,4},{5,9},{9,5},{6,10},{10,6},{7,11},{11,7},{20,24},{24,20... | collective-permute-start | bytes 258056 | tf_op jit(solution)/shard_map/ppermute | solution.py:58
  26.3 0.5 shard_map.206
  26.8 3.1 %collective-permute-start.13 = (bf16[336,128]{1,0:T(8,128)(2,1)S(1)}, bf16[336,128]{1,0:T(8,128)(2,1)S(1)}, u32[]{:S(2)}, u32[]{:S(2)}) collective-permute-start(bf16[336,128]{1,0:T(8,128)(2,1)S(1)} %get-tuple-element.67), channel_id=1, source_target_pairs={{0,4},{8,12},{4,0},{12,8},{1,5},{9,13},{5,1},{13,9},{2,6},{10,14},... | collective-permute-start | bytes 258056 | tf_op jit(solution)/shard_map/ppermute | solution.py:58
  29.8 0.8 %collective-permute-start.14 = (bf16[336,128]{1,0:T(8,128)(2,1)S(1)}, bf16[336,128]{1,0:T(8,128)(2,1)S(1)}, u32[]{:S(2)}, u32[]{:S(2)}) collective-permute-start(bf16[336,128]{1,0:T(8,128)(2,1)S(1)} %get-tuple-element.68), channel_id=1, source_target_pairs={{4,8},{8,4},{5,9},{9,5},{6,10},{10,6},{7,11},{11,7},{20,24},{24,20... | collective-permute-start | bytes 258056 | tf_op jit(solution)/shard_map/ppermute | solution.py:58
  30.7 0.7 %shard_map.200.part_ref = f32[336,512]{1,0:T(8,128)S(1)} custom-call(f32[336,512]{1,0:T(8,128)S(1)} %get-tuple-element.54.state_ref, f32[336,2]{1,0:T(8,128)S(1)} %get-tuple-element.47.band_ref, s32[4,128]{1,0:T(4,128)S(1)} %copy-done.8, f32[4,128]{1,0:T(4,128)S(1)} %copy-done.7), custom_call_target="tpu_custom_call" | custom-call | flops 575000000 | tf_op jit(solution)/shard_map/pallas_call | solution.py:31
  31.4 0.4 shard_map.201
  31.9 0.1 collective-permute-start.7
  32.0 1.1 %shard_map.207.part_ref = f32[336,512]{1,0:T(8,128)S(1)} custom-call(f32[336,512]{1,0:T(8,128)S(1)} %get-tuple-element.66.state_ref, bf16[4,768,512]{2,1,0:T(8,128)(2,1)S(1)} %get-tuple-element.61.hot_ref, f32[4,336,512]{2,1,0:T(8,128)S(1)} %get-tuple-element.62.weight_ref), custom_call_target="tpu_custom_call" | custom-call | flops 1150000000 | tf_op jit(solution)/shard_map/pallas_call | solution.py:31
  33.1 0.8 %shard_map.208 = (f32[336,512]{1,0:T(8,128)S(1)}, f32[128,512]{1,0:T(8,128)S(1)}, bf16[128,512]{1,0:T(8,128)(2,1)S(1)}) custom-call(f32[336,512]{1,0:T(8,128)S(1)} %shard_map.207.part_ref, bf16[336,128]{1,0:T(8,128)(2,1)S(1)} %collective-permute-done.13.even_ref, bf16[336,128]{1,0:T(8,128)(2,1)S(1)} %collective-permute-done.14.odd_ref, ...), custom_call_target="tpu_custom_call" | custom-call | flops 920000000 | tf_op jit(solution)/shard_map/pallas_call | solution.py:31
  33.9 0.6 collective-permute-start.15
  34.5 0.4 shard_map.209
  34.9 2.9 %collective-permute-start.17 = (bf16[336,256]{1,0:T(8,128)(2,1)S(1)}, bf16[336,256]{1,0:T(8,128)(2,1)S(1)}, u32[]{:S(2)}, u32[]{:S(2)}) collective-permute-start(bf16[336,256]{1,0:T(8,128)(2,1)S(1)} %shard_map.209), channel_id=1, source_target_pairs={{0,8},{4,12},{8,0},{12,4},{1,9},{5,13},{9,1},{13,5},{2,10},{6,14},... | collective-permute-start | bytes 516104 | tf_op jit(solution)/shard_map/ppermute | solution.py:63
  37.8 1.6 %collective-permute-start.8 = (bf16[128,512]{1,0:T(8,128)(2,1)S(1)}, bf16[128,512]{1,0:T(8,128)(2,1)S(1)}, u32[]{:S(2)}, u32[]{:S(2)}) collective-permute-start(bf16[128,512]{1,0:T(8,128)(2,1)S(1)} %get-tuple-element.90), channel_id=1, source_target_pairs={{0,2},{2,0},{1,3},{3,1},{4,6},{6,4},{5,7},{7,5},{8,10},{10,8},{9,1... | collective-permute-start | bytes 393224 | tf_op jit(solution)/shard_map/ppermute | solution.py:63
  39.4 0.6 collective-permute-start.16
  40.0 4.2 %collective-permute-done.8.got_ref = bf16[128,512]{1,0:T(8,128)(2,1)S(1)} collective-permute-done((bf16[128,512]{1,0:T(8,128)(2,1)S(1)}, bf16[128,512]{1,0:T(8,128)(2,1)S(1)}, u32[]{:S(2)}, u32[]{:S(2)}) %collective-permute-start.8) | collective-permute-done | bytes 131104 | tf_op jit(solution)/shard_map/ppermute | solution.py:63
  44.2 0.1 shard_map.202.mine_ref.grid_ref
  44.3 0.1 collective-permute-start.9
  44.3 2.1 %collective-permute-done.17.after_ref.early_ref = bf16[336,256]{1,0:T(8,128)(2,1)S(1)} collective-permute-done((bf16[336,256]{1,0:T(8,128)(2,1)S(1)}, bf16[336,256]{1,0:T(8,128)(2,1)S(1)}, u32[]{:S(2)}, u32[]{:S(2)}) %collective-permute-start.17) | collective-permute-done | bytes 172064 | tf_op jit(solution)/shard_map/ppermute | solution.py:63
  46.5 0.3 shard_map.210
  46.8 0.1 collective-permute-start.19
  46.8 0.2 collective-permute-start.18
  47.0 0.2 shard_map.203.grid_ref.gstate_ref
  47.3 0.9 %collective-permute-done.19.other_ref = bf16[128,512]{1,0:T(8,128)(2,1)S(1)} collective-permute-done((bf16[128,512]{1,0:T(8,128)(2,1)S(1)}, bf16[128,512]{1,0:T(8,128)(2,1)S(1)}, u32[]{:S(2)}, u32[]{:S(2)}) %collective-permute-start.19) | collective-permute-done | bytes 131104 | tf_op jit(solution)/shard_map/ppermute | solution.py:431
  48.2 0.9 %shard_map.211 = (f32[336,512]{1,0:T(8,128)S(1)}, bf16[336,256]{1,0:T(8,128)(2,1)S(1)}, bf16[336,256]{1,0:T(8,128)(2,1)S(1)}, bf16[336,256]{1,0:T(8,128)(2,1)S(1)}) custom-call(f32[336,512]{1,0:T(8,128)S(1)} %shard_map.203.grid_ref.gstate_ref, f32[336,512]{1,0:T(8,128)S(1)} %get-tuple-element.73.mesh_ref.moved_ref, ...), custom_call_target="tpu_custom_call" | custom-call | flops 920000000 | tf_op jit(solution)/shard_map/pallas_call | solution.py:31
  49.0 2.4 %collective-permute-start.20 = (bf16[336,256]{1,0:T(8,128)(2,1)S(1)}, bf16[336,256]{1,0:T(8,128)(2,1)S(1)}, u32[]{:S(2)}, u32[]{:S(2)}) collective-permute-start(bf16[336,256]{1,0:T(8,128)(2,1)S(1)} %get-tuple-element.80), channel_id=1, source_target_pairs={{0,12},{4,8},{8,4},{12,0},{1,13},{5,9},{9,5},{13,1},{2,14},{6,10},... | collective-permute-start | bytes 516104 | tf_op jit(solution)/shard_map/ppermute | solution.py:63
  51.4 0.1 collective-permute-start.22
  51.6 1.8 %collective-permute-done.18.mine_ref = bf16[128,256]{1,0:T(8,128)(2,1)S(1)} collective-permute-done((bf16[128,256]{1,0:T(8,128)(2,1)S(1)}, bf16[128,256]{1,0:T(8,128)(2,1)S(1)}, u32[]{:S(2)}, u32[]{:S(2)}) %collective-permute-start.18) | collective-permute-done | bytes 65568 | tf_op jit(solution)/shard_map/ppermute | solution.py:63
  53.4 0.0 collective-permute-start.21
  53.4 1.2 %collective-permute-done.21.other_ref = bf16[128,256]{1,0:T(8,128)(2,1)S(1)} collective-permute-done((bf16[128,256]{1,0:T(8,128)(2,1)S(1)}, bf16[128,256]{1,0:T(8,128)(2,1)S(1)}, u32[]{:S(2)}, u32[]{:S(2)}) %collective-permute-start.21) | collective-permute-done | bytes 65568 | tf_op jit(solution)/shard_map/ppermute | solution.py:431
  54.6 0.2 shard_map.212.rest_1_
  54.9 3.3 %collective-permute-done.20.rest_0_ = bf16[336,256]{1,0:T(8,128)(2,1)S(1)} collective-permute-done((bf16[336,256]{1,0:T(8,128)(2,1)S(1)}, bf16[336,256]{1,0:T(8,128)(2,1)S(1)}, u32[]{:S(2)}, u32[]{:S(2)}) %collective-permute-start.20) | collective-permute-done | bytes 172064 | tf_op jit(solution)/shard_map/ppermute | solution.py:63
  58.2 2.9 %collective-permute-done.22.rest_2_ = bf16[336,256]{1,0:T(8,128)(2,1)S(1)} collective-permute-done((bf16[336,256]{1,0:T(8,128)(2,1)S(1)}, bf16[336,256]{1,0:T(8,128)(2,1)S(1)}, u32[]{:S(2)}, u32[]{:S(2)}) %collective-permute-start.22) | collective-permute-done | bytes 172064 | tf_op jit(solution)/shard_map/ppermute | solution.py:63
  61.1 1.9 %shard_map.213 = (f32[1296,128]{1,0:T(8,128)}, f32[18,18,512]{2,1,0:T(8,128)}) custom-call(f32[336,512]{1,0:T(8,128)S(1)} %shard_map.203.grid_ref.gstate_ref, f32[336,512]{1,0:T(8,128)S(1)} %get-tuple-element.77.mstate_ref, bf16[512,512]{1,0:T(8,128)(2,1)S(1)} %get-tuple-element.78.gland_ref, bf16[512,512]{1,0:T(8,128)(2,1)S(1)} %get-tuple-element.79.mland_ref, ...), custom_call_target="tpu_custom_call" | custom-call | flops 2184999936 | tf_op jit(solution)/shard_map/pallas_call | solution.py:31
  (36 shorter events, 0.2 us)
Async XLA Ops:
  0.6 5.6 %copy-start.12 = (f32[4,512]{1,0:T(4,128)S(1)}, f32[4,512]{1,0:T(4,128)}, u32[]{:S(2)}) copy-start(f32[4,512]{1,0:T(4,128)} %param.24) | copy-start | bytes 24580
  0.6 5.6 %copy-start.13 = (f32[4,512]{1,0:T(4,128)S(1)}, f32[4,512]{1,0:T(4,128)}, u32[]{:S(2)}) copy-start(f32[4,512]{1,0:T(4,128)} %param.25) | copy-start | bytes 24580
  0.7 5.7 %copy-start = (s32[4,512]{1,0:T(4,128)S(1)}, s32[4,512]{1,0:T(4,128)}, u32[]{:S(2)}) copy-start(s32[4,512]{1,0:T(4,128)} %index_ref.1) | copy-start | bytes 24580
  0.7 5.7 %copy-start.7 = (f32[4,128]{1,0:T(4,128)S(1)}, f32[4,128]{1,0:T(4,128)}, u32[]{:S(2)}) copy-start(f32[4,128]{1,0:T(4,128)} %speed_ref.7) | copy-start | bytes 6148
  0.7 5.7 %copy-start.8 = (s32[4,128]{1,0:T(4,128)S(1)}, s32[4,128]{1,0:T(4,128)}, u32[]{:S(2)}) copy-start(s32[4,128]{1,0:T(4,128)} %sea_ref.9) | copy-start | bytes 6148
  2.5 7.5 %collective-permute-start = (bf16[336,256]{1,0:T(8,128)(2,1)S(1)}, bf16[336,256]{1,0:T(8,128)(2,1)S(1)}, u32[]{:S(2)}, u32[]{:S(2)}) collective-permute-start(bf16[336,256]{1,0:T(8,128)(2,1)S(1)} %get-tuple-element.45), channel_id=1, source_target_pairs={{0,4},{8,12},{4,0},{12,8},{1,5},{9,13},{5,1},{13,9},{2,6},{10,14},... | collective-permute-start | bytes 516104 | tf_op jit(solution)/shard_map/ppermute | solution.py:58
  5.6 4.4 %collective-permute-start.1 = (bf16[336,256]{1,0:T(8,128)(2,1)S(1)}, bf16[336,256]{1,0:T(8,128)(2,1)S(1)}, u32[]{:S(2)}, u32[]{:S(2)}) collective-permute-start(bf16[336,256]{1,0:T(8,128)(2,1)S(1)} %get-tuple-element.46), channel_id=1, source_target_pairs={{4,8},{8,4},{5,9},{9,5},{6,10},{10,6},{7,11},{11,7},{20,24},{24,20... | collective-permute-start | bytes 516104 | tf_op jit(solution)/shard_map/ppermute | solution.py:58
  10.4 1.5 %collective-permute-start.2 = (bf16[128,512]{1,0:T(8,128)(2,1)S(1)}, bf16[128,512]{1,0:T(8,128)(2,1)S(1)}, u32[]{:S(2)}, u32[]{:S(2)}) collective-permute-start(bf16[128,512]{1,0:T(8,128)(2,1)S(1)} %get-tuple-element.51.after_ref), channel_id=1, source_target_pairs={{0,1},{1,0},{2,3},{3,2},{4,5},{5,4},{6,7},{7,6},{8,9},{9,8},{10,11... | collective-permute-start | bytes 393224 | tf_op jit(solution)/shard_map/ppermute | solution.py:431
  10.5 4.2 %copy-start.1 = (s32[4,1,4,128]{3,2,1,0:T(4,128)S(1)}, s32[4,1,4,128]{3,2,1,0:T(4,128)}, u32[]{:S(2)}) copy-start(s32[4,1,4,128]{3,2,1,0:T(4,128)} %gi_ref.1) | copy-start | bytes 24580
  10.5 4.2 %copy-start.2 = (f32[4,1,4,128]{3,2,1,0:T(4,128)S(1)}, f32[4,1,4,128]{3,2,1,0:T(4,128)}, u32[]{:S(2)}) copy-start(f32[4,1,4,128]{3,2,1,0:T(4,128)} %gw_ref.1) | copy-start | bytes 24580
  10.5 4.2 %copy-start.3 = (s32[3,1,4,128]{3,2,1,0:T(4,128)S(1)}, s32[3,1,4,128]{3,2,1,0:T(4,128)}, u32[]{:S(2)}) copy-start(s32[3,1,4,128]{3,2,1,0:T(4,128)} %mi_ref.1) | copy-start | bytes 18436
  10.5 4.2 %copy-start.4 = (f32[3,1,4,128]{3,2,1,0:T(4,128)S(1)}, f32[3,1,4,128]{3,2,1,0:T(4,128)}, u32[]{:S(2)}) copy-start(f32[3,1,4,128]{3,2,1,0:T(4,128)} %mw_ref.1) | copy-start | bytes 18436
  10.5 4.2 %copy-start.5 = (s32[1,4,128]{2,1,0:T(4,128)S(1)}, s32[1,4,128]{2,1,0:T(4,128)}, u32[]{:S(2)}) copy-start(s32[1,4,128]{2,1,0:T(4,128)} %gt_ref.1) | copy-start | bytes 6148
  10.6 4.2 %copy-start.6 = (s32[1,4,128]{2,1,0:T(4,128)S(1)}, s32[1,4,128]{2,1,0:T(4,128)}, u32[]{:S(2)}) copy-start(s32[1,4,128]{2,1,0:T(4,128)} %mt_ref.1) | copy-start | bytes 6148
  10.6 4.2 %copy-start.10 = (s32[1,4]{1,0:T(1,128)S(1)}, s32[1,4]{1,0:T(1,128)}, u32[]{:S(2)}) copy-start(s32[1,4]{1,0:T(1,128)} %gc_ref.1) | copy-start | bytes 52
  10.6 4.2 %copy-start.11 = (s32[1,4]{1,0:T(1,128)S(1)}, s32[1,4]{1,0:T(1,128)}, u32[]{:S(2)}) copy-start(s32[1,4]{1,0:T(1,128)} %mc_ref.1) | copy-start | bytes 52
  11.4 2.3 %collective-permute-start.10 = (bf16[128,512]{1,0:T(8,128)(2,1)S(1)}, bf16[128,512]{1,0:T(8,128)(2,1)S(1)}, u32[]{:S(2)}, u32[]{:S(2)}) collective-permute-start(bf16[128,512]{1,0:T(8,128)(2,1)S(1)} %get-tuple-element.65), channel_id=1, source_target_pairs={{0,1},{1,0},{2,3},{3,2},{4,5},{5,4},{6,7},{7,6},{8,9},{9,8},{10,11... | collective-permute-start | bytes 393224 | tf_op jit(solution)/shard_map/ppermute | solution.py:431
  12.0 14.3 %copy-start.9 = (s32[2,128]{1,0:T(2,128)S(1)}, s32[2,128]{1,0:T(2,128)}, u32[]{:S(2)}) copy-start(s32[2,128]{1,0:T(2,128)} %halo_ref.1) | copy-start | bytes 3076
  12.0 6.4 %collective-permute-start.3 = (bf16[128,512]{1,0:T(8,128)(2,1)S(1)}, bf16[128,512]{1,0:T(8,128)(2,1)S(1)}, u32[]{:S(2)}, u32[]{:S(2)}) collective-permute-start(bf16[128,512]{1,0:T(8,128)(2,1)S(1)} %get-tuple-element.92.after_ref), channel_id=1, source_target_pairs={{0,2},{2,0},{1,3},{3,1},{4,6},{6,4},{5,7},{7,5},{8,10},{10,8},{9,1... | collective-permute-start | bytes 393224 | tf_op jit(solution)/shard_map/ppermute | solution.py:63
  13.8 6.6 %collective-permute-start.11 = (bf16[128,512]{1,0:T(8,128)(2,1)S(1)}, bf16[128,512]{1,0:T(8,128)(2,1)S(1)}, u32[]{:S(2)}, u32[]{:S(2)}) collective-permute-start(bf16[128,512]{1,0:T(8,128)(2,1)S(1)} %get-tuple-element.88), channel_id=1, source_target_pairs={{0,2},{2,0},{1,3},{3,1},{4,6},{6,4},{5,7},{7,5},{8,10},{10,8},{9,1... | collective-permute-start | bytes 393224 | tf_op jit(solution)/shard_map/ppermute | solution.py:63
  18.5 2.0 %collective-permute-start.4 = (bf16[128,512]{1,0:T(8,128)(2,1)S(1)}, bf16[128,512]{1,0:T(8,128)(2,1)S(1)}, u32[]{:S(2)}, u32[]{:S(2)}) collective-permute-start(bf16[128,512]{1,0:T(8,128)(2,1)S(1)} %shard_map.198.mine_ref), channel_id=1, source_target_pairs={{0,1},{1,0},{2,3},{3,2},{4,5},{5,4},{6,7},{7,6},{8,9},{9,8},{10,11... | collective-permute-start | bytes 393224 | tf_op jit(solution)/shard_map/ppermute | solution.py:431
  20.4 5.8 %collective-permute-start.12 = (bf16[128,512]{1,0:T(8,128)(2,1)S(1)}, bf16[128,512]{1,0:T(8,128)(2,1)S(1)}, u32[]{:S(2)}, u32[]{:S(2)}) collective-permute-start(bf16[128,512]{1,0:T(8,128)(2,1)S(1)} %shard_map.205.mine_ref), channel_id=1, source_target_pairs={{0,1},{1,0},{2,3},{3,2},{4,5},{5,4},{6,7},{7,6},{8,9},{9,8},{10,11... | collective-permute-start | bytes 393224 | tf_op jit(solution)/shard_map/ppermute | solution.py:431
  20.8 10.6 %collective-permute-start.5 = (bf16[336,128]{1,0:T(8,128)(2,1)S(1)}, bf16[336,128]{1,0:T(8,128)(2,1)S(1)}, u32[]{:S(2)}, u32[]{:S(2)}) collective-permute-start(bf16[336,128]{1,0:T(8,128)(2,1)S(1)} %get-tuple-element.55), channel_id=1, source_target_pairs={{0,4},{8,12},{4,0},{12,8},{1,5},{9,13},{5,1},{13,9},{2,6},{10,14},... | collective-permute-start | bytes 258056 | tf_op jit(solution)/shard_map/ppermute | solution.py:58
  25.6 5.8 %collective-permute-start.6 = (bf16[336,128]{1,0:T(8,128)(2,1)S(1)}, bf16[336,128]{1,0:T(8,128)(2,1)S(1)}, u32[]{:S(2)}, u32[]{:S(2)}) collective-permute-start(bf16[336,128]{1,0:T(8,128)(2,1)S(1)} %get-tuple-element.56), channel_id=1, source_target_pairs={{4,8},{8,4},{5,9},{9,5},{6,10},{10,6},{7,11},{11,7},{20,24},{24,20... | collective-permute-start | bytes 258056 | tf_op jit(solution)/shard_map/ppermute | solution.py:58
  26.8 6.3 %collective-permute-start.13 = (bf16[336,128]{1,0:T(8,128)(2,1)S(1)}, bf16[336,128]{1,0:T(8,128)(2,1)S(1)}, u32[]{:S(2)}, u32[]{:S(2)}) collective-permute-start(bf16[336,128]{1,0:T(8,128)(2,1)S(1)} %get-tuple-element.67), channel_id=1, source_target_pairs={{0,4},{8,12},{4,0},{12,8},{1,5},{9,13},{5,1},{13,9},{2,6},{10,14},... | collective-permute-start | bytes 258056 | tf_op jit(solution)/shard_map/ppermute | solution.py:58
  29.8 3.2 %collective-permute-start.14 = (bf16[336,128]{1,0:T(8,128)(2,1)S(1)}, bf16[336,128]{1,0:T(8,128)(2,1)S(1)}, u32[]{:S(2)}, u32[]{:S(2)}) collective-permute-start(bf16[336,128]{1,0:T(8,128)(2,1)S(1)} %get-tuple-element.68), channel_id=1, source_target_pairs={{4,8},{8,4},{5,9},{9,5},{6,10},{10,6},{7,11},{11,7},{20,24},{24,20... | collective-permute-start | bytes 258056 | tf_op jit(solution)/shard_map/ppermute | solution.py:58
  31.9 5.9 %collective-permute-start.7 = (bf16[128,512]{1,0:T(8,128)(2,1)S(1)}, bf16[128,512]{1,0:T(8,128)(2,1)S(1)}, u32[]{:S(2)}, u32[]{:S(2)}) collective-permute-start(bf16[128,512]{1,0:T(8,128)(2,1)S(1)} %get-tuple-element.59.after_ref), channel_id=1, source_target_pairs={{0,1},{1,0},{2,3},{3,2},{4,5},{5,4},{6,7},{7,6},{8,9},{9,8},{10,11... | collective-permute-start | bytes 393224 | tf_op jit(solution)/shard_map/ppermute | solution.py:431
  33.9 5.4 %collective-permute-start.15 = (bf16[128,512]{1,0:T(8,128)(2,1)S(1)}, bf16[128,512]{1,0:T(8,128)(2,1)S(1)}, u32[]{:S(2)}, u32[]{:S(2)}) collective-permute-start(bf16[128,512]{1,0:T(8,128)(2,1)S(1)} %get-tuple-element.70), channel_id=1, source_target_pairs={{0,1},{1,0},{2,3},{3,2},{4,5},{5,4},{6,7},{7,6},{8,9},{9,8},{10,11... | collective-permute-start | bytes 393224 | tf_op jit(solution)/shard_map/ppermute | solution.py:431
  34.9 11.6 %collective-permute-start.17 = (bf16[336,256]{1,0:T(8,128)(2,1)S(1)}, bf16[336,256]{1,0:T(8,128)(2,1)S(1)}, u32[]{:S(2)}, u32[]{:S(2)}) collective-permute-start(bf16[336,256]{1,0:T(8,128)(2,1)S(1)} %shard_map.209), channel_id=1, source_target_pairs={{0,8},{4,12},{8,0},{12,4},{1,9},{5,13},{9,1},{13,5},{2,10},{6,14},... | collective-permute-start | bytes 516104 | tf_op jit(solution)/shard_map/ppermute | solution.py:63
  37.8 6.4 %collective-permute-start.8 = (bf16[128,512]{1,0:T(8,128)(2,1)S(1)}, bf16[128,512]{1,0:T(8,128)(2,1)S(1)}, u32[]{:S(2)}, u32[]{:S(2)}) collective-permute-start(bf16[128,512]{1,0:T(8,128)(2,1)S(1)} %get-tuple-element.90), channel_id=1, source_target_pairs={{0,2},{2,0},{1,3},{3,1},{4,6},{6,4},{5,7},{7,5},{8,10},{10,8},{9,1... | collective-permute-start | bytes 393224 | tf_op jit(solution)/shard_map/ppermute | solution.py:63
  39.4 7.1 %collective-permute-start.16 = (bf16[128,512]{1,0:T(8,128)(2,1)S(1)}, bf16[128,512]{1,0:T(8,128)(2,1)S(1)}, u32[]{:S(2)}, u32[]{:S(2)}) collective-permute-start(bf16[128,512]{1,0:T(8,128)(2,1)S(1)} %get-tuple-element.86), channel_id=1, source_target_pairs={{0,2},{2,0},{1,3},{3,1},{4,6},{6,4},{5,7},{7,5},{8,10},{10,8},{9,1... | collective-permute-start | bytes 393224 | tf_op jit(solution)/shard_map/ppermute | solution.py:63
  44.3 2.8 %collective-permute-start.9 = (bf16[128,512]{1,0:T(8,128)(2,1)S(1)}, bf16[128,512]{1,0:T(8,128)(2,1)S(1)}, u32[]{:S(2)}, u32[]{:S(2)}) collective-permute-start(bf16[128,512]{1,0:T(8,128)(2,1)S(1)} %shard_map.202.mine_ref.grid_ref), channel_id=1, source_target_pairs={{0,1},{1,0},{2,3},{3,2},{4,5},{5,4},{6,7},{7,6},{8,9},{9,8},{10,11... | collective-permute-start | bytes 393224 | tf_op jit(solution)/shard_map/ppermute | solution.py:431
  46.8 1.4 %collective-permute-start.19 = (bf16[128,512]{1,0:T(8,128)(2,1)S(1)}, bf16[128,512]{1,0:T(8,128)(2,1)S(1)}, u32[]{:S(2)}, u32[]{:S(2)}) collective-permute-start(bf16[128,512]{1,0:T(8,128)(2,1)S(1)} %get-tuple-element.75.mine_ref), channel_id=1, source_target_pairs={{0,1},{1,0},{2,3},{3,2},{4,5},{5,4},{6,7},{7,6},{8,9},{9,8},{10,11... | collective-permute-start | bytes 393224 | tf_op jit(solution)/shard_map/ppermute | solution.py:431
  46.8 6.5 %collective-permute-start.18 = (bf16[128,256]{1,0:T(8,128)(2,1)S(1)}, bf16[128,256]{1,0:T(8,128)(2,1)S(1)}, u32[]{:S(2)}, u32[]{:S(2)}) collective-permute-start(bf16[128,256]{1,0:T(8,128)(2,1)S(1)} %get-tuple-element.74), channel_id=1, source_target_pairs={{0,8},{4,12},{8,0},{12,4},{1,9},{5,13},{9,1},{13,5},{2,10},{6,14},... | collective-permute-start | bytes 196616 | tf_op jit(solution)/shard_map/ppermute | solution.py:63
  49.0 9.2 %collective-permute-start.20 = (bf16[336,256]{1,0:T(8,128)(2,1)S(1)}, bf16[336,256]{1,0:T(8,128)(2,1)S(1)}, u32[]{:S(2)}, u32[]{:S(2)}) collective-permute-start(bf16[336,256]{1,0:T(8,128)(2,1)S(1)} %get-tuple-element.80), channel_id=1, source_target_pairs={{0,12},{4,8},{8,4},{12,0},{1,13},{5,9},{9,5},{13,1},{2,14},{6,10},... | collective-permute-start | bytes 516104 | tf_op jit(solution)/shard_map/ppermute | solution.py:63
  51.4 9.7 %collective-permute-start.22 = (bf16[336,256]{1,0:T(8,128)(2,1)S(1)}, bf16[336,256]{1,0:T(8,128)(2,1)S(1)}, u32[]{:S(2)}, u32[]{:S(2)}) collective-permute-start(bf16[336,256]{1,0:T(8,128)(2,1)S(1)} %get-tuple-element.82), channel_id=1, source_target_pairs={{0,4},{4,0},{8,12},{12,8},{1,5},{5,1},{9,13},{13,9},{2,6},{6,2},{1... | collective-permute-start | bytes 516104 | tf_op jit(solution)/shard_map/ppermute | solution.py:63
  53.4 1.3 %collective-permute-start.21 = (bf16[128,256]{1,0:T(8,128)(2,1)S(1)}, bf16[128,256]{1,0:T(8,128)(2,1)S(1)}, u32[]{:S(2)}, u32[]{:S(2)}) collective-permute-start(bf16[128,256]{1,0:T(8,128)(2,1)S(1)} %collective-permute-done.18.mine_ref), channel_id=1, source_target_pairs={{0,1},{1,0},{2,3},{3,2},{4,5},{5,4},{6,7},{7,6},{8,9},{9,8},{10,11... | collective-permute-start | bytes 196616 | tf_op jit(solution)/shard_map/ppermute | solution.py:431

commit v6 on v5

--- a/solution.py
+++ b/solution.py
@@ -573,7 +573,7 @@
                 mstate, hot, weight
             )
 
-    split = peers // 2
+    split = peers - 1
     slot_shape = ((padded, 2 * cap), BF16)
     (early,) = kernel_call(
         functools.partial(early_kernel, bands=bands, peer=split), [slot_shape], (), 0.4

time: 63.3 us -> 61.8 us (0.976)
  waiting for transfers between devices: 19.9 us -> 18 us
    ppermute x8, waiting for transfers between devices: 17.6 us -> 16.6 us  [peer_swap(): return lax.ppermute(array, axis, [(i, i ^ step) for i in range(size)])]
    ppermute x9, waiting for transfers between devices: 2.14 us -> 1.27 us  [core_swap(): return lax.ppermute(array, 'dr', [(0, 1), (1, 0)])]
  transfers between devices with their start and end apart: 23 -> 23, of which waited for: 10 -> 9; matrix products, arithmetic and copies ran while one was open for 0% -> 0% of each run, Pallas kernels for 20% -> 20%
where the time goes in v6:
time: 61.8 us; the launch traced here: 61.6 us
  starting transfers between devices  25.4 us (41%)
  waiting for transfers between devices  18 us (29%)
  Pallas kernels  16.6 us (27%)
  between operations  1.27 us (2%)
    ppermute x8, waiting for transfers between devices, peer_swap(): return lax.ppermute(array, axis, [(i, i ^ step) for i in range(size)])  16.6 us
    pallas_call x20, Pallas kernels, run(): pl.pallas_call(body, out_shape=[jax.ShapeDtypeStruct(s, t) for s, t in ou...  16.6 us
    ppermute x6, starting transfers between devices, pair_swap(): return lax.ppermute(array, axis, pairs + [(j, i) for i, j in pairs])  13.1 us
    ppermute x8, starting transfers between devices, peer_swap(): return lax.ppermute(array, axis, [(i, i ^ step) for i in range(size)])  10.8 us
    ppermute x9, starting transfers between devices, core_swap(): return lax.ppermute(array, 'dr', [(0, 1), (1, 0)])  1.53 us
    ppermute x9, waiting for transfers between devices, core_swap(): return lax.ppermute(array, 'dr', [(0, 1), (1, 0)])  1.27 us
  transfers between devices with their start and end apart: 23, of which 9 were waited for; matrix products, arithmetic and copies ran while one was open for 0% of the time, Pallas kernels for 20%

profile of v6, /device:TPU:0, one launch (start us, length us, event | category | flops | bytes accessed | tf_op | source)
XLA Modules:
  0.0 61.6 jit_solution(17398386219212916839)
XLA Ops:
  0.7 1.8 %shard_map.195 = (bf16[336,256]{1,0:T(8,128)(2,1)S(1)}, bf16[336,256]{1,0:T(8,128)(2,1)S(1)}) custom-call(f32[1296,128]{1,0:T(8,128)} %bitcast.3, f32[18,18,512]{2,1,0:T(8,128)} %mesh_hbm.3, s32[2,128]{1,0:T(2,128)} %halo_ref.1), custom_call_target="tpu_custom_call" | custom-call | flops 2070000000 | tf_op jit(solution)/shard_map/pallas_call | solution.py:31
  2.5 3.1 %collective-permute-start = (bf16[336,256]{1,0:T(8,128)(2,1)S(1)}, bf16[336,256]{1,0:T(8,128)(2,1)S(1)}, u32[]{:S(2)}, u32[]{:S(2)}) collective-permute-start(bf16[336,256]{1,0:T(8,128)(2,1)S(1)} %get-tuple-element.45), channel_id=1, source_target_pairs={{0,4},{8,12},{4,0},{12,8},{1,5},{9,13},{5,1},{13,9},{2,6},{10,14},... | collective-permute-start | bytes 516104 | tf_op jit(solution)/shard_map/ppermute | solution.py:58
  5.6 0.7 %collective-permute-start.1 = (bf16[336,256]{1,0:T(8,128)(2,1)S(1)}, bf16[336,256]{1,0:T(8,128)(2,1)S(1)}, u32[]{:S(2)}, u32[]{:S(2)}) collective-permute-start(bf16[336,256]{1,0:T(8,128)(2,1)S(1)} %get-tuple-element.46), channel_id=1, source_target_pairs={{4,8},{8,4},{5,9},{9,5},{6,10},{10,6},{7,11},{11,7},{20,24},{24,20... | collective-permute-start | bytes 516104 | tf_op jit(solution)/shard_map/ppermute | solution.py:58
  6.3 0.1 cosine_multiply_fusion
  6.4 3.4 %shard_map.194 = (f32[336,512]{1,0:T(8,128)S(1)}, f32[336,512]{1,0:T(8,128)S(1)}, bf16[4,768,512]{2,1,0:T(8,128)(2,1)S(1)}, f32[4,336,512]{2,1,0:T(8,128)S(1)}, ...) custom-call(f32[1296,128]{1,0:T(8,128)} %bitcast.4, f32[18,18,512]{2,1,0:T(8,128)} %mesh_hbm.3, ...), custom_call_target="tpu_custom_call" | custom-call | flops 3910000128 | tf_op jit(solution)/shard_map/pallas_call | solution.py:31
  9.8 0.1 collective-permute-done.even_ref
  10.0 0.0 collective-permute-done.1.odd_ref
  10.0 0.4 shard_map.196
  10.4 0.1 collective-permute-start.2
  10.5 0.0 copy-start.1
  10.5 0.0 copy-start.2
  10.5 0.0 copy-start.3
  10.5 0.0 copy-start.4
  10.5 0.0 copy-start.5
  10.6 0.0 copy-start.6
  10.6 0.0 copy-start.10
  10.6 0.0 copy-start.11
  10.6 0.8 %shard_map.204 = (f32[336,512]{1,0:T(8,128)S(1)}, f32[128,512]{1,0:T(8,128)S(1)}, bf16[128,512]{1,0:T(8,128)(2,1)S(1)}) custom-call(f32[336,512]{1,0:T(8,128)S(1)} %get-tuple-element.60.part_ref, bf16[336,256]{1,0:T(8,128)(2,1)S(1)} %collective-permute-done.even_ref, bf16[336,256]{1,0:T(8,128)(2,1)S(1)} %collective-permute-done.1.odd_ref, ...), custom_call_target="tpu_custom_call" | custom-call | flops 920000000 | tf_op jit(solution)/shard_map/pallas_call | solution.py:31
  11.4 0.5 collective-permute-start.10
  12.0 1.7 %collective-permute-start.3 = (bf16[128,512]{1,0:T(8,128)(2,1)S(1)}, bf16[128,512]{1,0:T(8,128)(2,1)S(1)}, u32[]{:S(2)}, u32[]{:S(2)}) collective-permute-start(bf16[128,512]{1,0:T(8,128)(2,1)S(1)} %get-tuple-element.92.after_ref), channel_id=1, source_target_pairs={{0,2},{2,0},{1,3},{3,1},{4,6},{6,4},{5,7},{7,5},{8,10},{10,8},{9,1... | collective-permute-start | bytes 393224 | tf_op jit(solution)/shard_map/ppermute | solution.py:63
  13.7 0.0 collective-permute-done.10
  13.8 0.9 %collective-permute-start.11 = (bf16[128,512]{1,0:T(8,128)(2,1)S(1)}, bf16[128,512]{1,0:T(8,128)(2,1)S(1)}, u32[]{:S(2)}, u32[]{:S(2)}) collective-permute-start(bf16[128,512]{1,0:T(8,128)(2,1)S(1)} %get-tuple-element.88), channel_id=1, source_target_pairs={{0,2},{2,0},{1,3},{3,1},{4,6},{6,4},{5,7},{7,5},{8,10},{10,8},{9,1... | collective-permute-start | bytes 393224 | tf_op jit(solution)/shard_map/ppermute | solution.py:63
  14.8 2.2 %shard_map.197 = (bf16[512,512]{1,0:T(8,128)(2,1)S(1)}, bf16[512,512]{1,0:T(8,128)(2,1)S(1)}, f32[2,512]{1,0:T(2,128)S(1)}, bf16[512,512]{1,0:T(8,128)(2,1)S(1)}, bf16[512,512]{1,0:T(8,128)(2,1)S(1)}) custom-call(s32[4,1,4,128]{3,2,1,0:T(4,128)S(1)} %copy-done.1, f32[4,1,4,128]{3,2,1,0:T(4,128)S(1)} %copy-done.2, s32[1,4]{1,0:T(1,128)S(1)} %copy-done.10, ...), custom_call_target="tpu_custom_call" | custom-call | flops 575000000 | tf_op jit(solution)/shard_map/pallas_call | solution.py:31
  16.9 1.5 %collective-permute-done.3.got_ref = bf16[128,512]{1,0:T(8,128)(2,1)S(1)} collective-permute-done((bf16[128,512]{1,0:T(8,128)(2,1)S(1)}, bf16[128,512]{1,0:T(8,128)(2,1)S(1)}, u32[]{:S(2)}, u32[]{:S(2)}) %collective-permute-start.3) | collective-permute-done | bytes 131104 | tf_op jit(solution)/shard_map/ppermute | solution.py:63
  18.4 0.1 shard_map.198.mine_ref
  18.5 0.1 collective-permute-start.4
  18.6 1.7 %collective-permute-done.11.got_ref = bf16[128,512]{1,0:T(8,128)(2,1)S(1)} collective-permute-done((bf16[128,512]{1,0:T(8,128)(2,1)S(1)}, bf16[128,512]{1,0:T(8,128)(2,1)S(1)}, u32[]{:S(2)}, u32[]{:S(2)}) %collective-permute-start.11) | collective-permute-done | bytes 131104 | tf_op jit(solution)/shard_map/ppermute | solution.py:63
  20.3 0.1 shard_map.205.mine_ref
  20.4 0.1 collective-permute-start.12
  20.5 0.0 collective-permute-done.4.other_ref
  20.5 0.3 shard_map.199
  20.8 4.8 %collective-permute-start.5 = (bf16[336,128]{1,0:T(8,128)(2,1)S(1)}, bf16[336,128]{1,0:T(8,128)(2,1)S(1)}, u32[]{:S(2)}, u32[]{:S(2)}) collective-permute-start(bf16[336,128]{1,0:T(8,128)(2,1)S(1)} %get-tuple-element.55), channel_id=1, source_target_pairs={{0,4},{8,12},{4,0},{12,8},{1,5},{9,13},{5,1},{13,9},{2,6},{10,14},... | collective-permute-start | bytes 258056 | tf_op jit(solution)/shard_map/ppermute | solution.py:58
  25.6 0.7 %collective-permute-start.6 = (bf16[336,128]{1,0:T(8,128)(2,1)S(1)}, bf16[336,128]{1,0:T(8,128)(2,1)S(1)}, u32[]{:S(2)}, u32[]{:S(2)}) collective-permute-start(bf16[336,128]{1,0:T(8,128)(2,1)S(1)} %get-tuple-element.56), channel_id=1, source_target_pairs={{4,8},{8,4},{5,9},{9,5},{6,10},{10,6},{7,11},{11,7},{20,24},{24,20... | collective-permute-start | bytes 258056 | tf_op jit(solution)/shard_map/ppermute | solution.py:58
  26.3 0.0 collective-permute-done.12.other_ref
  26.3 0.5 shard_map.206
  26.8 3.1 %collective-permute-start.13 = (bf16[336,128]{1,0:T(8,128)(2,1)S(1)}, bf16[336,128]{1,0:T(8,128)(2,1)S(1)}, u32[]{:S(2)}, u32[]{:S(2)}) collective-permute-start(bf16[336,128]{1,0:T(8,128)(2,1)S(1)} %get-tuple-element.67), channel_id=1, source_target_pairs={{0,4},{8,12},{4,0},{12,8},{1,5},{9,13},{5,1},{13,9},{2,6},{10,14},... | collective-permute-start | bytes 258056 | tf_op jit(solution)/shard_map/ppermute | solution.py:58
  29.8 0.8 %collective-permute-start.14 = (bf16[336,128]{1,0:T(8,128)(2,1)S(1)}, bf16[336,128]{1,0:T(8,128)(2,1)S(1)}, u32[]{:S(2)}, u32[]{:S(2)}) collective-permute-start(bf16[336,128]{1,0:T(8,128)(2,1)S(1)} %get-tuple-element.68), channel_id=1, source_target_pairs={{4,8},{8,4},{5,9},{9,5},{6,10},{10,6},{7,11},{11,7},{20,24},{24,20... | collective-permute-start | bytes 258056 | tf_op jit(solution)/shard_map/ppermute | solution.py:58
  30.7 0.7 %shard_map.200.part_ref = f32[336,512]{1,0:T(8,128)S(1)} custom-call(f32[336,512]{1,0:T(8,128)S(1)} %get-tuple-element.54.state_ref, f32[336,2]{1,0:T(8,128)S(1)} %get-tuple-element.47.band_ref, s32[4,128]{1,0:T(4,128)S(1)} %copy-done.8, f32[4,128]{1,0:T(4,128)S(1)} %copy-done.7), custom_call_target="tpu_custom_call" | custom-call | flops 575000000 | tf_op jit(solution)/shard_map/pallas_call | solution.py:31
  31.4 0.0 collective-permute-done.6.odd_ref
  31.4 0.4 shard_map.201
  31.9 0.1 collective-permute-start.7
  32.0 1.1 %shard_map.207.part_ref = f32[336,512]{1,0:T(8,128)S(1)} custom-call(f32[336,512]{1,0:T(8,128)S(1)} %get-tuple-element.66.state_ref, bf16[4,768,512]{2,1,0:T(8,128)(2,1)S(1)} %get-tuple-element.61.hot_ref, f32[4,336,512]{2,1,0:T(8,128)S(1)} %get-tuple-element.62.weight_ref), custom_call_target="tpu_custom_call" | custom-call | flops 1150000000 | tf_op jit(solution)/shard_map/pallas_call | solution.py:31
  33.1 0.8 %shard_map.208 = (f32[336,512]{1,0:T(8,128)S(1)}, f32[128,512]{1,0:T(8,128)S(1)}, bf16[128,512]{1,0:T(8,128)(2,1)S(1)}) custom-call(f32[336,512]{1,0:T(8,128)S(1)} %shard_map.207.part_ref, bf16[336,128]{1,0:T(8,128)(2,1)S(1)} %collective-permute-done.13.even_ref, bf16[336,128]{1,0:T(8,128)(2,1)S(1)} %collective-permute-done.14.odd_ref, ...), custom_call_target="tpu_custom_call" | custom-call | flops 920000000 | tf_op jit(solution)/shard_map/pallas_call | solution.py:31
  33.9 0.6 collective-permute-start.15
  34.5 0.4 shard_map.209
  34.9 1.3 %collective-permute-start.17 = (bf16[336,256]{1,0:T(8,128)(2,1)S(1)}, bf16[336,256]{1,0:T(8,128)(2,1)S(1)}, u32[]{:S(2)}, u32[]{:S(2)}) collective-permute-start(bf16[336,256]{1,0:T(8,128)(2,1)S(1)} %shard_map.209), channel_id=1, source_target_pairs={{0,12},{4,8},{8,4},{12,0},{1,13},{5,9},{9,5},{13,1},{2,14},{6,10},... | collective-permute-start | bytes 516104 | tf_op jit(solution)/shard_map/ppermute | solution.py:63
  36.2 1.6 %collective-permute-start.8 = (bf16[128,512]{1,0:T(8,128)(2,1)S(1)}, bf16[128,512]{1,0:T(8,128)(2,1)S(1)}, u32[]{:S(2)}, u32[]{:S(2)}) collective-permute-start(bf16[128,512]{1,0:T(8,128)(2,1)S(1)} %get-tuple-element.90), channel_id=1, source_target_pairs={{0,2},{2,0},{1,3},{3,1},{4,6},{6,4},{5,7},{7,5},{8,10},{10,8},{9,1... | collective-permute-start | bytes 393224 | tf_op jit(solution)/shard_map/ppermute | solution.py:63
  37.8 0.6 collective-permute-start.16
  38.4 4.3 %collective-permute-done.8.got_ref = bf16[128,512]{1,0:T(8,128)(2,1)S(1)} collective-permute-done((bf16[128,512]{1,0:T(8,128)(2,1)S(1)}, bf16[128,512]{1,0:T(8,128)(2,1)S(1)}, u32[]{:S(2)}, u32[]{:S(2)}) %collective-permute-start.8) | collective-permute-done | bytes 131104 | tf_op jit(solution)/shard_map/ppermute | solution.py:63
  42.6 0.1 shard_map.202.mine_ref.grid_ref
  42.7 0.1 collective-permute-start.9
  42.8 0.3 collective-permute-done.17.after_ref.early_ref
  43.1 1.0 %collective-permute-done.16.got_ref = bf16[128,512]{1,0:T(8,128)(2,1)S(1)} collective-permute-done((bf16[128,512]{1,0:T(8,128)(2,1)S(1)}, bf16[128,512]{1,0:T(8,128)(2,1)S(1)}, u32[]{:S(2)}, u32[]{:S(2)}) %collective-permute-start.16) | collective-permute-done | bytes 131104 | tf_op jit(solution)/shard_map/ppermute | solution.py:63
  44.2 0.3 shard_map.210
  44.4 0.1 collective-permute-start.19
  44.5 2.7 %collective-permute-start.18 = (bf16[128,256]{1,0:T(8,128)(2,1)S(1)}, bf16[128,256]{1,0:T(8,128)(2,1)S(1)}, u32[]{:S(2)}, u32[]{:S(2)}) collective-permute-start(bf16[128,256]{1,0:T(8,128)(2,1)S(1)} %get-tuple-element.74), channel_id=1, source_target_pairs={{0,12},{4,8},{8,4},{12,0},{1,13},{5,9},{9,5},{13,1},{2,14},{6,10},... | collective-permute-start | bytes 196616 | tf_op jit(solution)/shard_map/ppermute | solution.py:63
  47.2 0.2 shard_map.203.grid_ref.gstate_ref
  47.5 0.9 %shard_map.211 = (f32[336,512]{1,0:T(8,128)S(1)}, bf16[336,256]{1,0:T(8,128)(2,1)S(1)}, bf16[336,256]{1,0:T(8,128)(2,1)S(1)}, bf16[336,256]{1,0:T(8,128)(2,1)S(1)}) custom-call(f32[336,512]{1,0:T(8,128)S(1)} %shard_map.203.grid_ref.gstate_ref, f32[336,512]{1,0:T(8,128)S(1)} %get-tuple-element.73.mesh_ref.moved_ref, ...), custom_call_target="tpu_custom_call" | custom-call | flops 920000000 | tf_op jit(solution)/shard_map/pallas_call | solution.py:31
  48.3 2.0 %collective-permute-start.21 = (bf16[336,256]{1,0:T(8,128)(2,1)S(1)}, bf16[336,256]{1,0:T(8,128)(2,1)S(1)}, u32[]{:S(2)}, u32[]{:S(2)}) collective-permute-start(bf16[336,256]{1,0:T(8,128)(2,1)S(1)} %get-tuple-element.81), channel_id=1, source_target_pairs={{0,8},{4,12},{8,0},{12,4},{1,9},{5,13},{9,1},{13,5},{2,10},{6,14},... | collective-permute-start | bytes 516104 | tf_op jit(solution)/shard_map/ppermute | solution.py:63
  50.4 0.5 collective-permute-done.18.mine_ref
  50.9 1.3 %collective-permute-done.20.other_ref = bf16[128,256]{1,0:T(8,128)(2,1)S(1)} collective-permute-done((bf16[128,256]{1,0:T(8,128)(2,1)S(1)}, bf16[128,256]{1,0:T(8,128)(2,1)S(1)}, u32[]{:S(2)}, u32[]{:S(2)}) %collective-permute-start.20) | collective-permute-done | bytes 65568 | tf_op jit(solution)/shard_map/ppermute | solution.py:431
  52.1 0.2 shard_map.212.rest_0_
  52.4 7.2 %collective-permute-done.21.rest_1_ = bf16[336,256]{1,0:T(8,128)(2,1)S(1)} collective-permute-done((bf16[336,256]{1,0:T(8,128)(2,1)S(1)}, bf16[336,256]{1,0:T(8,128)(2,1)S(1)}, u32[]{:S(2)}, u32[]{:S(2)}) %collective-permute-start.21) | collective-permute-done | bytes 172064 | tf_op jit(solution)/shard_map/ppermute | solution.py:63
  59.6 1.9 %shard_map.213 = (f32[1296,128]{1,0:T(8,128)}, f32[18,18,512]{2,1,0:T(8,128)}) custom-call(f32[336,512]{1,0:T(8,128)S(1)} %shard_map.203.grid_ref.gstate_ref, f32[336,512]{1,0:T(8,128)S(1)} %get-tuple-element.77.mstate_ref, bf16[512,512]{1,0:T(8,128)(2,1)S(1)} %get-tuple-element.78.gland_ref, bf16[512,512]{1,0:T(8,128)(2,1)S(1)} %get-tuple-element.79.mland_ref, ...), custom_call_target="tpu_custom_call" | custom-call | flops 2184999936 | tf_op jit(solution)/shard_map/pallas_call | solution.py:31
  (36 shorter events, 0.2 us)
Async XLA Ops:
  0.6 5.6 %copy-start.12 = (f32[4,512]{1,0:T(4,128)S(1)}, f32[4,512]{1,0:T(4,128)}, u32[]{:S(2)}) copy-start(f32[4,512]{1,0:T(4,128)} %param.24) | copy-start | bytes 24580
  0.6 5.6 %copy-start.13 = (f32[4,512]{1,0:T(4,128)S(1)}, f32[4,512]{1,0:T(4,128)}, u32[]{:S(2)}) copy-start(f32[4,512]{1,0:T(4,128)} %param.25) | copy-start | bytes 24580
  0.7 5.7 %copy-start = (s32[4,512]{1,0:T(4,128)S(1)}, s32[4,512]{1,0:T(4,128)}, u32[]{:S(2)}) copy-start(s32[4,512]{1,0:T(4,128)} %index_ref.1) | copy-start | bytes 24580
  0.7 5.7 %copy-start.7 = (f32[4,128]{1,0:T(4,128)S(1)}, f32[4,128]{1,0:T(4,128)}, u32[]{:S(2)}) copy-start(f32[4,128]{1,0:T(4,128)} %speed_ref.7) | copy-start | bytes 6148
  0.7 5.7 %copy-start.8 = (s32[4,128]{1,0:T(4,128)S(1)}, s32[4,128]{1,0:T(4,128)}, u32[]{:S(2)}) copy-start(s32[4,128]{1,0:T(4,128)} %sea_ref.9) | copy-start | bytes 6148
  2.5 7.5 %collective-permute-start = (bf16[336,256]{1,0:T(8,128)(2,1)S(1)}, bf16[336,256]{1,0:T(8,128)(2,1)S(1)}, u32[]{:S(2)}, u32[]{:S(2)}) collective-permute-start(bf16[336,256]{1,0:T(8,128)(2,1)S(1)} %get-tuple-element.45), channel_id=1, source_target_pairs={{0,4},{8,12},{4,0},{12,8},{1,5},{9,13},{5,1},{13,9},{2,6},{10,14},... | collective-permute-start | bytes 516104 | tf_op jit(solution)/shard_map/ppermute | solution.py:58
  5.6 4.4 %collective-permute-start.1 = (bf16[336,256]{1,0:T(8,128)(2,1)S(1)}, bf16[336,256]{1,0:T(8,128)(2,1)S(1)}, u32[]{:S(2)}, u32[]{:S(2)}) collective-permute-start(bf16[336,256]{1,0:T(8,128)(2,1)S(1)} %get-tuple-element.46), channel_id=1, source_target_pairs={{4,8},{8,4},{5,9},{9,5},{6,10},{10,6},{7,11},{11,7},{20,24},{24,20... | collective-permute-start | bytes 516104 | tf_op jit(solution)/shard_map/ppermute | solution.py:58
  10.4 1.5 %collective-permute-start.2 = (bf16[128,512]{1,0:T(8,128)(2,1)S(1)}, bf16[128,512]{1,0:T(8,128)(2,1)S(1)}, u32[]{:S(2)}, u32[]{:S(2)}) collective-permute-start(bf16[128,512]{1,0:T(8,128)(2,1)S(1)} %get-tuple-element.51.after_ref), channel_id=1, source_target_pairs={{0,1},{1,0},{2,3},{3,2},{4,5},{5,4},{6,7},{7,6},{8,9},{9,8},{10,11... | collective-permute-start | bytes 393224 | tf_op jit(solution)/shard_map/ppermute | solution.py:431
  10.5 4.2 %copy-start.1 = (s32[4,1,4,128]{3,2,1,0:T(4,128)S(1)}, s32[4,1,4,128]{3,2,1,0:T(4,128)}, u32[]{:S(2)}) copy-start(s32[4,1,4,128]{3,2,1,0:T(4,128)} %gi_ref.1) | copy-start | bytes 24580
  10.5 4.2 %copy-start.2 = (f32[4,1,4,128]{3,2,1,0:T(4,128)S(1)}, f32[4,1,4,128]{3,2,1,0:T(4,128)}, u32[]{:S(2)}) copy-start(f32[4,1,4,128]{3,2,1,0:T(4,128)} %gw_ref.1) | copy-start | bytes 24580
  10.5 4.2 %copy-start.3 = (s32[3,1,4,128]{3,2,1,0:T(4,128)S(1)}, s32[3,1,4,128]{3,2,1,0:T(4,128)}, u32[]{:S(2)}) copy-start(s32[3,1,4,128]{3,2,1,0:T(4,128)} %mi_ref.1) | copy-start | bytes 18436
  10.5 4.2 %copy-start.4 = (f32[3,1,4,128]{3,2,1,0:T(4,128)S(1)}, f32[3,1,4,128]{3,2,1,0:T(4,128)}, u32[]{:S(2)}) copy-start(f32[3,1,4,128]{3,2,1,0:T(4,128)} %mw_ref.1) | copy-start | bytes 18436
  10.5 4.2 %copy-start.5 = (s32[1,4,128]{2,1,0:T(4,128)S(1)}, s32[1,4,128]{2,1,0:T(4,128)}, u32[]{:S(2)}) copy-start(s32[1,4,128]{2,1,0:T(4,128)} %gt_ref.1) | copy-start | bytes 6148
  10.6 4.2 %copy-start.6 = (s32[1,4,128]{2,1,0:T(4,128)S(1)}, s32[1,4,128]{2,1,0:T(4,128)}, u32[]{:S(2)}) copy-start(s32[1,4,128]{2,1,0:T(4,128)} %mt_ref.1) | copy-start | bytes 6148
  10.6 4.2 %copy-start.10 = (s32[1,4]{1,0:T(1,128)S(1)}, s32[1,4]{1,0:T(1,128)}, u32[]{:S(2)}) copy-start(s32[1,4]{1,0:T(1,128)} %gc_ref.1) | copy-start | bytes 52
  10.6 4.2 %copy-start.11 = (s32[1,4]{1,0:T(1,128)S(1)}, s32[1,4]{1,0:T(1,128)}, u32[]{:S(2)}) copy-start(s32[1,4]{1,0:T(1,128)} %mc_ref.1) | copy-start | bytes 52
  11.4 2.3 %collective-permute-start.10 = (bf16[128,512]{1,0:T(8,128)(2,1)S(1)}, bf16[128,512]{1,0:T(8,128)(2,1)S(1)}, u32[]{:S(2)}, u32[]{:S(2)}) collective-permute-start(bf16[128,512]{1,0:T(8,128)(2,1)S(1)} %get-tuple-element.65), channel_id=1, source_target_pairs={{0,1},{1,0},{2,3},{3,2},{4,5},{5,4},{6,7},{7,6},{8,9},{9,8},{10,11... | collective-permute-start | bytes 393224 | tf_op jit(solution)/shard_map/ppermute | solution.py:431
  12.0 14.3 %copy-start.9 = (s32[2,128]{1,0:T(2,128)S(1)}, s32[2,128]{1,0:T(2,128)}, u32[]{:S(2)}) copy-start(s32[2,128]{1,0:T(2,128)} %halo_ref.1) | copy-start | bytes 3076
  12.0 6.4 %collective-permute-start.3 = (bf16[128,512]{1,0:T(8,128)(2,1)S(1)}, bf16[128,512]{1,0:T(8,128)(2,1)S(1)}, u32[]{:S(2)}, u32[]{:S(2)}) collective-permute-start(bf16[128,512]{1,0:T(8,128)(2,1)S(1)} %get-tuple-element.92.after_ref), channel_id=1, source_target_pairs={{0,2},{2,0},{1,3},{3,1},{4,6},{6,4},{5,7},{7,5},{8,10},{10,8},{9,1... | collective-permute-start | bytes 393224 | tf_op jit(solution)/shard_map/ppermute | solution.py:63
  13.8 6.6 %collective-permute-start.11 = (bf16[128,512]{1,0:T(8,128)(2,1)S(1)}, bf16[128,512]{1,0:T(8,128)(2,1)S(1)}, u32[]{:S(2)}, u32[]{:S(2)}) collective-permute-start(bf16[128,512]{1,0:T(8,128)(2,1)S(1)} %get-tuple-element.88), channel_id=1, source_target_pairs={{0,2},{2,0},{1,3},{3,1},{4,6},{6,4},{5,7},{7,5},{8,10},{10,8},{9,1... | collective-permute-start | bytes 393224 | tf_op jit(solution)/shard_map/ppermute | solution.py:63
  18.5 2.0 %collective-permute-start.4 = (bf16[128,512]{1,0:T(8,128)(2,1)S(1)}, bf16[128,512]{1,0:T(8,128)(2,1)S(1)}, u32[]{:S(2)}, u32[]{:S(2)}) collective-permute-start(bf16[128,512]{1,0:T(8,128)(2,1)S(1)} %shard_map.198.mine_ref), channel_id=1, source_target_pairs={{0,1},{1,0},{2,3},{3,2},{4,5},{5,4},{6,7},{7,6},{8,9},{9,8},{10,11... | collective-permute-start | bytes 393224 | tf_op jit(solution)/shard_map/ppermute | solution.py:431
  20.4 5.8 %collective-permute-start.12 = (bf16[128,512]{1,0:T(8,128)(2,1)S(1)}, bf16[128,512]{1,0:T(8,128)(2,1)S(1)}, u32[]{:S(2)}, u32[]{:S(2)}) collective-permute-start(bf16[128,512]{1,0:T(8,128)(2,1)S(1)} %shard_map.205.mine_ref), channel_id=1, source_target_pairs={{0,1},{1,0},{2,3},{3,2},{4,5},{5,4},{6,7},{7,6},{8,9},{9,8},{10,11... | collective-permute-start | bytes 393224 | tf_op jit(solution)/shard_map/ppermute | solution.py:431
  20.8 10.6 %collective-permute-start.5 = (bf16[336,128]{1,0:T(8,128)(2,1)S(1)}, bf16[336,128]{1,0:T(8,128)(2,1)S(1)}, u32[]{:S(2)}, u32[]{:S(2)}) collective-permute-start(bf16[336,128]{1,0:T(8,128)(2,1)S(1)} %get-tuple-element.55), channel_id=1, source_target_pairs={{0,4},{8,12},{4,0},{12,8},{1,5},{9,13},{5,1},{13,9},{2,6},{10,14},... | collective-permute-start | bytes 258056 | tf_op jit(solution)/shard_map/ppermute | solution.py:58
  25.6 5.8 %collective-permute-start.6 = (bf16[336,128]{1,0:T(8,128)(2,1)S(1)}, bf16[336,128]{1,0:T(8,128)(2,1)S(1)}, u32[]{:S(2)}, u32[]{:S(2)}) collective-permute-start(bf16[336,128]{1,0:T(8,128)(2,1)S(1)} %get-tuple-element.56), channel_id=1, source_target_pairs={{4,8},{8,4},{5,9},{9,5},{6,10},{10,6},{7,11},{11,7},{20,24},{24,20... | collective-permute-start | bytes 258056 | tf_op jit(solution)/shard_map/ppermute | solution.py:58
  26.8 6.3 %collective-permute-start.13 = (bf16[336,128]{1,0:T(8,128)(2,1)S(1)}, bf16[336,128]{1,0:T(8,128)(2,1)S(1)}, u32[]{:S(2)}, u32[]{:S(2)}) collective-permute-start(bf16[336,128]{1,0:T(8,128)(2,1)S(1)} %get-tuple-element.67), channel_id=1, source_target_pairs={{0,4},{8,12},{4,0},{12,8},{1,5},{9,13},{5,1},{13,9},{2,6},{10,14},... | collective-permute-start | bytes 258056 | tf_op jit(solution)/shard_map/ppermute | solution.py:58
  29.8 3.2 %collective-permute-start.14 = (bf16[336,128]{1,0:T(8,128)(2,1)S(1)}, bf16[336,128]{1,0:T(8,128)(2,1)S(1)}, u32[]{:S(2)}, u32[]{:S(2)}) collective-permute-start(bf16[336,128]{1,0:T(8,128)(2,1)S(1)} %get-tuple-element.68), channel_id=1, source_target_pairs={{4,8},{8,4},{5,9},{9,5},{6,10},{10,6},{7,11},{11,7},{20,24},{24,20... | collective-permute-start | bytes 258056 | tf_op jit(solution)/shard_map/ppermute | solution.py:58
  31.9 4.2 %collective-permute-start.7 = (bf16[128,512]{1,0:T(8,128)(2,1)S(1)}, bf16[128,512]{1,0:T(8,128)(2,1)S(1)}, u32[]{:S(2)}, u32[]{:S(2)}) collective-permute-start(bf16[128,512]{1,0:T(8,128)(2,1)S(1)} %get-tuple-element.59.after_ref), channel_id=1, source_target_pairs={{0,1},{1,0},{2,3},{3,2},{4,5},{5,4},{6,7},{7,6},{8,9},{9,8},{10,11... | collective-permute-start | bytes 393224 | tf_op jit(solution)/shard_map/ppermute | solution.py:431
  33.9 3.8 %collective-permute-start.15 = (bf16[128,512]{1,0:T(8,128)(2,1)S(1)}, bf16[128,512]{1,0:T(8,128)(2,1)S(1)}, u32[]{:S(2)}, u32[]{:S(2)}) collective-permute-start(bf16[128,512]{1,0:T(8,128)(2,1)S(1)} %get-tuple-element.70), channel_id=1, source_target_pairs={{0,1},{1,0},{2,3},{3,2},{4,5},{5,4},{6,7},{7,6},{8,9},{9,8},{10,11... | collective-permute-start | bytes 393224 | tf_op jit(solution)/shard_map/ppermute | solution.py:431
  34.9 8.3 %collective-permute-start.17 = (bf16[336,256]{1,0:T(8,128)(2,1)S(1)}, bf16[336,256]{1,0:T(8,128)(2,1)S(1)}, u32[]{:S(2)}, u32[]{:S(2)}) collective-permute-start(bf16[336,256]{1,0:T(8,128)(2,1)S(1)} %shard_map.209), channel_id=1, source_target_pairs={{0,12},{4,8},{8,4},{12,0},{1,13},{5,9},{9,5},{13,1},{2,14},{6,10},... | collective-permute-start | bytes 516104 | tf_op jit(solution)/shard_map/ppermute | solution.py:63
  36.2 6.5 %collective-permute-start.8 = (bf16[128,512]{1,0:T(8,128)(2,1)S(1)}, bf16[128,512]{1,0:T(8,128)(2,1)S(1)}, u32[]{:S(2)}, u32[]{:S(2)}) collective-permute-start(bf16[128,512]{1,0:T(8,128)(2,1)S(1)} %get-tuple-element.90), channel_id=1, source_target_pairs={{0,2},{2,0},{1,3},{3,1},{4,6},{6,4},{5,7},{7,5},{8,10},{10,8},{9,1... | collective-permute-start | bytes 393224 | tf_op jit(solution)/shard_map/ppermute | solution.py:63
  37.8 6.4 %collective-permute-start.16 = (bf16[128,512]{1,0:T(8,128)(2,1)S(1)}, bf16[128,512]{1,0:T(8,128)(2,1)S(1)}, u32[]{:S(2)}, u32[]{:S(2)}) collective-permute-start(bf16[128,512]{1,0:T(8,128)(2,1)S(1)} %get-tuple-element.86), channel_id=1, source_target_pairs={{0,2},{2,0},{1,3},{3,1},{4,6},{6,4},{5,7},{7,5},{8,10},{10,8},{9,1... | collective-permute-start | bytes 393224 | tf_op jit(solution)/shard_map/ppermute | solution.py:63
  42.7 4.5 %collective-permute-start.9 = (bf16[128,512]{1,0:T(8,128)(2,1)S(1)}, bf16[128,512]{1,0:T(8,128)(2,1)S(1)}, u32[]{:S(2)}, u32[]{:S(2)}) collective-permute-start(bf16[128,512]{1,0:T(8,128)(2,1)S(1)} %shard_map.202.mine_ref.grid_ref), channel_id=1, source_target_pairs={{0,1},{1,0},{2,3},{3,2},{4,5},{5,4},{6,7},{7,6},{8,9},{9,8},{10,11... | collective-permute-start | bytes 393224 | tf_op jit(solution)/shard_map/ppermute | solution.py:431
  44.4 3.0 %collective-permute-start.19 = (bf16[128,512]{1,0:T(8,128)(2,1)S(1)}, bf16[128,512]{1,0:T(8,128)(2,1)S(1)}, u32[]{:S(2)}, u32[]{:S(2)}) collective-permute-start(bf16[128,512]{1,0:T(8,128)(2,1)S(1)} %get-tuple-element.75.mine_ref), channel_id=1, source_target_pairs={{0,1},{1,0},{2,3},{3,2},{4,5},{5,4},{6,7},{7,6},{8,9},{9,8},{10,11... | collective-permute-start | bytes 393224 | tf_op jit(solution)/shard_map/ppermute | solution.py:431
  44.5 6.4 %collective-permute-start.18 = (bf16[128,256]{1,0:T(8,128)(2,1)S(1)}, bf16[128,256]{1,0:T(8,128)(2,1)S(1)}, u32[]{:S(2)}, u32[]{:S(2)}) collective-permute-start(bf16[128,256]{1,0:T(8,128)(2,1)S(1)} %get-tuple-element.74), channel_id=1, source_target_pairs={{0,12},{4,8},{8,4},{12,0},{1,13},{5,9},{9,5},{13,1},{2,14},{6,10},... | collective-permute-start | bytes 196616 | tf_op jit(solution)/shard_map/ppermute | solution.py:63
  48.3 11.3 %collective-permute-start.21 = (bf16[336,256]{1,0:T(8,128)(2,1)S(1)}, bf16[336,256]{1,0:T(8,128)(2,1)S(1)}, u32[]{:S(2)}, u32[]{:S(2)}) collective-permute-start(bf16[336,256]{1,0:T(8,128)(2,1)S(1)} %get-tuple-element.81), channel_id=1, source_target_pairs={{0,8},{4,12},{8,0},{12,4},{1,9},{5,13},{9,1},{13,5},{2,10},{6,14},... | collective-permute-start | bytes 516104 | tf_op jit(solution)/shard_map/ppermute | solution.py:63
  50.4 9.2 %collective-permute-start.22 = (bf16[336,256]{1,0:T(8,128)(2,1)S(1)}, bf16[336,256]{1,0:T(8,128)(2,1)S(1)}, u32[]{:S(2)}, u32[]{:S(2)}) collective-permute-start(bf16[336,256]{1,0:T(8,128)(2,1)S(1)} %get-tuple-element.82), channel_id=1, source_target_pairs={{0,4},{4,0},{8,12},{12,8},{1,5},{5,1},{9,13},{13,9},{2,6},{6,2},{1... | collective-permute-start | bytes 516104 | tf_op jit(solution)/shard_map/ppermute | solution.py:63
  50.9 1.3 %collective-permute-start.20 = (bf16[128,256]{1,0:T(8,128)(2,1)S(1)}, bf16[128,256]{1,0:T(8,128)(2,1)S(1)}, u32[]{:S(2)}, u32[]{:S(2)}) collective-permute-start(bf16[128,256]{1,0:T(8,128)(2,1)S(1)} %collective-permute-done.18.mine_ref), channel_id=1, source_target_pairs={{0,1},{1,0},{2,3},{3,2},{4,5},{5,4},{6,7},{7,6},{8,9},{9,8},{10,11... | collective-permute-start | bytes 196616 | tf_op jit(solution)/shard_map/ppermute | solution.py:431

commit v7 on v6

--- a/solution.py
+++ b/solution.py
@@ -67,18 +67,6 @@
     return lax.rem(lax.axis_index("sp"), 2) == 0
 
 
-def messages(mesh, low_row, high_row, halo_ref, even_ref, odd_ref):
-    even = on_even()
-    nodes = mesh.shape[1]
-    cols = low_row.shape[1]
-    to_lower = dot(mesh, one_hot(halo_ref[0:1, :], nodes)).astype(BF16)
-    to_upper = dot(mesh, one_hot(halo_ref[1:2, :], nodes)).astype(BF16)
-    even_ref[:, :cols] = jnp.where(even, high_row, low_row)
-    odd_ref[:, :cols] = jnp.where(even, low_row, high_row)
-    even_ref[:, cols:] = jnp.where(even, to_upper, to_lower)
-    odd_ref[:, cols:] = jnp.where(even, to_lower, to_upper)
-
-
 def pack_rows(source_ref, packed_ref, at):
     freqs, dirs, width = source_ref.shape
     for f in range(freqs):
@@ -89,8 +77,8 @@
 
 
 def begin_kernel(
-    grid_hbm, mesh_hbm, halo_hbm, even_ref, odd_ref, grid_ref, mesh_ref, halo_ref, packed_ref, sem,
-    *, rows,
+    grid_hbm, mesh_hbm, halo_hbm, even_ref, odd_ref, grid_ref, mesh_ref, halo_ref, packed_ref,
+    pick_ref, sem, *, rows,
 ):
     copies = [
         pltpu.make_async_copy(halo_hbm, halo_ref, sem.at[0]),
@@ -99,17 +87,25 @@
     ]
     for copy in copies:
         copy.start()
+    even = on_even()
     bands = grid_ref.shape[0] // rows
-    blank = jnp.zeros((packed_ref.shape[0] - bands, grid_ref.shape[1]), F32)
+    cols = grid_ref.shape[1]
+    listed = halo_ref.shape[1]
     copies[0].wait()
+    lower, upper = halo_ref[0:1, :], halo_ref[1:2, :]
+    pick_ref[:, :listed] = one_hot(jnp.where(even, upper, lower), pick_ref.shape[0])
+    pick_ref[:, listed:] = one_hot(jnp.where(even, lower, upper), pick_ref.shape[0])
     copies[1].wait()
     pack_rows(mesh_ref, packed_ref, 0)
+    picked = dot(packed_ref[...].astype(BF16), pick_ref[...]).astype(BF16)
+    even_ref[:, cols:] = picked[:, :listed]
+    odd_ref[:, cols:] = picked[:, listed:]
     copies[2].wait()
+    blank = jnp.zeros((packed_ref.shape[0] - bands, cols), F32)
     low = jnp.concatenate([grid_ref[pl.ds(0, bands, stride=rows), :], blank], axis=0)
     high = jnp.concatenate([grid_ref[pl.ds(rows - 1, bands, stride=rows), :], blank], axis=0)
-    messages(
-        packed_ref[...].astype(BF16), low.astype(BF16), high.astype(BF16), halo_ref, even_ref, odd_ref
-    )
+    even_ref[:, :cols] = jnp.where(even, high, low).astype(BF16)
+    odd_ref[:, :cols] = jnp.where(even, low, high).astype(BF16)
 
 
 def own_grid(state_ref, band_ref, sea_ref, speed_ref, part_ref):
@@ -316,9 +312,9 @@
                 total = total + scaled
             mix_ref[:, p * cap : (p + 1) * cap] = mix.astype(BF16)
             sums_ref[kind : kind + 1, p * cap : (p + 1) * cap] = total
-            land_ref[:, p * cap : (p + 1) * cap] = one_hot(
-                target_ref[0, pl.ds(peer, 1), :], land_ref.shape[0]
-            )
+            hit = lax.broadcasted_iota(jnp.int32, (land_ref.shape[1], cap), 0)
+            hit = jnp.where(hit == target_ref[0, pl.ds(peer, 1), :], 1.0, 0.0)
+            land_ref[p * cap : (p + 1) * cap, :] = hit.T.astype(BF16)
 
 
 def slot_values(source_refs, mix_refs, sums_ref, p, cap, bands, out_ref):
@@ -370,12 +366,6 @@
     half = mine_ref.shape[0]
     moved = dot(wout_ref[:, :half], mine_ref[...]) + dot(wout_ref[:, half:], other_ref[...])
     out_ref[...] = (early_ref[...].astype(F32) + DT_STEP * moved).astype(BF16)
-
-
-def land(values, land_ref):
-    return lax.dot_general(
-        values, land_ref[...], (((1,), (1,)), ((), ())), preferred_element_type=F32
-    )
 
 
 def end_kernel(gstate_ref, mstate_ref, gland_ref, mland_ref, sea_ref, *rest, bands):
@@ -388,16 +378,16 @@
     for kind in (0, 1):
         for p, got in enumerate(got_refs):
             values_ref[kind, :, p * cap : (p + 1) * cap] = got[:, kind * cap : (kind + 1) * cap]
-    sum_ref[:, gp:] = land(values_ref[0], gland_ref)
+    sum_ref[:, gp:] = dot(values_ref[0], gland_ref[...])
     cover = sum_ref[bands : bands + 1, gp:]
     rate = BLEND_RATE / (1.0 + cover)
     keep = 1.0 - rate * cover
+    sum_ref[:, gp:] = keep * mstate_ref[...] + rate * sum_ref[:, gp:]
     for f in range(freqs):
-        here = slice(f * dirs, (f + 1) * dirs)
-        mesh_ref[f] = keep * mstate_ref[here, :] + rate * sum_ref[here, gp:]
+        mesh_ref[f] = sum_ref[f * dirs : (f + 1) * dirs, gp:]
     mesh_copy = pltpu.make_async_copy(mesh_ref, mesh_hbm, sem.at[0])
     mesh_copy.start()
-    sum_ref[:, :gp] = land(values_ref[1], mland_ref)
+    sum_ref[:, :gp] = dot(values_ref[1], mland_ref[...])
     cover = sum_ref[bands : bands + 1, :gp]
     rate = BLEND_RATE / (1.0 + cover)
     keep = 1.0 - rate * cover
@@ -461,6 +451,7 @@
             (mesh_spec.shape, F32),
             (halo_list.shape, jnp.int32),
             mesh_shape,
+            ((nodes, 2 * listed), BF16),
             pltpu.SemaphoreType.DMA((3,)),
         ],
         1.8,
@@ -540,8 +531,8 @@
                     ((gp, peers * cap), BF16),
                     ((nodes, peers * cap), BF16),
                     ((2, peers * cap), F32),
-                    ((nodes, peers * cap), BF16),
-                    ((gp, peers * cap), BF16),
+                    ((peers * cap, nodes), BF16),
+                    ((peers * cap, gp), BF16),
                 ],
                 (),
                 0.5,

time: 61.8 us -> 61.5 us (level)
  no operation moved by 1% of the time
where the time goes in v7:
time: 61.5 us; the launch traced here: 61.3 us
  starting transfers between devices  25.5 us (41%)
  waiting for transfers between devices  18.1 us (29%)
  Pallas kernels  16.2 us (26%)
  between operations  1.27 us (2%)
    ppermute x8, waiting for transfers between devices, peer_swap(): return lax.ppermute(array, axis, [(i, i ^ step) for i in range(size)])  16.7 us
    pallas_call x20, Pallas kernels, run(): pl.pallas_call(body, out_shape=[jax.ShapeDtypeStruct(s, t) for s, t in ou...  16.2 us
    ppermute x6, starting transfers between devices, pair_swap(): return lax.ppermute(array, axis, pairs + [(j, i) for i, j in pairs])  13.1 us
    ppermute x8, starting transfers between devices, peer_swap(): return lax.ppermute(array, axis, [(i, i ^ step) for i in range(size)])  10.8 us
    ppermute x9, starting transfers between devices, core_swap(): return lax.ppermute(array, 'dr', [(0, 1), (1, 0)])  1.53 us
    ppermute x9, waiting for transfers between devices, core_swap(): return lax.ppermute(array, 'dr', [(0, 1), (1, 0)])  1.27 us
  transfers between devices with their start and end apart: 23, of which 9 were waited for; matrix products, arithmetic and copies ran while one was open for 0% of the time, Pallas kernels for 20%

profile of v7, /device:TPU:0, one launch (start us, length us, event | category | flops | bytes accessed | tf_op | source)
XLA Modules:
  0.0 61.3 jit_solution(2657341026155479804)
XLA Ops:
  0.7 1.5 %shard_map.195 = (bf16[336,256]{1,0:T(8,128)(2,1)S(1)}, bf16[336,256]{1,0:T(8,128)(2,1)S(1)}) custom-call(f32[1296,128]{1,0:T(8,128)} %bitcast.3, f32[18,18,512]{2,1,0:T(8,128)} %mesh_hbm.3, s32[2,128]{1,0:T(2,128)} %halo_ref.1), custom_call_target="tpu_custom_call" | custom-call | flops 2070000000 | tf_op jit(solution)/shard_map/pallas_call | solution.py:31
  2.2 3.1 %collective-permute-start = (bf16[336,256]{1,0:T(8,128)(2,1)S(1)}, bf16[336,256]{1,0:T(8,128)(2,1)S(1)}, u32[]{:S(2)}, u32[]{:S(2)}) collective-permute-start(bf16[336,256]{1,0:T(8,128)(2,1)S(1)} %get-tuple-element.45), channel_id=1, source_target_pairs={{0,4},{8,12},{4,0},{12,8},{1,5},{9,13},{5,1},{13,9},{2,6},{10,14},... | collective-permute-start | bytes 516104 | tf_op jit(solution)/shard_map/ppermute | solution.py:58
  5.3 0.7 %collective-permute-start.1 = (bf16[336,256]{1,0:T(8,128)(2,1)S(1)}, bf16[336,256]{1,0:T(8,128)(2,1)S(1)}, u32[]{:S(2)}, u32[]{:S(2)}) collective-permute-start(bf16[336,256]{1,0:T(8,128)(2,1)S(1)} %get-tuple-element.46), channel_id=1, source_target_pairs={{4,8},{8,4},{5,9},{9,5},{6,10},{10,6},{7,11},{11,7},{20,24},{24,20... | collective-permute-start | bytes 516104 | tf_op jit(solution)/shard_map/ppermute | solution.py:58
  6.0 0.1 cosine_multiply_fusion
  6.1 3.4 %shard_map.194 = (f32[336,512]{1,0:T(8,128)S(1)}, f32[336,512]{1,0:T(8,128)S(1)}, bf16[4,768,512]{2,1,0:T(8,128)(2,1)S(1)}, f32[4,336,512]{2,1,0:T(8,128)S(1)}, ...) custom-call(f32[1296,128]{1,0:T(8,128)} %bitcast.4, f32[18,18,512]{2,1,0:T(8,128)} %mesh_hbm.3, ...), custom_call_target="tpu_custom_call" | custom-call | flops 3910000128 | tf_op jit(solution)/shard_map/pallas_call | solution.py:31
  9.6 0.1 collective-permute-done.even_ref
  9.7 0.0 collective-permute-done.1.odd_ref
  9.7 0.4 shard_map.196
  10.1 0.1 collective-permute-start.2
  10.2 0.0 copy-start.1
  10.2 0.0 copy-start.2
  10.3 0.0 copy-start.3
  10.3 0.0 copy-start.4
  10.3 0.0 copy-start.5
  10.3 0.0 copy-start.6
  10.3 0.0 copy-start.10
  10.3 0.0 copy-start.11
  10.3 0.8 %shard_map.204 = (f32[336,512]{1,0:T(8,128)S(1)}, f32[128,512]{1,0:T(8,128)S(1)}, bf16[128,512]{1,0:T(8,128)(2,1)S(1)}) custom-call(f32[336,512]{1,0:T(8,128)S(1)} %get-tuple-element.60.part_ref, bf16[336,256]{1,0:T(8,128)(2,1)S(1)} %collective-permute-done.even_ref, bf16[336,256]{1,0:T(8,128)(2,1)S(1)} %collective-permute-done.1.odd_ref, ...), custom_call_target="tpu_custom_call" | custom-call | flops 920000000 | tf_op jit(solution)/shard_map/pallas_call | solution.py:31
  11.2 0.5 collective-permute-start.10
  11.7 0.0 collective-permute-done.2
  11.7 1.7 %collective-permute-start.3 = (bf16[128,512]{1,0:T(8,128)(2,1)S(1)}, bf16[128,512]{1,0:T(8,128)(2,1)S(1)}, u32[]{:S(2)}, u32[]{:S(2)}) collective-permute-start(bf16[128,512]{1,0:T(8,128)(2,1)S(1)} %get-tuple-element.92.after_ref), channel_id=1, source_target_pairs={{0,2},{2,0},{1,3},{3,1},{4,6},{6,4},{5,7},{7,5},{8,10},{10,8},{9,1... | collective-permute-start | bytes 393224 | tf_op jit(solution)/shard_map/ppermute | solution.py:63
  13.4 0.0 collective-permute-done.10
  13.5 0.9 %collective-permute-start.11 = (bf16[128,512]{1,0:T(8,128)(2,1)S(1)}, bf16[128,512]{1,0:T(8,128)(2,1)S(1)}, u32[]{:S(2)}, u32[]{:S(2)}) collective-permute-start(bf16[128,512]{1,0:T(8,128)(2,1)S(1)} %get-tuple-element.88), channel_id=1, source_target_pairs={{0,2},{2,0},{1,3},{3,1},{4,6},{6,4},{5,7},{7,5},{8,10},{10,8},{9,1... | collective-permute-start | bytes 393224 | tf_op jit(solution)/shard_map/ppermute | solution.py:63
  14.5 2.1 %shard_map.197 = (bf16[512,512]{1,0:T(8,128)(2,1)S(1)}, bf16[512,512]{1,0:T(8,128)(2,1)S(1)}, f32[2,512]{1,0:T(2,128)S(1)}, bf16[512,512]{1,0:T(8,128)(2,1)S(1)}, bf16[512,512]{1,0:T(8,128)(2,1)S(1)}) custom-call(s32[4,1,4,128]{3,2,1,0:T(4,128)S(1)} %copy-done.1, f32[4,1,4,128]{3,2,1,0:T(4,128)S(1)} %copy-done.2, s32[1,4]{1,0:T(1,128)S(1)} %copy-done.10, ...), custom_call_target="tpu_custom_call" | custom-call | flops 575000000 | tf_op jit(solution)/shard_map/pallas_call | solution.py:31
  16.6 1.5 %collective-permute-done.3.got_ref = bf16[128,512]{1,0:T(8,128)(2,1)S(1)} collective-permute-done((bf16[128,512]{1,0:T(8,128)(2,1)S(1)}, bf16[128,512]{1,0:T(8,128)(2,1)S(1)}, u32[]{:S(2)}, u32[]{:S(2)}) %collective-permute-start.3) | collective-permute-done | bytes 131104 | tf_op jit(solution)/shard_map/ppermute | solution.py:63
  18.2 0.1 shard_map.198.mine_ref
  18.2 0.1 collective-permute-start.4
  18.3 1.7 %collective-permute-done.11.got_ref = bf16[128,512]{1,0:T(8,128)(2,1)S(1)} collective-permute-done((bf16[128,512]{1,0:T(8,128)(2,1)S(1)}, bf16[128,512]{1,0:T(8,128)(2,1)S(1)}, u32[]{:S(2)}, u32[]{:S(2)}) %collective-permute-start.11) | collective-permute-done | bytes 131104 | tf_op jit(solution)/shard_map/ppermute | solution.py:63
  20.1 0.1 shard_map.205.mine_ref
  20.1 0.1 collective-permute-start.12
  20.2 0.3 shard_map.199
  20.5 4.8 %collective-permute-start.5 = (bf16[336,128]{1,0:T(8,128)(2,1)S(1)}, bf16[336,128]{1,0:T(8,128)(2,1)S(1)}, u32[]{:S(2)}, u32[]{:S(2)}) collective-permute-start(bf16[336,128]{1,0:T(8,128)(2,1)S(1)} %get-tuple-element.55), channel_id=1, source_target_pairs={{0,4},{8,12},{4,0},{12,8},{1,5},{9,13},{5,1},{13,9},{2,6},{10,14},... | collective-permute-start | bytes 258056 | tf_op jit(solution)/shard_map/ppermute | solution.py:58
  25.3 0.7 %collective-permute-start.6 = (bf16[336,128]{1,0:T(8,128)(2,1)S(1)}, bf16[336,128]{1,0:T(8,128)(2,1)S(1)}, u32[]{:S(2)}, u32[]{:S(2)}) collective-permute-start(bf16[336,128]{1,0:T(8,128)(2,1)S(1)} %get-tuple-element.56), channel_id=1, source_target_pairs={{4,8},{8,4},{5,9},{9,5},{6,10},{10,6},{7,11},{11,7},{20,24},{24,20... | collective-permute-start | bytes 258056 | tf_op jit(solution)/shard_map/ppermute | solution.py:58
  26.0 0.5 shard_map.206
  26.5 3.1 %collective-permute-start.13 = (bf16[336,128]{1,0:T(8,128)(2,1)S(1)}, bf16[336,128]{1,0:T(8,128)(2,1)S(1)}, u32[]{:S(2)}, u32[]{:S(2)}) collective-permute-start(bf16[336,128]{1,0:T(8,128)(2,1)S(1)} %get-tuple-element.67), channel_id=1, source_target_pairs={{0,4},{8,12},{4,0},{12,8},{1,5},{9,13},{5,1},{13,9},{2,6},{10,14},... | collective-permute-start | bytes 258056 | tf_op jit(solution)/shard_map/ppermute | solution.py:58
  29.6 0.8 %collective-permute-start.14 = (bf16[336,128]{1,0:T(8,128)(2,1)S(1)}, bf16[336,128]{1,0:T(8,128)(2,1)S(1)}, u32[]{:S(2)}, u32[]{:S(2)}) collective-permute-start(bf16[336,128]{1,0:T(8,128)(2,1)S(1)} %get-tuple-element.68), channel_id=1, source_target_pairs={{4,8},{8,4},{5,9},{9,5},{6,10},{10,6},{7,11},{11,7},{20,24},{24,20... | collective-permute-start | bytes 258056 | tf_op jit(solution)/shard_map/ppermute | solution.py:58
  30.4 0.7 %shard_map.200.part_ref = f32[336,512]{1,0:T(8,128)S(1)} custom-call(f32[336,512]{1,0:T(8,128)S(1)} %get-tuple-element.54.state_ref, f32[336,2]{1,0:T(8,128)S(1)} %get-tuple-element.47.band_ref, s32[4,128]{1,0:T(4,128)S(1)} %copy-done.8, f32[4,128]{1,0:T(4,128)S(1)} %copy-done.7), custom_call_target="tpu_custom_call" | custom-call | flops 575000000 | tf_op jit(solution)/shard_map/pallas_call | solution.py:31
  31.2 0.4 shard_map.201
  31.6 0.1 collective-permute-start.7
  31.7 1.1 %shard_map.207.part_ref = f32[336,512]{1,0:T(8,128)S(1)} custom-call(f32[336,512]{1,0:T(8,128)S(1)} %get-tuple-element.66.state_ref, bf16[4,768,512]{2,1,0:T(8,128)(2,1)S(1)} %get-tuple-element.61.hot_ref, f32[4,336,512]{2,1,0:T(8,128)S(1)} %get-tuple-element.62.weight_ref), custom_call_target="tpu_custom_call" | custom-call | flops 1150000000 | tf_op jit(solution)/shard_map/pallas_call | solution.py:31
  32.8 0.0 collective-permute-done.13.even_ref
  32.8 0.0 collective-permute-done.14.odd_ref
  32.8 0.8 %shard_map.208 = (f32[336,512]{1,0:T(8,128)S(1)}, f32[128,512]{1,0:T(8,128)S(1)}, bf16[128,512]{1,0:T(8,128)(2,1)S(1)}) custom-call(f32[336,512]{1,0:T(8,128)S(1)} %shard_map.207.part_ref, bf16[336,128]{1,0:T(8,128)(2,1)S(1)} %collective-permute-done.13.even_ref, bf16[336,128]{1,0:T(8,128)(2,1)S(1)} %collective-permute-done.14.odd_ref, ...), custom_call_target="tpu_custom_call" | custom-call | flops 920000000 | tf_op jit(solution)/shard_map/pallas_call | solution.py:31
  33.6 0.6 collective-permute-start.15
  34.2 0.4 shard_map.209
  34.6 1.2 %collective-permute-start.17 = (bf16[336,256]{1,0:T(8,128)(2,1)S(1)}, bf16[336,256]{1,0:T(8,128)(2,1)S(1)}, u32[]{:S(2)}, u32[]{:S(2)}) collective-permute-start(bf16[336,256]{1,0:T(8,128)(2,1)S(1)} %shard_map.209), channel_id=1, source_target_pairs={{0,12},{4,8},{8,4},{12,0},{1,13},{5,9},{9,5},{13,1},{2,14},{6,10},... | collective-permute-start | bytes 516104 | tf_op jit(solution)/shard_map/ppermute | solution.py:63
  35.9 1.6 %collective-permute-start.8 = (bf16[128,512]{1,0:T(8,128)(2,1)S(1)}, bf16[128,512]{1,0:T(8,128)(2,1)S(1)}, u32[]{:S(2)}, u32[]{:S(2)}) collective-permute-start(bf16[128,512]{1,0:T(8,128)(2,1)S(1)} %get-tuple-element.90), channel_id=1, source_target_pairs={{0,2},{2,0},{1,3},{3,1},{4,6},{6,4},{5,7},{7,5},{8,10},{10,8},{9,1... | collective-permute-start | bytes 393224 | tf_op jit(solution)/shard_map/ppermute | solution.py:63
  37.5 0.6 collective-permute-start.16
  38.1 4.3 %collective-permute-done.8.got_ref = bf16[128,512]{1,0:T(8,128)(2,1)S(1)} collective-permute-done((bf16[128,512]{1,0:T(8,128)(2,1)S(1)}, bf16[128,512]{1,0:T(8,128)(2,1)S(1)}, u32[]{:S(2)}, u32[]{:S(2)}) %collective-permute-start.8) | collective-permute-done | bytes 131104 | tf_op jit(solution)/shard_map/ppermute | solution.py:63
  42.3 0.1 shard_map.202.mine_ref.grid_ref
  42.4 0.1 collective-permute-start.9
  42.5 0.3 collective-permute-done.17.after_ref.early_ref
  42.9 1.0 %collective-permute-done.16.got_ref = bf16[128,512]{1,0:T(8,128)(2,1)S(1)} collective-permute-done((bf16[128,512]{1,0:T(8,128)(2,1)S(1)}, bf16[128,512]{1,0:T(8,128)(2,1)S(1)}, u32[]{:S(2)}, u32[]{:S(2)}) %collective-permute-start.16) | collective-permute-done | bytes 131104 | tf_op jit(solution)/shard_map/ppermute | solution.py:63
  43.9 0.3 shard_map.210
  44.2 0.1 collective-permute-start.19
  44.2 2.7 %collective-permute-start.18 = (bf16[128,256]{1,0:T(8,128)(2,1)S(1)}, bf16[128,256]{1,0:T(8,128)(2,1)S(1)}, u32[]{:S(2)}, u32[]{:S(2)}) collective-permute-start(bf16[128,256]{1,0:T(8,128)(2,1)S(1)} %get-tuple-element.74), channel_id=1, source_target_pairs={{0,12},{4,8},{8,4},{12,0},{1,13},{5,9},{9,5},{13,1},{2,14},{6,10},... | collective-permute-start | bytes 196616 | tf_op jit(solution)/shard_map/ppermute | solution.py:63
  47.0 0.2 shard_map.203.grid_ref.gstate_ref
  47.2 0.9 %shard_map.211 = (f32[336,512]{1,0:T(8,128)S(1)}, bf16[336,256]{1,0:T(8,128)(2,1)S(1)}, bf16[336,256]{1,0:T(8,128)(2,1)S(1)}, bf16[336,256]{1,0:T(8,128)(2,1)S(1)}) custom-call(f32[336,512]{1,0:T(8,128)S(1)} %shard_map.203.grid_ref.gstate_ref, f32[336,512]{1,0:T(8,128)S(1)} %get-tuple-element.73.mesh_ref.moved_ref, ...), custom_call_target="tpu_custom_call" | custom-call | flops 920000000 | tf_op jit(solution)/shard_map/pallas_call | solution.py:31
  48.1 2.0 %collective-permute-start.21 = (bf16[336,256]{1,0:T(8,128)(2,1)S(1)}, bf16[336,256]{1,0:T(8,128)(2,1)S(1)}, u32[]{:S(2)}, u32[]{:S(2)}) collective-permute-start(bf16[336,256]{1,0:T(8,128)(2,1)S(1)} %get-tuple-element.81), channel_id=1, source_target_pairs={{0,8},{4,12},{8,0},{12,4},{1,9},{5,13},{9,1},{13,5},{2,10},{6,14},... | collective-permute-start | bytes 516104 | tf_op jit(solution)/shard_map/ppermute | solution.py:63
  50.1 0.5 collective-permute-done.18.mine_ref
  50.6 1.3 %collective-permute-done.20.other_ref = bf16[128,256]{1,0:T(8,128)(2,1)S(1)} collective-permute-done((bf16[128,256]{1,0:T(8,128)(2,1)S(1)}, bf16[128,256]{1,0:T(8,128)(2,1)S(1)}, u32[]{:S(2)}, u32[]{:S(2)}) %collective-permute-start.20) | collective-permute-done | bytes 65568 | tf_op jit(solution)/shard_map/ppermute | solution.py:421
  51.9 0.2 shard_map.212.rest_0_
  52.1 7.2 %collective-permute-done.21.rest_1_ = bf16[336,256]{1,0:T(8,128)(2,1)S(1)} collective-permute-done((bf16[336,256]{1,0:T(8,128)(2,1)S(1)}, bf16[336,256]{1,0:T(8,128)(2,1)S(1)}, u32[]{:S(2)}, u32[]{:S(2)}) %collective-permute-start.21) | collective-permute-done | bytes 172064 | tf_op jit(solution)/shard_map/ppermute | solution.py:63
  59.3 1.8 %shard_map.213 = (f32[1296,128]{1,0:T(8,128)}, f32[18,18,512]{2,1,0:T(8,128)}) custom-call(f32[336,512]{1,0:T(8,128)S(1)} %shard_map.203.grid_ref.gstate_ref, f32[336,512]{1,0:T(8,128)S(1)} %get-tuple-element.77.mstate_ref, bf16[512,512]{1,0:T(8,128)(2,1)S(1)} %get-tuple-element.78.gland_ref, bf16[512,512]{1,0:T(8,128)(2,1)S(1)} %get-tuple-element.79.mland_ref, ...), custom_call_target="tpu_custom_call" | custom-call | flops 2184999936 | tf_op jit(solution)/shard_map/pallas_call | solution.py:31
  (36 shorter events, 0.2 us)
Async XLA Ops:
  0.6 5.4 %copy-start.12 = (f32[4,512]{1,0:T(4,128)S(1)}, f32[4,512]{1,0:T(4,128)}, u32[]{:S(2)}) copy-start(f32[4,512]{1,0:T(4,128)} %param.24) | copy-start | bytes 24580
  0.6 5.4 %copy-start.13 = (f32[4,512]{1,0:T(4,128)S(1)}, f32[4,512]{1,0:T(4,128)}, u32[]{:S(2)}) copy-start(f32[4,512]{1,0:T(4,128)} %param.25) | copy-start | bytes 24580
  0.7 5.5 %copy-start = (s32[4,512]{1,0:T(4,128)S(1)}, s32[4,512]{1,0:T(4,128)}, u32[]{:S(2)}) copy-start(s32[4,512]{1,0:T(4,128)} %index_ref.1) | copy-start | bytes 24580
  0.7 5.5 %copy-start.7 = (f32[4,128]{1,0:T(4,128)S(1)}, f32[4,128]{1,0:T(4,128)}, u32[]{:S(2)}) copy-start(f32[4,128]{1,0:T(4,128)} %speed_ref.7) | copy-start | bytes 6148
  0.7 5.5 %copy-start.8 = (s32[4,128]{1,0:T(4,128)S(1)}, s32[4,128]{1,0:T(4,128)}, u32[]{:S(2)}) copy-start(s32[4,128]{1,0:T(4,128)} %sea_ref.9) | copy-start | bytes 6148
  2.2 7.5 %collective-permute-start = (bf16[336,256]{1,0:T(8,128)(2,1)S(1)}, bf16[336,256]{1,0:T(8,128)(2,1)S(1)}, u32[]{:S(2)}, u32[]{:S(2)}) collective-permute-start(bf16[336,256]{1,0:T(8,128)(2,1)S(1)} %get-tuple-element.45), channel_id=1, source_target_pairs={{0,4},{8,12},{4,0},{12,8},{1,5},{9,13},{5,1},{13,9},{2,6},{10,14},... | collective-permute-start | bytes 516104 | tf_op jit(solution)/shard_map/ppermute | solution.py:58
  5.3 4.4 %collective-permute-start.1 = (bf16[336,256]{1,0:T(8,128)(2,1)S(1)}, bf16[336,256]{1,0:T(8,128)(2,1)S(1)}, u32[]{:S(2)}, u32[]{:S(2)}) collective-permute-start(bf16[336,256]{1,0:T(8,128)(2,1)S(1)} %get-tuple-element.46), channel_id=1, source_target_pairs={{4,8},{8,4},{5,9},{9,5},{6,10},{10,6},{7,11},{11,7},{20,24},{24,20... | collective-permute-start | bytes 516104 | tf_op jit(solution)/shard_map/ppermute | solution.py:58
  10.1 1.5 %collective-permute-start.2 = (bf16[128,512]{1,0:T(8,128)(2,1)S(1)}, bf16[128,512]{1,0:T(8,128)(2,1)S(1)}, u32[]{:S(2)}, u32[]{:S(2)}) collective-permute-start(bf16[128,512]{1,0:T(8,128)(2,1)S(1)} %get-tuple-element.51.after_ref), channel_id=1, source_target_pairs={{0,1},{1,0},{2,3},{3,2},{4,5},{5,4},{6,7},{7,6},{8,9},{9,8},{10,11... | collective-permute-start | bytes 393224 | tf_op jit(solution)/shard_map/ppermute | solution.py:421
  10.2 4.2 %copy-start.1 = (s32[4,1,4,128]{3,2,1,0:T(4,128)S(1)}, s32[4,1,4,128]{3,2,1,0:T(4,128)}, u32[]{:S(2)}) copy-start(s32[4,1,4,128]{3,2,1,0:T(4,128)} %gi_ref.1) | copy-start | bytes 24580
  10.2 4.2 %copy-start.2 = (f32[4,1,4,128]{3,2,1,0:T(4,128)S(1)}, f32[4,1,4,128]{3,2,1,0:T(4,128)}, u32[]{:S(2)}) copy-start(f32[4,1,4,128]{3,2,1,0:T(4,128)} %gw_ref.1) | copy-start | bytes 24580
  10.3 4.2 %copy-start.3 = (s32[3,1,4,128]{3,2,1,0:T(4,128)S(1)}, s32[3,1,4,128]{3,2,1,0:T(4,128)}, u32[]{:S(2)}) copy-start(s32[3,1,4,128]{3,2,1,0:T(4,128)} %mi_ref.1) | copy-start | bytes 18436
  10.3 4.2 %copy-start.4 = (f32[3,1,4,128]{3,2,1,0:T(4,128)S(1)}, f32[3,1,4,128]{3,2,1,0:T(4,128)}, u32[]{:S(2)}) copy-start(f32[3,1,4,128]{3,2,1,0:T(4,128)} %mw_ref.1) | copy-start | bytes 18436
  10.3 4.2 %copy-start.5 = (s32[1,4,128]{2,1,0:T(4,128)S(1)}, s32[1,4,128]{2,1,0:T(4,128)}, u32[]{:S(2)}) copy-start(s32[1,4,128]{2,1,0:T(4,128)} %gt_ref.1) | copy-start | bytes 6148
  10.3 4.2 %copy-start.6 = (s32[1,4,128]{2,1,0:T(4,128)S(1)}, s32[1,4,128]{2,1,0:T(4,128)}, u32[]{:S(2)}) copy-start(s32[1,4,128]{2,1,0:T(4,128)} %mt_ref.1) | copy-start | bytes 6148
  10.3 4.2 %copy-start.10 = (s32[1,4]{1,0:T(1,128)S(1)}, s32[1,4]{1,0:T(1,128)}, u32[]{:S(2)}) copy-start(s32[1,4]{1,0:T(1,128)} %gc_ref.1) | copy-start | bytes 52
  10.3 4.2 %copy-start.11 = (s32[1,4]{1,0:T(1,128)S(1)}, s32[1,4]{1,0:T(1,128)}, u32[]{:S(2)}) copy-start(s32[1,4]{1,0:T(1,128)} %mc_ref.1) | copy-start | bytes 52
  11.2 2.3 %collective-permute-start.10 = (bf16[128,512]{1,0:T(8,128)(2,1)S(1)}, bf16[128,512]{1,0:T(8,128)(2,1)S(1)}, u32[]{:S(2)}, u32[]{:S(2)}) collective-permute-start(bf16[128,512]{1,0:T(8,128)(2,1)S(1)} %get-tuple-element.65), channel_id=1, source_target_pairs={{0,1},{1,0},{2,3},{3,2},{4,5},{5,4},{6,7},{7,6},{8,9},{9,8},{10,11... | collective-permute-start | bytes 393224 | tf_op jit(solution)/shard_map/ppermute | solution.py:421
  11.7 14.3 %copy-start.9 = (s32[2,128]{1,0:T(2,128)S(1)}, s32[2,128]{1,0:T(2,128)}, u32[]{:S(2)}) copy-start(s32[2,128]{1,0:T(2,128)} %halo_ref.1) | copy-start | bytes 3076
  11.7 6.4 %collective-permute-start.3 = (bf16[128,512]{1,0:T(8,128)(2,1)S(1)}, bf16[128,512]{1,0:T(8,128)(2,1)S(1)}, u32[]{:S(2)}, u32[]{:S(2)}) collective-permute-start(bf16[128,512]{1,0:T(8,128)(2,1)S(1)} %get-tuple-element.92.after_ref), channel_id=1, source_target_pairs={{0,2},{2,0},{1,3},{3,1},{4,6},{6,4},{5,7},{7,5},{8,10},{10,8},{9,1... | collective-permute-start | bytes 393224 | tf_op jit(solution)/shard_map/ppermute | solution.py:63
  13.5 6.6 %collective-permute-start.11 = (bf16[128,512]{1,0:T(8,128)(2,1)S(1)}, bf16[128,512]{1,0:T(8,128)(2,1)S(1)}, u32[]{:S(2)}, u32[]{:S(2)}) collective-permute-start(bf16[128,512]{1,0:T(8,128)(2,1)S(1)} %get-tuple-element.88), channel_id=1, source_target_pairs={{0,2},{2,0},{1,3},{3,1},{4,6},{6,4},{5,7},{7,5},{8,10},{10,8},{9,1... | collective-permute-start | bytes 393224 | tf_op jit(solution)/shard_map/ppermute | solution.py:63
  18.2 2.0 %collective-permute-start.4 = (bf16[128,512]{1,0:T(8,128)(2,1)S(1)}, bf16[128,512]{1,0:T(8,128)(2,1)S(1)}, u32[]{:S(2)}, u32[]{:S(2)}) collective-permute-start(bf16[128,512]{1,0:T(8,128)(2,1)S(1)} %shard_map.198.mine_ref), channel_id=1, source_target_pairs={{0,1},{1,0},{2,3},{3,2},{4,5},{5,4},{6,7},{7,6},{8,9},{9,8},{10,11... | collective-permute-start | bytes 393224 | tf_op jit(solution)/shard_map/ppermute | solution.py:421
  20.1 5.8 %collective-permute-start.12 = (bf16[128,512]{1,0:T(8,128)(2,1)S(1)}, bf16[128,512]{1,0:T(8,128)(2,1)S(1)}, u32[]{:S(2)}, u32[]{:S(2)}) collective-permute-start(bf16[128,512]{1,0:T(8,128)(2,1)S(1)} %shard_map.205.mine_ref), channel_id=1, source_target_pairs={{0,1},{1,0},{2,3},{3,2},{4,5},{5,4},{6,7},{7,6},{8,9},{9,8},{10,11... | collective-permute-start | bytes 393224 | tf_op jit(solution)/shard_map/ppermute | solution.py:421
  20.5 10.6 %collective-permute-start.5 = (bf16[336,128]{1,0:T(8,128)(2,1)S(1)}, bf16[336,128]{1,0:T(8,128)(2,1)S(1)}, u32[]{:S(2)}, u32[]{:S(2)}) collective-permute-start(bf16[336,128]{1,0:T(8,128)(2,1)S(1)} %get-tuple-element.55), channel_id=1, source_target_pairs={{0,4},{8,12},{4,0},{12,8},{1,5},{9,13},{5,1},{13,9},{2,6},{10,14},... | collective-permute-start | bytes 258056 | tf_op jit(solution)/shard_map/ppermute | solution.py:58
  25.3 5.8 %collective-permute-start.6 = (bf16[336,128]{1,0:T(8,128)(2,1)S(1)}, bf16[336,128]{1,0:T(8,128)(2,1)S(1)}, u32[]{:S(2)}, u32[]{:S(2)}) collective-permute-start(bf16[336,128]{1,0:T(8,128)(2,1)S(1)} %get-tuple-element.56), channel_id=1, source_target_pairs={{4,8},{8,4},{5,9},{9,5},{6,10},{10,6},{7,11},{11,7},{20,24},{24,20... | collective-permute-start | bytes 258056 | tf_op jit(solution)/shard_map/ppermute | solution.py:58
  26.5 6.3 %collective-permute-start.13 = (bf16[336,128]{1,0:T(8,128)(2,1)S(1)}, bf16[336,128]{1,0:T(8,128)(2,1)S(1)}, u32[]{:S(2)}, u32[]{:S(2)}) collective-permute-start(bf16[336,128]{1,0:T(8,128)(2,1)S(1)} %get-tuple-element.67), channel_id=1, source_target_pairs={{0,4},{8,12},{4,0},{12,8},{1,5},{9,13},{5,1},{13,9},{2,6},{10,14},... | collective-permute-start | bytes 258056 | tf_op jit(solution)/shard_map/ppermute | solution.py:58
  29.6 3.2 %collective-permute-start.14 = (bf16[336,128]{1,0:T(8,128)(2,1)S(1)}, bf16[336,128]{1,0:T(8,128)(2,1)S(1)}, u32[]{:S(2)}, u32[]{:S(2)}) collective-permute-start(bf16[336,128]{1,0:T(8,128)(2,1)S(1)} %get-tuple-element.68), channel_id=1, source_target_pairs={{4,8},{8,4},{5,9},{9,5},{6,10},{10,6},{7,11},{11,7},{20,24},{24,20... | collective-permute-start | bytes 258056 | tf_op jit(solution)/shard_map/ppermute | solution.py:58
  31.6 4.2 %collective-permute-start.7 = (bf16[128,512]{1,0:T(8,128)(2,1)S(1)}, bf16[128,512]{1,0:T(8,128)(2,1)S(1)}, u32[]{:S(2)}, u32[]{:S(2)}) collective-permute-start(bf16[128,512]{1,0:T(8,128)(2,1)S(1)} %get-tuple-element.59.after_ref), channel_id=1, source_target_pairs={{0,1},{1,0},{2,3},{3,2},{4,5},{5,4},{6,7},{7,6},{8,9},{9,8},{10,11... | collective-permute-start | bytes 393224 | tf_op jit(solution)/shard_map/ppermute | solution.py:421
  33.6 3.8 %collective-permute-start.15 = (bf16[128,512]{1,0:T(8,128)(2,1)S(1)}, bf16[128,512]{1,0:T(8,128)(2,1)S(1)}, u32[]{:S(2)}, u32[]{:S(2)}) collective-permute-start(bf16[128,512]{1,0:T(8,128)(2,1)S(1)} %get-tuple-element.70), channel_id=1, source_target_pairs={{0,1},{1,0},{2,3},{3,2},{4,5},{5,4},{6,7},{7,6},{8,9},{9,8},{10,11... | collective-permute-start | bytes 393224 | tf_op jit(solution)/shard_map/ppermute | solution.py:421
  34.6 8.3 %collective-permute-start.17 = (bf16[336,256]{1,0:T(8,128)(2,1)S(1)}, bf16[336,256]{1,0:T(8,128)(2,1)S(1)}, u32[]{:S(2)}, u32[]{:S(2)}) collective-permute-start(bf16[336,256]{1,0:T(8,128)(2,1)S(1)} %shard_map.209), channel_id=1, source_target_pairs={{0,12},{4,8},{8,4},{12,0},{1,13},{5,9},{9,5},{13,1},{2,14},{6,10},... | collective-permute-start | bytes 516104 | tf_op jit(solution)/shard_map/ppermute | solution.py:63
  35.9 6.5 %collective-permute-start.8 = (bf16[128,512]{1,0:T(8,128)(2,1)S(1)}, bf16[128,512]{1,0:T(8,128)(2,1)S(1)}, u32[]{:S(2)}, u32[]{:S(2)}) collective-permute-start(bf16[128,512]{1,0:T(8,128)(2,1)S(1)} %get-tuple-element.90), channel_id=1, source_target_pairs={{0,2},{2,0},{1,3},{3,1},{4,6},{6,4},{5,7},{7,5},{8,10},{10,8},{9,1... | collective-permute-start | bytes 393224 | tf_op jit(solution)/shard_map/ppermute | solution.py:63
  37.5 6.4 %collective-permute-start.16 = (bf16[128,512]{1,0:T(8,128)(2,1)S(1)}, bf16[128,512]{1,0:T(8,128)(2,1)S(1)}, u32[]{:S(2)}, u32[]{:S(2)}) collective-permute-start(bf16[128,512]{1,0:T(8,128)(2,1)S(1)} %get-tuple-element.86), channel_id=1, source_target_pairs={{0,2},{2,0},{1,3},{3,1},{4,6},{6,4},{5,7},{7,5},{8,10},{10,8},{9,1... | collective-permute-start | bytes 393224 | tf_op jit(solution)/shard_map/ppermute | solution.py:63
  42.4 4.5 %collective-permute-start.9 = (bf16[128,512]{1,0:T(8,128)(2,1)S(1)}, bf16[128,512]{1,0:T(8,128)(2,1)S(1)}, u32[]{:S(2)}, u32[]{:S(2)}) collective-permute-start(bf16[128,512]{1,0:T(8,128)(2,1)S(1)} %shard_map.202.mine_ref.grid_ref), channel_id=1, source_target_pairs={{0,1},{1,0},{2,3},{3,2},{4,5},{5,4},{6,7},{7,6},{8,9},{9,8},{10,11... | collective-permute-start | bytes 393224 | tf_op jit(solution)/shard_map/ppermute | solution.py:421
  44.2 3.1 %collective-permute-start.19 = (bf16[128,512]{1,0:T(8,128)(2,1)S(1)}, bf16[128,512]{1,0:T(8,128)(2,1)S(1)}, u32[]{:S(2)}, u32[]{:S(2)}) collective-permute-start(bf16[128,512]{1,0:T(8,128)(2,1)S(1)} %get-tuple-element.75.mine_ref), channel_id=1, source_target_pairs={{0,1},{1,0},{2,3},{3,2},{4,5},{5,4},{6,7},{7,6},{8,9},{9,8},{10,11... | collective-permute-start | bytes 393224 | tf_op jit(solution)/shard_map/ppermute | solution.py:421
  44.2 6.4 %collective-permute-start.18 = (bf16[128,256]{1,0:T(8,128)(2,1)S(1)}, bf16[128,256]{1,0:T(8,128)(2,1)S(1)}, u32[]{:S(2)}, u32[]{:S(2)}) collective-permute-start(bf16[128,256]{1,0:T(8,128)(2,1)S(1)} %get-tuple-element.74), channel_id=1, source_target_pairs={{0,12},{4,8},{8,4},{12,0},{1,13},{5,9},{9,5},{13,1},{2,14},{6,10},... | collective-permute-start | bytes 196616 | tf_op jit(solution)/shard_map/ppermute | solution.py:63
  48.1 11.2 %collective-permute-start.21 = (bf16[336,256]{1,0:T(8,128)(2,1)S(1)}, bf16[336,256]{1,0:T(8,128)(2,1)S(1)}, u32[]{:S(2)}, u32[]{:S(2)}) collective-permute-start(bf16[336,256]{1,0:T(8,128)(2,1)S(1)} %get-tuple-element.81), channel_id=1, source_target_pairs={{0,8},{4,12},{8,0},{12,4},{1,9},{5,13},{9,1},{13,5},{2,10},{6,14},... | collective-permute-start | bytes 516104 | tf_op jit(solution)/shard_map/ppermute | solution.py:63
  50.1 9.2 %collective-permute-start.22 = (bf16[336,256]{1,0:T(8,128)(2,1)S(1)}, bf16[336,256]{1,0:T(8,128)(2,1)S(1)}, u32[]{:S(2)}, u32[]{:S(2)}) collective-permute-start(bf16[336,256]{1,0:T(8,128)(2,1)S(1)} %get-tuple-element.82), channel_id=1, source_target_pairs={{0,4},{4,0},{8,12},{12,8},{1,5},{5,1},{9,13},{13,9},{2,6},{6,2},{1... | collective-permute-start | bytes 516104 | tf_op jit(solution)/shard_map/ppermute | solution.py:63
  50.6 1.3 %collective-permute-start.20 = (bf16[128,256]{1,0:T(8,128)(2,1)S(1)}, bf16[128,256]{1,0:T(8,128)(2,1)S(1)}, u32[]{:S(2)}, u32[]{:S(2)}) collective-permute-start(bf16[128,256]{1,0:T(8,128)(2,1)S(1)} %collective-permute-done.18.mine_ref), channel_id=1, source_target_pairs={{0,1},{1,0},{2,3},{3,2},{4,5},{5,4},{6,7},{7,6},{8,9},{9,8},{10,11... | collective-permute-start | bytes 196616 | tf_op jit(solution)/shard_map/ppermute | solution.py:421

commit v8 on v7

--- a/solution.py
+++ b/solution.py
@@ -141,9 +141,9 @@
 
 
 def prepare_kernel(
-    grid_hbm, mesh_hbm, table_hbm, win_hbm, wout_hbm, index_ref, pq_ref, sea_ref, speed_ref,
+    grid_hbm, mesh_hbm, table_hbm, first_ref, second_ref, index_ref, pq_ref, sea_ref, speed_ref,
     gpart_ref, mpart_ref, hot_ref, weight_ref, band_ref, win_ref, wout_ref,
-    grid_ref, mesh_ref, layer_ref, gstate_ref, mstate_ref, near_ref, pack_ref, sem,
+    grid_ref, mesh_ref, gstate_ref, mstate_ref, near_ref, pack_ref, sem,
 ):
     fr, dr = lax.axis_index("fr"), lax.axis_index("dr")
     rows, cols = sea_ref.shape
@@ -153,8 +153,6 @@
         pltpu.make_async_copy(table_hbm.at[fr, dr], band_ref, sem.at[0]),
         pltpu.make_async_copy(mesh_hbm, mesh_ref, sem.at[1]),
         pltpu.make_async_copy(grid_hbm, grid_ref, sem.at[2]),
-        pltpu.make_async_copy(win_hbm, layer_ref.at[0], sem.at[3]),
-        pltpu.make_async_copy(wout_hbm, layer_ref.at[1], sem.at[4]),
     ]
     for copy in copies:
         copy.start()
@@ -178,13 +176,11 @@
         gstate_ref[:bands, x * cols : (x + 1) * cols] = grid_ref[pl.ds(x, bands, stride=rows), :]
     own_grid(gstate_ref, band_ref, sea_ref, speed_ref, gpart_ref)
     half = pack_ref.shape[1] // 2
-    copies[3].wait()
-    pack_rows(layer_ref.at[0], pack_ref, 0)
+    pack_rows(first_ref, pack_ref, 0)
     one, two = pack_ref[:, :half].T.astype(BF16), pack_ref[:, half:].T.astype(BF16)
     win_ref[:half, :] = jnp.where(dr == 0, one, two)
     win_ref[half:, :] = jnp.where(dr == 0, two, one)
-    copies[4].wait()
-    pack_rows(layer_ref.at[1], pack_ref, 0)
+    pack_rows(second_ref, pack_ref, 0)
     one, two = pack_ref[:, :half].astype(BF16), pack_ref[:, half:].astype(BF16)
     wout_ref[:, :half] = jnp.where(dr == 0, one, two)
     wout_ref[:, half:] = jnp.where(dr == 0, two, one)
@@ -476,15 +472,14 @@
         [
             (grid_flat.shape, F32),
             (mesh_spec.shape, F32),
-            ((2,) + w_in.shape, BF16),
             grid_shape,
             mesh_shape,
             near_scratch,
             ((padded, hid), F32),
-            pltpu.SemaphoreType.DMA((5,)),
+            pltpu.SemaphoreType.DMA((3,)),
         ],
         3.4,
-        spaces=[HBM] * 5 + [VMEM] * 4,
+        spaces=[HBM] * 3 + [VMEM] * 6,
     )(
         grid_flat, mesh_spec, table, w_in, jnp.transpose(w_out, (1, 2, 0)),
         nb_index, pq, grid_sea, grid_speed,

time: 61.5 us -> 61.6 us (level)
  no operation moved by 1% of the time
where the time goes in v8:
time: 61.6 us; the launch traced here: 61.4 us
  starting transfers between devices  25.4 us (41%)
  waiting for transfers between devices  18.2 us (30%)
  Pallas kernels  16.1 us (26%)
  between operations  1.3 us (2%)
    ppermute x8, waiting for transfers between devices, peer_swap(): return lax.ppermute(array, axis, [(i, i ^ step) for i in range(size)])  16.7 us
    pallas_call x20, Pallas kernels, run(): pl.pallas_call(body, out_shape=[jax.ShapeDtypeStruct(s, t) for s, t in ou...  16.1 us
    ppermute x6, starting transfers between devices, pair_swap(): return lax.ppermute(array, axis, pairs + [(j, i) for i, j in pairs])  13.1 us
    ppermute x8, starting transfers between devices, peer_swap(): return lax.ppermute(array, axis, [(i, i ^ step) for i in range(size)])  10.8 us
    ppermute x9, starting transfers between devices, core_swap(): return lax.ppermute(array, 'dr', [(0, 1), (1, 0)])  1.52 us
    ppermute x9, waiting for transfers between devices, core_swap(): return lax.ppermute(array, 'dr', [(0, 1), (1, 0)])  1.27 us
  transfers between devices with their start and end apart: 23, of which 9 were waited for; matrix products, arithmetic and copies ran while one was open for 0% of the time, Pallas kernels for 20%

profile of v8, /device:TPU:0, one launch (start us, length us, event | category | flops | bytes accessed | tf_op | source)
XLA Modules:
  0.0 61.4 jit_solution(434202112332880175)
XLA Ops:
  0.7 1.6 %shard_map.195 = (bf16[336,256]{1,0:T(8,128)(2,1)S(1)}, bf16[336,256]{1,0:T(8,128)(2,1)S(1)}) custom-call(f32[1296,128]{1,0:T(8,128)} %bitcast.4, f32[18,18,512]{2,1,0:T(8,128)} %mesh_hbm.3, s32[2,128]{1,0:T(2,128)} %halo_ref.1), custom_call_target="tpu_custom_call" | custom-call | flops 2070000000 | tf_op jit(solution)/shard_map/pallas_call | solution.py:31
  2.3 3.1 %collective-permute-start = (bf16[336,256]{1,0:T(8,128)(2,1)S(1)}, bf16[336,256]{1,0:T(8,128)(2,1)S(1)}, u32[]{:S(2)}, u32[]{:S(2)}) collective-permute-start(bf16[336,256]{1,0:T(8,128)(2,1)S(1)} %get-tuple-element.45), channel_id=1, source_target_pairs={{0,4},{8,12},{4,0},{12,8},{1,5},{9,13},{5,1},{13,9},{2,6},{10,14},... | collective-permute-start | bytes 516104 | tf_op jit(solution)/shard_map/ppermute | solution.py:58
  5.4 0.7 %collective-permute-start.1 = (bf16[336,256]{1,0:T(8,128)(2,1)S(1)}, bf16[336,256]{1,0:T(8,128)(2,1)S(1)}, u32[]{:S(2)}, u32[]{:S(2)}) collective-permute-start(bf16[336,256]{1,0:T(8,128)(2,1)S(1)} %get-tuple-element.46), channel_id=1, source_target_pairs={{4,8},{8,4},{5,9},{9,5},{6,10},{10,6},{7,11},{11,7},{20,24},{24,20... | collective-permute-start | bytes 516104 | tf_op jit(solution)/shard_map/ppermute | solution.py:58
  6.1 0.1 cosine_multiply_fusion
  6.2 3.3 %shard_map.194 = (f32[336,512]{1,0:T(8,128)S(1)}, f32[336,512]{1,0:T(8,128)S(1)}, bf16[4,768,512]{2,1,0:T(8,128)(2,1)S(1)}, f32[4,336,512]{2,1,0:T(8,128)S(1)}, ...) custom-call(f32[1296,128]{1,0:T(8,128)} %bitcast.5, f32[18,18,512]{2,1,0:T(8,128)} %mesh_hbm.3, ...), custom_call_target="tpu_custom_call" | custom-call | flops 3910000128 | tf_op jit(solution)/shard_map/pallas_call | solution.py:31
  9.6 0.2 collective-permute-done.even_ref
  9.8 0.4 shard_map.196
  10.2 0.1 collective-permute-start.2
  10.3 0.0 copy-start.3
  10.3 0.0 copy-start.4
  10.3 0.0 copy-start.5
  10.3 0.0 copy-start.6
  10.4 0.0 copy-start.7
  10.4 0.0 copy-start.8
  10.4 0.0 copy-start.12
  10.4 0.0 copy-start.13
  10.4 0.8 %shard_map.204 = (f32[336,512]{1,0:T(8,128)S(1)}, f32[128,512]{1,0:T(8,128)S(1)}, bf16[128,512]{1,0:T(8,128)(2,1)S(1)}) custom-call(f32[336,512]{1,0:T(8,128)S(1)} %get-tuple-element.60.part_ref, bf16[336,256]{1,0:T(8,128)(2,1)S(1)} %collective-permute-done.even_ref, bf16[336,256]{1,0:T(8,128)(2,1)S(1)} %collective-permute-done.1.odd_ref, ...), custom_call_target="tpu_custom_call" | custom-call | flops 920000000 | tf_op jit(solution)/shard_map/pallas_call | solution.py:31
  11.2 0.5 collective-permute-start.10
  11.8 1.7 %collective-permute-start.3 = (bf16[128,512]{1,0:T(8,128)(2,1)S(1)}, bf16[128,512]{1,0:T(8,128)(2,1)S(1)}, u32[]{:S(2)}, u32[]{:S(2)}) collective-permute-start(bf16[128,512]{1,0:T(8,128)(2,1)S(1)} %get-tuple-element.92.after_ref), channel_id=1, source_target_pairs={{0,2},{2,0},{1,3},{3,1},{4,6},{6,4},{5,7},{7,5},{8,10},{10,8},{9,1... | collective-permute-start | bytes 393224 | tf_op jit(solution)/shard_map/ppermute | solution.py:63
  13.6 0.9 %collective-permute-start.11 = (bf16[128,512]{1,0:T(8,128)(2,1)S(1)}, bf16[128,512]{1,0:T(8,128)(2,1)S(1)}, u32[]{:S(2)}, u32[]{:S(2)}) collective-permute-start(bf16[128,512]{1,0:T(8,128)(2,1)S(1)} %get-tuple-element.88), channel_id=1, source_target_pairs={{0,2},{2,0},{1,3},{3,1},{4,6},{6,4},{5,7},{7,5},{8,10},{10,8},{9,1... | collective-permute-start | bytes 393224 | tf_op jit(solution)/shard_map/ppermute | solution.py:63
  14.6 2.1 %shard_map.197 = (bf16[512,512]{1,0:T(8,128)(2,1)S(1)}, bf16[512,512]{1,0:T(8,128)(2,1)S(1)}, f32[2,512]{1,0:T(2,128)S(1)}, bf16[512,512]{1,0:T(8,128)(2,1)S(1)}, bf16[512,512]{1,0:T(8,128)(2,1)S(1)}) custom-call(s32[4,1,4,128]{3,2,1,0:T(4,128)S(1)} %copy-done.3, f32[4,1,4,128]{3,2,1,0:T(4,128)S(1)} %copy-done.4, s32[1,4]{1,0:T(1,128)S(1)} %copy-done.12, ...), custom_call_target="tpu_custom_call" | custom-call | flops 575000000 | tf_op jit(solution)/shard_map/pallas_call | solution.py:31
  16.7 1.6 %collective-permute-done.3.got_ref = bf16[128,512]{1,0:T(8,128)(2,1)S(1)} collective-permute-done((bf16[128,512]{1,0:T(8,128)(2,1)S(1)}, bf16[128,512]{1,0:T(8,128)(2,1)S(1)}, u32[]{:S(2)}, u32[]{:S(2)}) %collective-permute-start.3) | collective-permute-done | bytes 131104 | tf_op jit(solution)/shard_map/ppermute | solution.py:63
  18.2 0.1 shard_map.198.mine_ref
  18.3 0.1 collective-permute-start.4
  18.4 1.7 %collective-permute-done.11.got_ref = bf16[128,512]{1,0:T(8,128)(2,1)S(1)} collective-permute-done((bf16[128,512]{1,0:T(8,128)(2,1)S(1)}, bf16[128,512]{1,0:T(8,128)(2,1)S(1)}, u32[]{:S(2)}, u32[]{:S(2)}) %collective-permute-start.11) | collective-permute-done | bytes 131104 | tf_op jit(solution)/shard_map/ppermute | solution.py:63
  20.1 0.1 shard_map.205.mine_ref
  20.2 0.1 collective-permute-start.12
  20.3 0.0 collective-permute-done.4.other_ref
  20.3 0.3 shard_map.199
  20.6 4.8 %collective-permute-start.5 = (bf16[336,128]{1,0:T(8,128)(2,1)S(1)}, bf16[336,128]{1,0:T(8,128)(2,1)S(1)}, u32[]{:S(2)}, u32[]{:S(2)}) collective-permute-start(bf16[336,128]{1,0:T(8,128)(2,1)S(1)} %get-tuple-element.55), channel_id=1, source_target_pairs={{0,4},{8,12},{4,0},{12,8},{1,5},{9,13},{5,1},{13,9},{2,6},{10,14},... | collective-permute-start | bytes 258056 | tf_op jit(solution)/shard_map/ppermute | solution.py:58
  25.4 0.7 %collective-permute-start.6 = (bf16[336,128]{1,0:T(8,128)(2,1)S(1)}, bf16[336,128]{1,0:T(8,128)(2,1)S(1)}, u32[]{:S(2)}, u32[]{:S(2)}) collective-permute-start(bf16[336,128]{1,0:T(8,128)(2,1)S(1)} %get-tuple-element.56), channel_id=1, source_target_pairs={{4,8},{8,4},{5,9},{9,5},{6,10},{10,6},{7,11},{11,7},{20,24},{24,20... | collective-permute-start | bytes 258056 | tf_op jit(solution)/shard_map/ppermute | solution.py:58
  26.1 0.0 collective-permute-done.12.other_ref
  26.1 0.5 shard_map.206
  26.6 3.1 %collective-permute-start.13 = (bf16[336,128]{1,0:T(8,128)(2,1)S(1)}, bf16[336,128]{1,0:T(8,128)(2,1)S(1)}, u32[]{:S(2)}, u32[]{:S(2)}) collective-permute-start(bf16[336,128]{1,0:T(8,128)(2,1)S(1)} %get-tuple-element.67), channel_id=1, source_target_pairs={{0,4},{8,12},{4,0},{12,8},{1,5},{9,13},{5,1},{13,9},{2,6},{10,14},... | collective-permute-start | bytes 258056 | tf_op jit(solution)/shard_map/ppermute | solution.py:58
  29.6 0.8 %collective-permute-start.14 = (bf16[336,128]{1,0:T(8,128)(2,1)S(1)}, bf16[336,128]{1,0:T(8,128)(2,1)S(1)}, u32[]{:S(2)}, u32[]{:S(2)}) collective-permute-start(bf16[336,128]{1,0:T(8,128)(2,1)S(1)} %get-tuple-element.68), channel_id=1, source_target_pairs={{4,8},{8,4},{5,9},{9,5},{6,10},{10,6},{7,11},{11,7},{20,24},{24,20... | collective-permute-start | bytes 258056 | tf_op jit(solution)/shard_map/ppermute | solution.py:58
  30.5 0.7 %shard_map.200.part_ref = f32[336,512]{1,0:T(8,128)S(1)} custom-call(f32[336,512]{1,0:T(8,128)S(1)} %get-tuple-element.54.state_ref, f32[336,2]{1,0:T(8,128)S(1)} %get-tuple-element.47.band_ref, s32[4,128]{1,0:T(4,128)S(1)} %copy-done.10, f32[4,128]{1,0:T(4,128)S(1)} %copy-done.9), custom_call_target="tpu_custom_call" | custom-call | flops 575000000 | tf_op jit(solution)/shard_map/pallas_call | solution.py:31
  31.2 0.0 collective-permute-done.5.even_ref
  31.2 0.4 shard_map.201
  31.7 0.1 collective-permute-start.7
  31.8 1.1 %shard_map.207.part_ref = f32[336,512]{1,0:T(8,128)S(1)} custom-call(f32[336,512]{1,0:T(8,128)S(1)} %get-tuple-element.66.state_ref, bf16[4,768,512]{2,1,0:T(8,128)(2,1)S(1)} %get-tuple-element.61.hot_ref, f32[4,336,512]{2,1,0:T(8,128)S(1)} %get-tuple-element.62.weight_ref), custom_call_target="tpu_custom_call" | custom-call | flops 1150000000 | tf_op jit(solution)/shard_map/pallas_call | solution.py:31
  32.9 0.0 collective-permute-done.14.odd_ref
  32.9 0.8 %shard_map.208 = (f32[336,512]{1,0:T(8,128)S(1)}, f32[128,512]{1,0:T(8,128)S(1)}, bf16[128,512]{1,0:T(8,128)(2,1)S(1)}) custom-call(f32[336,512]{1,0:T(8,128)S(1)} %shard_map.207.part_ref, bf16[336,128]{1,0:T(8,128)(2,1)S(1)} %collective-permute-done.13.even_ref, bf16[336,128]{1,0:T(8,128)(2,1)S(1)} %collective-permute-done.14.odd_ref, ...), custom_call_target="tpu_custom_call" | custom-call | flops 920000000 | tf_op jit(solution)/shard_map/pallas_call | solution.py:31
  33.7 0.6 collective-permute-start.15
  34.3 0.4 shard_map.209
  34.7 1.3 %collective-permute-start.17 = (bf16[336,256]{1,0:T(8,128)(2,1)S(1)}, bf16[336,256]{1,0:T(8,128)(2,1)S(1)}, u32[]{:S(2)}, u32[]{:S(2)}) collective-permute-start(bf16[336,256]{1,0:T(8,128)(2,1)S(1)} %shard_map.209), channel_id=1, source_target_pairs={{0,12},{4,8},{8,4},{12,0},{1,13},{5,9},{9,5},{13,1},{2,14},{6,10},... | collective-permute-start | bytes 516104 | tf_op jit(solution)/shard_map/ppermute | solution.py:63
  36.0 1.5 %collective-permute-start.8 = (bf16[128,512]{1,0:T(8,128)(2,1)S(1)}, bf16[128,512]{1,0:T(8,128)(2,1)S(1)}, u32[]{:S(2)}, u32[]{:S(2)}) collective-permute-start(bf16[128,512]{1,0:T(8,128)(2,1)S(1)} %get-tuple-element.90), channel_id=1, source_target_pairs={{0,2},{2,0},{1,3},{3,1},{4,6},{6,4},{5,7},{7,5},{8,10},{10,8},{9,1... | collective-permute-start | bytes 393224 | tf_op jit(solution)/shard_map/ppermute | solution.py:63
  37.5 0.0 collective-permute-done.15
  37.5 0.6 %collective-permute-start.16 = (bf16[128,512]{1,0:T(8,128)(2,1)S(1)}, bf16[128,512]{1,0:T(8,128)(2,1)S(1)}, u32[]{:S(2)}, u32[]{:S(2)}) collective-permute-start(bf16[128,512]{1,0:T(8,128)(2,1)S(1)} %get-tuple-element.86), channel_id=1, source_target_pairs={{0,2},{2,0},{1,3},{3,1},{4,6},{6,4},{5,7},{7,5},{8,10},{10,8},{9,1... | collective-permute-start | bytes 393224 | tf_op jit(solution)/shard_map/ppermute | solution.py:63
  38.2 4.3 %collective-permute-done.8.got_ref = bf16[128,512]{1,0:T(8,128)(2,1)S(1)} collective-permute-done((bf16[128,512]{1,0:T(8,128)(2,1)S(1)}, bf16[128,512]{1,0:T(8,128)(2,1)S(1)}, u32[]{:S(2)}, u32[]{:S(2)}) %collective-permute-start.8) | collective-permute-done | bytes 131104 | tf_op jit(solution)/shard_map/ppermute | solution.py:63
  42.4 0.1 shard_map.202.mine_ref.grid_ref
  42.5 0.1 collective-permute-start.9
  42.6 0.3 collective-permute-done.17.after_ref.early_ref
  42.9 1.1 %collective-permute-done.16.got_ref = bf16[128,512]{1,0:T(8,128)(2,1)S(1)} collective-permute-done((bf16[128,512]{1,0:T(8,128)(2,1)S(1)}, bf16[128,512]{1,0:T(8,128)(2,1)S(1)}, u32[]{:S(2)}, u32[]{:S(2)}) %collective-permute-start.16) | collective-permute-done | bytes 131104 | tf_op jit(solution)/shard_map/ppermute | solution.py:63
  44.0 0.3 shard_map.210
  44.3 0.1 collective-permute-start.19
  44.3 2.7 %collective-permute-start.18 = (bf16[128,256]{1,0:T(8,128)(2,1)S(1)}, bf16[128,256]{1,0:T(8,128)(2,1)S(1)}, u32[]{:S(2)}, u32[]{:S(2)}) collective-permute-start(bf16[128,256]{1,0:T(8,128)(2,1)S(1)} %get-tuple-element.74), channel_id=1, source_target_pairs={{0,12},{4,8},{8,4},{12,0},{1,13},{5,9},{9,5},{13,1},{2,14},{6,10},... | collective-permute-start | bytes 196616 | tf_op jit(solution)/shard_map/ppermute | solution.py:63
  47.0 0.2 shard_map.203.grid_ref.gstate_ref
  47.3 0.9 %shard_map.211 = (f32[336,512]{1,0:T(8,128)S(1)}, bf16[336,256]{1,0:T(8,128)(2,1)S(1)}, bf16[336,256]{1,0:T(8,128)(2,1)S(1)}, bf16[336,256]{1,0:T(8,128)(2,1)S(1)}) custom-call(f32[336,512]{1,0:T(8,128)S(1)} %shard_map.203.grid_ref.gstate_ref, f32[336,512]{1,0:T(8,128)S(1)} %get-tuple-element.73.mesh_ref.moved_ref, ...), custom_call_target="tpu_custom_call" | custom-call | flops 920000000 | tf_op jit(solution)/shard_map/pallas_call | solution.py:31
  48.1 2.0 %collective-permute-start.21 = (bf16[336,256]{1,0:T(8,128)(2,1)S(1)}, bf16[336,256]{1,0:T(8,128)(2,1)S(1)}, u32[]{:S(2)}, u32[]{:S(2)}) collective-permute-start(bf16[336,256]{1,0:T(8,128)(2,1)S(1)} %get-tuple-element.81), channel_id=1, source_target_pairs={{0,8},{4,12},{8,0},{12,4},{1,9},{5,13},{9,1},{13,5},{2,10},{6,14},... | collective-permute-start | bytes 516104 | tf_op jit(solution)/shard_map/ppermute | solution.py:63
  50.2 0.6 collective-permute-done.18.mine_ref
  50.7 1.3 %collective-permute-done.20.other_ref = bf16[128,256]{1,0:T(8,128)(2,1)S(1)} collective-permute-done((bf16[128,256]{1,0:T(8,128)(2,1)S(1)}, bf16[128,256]{1,0:T(8,128)(2,1)S(1)}, u32[]{:S(2)}, u32[]{:S(2)}) %collective-permute-start.20) | collective-permute-done | bytes 65568 | tf_op jit(solution)/shard_map/ppermute | solution.py:417
  52.0 0.2 shard_map.212.rest_0_
  52.2 7.2 %collective-permute-done.21.rest_1_ = bf16[336,256]{1,0:T(8,128)(2,1)S(1)} collective-permute-done((bf16[336,256]{1,0:T(8,128)(2,1)S(1)}, bf16[336,256]{1,0:T(8,128)(2,1)S(1)}, u32[]{:S(2)}, u32[]{:S(2)}) %collective-permute-start.21) | collective-permute-done | bytes 172064 | tf_op jit(solution)/shard_map/ppermute | solution.py:63
  59.4 1.8 %shard_map.213 = (f32[1296,128]{1,0:T(8,128)}, f32[18,18,512]{2,1,0:T(8,128)}) custom-call(f32[336,512]{1,0:T(8,128)S(1)} %shard_map.203.grid_ref.gstate_ref, f32[336,512]{1,0:T(8,128)S(1)} %get-tuple-element.77.mstate_ref, bf16[512,512]{1,0:T(8,128)(2,1)S(1)} %get-tuple-element.78.gland_ref, bf16[512,512]{1,0:T(8,128)(2,1)S(1)} %get-tuple-element.79.mland_ref, ...), custom_call_target="tpu_custom_call" | custom-call | flops 2184999936 | tf_op jit(solution)/shard_map/pallas_call | solution.py:31
  (40 shorter events, 0.2 us)
Async XLA Ops:
  0.6 5.4 %copy-start.14 = (f32[4,512]{1,0:T(4,128)S(1)}, f32[4,512]{1,0:T(4,128)}, u32[]{:S(2)}) copy-start(f32[4,512]{1,0:T(4,128)} %param.24) | copy-start | bytes 24580
  0.6 5.4 %copy-start.15 = (f32[4,512]{1,0:T(4,128)S(1)}, f32[4,512]{1,0:T(4,128)}, u32[]{:S(2)}) copy-start(f32[4,512]{1,0:T(4,128)} %param.25) | copy-start | bytes 24580
  0.7 5.5 %copy-start = (bf16[18,18,256]{2,1,0:T(8,128)(2,1)S(1)}, bf16[18,18,256]{2,1,0:T(8,128)(2,1)}, u32[]{:S(2)}) copy-start(bf16[18,18,256]{2,1,0:T(8,128)(2,1)} %first_ref.1) | copy-start | bytes 497668
  0.7 5.5 %copy-start.1 = (bf16[256,18,18]{0,2,1:T(8,128)(2,1)S(1)}, bf16[256,18,18]{0,2,1:T(8,128)(2,1)}, u32[]{:S(2)}) copy-start(bf16[256,18,18]{0,2,1:T(8,128)(2,1)} %param.28) | copy-start | bytes 497668
  0.7 5.5 %copy-start.2 = (s32[4,512]{1,0:T(4,128)S(1)}, s32[4,512]{1,0:T(4,128)}, u32[]{:S(2)}) copy-start(s32[4,512]{1,0:T(4,128)} %index_ref.1) | copy-start | bytes 24580
  0.7 5.5 %copy-start.9 = (f32[4,128]{1,0:T(4,128)S(1)}, f32[4,128]{1,0:T(4,128)}, u32[]{:S(2)}) copy-start(f32[4,128]{1,0:T(4,128)} %speed_ref.7) | copy-start | bytes 6148
  0.7 5.5 %copy-start.10 = (s32[4,128]{1,0:T(4,128)S(1)}, s32[4,128]{1,0:T(4,128)}, u32[]{:S(2)}) copy-start(s32[4,128]{1,0:T(4,128)} %sea_ref.9) | copy-start | bytes 6148
  2.3 7.5 %collective-permute-start = (bf16[336,256]{1,0:T(8,128)(2,1)S(1)}, bf16[336,256]{1,0:T(8,128)(2,1)S(1)}, u32[]{:S(2)}, u32[]{:S(2)}) collective-permute-start(bf16[336,256]{1,0:T(8,128)(2,1)S(1)} %get-tuple-element.45), channel_id=1, source_target_pairs={{0,4},{8,12},{4,0},{12,8},{1,5},{9,13},{5,1},{13,9},{2,6},{10,14},... | collective-permute-start | bytes 516104 | tf_op jit(solution)/shard_map/ppermute | solution.py:58
  5.4 4.4 %collective-permute-start.1 = (bf16[336,256]{1,0:T(8,128)(2,1)S(1)}, bf16[336,256]{1,0:T(8,128)(2,1)S(1)}, u32[]{:S(2)}, u32[]{:S(2)}) collective-permute-start(bf16[336,256]{1,0:T(8,128)(2,1)S(1)} %get-tuple-element.46), channel_id=1, source_target_pairs={{4,8},{8,4},{5,9},{9,5},{6,10},{10,6},{7,11},{11,7},{20,24},{24,20... | collective-permute-start | bytes 516104 | tf_op jit(solution)/shard_map/ppermute | solution.py:58
  10.2 1.5 %collective-permute-start.2 = (bf16[128,512]{1,0:T(8,128)(2,1)S(1)}, bf16[128,512]{1,0:T(8,128)(2,1)S(1)}, u32[]{:S(2)}, u32[]{:S(2)}) collective-permute-start(bf16[128,512]{1,0:T(8,128)(2,1)S(1)} %get-tuple-element.51.after_ref), channel_id=1, source_target_pairs={{0,1},{1,0},{2,3},{3,2},{4,5},{5,4},{6,7},{7,6},{8,9},{9,8},{10,11... | collective-permute-start | bytes 393224 | tf_op jit(solution)/shard_map/ppermute | solution.py:417
  10.3 4.2 %copy-start.3 = (s32[4,1,4,128]{3,2,1,0:T(4,128)S(1)}, s32[4,1,4,128]{3,2,1,0:T(4,128)}, u32[]{:S(2)}) copy-start(s32[4,1,4,128]{3,2,1,0:T(4,128)} %gi_ref.1) | copy-start | bytes 24580
  10.3 4.2 %copy-start.4 = (f32[4,1,4,128]{3,2,1,0:T(4,128)S(1)}, f32[4,1,4,128]{3,2,1,0:T(4,128)}, u32[]{:S(2)}) copy-start(f32[4,1,4,128]{3,2,1,0:T(4,128)} %gw_ref.1) | copy-start | bytes 24580
  10.3 4.2 %copy-start.5 = (s32[3,1,4,128]{3,2,1,0:T(4,128)S(1)}, s32[3,1,4,128]{3,2,1,0:T(4,128)}, u32[]{:S(2)}) copy-start(s32[3,1,4,128]{3,2,1,0:T(4,128)} %mi_ref.1) | copy-start | bytes 18436
  10.3 4.2 %copy-start.6 = (f32[3,1,4,128]{3,2,1,0:T(4,128)S(1)}, f32[3,1,4,128]{3,2,1,0:T(4,128)}, u32[]{:S(2)}) copy-start(f32[3,1,4,128]{3,2,1,0:T(4,128)} %mw_ref.1) | copy-start | bytes 18436
  10.4 4.2 %copy-start.7 = (s32[1,4,128]{2,1,0:T(4,128)S(1)}, s32[1,4,128]{2,1,0:T(4,128)}, u32[]{:S(2)}) copy-start(s32[1,4,128]{2,1,0:T(4,128)} %gt_ref.1) | copy-start | bytes 6148
  10.4 4.2 %copy-start.8 = (s32[1,4,128]{2,1,0:T(4,128)S(1)}, s32[1,4,128]{2,1,0:T(4,128)}, u32[]{:S(2)}) copy-start(s32[1,4,128]{2,1,0:T(4,128)} %mt_ref.1) | copy-start | bytes 6148
  10.4 4.2 %copy-start.12 = (s32[1,4]{1,0:T(1,128)S(1)}, s32[1,4]{1,0:T(1,128)}, u32[]{:S(2)}) copy-start(s32[1,4]{1,0:T(1,128)} %gc_ref.1) | copy-start | bytes 52
  10.4 4.2 %copy-start.13 = (s32[1,4]{1,0:T(1,128)S(1)}, s32[1,4]{1,0:T(1,128)}, u32[]{:S(2)}) copy-start(s32[1,4]{1,0:T(1,128)} %mc_ref.1) | copy-start | bytes 52
  11.2 2.3 %collective-permute-start.10 = (bf16[128,512]{1,0:T(8,128)(2,1)S(1)}, bf16[128,512]{1,0:T(8,128)(2,1)S(1)}, u32[]{:S(2)}, u32[]{:S(2)}) collective-permute-start(bf16[128,512]{1,0:T(8,128)(2,1)S(1)} %get-tuple-element.65), channel_id=1, source_target_pairs={{0,1},{1,0},{2,3},{3,2},{4,5},{5,4},{6,7},{7,6},{8,9},{9,8},{10,11... | collective-permute-start | bytes 393224 | tf_op jit(solution)/shard_map/ppermute | solution.py:417
  11.8 14.3 %copy-start.11 = (s32[2,128]{1,0:T(2,128)S(1)}, s32[2,128]{1,0:T(2,128)}, u32[]{:S(2)}) copy-start(s32[2,128]{1,0:T(2,128)} %halo_ref.1) | copy-start | bytes 3076
  11.8 6.4 %collective-permute-start.3 = (bf16[128,512]{1,0:T(8,128)(2,1)S(1)}, bf16[128,512]{1,0:T(8,128)(2,1)S(1)}, u32[]{:S(2)}, u32[]{:S(2)}) collective-permute-start(bf16[128,512]{1,0:T(8,128)(2,1)S(1)} %get-tuple-element.92.after_ref), channel_id=1, source_target_pairs={{0,2},{2,0},{1,3},{3,1},{4,6},{6,4},{5,7},{7,5},{8,10},{10,8},{9,1... | collective-permute-start | bytes 393224 | tf_op jit(solution)/shard_map/ppermute | solution.py:63
  13.6 6.6 %collective-permute-start.11 = (bf16[128,512]{1,0:T(8,128)(2,1)S(1)}, bf16[128,512]{1,0:T(8,128)(2,1)S(1)}, u32[]{:S(2)}, u32[]{:S(2)}) collective-permute-start(bf16[128,512]{1,0:T(8,128)(2,1)S(1)} %get-tuple-element.88), channel_id=1, source_target_pairs={{0,2},{2,0},{1,3},{3,1},{4,6},{6,4},{5,7},{7,5},{8,10},{10,8},{9,1... | collective-permute-start | bytes 393224 | tf_op jit(solution)/shard_map/ppermute | solution.py:63
  18.3 2.0 %collective-permute-start.4 = (bf16[128,512]{1,0:T(8,128)(2,1)S(1)}, bf16[128,512]{1,0:T(8,128)(2,1)S(1)}, u32[]{:S(2)}, u32[]{:S(2)}) collective-permute-start(bf16[128,512]{1,0:T(8,128)(2,1)S(1)} %shard_map.198.mine_ref), channel_id=1, source_target_pairs={{0,1},{1,0},{2,3},{3,2},{4,5},{5,4},{6,7},{7,6},{8,9},{9,8},{10,11... | collective-permute-start | bytes 393224 | tf_op jit(solution)/shard_map/ppermute | solution.py:417
  20.2 5.8 %collective-permute-start.12 = (bf16[128,512]{1,0:T(8,128)(2,1)S(1)}, bf16[128,512]{1,0:T(8,128)(2,1)S(1)}, u32[]{:S(2)}, u32[]{:S(2)}) collective-permute-start(bf16[128,512]{1,0:T(8,128)(2,1)S(1)} %shard_map.205.mine_ref), channel_id=1, source_target_pairs={{0,1},{1,0},{2,3},{3,2},{4,5},{5,4},{6,7},{7,6},{8,9},{9,8},{10,11... | collective-permute-start | bytes 393224 | tf_op jit(solution)/shard_map/ppermute | solution.py:417
  20.6 10.6 %collective-permute-start.5 = (bf16[336,128]{1,0:T(8,128)(2,1)S(1)}, bf16[336,128]{1,0:T(8,128)(2,1)S(1)}, u32[]{:S(2)}, u32[]{:S(2)}) collective-permute-start(bf16[336,128]{1,0:T(8,128)(2,1)S(1)} %get-tuple-element.55), channel_id=1, source_target_pairs={{0,4},{8,12},{4,0},{12,8},{1,5},{9,13},{5,1},{13,9},{2,6},{10,14},... | collective-permute-start | bytes 258056 | tf_op jit(solution)/shard_map/ppermute | solution.py:58
  25.4 5.8 %collective-permute-start.6 = (bf16[336,128]{1,0:T(8,128)(2,1)S(1)}, bf16[336,128]{1,0:T(8,128)(2,1)S(1)}, u32[]{:S(2)}, u32[]{:S(2)}) collective-permute-start(bf16[336,128]{1,0:T(8,128)(2,1)S(1)} %get-tuple-element.56), channel_id=1, source_target_pairs={{4,8},{8,4},{5,9},{9,5},{6,10},{10,6},{7,11},{11,7},{20,24},{24,20... | collective-permute-start | bytes 258056 | tf_op jit(solution)/shard_map/ppermute | solution.py:58
  26.6 6.3 %collective-permute-start.13 = (bf16[336,128]{1,0:T(8,128)(2,1)S(1)}, bf16[336,128]{1,0:T(8,128)(2,1)S(1)}, u32[]{:S(2)}, u32[]{:S(2)}) collective-permute-start(bf16[336,128]{1,0:T(8,128)(2,1)S(1)} %get-tuple-element.67), channel_id=1, source_target_pairs={{0,4},{8,12},{4,0},{12,8},{1,5},{9,13},{5,1},{13,9},{2,6},{10,14},... | collective-permute-start | bytes 258056 | tf_op jit(solution)/shard_map/ppermute | solution.py:58
  29.6 3.2 %collective-permute-start.14 = (bf16[336,128]{1,0:T(8,128)(2,1)S(1)}, bf16[336,128]{1,0:T(8,128)(2,1)S(1)}, u32[]{:S(2)}, u32[]{:S(2)}) collective-permute-start(bf16[336,128]{1,0:T(8,128)(2,1)S(1)} %get-tuple-element.68), channel_id=1, source_target_pairs={{4,8},{8,4},{5,9},{9,5},{6,10},{10,6},{7,11},{11,7},{20,24},{24,20... | collective-permute-start | bytes 258056 | tf_op jit(solution)/shard_map/ppermute | solution.py:58
  31.7 4.2 %collective-permute-start.7 = (bf16[128,512]{1,0:T(8,128)(2,1)S(1)}, bf16[128,512]{1,0:T(8,128)(2,1)S(1)}, u32[]{:S(2)}, u32[]{:S(2)}) collective-permute-start(bf16[128,512]{1,0:T(8,128)(2,1)S(1)} %get-tuple-element.59.after_ref), channel_id=1, source_target_pairs={{0,1},{1,0},{2,3},{3,2},{4,5},{5,4},{6,7},{7,6},{8,9},{9,8},{10,11... | collective-permute-start | bytes 393224 | tf_op jit(solution)/shard_map/ppermute | solution.py:417
  33.7 3.8 %collective-permute-start.15 = (bf16[128,512]{1,0:T(8,128)(2,1)S(1)}, bf16[128,512]{1,0:T(8,128)(2,1)S(1)}, u32[]{:S(2)}, u32[]{:S(2)}) collective-permute-start(bf16[128,512]{1,0:T(8,128)(2,1)S(1)} %get-tuple-element.70), channel_id=1, source_target_pairs={{0,1},{1,0},{2,3},{3,2},{4,5},{5,4},{6,7},{7,6},{8,9},{9,8},{10,11... | collective-permute-start | bytes 393224 | tf_op jit(solution)/shard_map/ppermute | solution.py:417
  34.7 8.3 %collective-permute-start.17 = (bf16[336,256]{1,0:T(8,128)(2,1)S(1)}, bf16[336,256]{1,0:T(8,128)(2,1)S(1)}, u32[]{:S(2)}, u32[]{:S(2)}) collective-permute-start(bf16[336,256]{1,0:T(8,128)(2,1)S(1)} %shard_map.209), channel_id=1, source_target_pairs={{0,12},{4,8},{8,4},{12,0},{1,13},{5,9},{9,5},{13,1},{2,14},{6,10},... | collective-permute-start | bytes 516104 | tf_op jit(solution)/shard_map/ppermute | solution.py:63
  36.0 6.5 %collective-permute-start.8 = (bf16[128,512]{1,0:T(8,128)(2,1)S(1)}, bf16[128,512]{1,0:T(8,128)(2,1)S(1)}, u32[]{:S(2)}, u32[]{:S(2)}) collective-permute-start(bf16[128,512]{1,0:T(8,128)(2,1)S(1)} %get-tuple-element.90), channel_id=1, source_target_pairs={{0,2},{2,0},{1,3},{3,1},{4,6},{6,4},{5,7},{7,5},{8,10},{10,8},{9,1... | collective-permute-start | bytes 393224 | tf_op jit(solution)/shard_map/ppermute | solution.py:63
  37.5 6.4 %collective-permute-start.16 = (bf16[128,512]{1,0:T(8,128)(2,1)S(1)}, bf16[128,512]{1,0:T(8,128)(2,1)S(1)}, u32[]{:S(2)}, u32[]{:S(2)}) collective-permute-start(bf16[128,512]{1,0:T(8,128)(2,1)S(1)} %get-tuple-element.86), channel_id=1, source_target_pairs={{0,2},{2,0},{1,3},{3,1},{4,6},{6,4},{5,7},{7,5},{8,10},{10,8},{9,1... | collective-permute-start | bytes 393224 | tf_op jit(solution)/shard_map/ppermute | solution.py:63
  42.5 4.5 %collective-permute-start.9 = (bf16[128,512]{1,0:T(8,128)(2,1)S(1)}, bf16[128,512]{1,0:T(8,128)(2,1)S(1)}, u32[]{:S(2)}, u32[]{:S(2)}) collective-permute-start(bf16[128,512]{1,0:T(8,128)(2,1)S(1)} %shard_map.202.mine_ref.grid_ref), channel_id=1, source_target_pairs={{0,1},{1,0},{2,3},{3,2},{4,5},{5,4},{6,7},{7,6},{8,9},{9,8},{10,11... | collective-permute-start | bytes 393224 | tf_op jit(solution)/shard_map/ppermute | solution.py:417
  44.3 3.0 %collective-permute-start.19 = (bf16[128,512]{1,0:T(8,128)(2,1)S(1)}, bf16[128,512]{1,0:T(8,128)(2,1)S(1)}, u32[]{:S(2)}, u32[]{:S(2)}) collective-permute-start(bf16[128,512]{1,0:T(8,128)(2,1)S(1)} %get-tuple-element.75.mine_ref), channel_id=1, source_target_pairs={{0,1},{1,0},{2,3},{3,2},{4,5},{5,4},{6,7},{7,6},{8,9},{9,8},{10,11... | collective-permute-start | bytes 393224 | tf_op jit(solution)/shard_map/ppermute | solution.py:417
  44.3 6.4 %collective-permute-start.18 = (bf16[128,256]{1,0:T(8,128)(2,1)S(1)}, bf16[128,256]{1,0:T(8,128)(2,1)S(1)}, u32[]{:S(2)}, u32[]{:S(2)}) collective-permute-start(bf16[128,256]{1,0:T(8,128)(2,1)S(1)} %get-tuple-element.74), channel_id=1, source_target_pairs={{0,12},{4,8},{8,4},{12,0},{1,13},{5,9},{9,5},{13,1},{2,14},{6,10},... | collective-permute-start | bytes 196616 | tf_op jit(solution)/shard_map/ppermute | solution.py:63
  48.1 11.3 %collective-permute-start.21 = (bf16[336,256]{1,0:T(8,128)(2,1)S(1)}, bf16[336,256]{1,0:T(8,128)(2,1)S(1)}, u32[]{:S(2)}, u32[]{:S(2)}) collective-permute-start(bf16[336,256]{1,0:T(8,128)(2,1)S(1)} %get-tuple-element.81), channel_id=1, source_target_pairs={{0,8},{4,12},{8,0},{12,4},{1,9},{5,13},{9,1},{13,5},{2,10},{6,14},... | collective-permute-start | bytes 516104 | tf_op jit(solution)/shard_map/ppermute | solution.py:63
  50.1 9.3 %collective-permute-start.22 = (bf16[336,256]{1,0:T(8,128)(2,1)S(1)}, bf16[336,256]{1,0:T(8,128)(2,1)S(1)}, u32[]{:S(2)}, u32[]{:S(2)}) collective-permute-start(bf16[336,256]{1,0:T(8,128)(2,1)S(1)} %get-tuple-element.82), channel_id=1, source_target_pairs={{0,4},{4,0},{8,12},{12,8},{1,5},{5,1},{9,13},{13,9},{2,6},{6,2},{1... | collective-permute-start | bytes 516104 | tf_op jit(solution)/shard_map/ppermute | solution.py:63
  50.7 1.3 %collective-permute-start.20 = (bf16[128,256]{1,0:T(8,128)(2,1)S(1)}, bf16[128,256]{1,0:T(8,128)(2,1)S(1)}, u32[]{:S(2)}, u32[]{:S(2)}) collective-permute-start(bf16[128,256]{1,0:T(8,128)(2,1)S(1)} %collective-permute-done.18.mine_ref), channel_id=1, source_target_pairs={{0,1},{1,0},{2,3},{3,2},{4,5},{5,4},{6,7},{7,6},{8,9},{9,8},{10,11... | collective-permute-start | bytes 196616 | tf_op jit(solution)/shard_map/ppermute | solution.py:417
